TPU v7x, 32 devices: a whole 2x2x4 slice. The times are simulated.
32 devices in a mesh: rows: 8 (over z, y), cols: 4 (over x, core).
Axes of the slice: x: 2, y: 2, z: 4, core: 2. Of those that a mesh axis runs over, the one named last changes fastest.
Arguments:
- embeddings: bfloat16 [8192, 1024], P('rows'), may hold values from -6 to 6
- knn_mean: bfloat16 [8192], P('rows'), may hold values from 0.29882812 to 0.8984375
- pair_rows: int32 [8, 4, 24], P('rows', 'cols'), may hold values from 0 to 31, as said below
- pair_cols: int32 [8, 4, 24], P('rows', 'cols'), may hold values from 0 to 31, as said below
- pair_count: int32 [8, 4], P('rows', 'cols'), may hold values from 2 to 24, as said below
- start_block: float32 [64, 8192], P(None, 'rows')
Outputs:
- block_vector: float32 [64, 8192], P(None, 'rows')
Inputs may be any that keep to these rules, and one draw needn't show every extreme that they name: `pair_count`: on every index of rows one device of cols has exactly 24 live slots. `pair_rows`: A live entry of device (i, j) is one of the row blocks i * 4 to (i + 1) * 4 - 1; the live pairs of one index of rows are all different, and each of its row blocks is paired with itself. Slots at pair_count and beyond are unused and repeat the device's first pair. `pair_cols`: the column block of a live pair of device (i, j) is a row block of rows index i - 1, i or i + 1.
All inputs are finite; a program needn't handle non-finite values.
Results may differ from a plain program's by a relative error of at most 0.0065.
Values may be sent and summed in bfloat16 or wider, within the bound.
No kernel may reach another device: no remote copies, remote signals or barrier semaphores. Data moves between devices by JAX's collectives and lax.ppermute only.
A program may use at most 64 MiB of HBM per device.

v0:
```python
import math

import jax
import jax.numpy as jnp
from jax import lax
from jax.sharding import PartitionSpec as P

K = 64
BLOCK = 256
ITERS = 2


sharpness = 10.0
epsilon = 1e-06


def extended(cells, sides, width):
    for axis, dim in sides:
        count = lax.axis_size(axis)
        ends = count - 1
        head = lax.slice_in_dim(cells, 0, width, axis=dim)
        tail = lax.slice_in_dim(cells, cells.shape[dim] - width, cells.shape[dim], axis=dim)
        cells = jnp.concatenate(
            [
                lax.ppermute(tail, axis, [(i, (i + 1) % count) for i in range(ends)]),
                cells,
                lax.ppermute(head, axis, [((i + 1) % count, i) for i in range(ends)]),
            ],
            axis=dim,
        )
    return cells


def unit_rows(embeddings):
    values = embeddings.astype(jnp.float32)
    scale = lax.rsqrt(jnp.mean(values * values, axis=1, keepdims=True) + epsilon)
    return (values * scale / math.sqrt(values.shape[1])).astype(jnp.bfloat16)


def make_affinity(row_unit, col_unit, row_mean, col_mean, row_block, col_block):
    size = row_unit.shape[0]
    scores = lax.dot_general(
        row_unit, col_unit, (((1,), (1,)), ((), ())), preferred_element_type=jnp.float32
    )
    denom = 0.5 * (row_mean.astype(jnp.float32)[:, None] + col_mean.astype(jnp.float32)[None, :])
    weights = jnp.exp(sharpness * scores / denom)
    offsets = jnp.arange(size, dtype=jnp.int32)
    same = (row_block * size + offsets)[:, None] == (col_block * size + offsets)[None, :]
    return jnp.where(same, jnp.zeros_like(weights), weights).astype(jnp.bfloat16)


def add_block(accum, piece, block_index):
    size = piece.shape[1]
    current = lax.dynamic_slice_in_dim(accum, block_index * size, size, 1)
    return lax.dynamic_update_slice_in_dim(accum, current + piece, block_index * size, 1)


def local(embeddings, knn_mean, pair_rows, pair_cols, pair_count, start_block):
    rows_here = embeddings.shape[0]
    blocks_here = rows_here // BLOCK
    slots = pair_rows.shape[2]
    group_index = lax.axis_index("rows")
    lanes = lax.axis_size("cols")
    lane_index = lax.axis_index("cols")
    total_rows = rows_here * lax.axis_size("rows")
    unit = unit_rows(embeddings)
    window_unit, window_mean = (
        extended(unit, (("rows", 0),), rows_here),
        extended(knn_mean, (("rows", 0),), rows_here),
    )
    all_rows, all_cols, all_counts = (
        lax.all_gather(pair_rows, "cols", axis=1, tiled=True),
        lax.all_gather(pair_cols, "cols", axis=1, tiled=True),
        lax.all_gather(pair_count, "cols", axis=1, tiled=True),
    )
    flat_rows = all_rows.reshape(-1)
    flat_cols = all_cols.reshape(-1)
    live = (jnp.arange(slots, dtype=jnp.int32)[None, :] < all_counts.reshape(-1)[:, None]).reshape(
        -1
    )
    live_rank = jnp.cumsum(live.astype(jnp.int32)) - 1
    wanted = lane_index + lanes * jnp.arange(slots, dtype=jnp.int32)
    picked = (live_rank[None, :] == wanted[:, None]) & live[None, :]
    my_rows = jnp.sum(jnp.where(picked, flat_rows[None, :], 0), axis=1)
    my_cols = jnp.sum(jnp.where(picked, flat_cols[None, :], 0), axis=1)
    live_total = jnp.sum(all_counts)
    live_count = jnp.maximum((live_total - lane_index + lanes - 1) // lanes, 0)
    local_rows = my_rows - group_index * blocks_here
    window_cols = my_cols - (group_index - 1) * blocks_here
    cache = jnp.zeros((slots, BLOCK, BLOCK), jnp.bfloat16)
    degree_part = jnp.zeros((1, rows_here), jnp.float32)
    vector = start_block
    for sweep in range(ITERS):
        narrow = extended(vector.astype(jnp.bfloat16), (("rows", 1),), rows_here)

        def accumulate(slot, state):
            vector_acc, degree_acc, stored = state
            row_block = local_rows[slot]
            col_block = window_cols[slot]
            if sweep == 0:
                row_unit = lax.dynamic_slice_in_dim(
                    window_unit, (blocks_here + row_block) * BLOCK, BLOCK, 0
                )
                col_unit = lax.dynamic_slice_in_dim(window_unit, col_block * BLOCK, BLOCK, 0)
                row_mean = lax.dynamic_slice_in_dim(
                    window_mean, (blocks_here + row_block) * BLOCK, BLOCK, 0
                )
                col_mean = lax.dynamic_slice_in_dim(window_mean, col_block * BLOCK, BLOCK, 0)
                affinity = make_affinity(
                    row_unit, col_unit, row_mean, col_mean, my_rows[slot], my_cols[slot]
                )
                stored = lax.dynamic_update_index_in_dim(stored, affinity, slot, 0)
                degree_acc = add_block(
                    degree_acc, jnp.sum(affinity.astype(jnp.float32), axis=1)[None, :], row_block
                )
            else:
                affinity = lax.dynamic_index_in_dim(stored, slot, 0, keepdims=False)
            source = lax.dynamic_slice_in_dim(narrow, col_block * BLOCK, BLOCK, 1)
            product = lax.dot_general(
                source, affinity, (((1,), (1,)), ((), ())), preferred_element_type=jnp.float32
            )
            vector_acc = add_block(vector_acc, product, row_block)
            return (vector_acc, degree_acc, stored)

        start_state = (jnp.zeros((K, rows_here), jnp.float32), degree_part, cache)
        partial_value, degree_part, cache = lax.fori_loop(0, live_count, accumulate, start_state)
        summed, degree = lax.psum((partial_value, degree_part), "cols")
        smoothed = summed / degree
        gram = (
            jnp.dot(
                smoothed,
                smoothed.T,
                precision=lax.Precision.HIGHEST,
                preferred_element_type=jnp.float32,
            )
            / total_rows
        )
        gram = lax.psum(gram, "rows")
        lower = jnp.linalg.cholesky(gram)
        vector = jax.scipy.linalg.solve_triangular(lower, smoothed, lower=True)
    return vector


def solution(mesh):
    in_specs = (
        P("rows", None),
        P("rows"),
        P("rows", "cols", None),
        P("rows", "cols", None),
        P("rows", "cols"),
        P(None, "rows"),
    )
    out_specs = P(None, "rows")
    return jax.shard_map(local, mesh=mesh, in_specs=in_specs, out_specs=out_specs, check_vma=False)
```

profile of v0, /device:TPU:0, one launch (start us, length us, event | category | flops | bytes accessed | tf_op | source)
XLA Modules:
  0.0 493.9 jit_solution(14880050352540177274)
XLA Ops:
  6.6 2.1 fusion.16
  8.7 2.1 fusion.18
  10.9 6.3 %collective-permute-start.2 = (bf16[1024,1024]{1,0:T(8,128)(2,1)S(1)}, bf16[1024,1024]{1,0:T(8,128)(2,1)}, u32[]{:S(2)}, u32[]{:S(2)}) collective-permute-start(bf16[1024,1024]{1,0:T(8,128)(2,1)S(1)} %fusion.18), channel_id=1, source_target_pairs={{0,4},{4,8},{8,12},{12,16},{16,20},{20,24},{24,28},{1,5},{5,9},{9,... | collective-permute-start | bytes 6291464 | tf_op jit(solution)/shard_map/ppermute | solution.py:25
  18.4 4.6 collective-permute-start
  23.0 1.3 collective-permute-start.1
  26.3 4.5 collective-permute-start.4
  30.8 4.9 all-reduce
  36.1 5.0 %all_gather.10 = s32[1,4,24]{2,0,1:T(1,128)S(1)} all-gather(s32[1,1,24]{2,0,1:T(1,128)S(1)} %bitcast.65), channel_id=1, replica_groups=mesh['rows'=8,'cols'=4] {'cols'}, dimensions={1}, use_global_device_ids=true | all-gather | bytes 480 | tf_op jit(solution)/shard_map/all_gather | solution.py:72
  42.4 5.0 %all_gather.11 = s32[1,4,24]{2,0,1:T(1,128)S(1)} all-gather(s32[1,1,24]{2,0,1:T(1,128)S(1)} %bitcast.66), channel_id=1, replica_groups=mesh['rows'=8,'cols'=4] {'cols'}, dimensions={1}, use_global_device_ids=true | all-gather | bytes 480 | tf_op jit(solution)/shard_map/all_gather | solution.py:73
  49.1 62.1 %collective-permute-done.4 = bf16[1024]{0:T(1024)(128)(2,1)S(1)} collective-permute-done((bf16[1024]{0:T(1024)(128)(2,1)S(1)}, bf16[1024]{0:T(1024)(128)(2,1)S(1)}, u32[]{:S(2)}, u32[]{:S(2)}) %collective-permute-start.4) | collective-permute-done | bytes 2080 | tf_op jit(solution)/shard_map/ppermute | solution.py:25
  115.1 2.1 collective-permute-done.5
  118.0 5.4 %pad_maximum_fusion = bf16[3072,1024]{1,0:T(8,128)(2,1)} fusion(bf16[1024,1024]{1,0:T(8,128)(2,1)} %collective-permute-done.3, bf16[1024,1024]{1,0:T(8,128)(2,1)S(1)} %fusion.18, bf16[1024,1024]{1,0:T(8,128)(2,1)} %collective-permute-done.2), kind=kLoop, calls=%fused_computation.27 | loop fusion | flops 18874368 | bytes 12582912 | tf_op jit(solution)/shard_map/concatenate | solution.py:23
  123.8 86.3 %while.24 = (s32[]{:T(128)}, f32[64,1024]{1,0:T(8,128)S(1)}, f32[1,1024]{1,0:T(1,128)S(1)}, bf16[24,256,256]{1,2,0:T(8,128)(2,1)S(1)}, s32[]{:T(128)}, /*index=5...) while((s32[]{:T(128)}, f32[64,1024]{1,0:T(8,128)S(1)}, ...), condition=%wide.region_7.8_spmd, body=%wide.region_5.7_spmd.sunk | while | flops 143213584 | bytes 1750485 | solution.py:126
  127.6 1.3 dynamic_slice.97
  131.4 1.6 convert_reduce_fusion.2
  142.2 1.6 convert_reduce_fusion.2
  149.2 1.3 dynamic_slice.97
  153.0 1.6 convert_reduce_fusion.2
  163.8 1.6 convert_reduce_fusion.2
  174.6 1.6 convert_reduce_fusion.2
  185.4 1.6 convert_reduce_fusion.2
  196.2 1.6 convert_reduce_fusion.2
  206.9 1.6 convert_reduce_fusion.2
  210.8 5.8 %psum.39 = f32[1024]{0:T(1024)S(1)} all-reduce(f32[1024]{0:T(1024)S(1)} %bitcast.63), channel_id=1, replica_groups=mesh['rows'=8,'cols'=4] {'cols'}, use_global_device_ids=true, to_apply=%region_9.10 | all-reduce | flops 1024 | bytes 8192 | tf_op jit(solution)/shard_map/psum | solution.py:127
  216.6 69.7 %all-reduce.4.cloned.1.call-done = f32[64,1024]{1,0:T(8,128)} async-done(((f32[64,1024]{1,0:T(8,128)}), f32[64,1024]{1,0:T(8,128)}) %all-reduce.4.cloned.1.call-update) | async-done | bytes 262160 | tf_op jit(solution)/shard_map/psum | solution.py:127
  286.3 1.4 convolution_multiply_fusion.2
  287.7 37.1 %psum.40 = f32[64,64]{0,1:T(8,128)S(1)} all-reduce(f32[64,64]{0,1:T(8,128)S(1)} %convolution_multiply_fusion.2), channel_id=1, replica_groups=mesh['rows'=8,'cols'=4] {'rows'}, use_global_device_ids=true, to_apply=%region_10.11 | all-reduce | flops 4096 | bytes 32768 | tf_op jit(solution)/shard_map/psum | solution.py:138
  324.9 5.8 %cholesky.44 = f32[64,64]{1,0:T(8,128)S(1)} custom-call(f32[64,64]{1,0:T(8,128)S(1)} %fusion.25), custom_call_target="Cholesky" | custom-call | tf_op jit(solution)/shard_map/jit(cholesky)/cholesky | solution.py:139
  332.1 4.9 custom-call.6
  337.0 1.4 convolution_convert_fusion
  338.4 1.3 collective-permute-start.6
  339.7 1.3 collective-permute-start.7
  342.2 4.4 collective-permute-done.7
  347.4 38.3 %while.25 = (s32[]{:T(128)}, f32[64,1024]{1,0:T(8,128)S(1)}, s32[]{:T(128)}, s32[24]{0:T(128)}, s32[24]{0:T(128)}, /*index=5*/bf16[64,3072]{1,0:T(8,128)(2,1)}, ...) while((s32[]{:T(128)}, f32[64,1024]{1,0:T(8,128)S(1)}, ...), condition=%wide.region_14.17_spmd, body=%wide.region_13.16_spmd.sunk | while | flops 8405005 | bytes 295199 | solution.py:126
  349.3 1.3 dynamic_slice.102
  354.1 1.3 dynamic_slice.102
  358.8 1.3 dynamic_slice.102
  363.6 1.3 dynamic_slice.102
  368.4 1.3 dynamic_slice.102
  373.2 1.3 dynamic_slice.102
  378.0 1.3 dynamic_slice.102
  382.8 1.3 dynamic_slice.102
  386.4 47.9 %all-reduce.6.cloned.1.call-done = f32[64,1024]{1,0:T(8,128)} async-done(((f32[64,1024]{1,0:T(8,128)}), f32[64,1024]{1,0:T(8,128)}) %all-reduce.6.cloned.1.call-update) | async-done | bytes 262160 | tf_op jit(solution)/shard_map/psum | solution.py:127
  434.3 1.4 convolution_multiply_fusion.1
  435.7 37.1 %psum.42 = f32[64,64]{0,1:T(8,128)S(1)} all-reduce(f32[64,64]{0,1:T(8,128)S(1)} %convolution_multiply_fusion.1), channel_id=1, replica_groups=mesh['rows'=8,'cols'=4] {'rows'}, use_global_device_ids=true, to_apply=%region_16.19 | all-reduce | flops 4096 | bytes 32768 | tf_op jit(solution)/shard_map/psum | solution.py:138
  472.9 5.8 %cholesky.55 = f32[64,64]{1,0:T(8,128)S(1)} custom-call(f32[64,64]{1,0:T(8,128)S(1)} %fusion.23), custom_call_target="Cholesky" | custom-call | tf_op jit(solution)/shard_map/jit(cholesky)/cholesky | solution.py:139
  480.1 4.9 custom-call.7
  485.0 2.1 fusion.19
  (147 shorter events, 80.0 us)
Async XLA Ops:
  6.5 18.4 %copy-start.6 = (u32[32]{0:T(128)S(1)}, u32[32]{0:T(128)}, u32[]{:S(2)}) copy-start(u32[32]{0:T(128)} %constant.140) | copy-start | bytes 388
  6.5 11.9 %copy-start.2 = (f32[64,1024]{1,0:T(8,128)S(1)}, f32[64,1024]{1,0:T(8,128)}, u32[]{:S(2)}) copy-start(f32[64,1024]{1,0:T(8,128)} %param.18) | copy-start | bytes 786436
  6.5 19.7 %copy-start.3 = (bf16[1024]{0:T(1024)(128)(2,1)S(1)}, bf16[1024]{0:T(1024)(128)(2,1)}, u32[]{:S(2)}) copy-start(bf16[1024]{0:T(1024)(128)(2,1)} %param.14) | copy-start | bytes 6148
  6.5 29.6 %copy-start.4 = (s32[1,1,24]{2,1,0:T(1,128)S(1)}, s32[1,1,24]{2,1,0:T(1,128)}, u32[]{:S(2)}) copy-start(s32[1,1,24]{2,1,0:T(1,128)} %param.15) | copy-start | bytes 292
  6.5 35.9 %copy-start.5 = (s32[1,1,24]{2,1,0:T(1,128)S(1)}, s32[1,1,24]{2,1,0:T(1,128)}, u32[]{:S(2)}) copy-start(s32[1,1,24]{2,1,0:T(1,128)} %param.16) | copy-start | bytes 292
  6.5 279.8 %all-reduce.4.cloned.1.call-start = ((), (), s32[]{:S(2)}) async-start(), calls=%async_computation | async-start | bytes 524288 | tf_op jit(solution)/shard_map/psum | solution.py:127
  10.9 107.1 %collective-permute-start.2 = (bf16[1024,1024]{1,0:T(8,128)(2,1)S(1)}, bf16[1024,1024]{1,0:T(8,128)(2,1)}, u32[]{:S(2)}, u32[]{:S(2)}) collective-permute-start(bf16[1024,1024]{1,0:T(8,128)(2,1)S(1)} %fusion.18), channel_id=1, source_target_pairs={{0,4},{4,8},{8,12},{12,16},{16,20},{20,24},{24,28},{1,5},{5,9},{9,... | collective-permute-start | bytes 6291464 | tf_op jit(solution)/shard_map/ppermute | solution.py:25
  17.1 100.8 %collective-permute-start.3 = (bf16[1024,1024]{1,0:T(8,128)(2,1)S(1)}, bf16[1024,1024]{1,0:T(8,128)(2,1)}, u32[]{:S(2)}, u32[]{:S(2)}) collective-permute-start(bf16[1024,1024]{1,0:T(8,128)(2,1)S(1)} %fusion.18), channel_id=1, source_target_pairs={{4,0},{8,4},{12,8},{16,12},{20,16},{24,20},{28,24},{5,1},{9,5},{13... | collective-permute-start | bytes 6291464 | tf_op jit(solution)/shard_map/ppermute | solution.py:27
  18.4 98.7 %collective-permute-start = (bf16[64,1024]{1,0:T(8,128)(2,1)S(1)}, bf16[64,1024]{1,0:T(8,128)(2,1)S(1)}, u32[]{:S(2)}, u32[]{:S(2)}) collective-permute-start(bf16[64,1024]{1,0:T(8,128)(2,1)S(1)} %convert_element_type.41), channel_id=1, source_target_pairs={{0,4},{4,8},{8,12},{12,16},{16,20},{20,24},{24,28},{1,5},{5,9},{9,... | collective-permute-start | bytes 393224 | tf_op jit(solution)/shard_map/ppermute | solution.py:25
  23.0 94.1 %collective-permute-start.1 = (bf16[64,1024]{1,0:T(8,128)(2,1)S(1)}, bf16[64,1024]{1,0:T(8,128)(2,1)S(1)}, u32[]{:S(2)}, u32[]{:S(2)}) collective-permute-start(bf16[64,1024]{1,0:T(8,128)(2,1)S(1)} %convert_element_type.41), channel_id=1, source_target_pairs={{4,0},{8,4},{12,8},{16,12},{20,16},{24,20},{28,24},{5,1},{9,5},{13... | collective-permute-start | bytes 393224 | tf_op jit(solution)/shard_map/ppermute | solution.py:27
  26.3 85.0 %collective-permute-start.4 = (bf16[1024]{0:T(1024)(128)(2,1)S(1)}, bf16[1024]{0:T(1024)(128)(2,1)S(1)}, u32[]{:S(2)}, u32[]{:S(2)}) collective-permute-start(bf16[1024]{0:T(1024)(128)(2,1)S(1)} %copy-done.3), channel_id=1, source_target_pairs={{0,4},{4,8},{8,12},{12,16},{16,20},{20,24},{24,28},{1,5},{5,9},{9,... | collective-permute-start | bytes 6152 | tf_op jit(solution)/shard_map/ppermute | solution.py:25
  111.2 5.9 %collective-permute-start.5 = (bf16[1024]{0:T(1024)(128)(2,1)S(1)}, bf16[1024]{0:T(1024)(128)(2,1)S(1)}, u32[]{:S(2)}, u32[]{:S(2)}) collective-permute-start(bf16[1024]{0:T(1024)(128)(2,1)S(1)} %copy-done.3), channel_id=1, source_target_pairs={{4,0},{8,4},{12,8},{16,12},{20,16},{24,20},{28,24},{5,1},{9,5},{13... | collective-permute-start | bytes 6152 | tf_op jit(solution)/shard_map/ppermute | solution.py:27
  210.1 0.7 copy-start
  210.8 223.5 %all-reduce.6.cloned.1.call-start = ((), (), s32[]{:S(2)}) async-start(), calls=%async_computation.1 | async-start | bytes 524288 | tf_op jit(solution)/shard_map/psum | solution.py:127
  338.4 3.8 collective-permute-start.6
  339.7 6.9 %collective-permute-start.7 = (bf16[64,1024]{1,0:T(8,128)(2,1)S(1)}, bf16[64,1024]{1,0:T(8,128)(2,1)S(1)}, u32[]{:S(2)}, u32[]{:S(2)}) collective-permute-start(bf16[64,1024]{1,0:T(8,128)(2,1)S(1)} %convolution_convert_fusion), channel_id=1, source_target_pairs={{4,0},{8,4},{12,8},{16,12},{20,16},{24,20},{28,24},{5,1},{9,5},{13... | collective-permute-start | bytes 393224 | tf_op jit(solution)/shard_map/ppermute | solution.py:27
  385.6 0.7 copy-start.1
Sparse Core Ops, SparseCore 0:
  210.9 75.3 all-reduce.3
  386.5 47.7 all-reduce.5
where the time goes:
time: 499 us; the launch traced here: 494 us
  waiting for transfers between devices  187 us (37%)
  blocking collectives  95 us (19%)
  local copies, waits for them, and re-layouts  65.4 us (13%)
  other arithmetic  40.6 us (8%)
  loops' own time  35.2 us (7%)
  matrix products  33.4 us (7%)
  starting transfers between devices  21.9 us (4%)
  between operations  15 us (3%)
    psum x2, waiting for transfers between devices, local(): summed, degree = lax.psum((partial_value, degree_part), 'cols')  118 us
    psum x2, blocking collectives, local(): gram = lax.psum(gram, 'rows')  74.2 us
    ppermute x4, waiting for transfers between devices, extended(): lax.ppermute(tail, axis, [(i, (i + 1) % count) for i in range(ends)])  63.3 us
    another operation x2, loops' own time, local(): lax.fori_loop(0, live_count, accumulate, start_state)  35.2 us
    dynamic_slice x16, local copies, waits for them, and re-layouts, accumulate(): row_block = local_rows[slot]  20.8 us
    dynamic_slice x16, local copies, waits for them, and re-layouts, accumulate(): col_block = window_cols[slot]  20.1 us
    ppermute x4, starting transfers between devices, extended(): lax.ppermute(tail, axis, [(i, (i + 1) % count) for i in range(ends)])  16.7 us
    dot_general x16, matrix products, accumulate(): lax.dot_general(source, affinity, (((1,), (1,)), ((), ())), preferred_ele...  14.5 us
  transfers between devices with their start and end apart: 10, of which 6 were waited for; matrix products, arithmetic and copies ran while one was open for 1% of the time, Pallas kernels for 0%

commit v1 on v0

v1 whole, which is shorter than its diff:
```python
import functools
import math

import jax
import jax.numpy as jnp
from jax import lax
from jax.experimental import pallas as pl
from jax.experimental.pallas import tpu as pltpu
from jax.sharding import PartitionSpec as P

BLOCK = 256
ONES = 16

sharpness = 10.0
epsilon = 1e-06

HIGHEST = lax.Precision.HIGHEST
f32 = jnp.float32
bf16 = jnp.bfloat16


def shift(cells, step):
    count = lax.axis_size("rows")
    return lax.ppermute(cells, "rows", [(i, (i + step) % count) for i in range(count)])


def swap(cells, axis, offset):
    count = lax.axis_size(axis)
    return lax.ppermute(cells, axis, [(i, i ^ offset) for i in range(count)])


def lane_swaps(cells):
    return [cells] + [swap(cells, "cols", d) for d in range(1, lax.axis_size("cols"))]


def row_stages(count):
    bits = count.bit_length() - 1
    stages = []
    low = 0
    while low < bits:
        wide = 1 if (bits - low) % 2 else 2
        stages.append([m << low for m in range(1, 1 << wide)])
        low += wide
    return stages


def nt(left, right):
    return lax.dot_general(left, right, (((1,), (1,)), ((), ())), preferred_element_type=f32)


def unit_rows(cells):
    values = cells.astype(f32)
    scale = lax.rsqrt(jnp.mean(values * values, axis=1, keepdims=True) + epsilon)
    return (values * (scale * (1.0 / math.sqrt(cells.shape[1])))).astype(bf16)


def diagonal(size):
    return lax.broadcasted_iota(jnp.int32, (size, size), 0) == lax.broadcasted_iota(
        jnp.int32, (size, size), 1
    )


def upright(row, eye):
    return jnp.sum(jnp.where(eye, row, 0.0), axis=1, keepdims=True)


def affinity(col_unit, row_unit, col_mean, row_mean):
    scores = nt(col_unit, row_unit)
    return jnp.exp((2.0 * sharpness) * scores / (col_mean + row_mean))


def with_ones(narrow):
    return jnp.concatenate([narrow, jnp.ones((ONES, narrow.shape[1]), bf16)], axis=0)


def pieces(values):
    first = values.astype(bf16)
    rest = values - first.astype(f32)
    second = rest.astype(bf16)
    third = (rest - second.astype(f32)).astype(bf16)
    return jnp.concatenate([first, second, third], axis=0)


def joined(product, size):
    return product[:size] + (product[size : 2 * size] + product[2 * size :])


def inverse_factor(gram):
    size = gram.shape[0]
    eye = jnp.where(diagonal(size), 1.0, 0.0).astype(f32)
    table = jnp.concatenate([gram, eye], axis=1)
    tile = 8
    parts = [table[g * tile : (g + 1) * tile] for g in range(size // tile)]
    inner = lax.broadcasted_iota(jnp.int32, (tile, 1), 0)
    scales = []
    for k in range(size):
        home, at = k // tile, k % tile
        row = parts[home][at : at + 1]
        pivot = row[:, k : k + 1]
        scales.append(lax.rsqrt(pivot))
        row_scaled = row / pivot
        for g in range(home, size // tile):
            column = parts[g][:, k : k + 1]
            if g == home:
                column = jnp.where(inner > at, column, 0.0)
            parts[g] = parts[g] - column * row_scaled
    out = []
    for g in range(size // tile):
        scale = jnp.concatenate(scales[g * tile : (g + 1) * tile], axis=0)
        out.append(parts[g][:, size:] * scale)
    return jnp.concatenate(out, axis=0)


def times(left, right):
    return jnp.dot(left, right, precision=HIGHEST, preferred_element_type=f32)


def gram_of(blocks, total):
    acc = None
    for block in blocks:
        term = lax.dot_general(
            block, block, (((1,), (1,)), ((), ())), precision=HIGHEST, preferred_element_type=f32
        )
        acc = term if acc is None else acc + term
    return acc * (1.0 / total)


def block_of(lane, d):
    return pl.ds(pl.multiple_of((lane ^ d) * BLOCK, BLOCK), BLOCK)


def own_kernel(lanes, cells_ref, mean_ref, start_ref, unit_ref, weight_ref, product_ref):
    lane = lax.axis_index("cols")
    for d in range(lanes):
        unit_ref[d] = unit_rows(cells_ref[block_of(lane, d), :])
    eye = diagonal(BLOCK)
    own = unit_ref[0]
    col_mean = upright(mean_ref[:, block_of(lane, 0)], eye)
    left = with_ones(start_ref[:, block_of(lane, 0)].astype(bf16))
    rows = product_ref.shape[1]
    for d in range(lanes):
        weights = affinity(own, unit_ref[d], col_mean, mean_ref[:, block_of(lane, d)])
        if d == 0:
            weights = jnp.where(eye, 0.0, weights)
        weights = weights.astype(bf16)
        weight_ref[d] = weights
        product_ref[d] = jnp.dot(left, weights, preferred_element_type=f32)[:rows]


def next_kernel(
    lanes,
    columns,
    unit_ref,
    cells_ref,
    side_ref,
    mean_ref,
    start_ref,
    own_ref,
    *rest,
):
    lists, (weight_ref, mask_ref, *product_refs, back_ref) = rest[:lanes], rest[lanes:]
    lane = lax.axis_index("cols")
    group = lax.axis_index("rows")
    blocks = lax.axis_size("rows") * lanes
    size = columns
    listed = jnp.concatenate([ref[...] for ref in lists], axis=0)
    here = [listed[4 * p : 4 * p + 1] * blocks + listed[4 * p + 1 : 4 * p + 2] for p in range(lanes)]
    after = [
        listed[4 * p + 2 : 4 * p + 3] * blocks + listed[4 * p + 3 : 4 * p + 4] for p in range(lanes)
    ]
    here = jnp.concatenate(here, axis=0)
    after = jnp.concatenate(after, axis=0)

    def live(codes, row_block, col_block):
        hit = jnp.where(codes == row_block * blocks + col_block, 1.0, 0.0)
        return jnp.max(jnp.max(hit, axis=1, keepdims=True), axis=0, keepdims=True)

    eye = diagonal(BLOCK)
    col_unit = unit_rows(cells_ref[...])
    col_mean = upright(side_ref[size : size + 1, :].astype(f32), eye)
    left = with_ones(side_ref[:size, :])
    rows = own_ref.shape[1]
    back = jnp.zeros((rows, BLOCK), f32)
    for d in range(lanes):
        row_block = group * lanes + (lane ^ d)
        own_live = live(here, row_block, group * lanes + lane)
        next_live = live(here, row_block, (group + 1) * lanes + lane)
        back_live = live(after, (group + 1) * lanes + lane, row_block)
        for at, value in ((0, own_live), (1, next_live), (2, back_live)):
            mask_ref[at * lanes + d : at * lanes + d + 1, :] = jnp.broadcast_to(
                value, (1, mask_ref.shape[1])
            )
        weights = affinity(col_unit, unit_ref[d], col_mean, mean_ref[:, block_of(lane, d)])
        weights = weights.astype(bf16)
        weight_ref[d] = weights
        product = jnp.dot(left, weights, preferred_element_type=f32)[:rows]
        product_refs[d][...] = own_live * own_ref[d] + next_live * product
        narrow = with_ones(start_ref[:, block_of(lane, d)].astype(bf16))
        back = back + back_live * nt(narrow, weights)[:rows]
    back_ref[...] = back


def smooth_kernel(size, *refs):
    *parts, smooth_ref, degree_ref = refs
    total = parts[0][...]
    for part in parts[1:]:
        total = total + part[...]
    degree = total[size : size + 1]
    smooth_ref[...] = total[:size] / degree
    degree_ref[...] = jnp.broadcast_to(degree, degree_ref.shape)


def sweep_kernel(lanes, total, own_ref, weight_ref, mask_ref, next_ref, *rest):
    blocks, (*product_refs, back_ref, gram_ref) = rest[:lanes], rest[lanes:]
    size = next_ref.shape[0]
    own_left = pieces(blocks[0][...])
    next_left = pieces(next_ref[...])
    back = jnp.zeros((size, BLOCK), f32)

    def mask(at, d):
        return mask_ref[at * lanes + d : at * lanes + d + 1, :]

    for d in range(lanes):
        own = joined(jnp.dot(own_left, own_ref[d], preferred_element_type=f32), size)
        after = joined(jnp.dot(next_left, weight_ref[d], preferred_element_type=f32), size)
        product_refs[d][...] = mask(0, d) * own + mask(1, d) * after
        left = own_left if d == 0 else pieces(blocks[d][...])
        back = back + mask(2, d) * joined(nt(left, weight_ref[d]), size)
    back_ref[...] = back
    gram_ref[...] = gram_of([block[...] for block in blocks], total)


def resmooth_kernel(degree_ref, *refs):
    *parts, smooth_ref = refs
    total = parts[0][...]
    for part in parts[1:]:
        total = total + part[...]
    smooth_ref[...] = total / degree_ref[0:1, :]


def first_solve_kernel(lanes, total, *refs):
    grams, blocks, smooth_ref, gram_ref = refs[: -lanes - 2], refs[-lanes - 2 : -2], refs[-2], refs[-1]
    gram = grams[0][...]
    for part in grams[1:]:
        gram = gram + part[...]
    inverse = inverse_factor(gram)
    solved = []
    for d in range(lanes):
        value = times(inverse, blocks[d][...])
        smooth_ref[d] = value
        solved.append(value)
    gram_ref[...] = gram_of(solved, total)


def last_solve_kernel(lanes, smooth_ref, *refs):
    *grams, out_ref = refs
    lane = lax.axis_index("cols")
    gram = grams[0][...]
    for part in grams[1:]:
        gram = gram + part[...]
    inverse = inverse_factor(gram)
    for d in range(lanes):
        out_ref[:, block_of(lane, d)] = times(inverse, smooth_ref[d])


def call(body, outs, *args):
    return pl.pallas_call(
        body,
        out_shape=[jax.ShapeDtypeStruct(shape, kind) for shape, kind in outs],
        in_specs=[pl.BlockSpec(memory_space=pltpu.VMEM)] * len(args),
        out_specs=[pl.BlockSpec(memory_space=pltpu.VMEM)] * len(outs),
        compiler_params=pltpu.CompilerParams(vmem_limit_bytes=40 * 1024 * 1024),
    )(*args)


def local(embeddings, knn_mean, pair_rows, pair_cols, pair_count, start_block):
    rows_here, width = embeddings.shape
    size = start_block.shape[0]
    slots = pair_rows.shape[2]
    lanes = lax.axis_size("cols")
    lane = lax.axis_index("cols")
    groups = lax.axis_size("rows")
    total = rows_here * groups
    assert rows_here == lanes * BLOCK and lanes & (lanes - 1) == 0 and groups & (groups - 1) == 0
    wide = size + 8

    first = lane * BLOCK
    next_cells = shift(lax.dynamic_slice_in_dim(embeddings, first, BLOCK, 0), -1)
    live = jnp.arange(slots, dtype=jnp.int32) < pair_count[0, 0]
    mine = jnp.stack([jnp.where(live, pair_rows[0, 0], -1), jnp.where(live, pair_cols[0, 0], -1)])
    mine = jnp.pad(mine, ((0, 0), (0, 128 - slots)), constant_values=-1)
    lists = lane_swaps(jnp.concatenate([mine, shift(mine, -1)], axis=0))
    side = jnp.concatenate(
        [
            lax.dynamic_slice_in_dim(start_block, first, BLOCK, 1).astype(bf16),
            jnp.broadcast_to(lax.dynamic_slice_in_dim(knn_mean, first, BLOCK, 0)[None], (16, BLOCK)),
        ],
        axis=0,
    )
    next_side = shift(side, -1)
    mean = knn_mean.astype(f32)[None, :]

    unit, own_weights, own_product = call(
        functools.partial(own_kernel, lanes),
        [
            ((lanes, BLOCK, width), bf16),
            ((lanes, BLOCK, BLOCK), bf16),
            ((lanes, wide, BLOCK), f32),
        ],
        embeddings,
        mean,
        start_block,
    )
    next_weights, masks, *products, back = call(
        functools.partial(next_kernel, lanes, size),
        [((lanes, BLOCK, BLOCK), bf16), ((16, BLOCK), f32)] + [((wide, BLOCK), f32)] * (lanes + 1),
        unit,
        next_cells,
        next_side,
        mean,
        start_block,
        own_product,
        *lists,
    )

    def scattered(products, back):
        came = [swap(products[d], "cols", d) for d in range(1, lanes)]
        return [products[0], *came, shift(back, 1)]

    smooth, degree = call(
        functools.partial(smooth_kernel, size),
        [((size, BLOCK), f32), ((8, BLOCK), f32)],
        *scattered(products, back),
    )

    *products, back, gram = call(
        functools.partial(sweep_kernel, lanes, total),
        [((size, BLOCK), f32)] * (lanes + 1) + [((size, size), f32)],
        own_weights,
        next_weights,
        masks,
        shift(smooth, -1),
        *lane_swaps(smooth),
    )
    (smooth,) = call(resmooth_kernel, [((size, BLOCK), f32)], degree, *scattered(products, back))

    def stages(gram):
        parts = [gram]
        for offsets in row_stages(groups):
            whole = sum(parts[1:], parts[0])
            parts = [whole] + [swap(whole, "rows", offset) for offset in offsets]
        return parts

    smooth, gram = call(
        functools.partial(first_solve_kernel, lanes, total),
        [((lanes, size, BLOCK), f32), ((size, size), f32)],
        *stages(gram),
        *lane_swaps(smooth),
    )
    (vector,) = call(
        functools.partial(last_solve_kernel, lanes),
        [((size, rows_here), f32)],
        smooth,
        *stages(gram),
    )
    return vector


def solution(mesh):
    in_specs = (
        P("rows", None),
        P("rows"),
        P("rows", "cols", None),
        P("rows", "cols", None),
        P("rows", "cols"),
        P(None, "rows"),
    )
    out_specs = P(None, "rows")
    return jax.shard_map(local, mesh=mesh, in_specs=in_specs, out_specs=out_specs, check_vma=False)
```

time: 499 us -> 92.9 us (0.19)
  waiting for transfers between devices: 187 us -> 43.3 us
  blocking collectives: 95 us -> 0 us
  local copies, waits for them, and re-layouts: 65.4 us -> 5.23 us
  other arithmetic: 40.6 us -> 1.4 us
  loops' own time: 35.2 us -> 0 us
  matrix products: 33.4 us -> 0 us
  Pallas kernels: 0 us -> 17.4 us
  between operations: 15 us -> 0.78 us
    psum x2 -> x0, waiting for transfers between devices: 118 us -> none  [local(): summed, degree = lax.psum((partial_value, degree_part), 'cols')]
    psum x3 -> x0, blocking collectives: 80 us -> none  [the longest x2 74.2 us: local(): gram = lax.psum(gram, 'rows')]
    dynamic_slice x48 -> x2, local copies, waits for them, and re-layouts: 61.2 us -> 1.83 us  [the longest x1 1.08 us: local(): lax.dynamic_slice_in_dim(embeddings, first, BLOCK, 0)]
    another operation x2 -> x0, loops' own time: 35.2 us -> none  [local(): lax.fori_loop(0, live_count, accumulate, start_state)]
    dot_general x26 -> x0, matrix products: 30 us -> none  [the longest x16 14.5 us: accumulate(): lax.dot_general(source, affinity, (((1,), (1,)), ((), ())), preferred_ele...]
    ppermute x8 -> x29, waiting for transfers between devices: 69.7 us -> 43.3 us  [the longest x23 29.1 us: swap(): return lax.ppermute(cells, axis, [(i, i ^ offset) for i in range(count)])]
    another operation x11 -> x1, other arithmetic: 24.3 us -> 0.01 us  [local(): jnp.stack([jnp.where(live, pair_rows[0, 0], -1), jnp.where(live, pair_col...]
    pallas_call x0 -> x7, Pallas kernels: none -> 17.4 us  [call(): pl.pallas_call(body, out_shape=[jax.ShapeDtypeStruct(shape, kind) for sha...]
  transfers between devices with their start and end apart: 10 -> 29, of which waited for: 6 -> 16; matrix products, arithmetic and copies ran while one was open for 1% -> 3% of each run, Pallas kernels for 0% -> 2%
where the time goes in v1:
time: 92.9 us; the launch traced here: 92.6 us
  waiting for transfers between devices  43.3 us (47%)
  starting transfers between devices  24.5 us (26%)
  Pallas kernels  17.4 us (19%)
  local copies, waits for them, and re-layouts  5.23 us (6%)
  other arithmetic  1.4 us (2%)
    ppermute x23, waiting for transfers between devices, swap(): return lax.ppermute(cells, axis, [(i, i ^ offset) for i in range(count)])  29.1 us
    pallas_call x7, Pallas kernels, call(): pl.pallas_call(body, out_shape=[jax.ShapeDtypeStruct(shape, kind) for sha...  17.4 us
    ppermute x23, starting transfers between devices, swap(): return lax.ppermute(cells, axis, [(i, i ^ offset) for i in range(count)])  14.3 us
    ppermute x6, waiting for transfers between devices, shift(): lax.ppermute(cells, 'rows', [(i, (i + step) % count) for i in range(count)])  14.2 us
    ppermute x6, starting transfers between devices, shift(): lax.ppermute(cells, 'rows', [(i, (i + step) % count) for i in range(count)])  10.2 us
    unnamed x4, local copies, waits for them, and re-layouts  2.54 us
  transfers between devices with their start and end apart: 29, of which 16 were waited for; matrix products, arithmetic and copies ran while one was open for 3% of the time, Pallas kernels for 2%

profile of v1, /device:TPU:0, one launch (start us, length us, event | category | flops | bytes accessed | tf_op | source)
XLA Modules:
  0.0 92.6 jit_solution(4813087809784495221)
XLA Ops:
  0.0 1.1 %constant_dynamic-slice_fusion = bf16[256,1024]{1,0:T(8,128)(2,1)S(1)} fusion(bf16[1024,1024]{1,0:T(8,128)(2,1)} %cells_ref.1, s32[]{:T(128)S(6)} %select_n.26), kind=kLoop, calls=%fused_computation.6 | loop fusion | bytes 1048580 | tf_op jit(solution)/shard_map/dynamic_slice | solution.py:288
  1.1 6.1 %collective-permute-start = (bf16[256,1024]{1,0:T(8,128)(2,1)S(1)}, bf16[256,1024]{1,0:T(8,128)(2,1)S(1)}, u32[]{:S(2)}, u32[]{:S(2)}) collective-permute-start(bf16[256,1024]{1,0:T(8,128)(2,1)S(1)} %constant_dynamic-slice_fusion), channel_id=1, source_target_pairs={{0,28},{4,0},{8,4},{12,8},{16,12},{20,16},{24,20},{28,24},{1,29},{... | collective-permute-start | bytes 1572872 | tf_op jit(solution)/shard_map/ppermute | solution.py:24
  7.8 0.7 compare_select_fusion
  8.5 0.6 collective-permute-start.2
  9.1 0.8 dynamic_slice.11
  9.8 0.8 dynamic-slice_convert_fusion
  10.7 1.5 %collective-permute-start.1 = (bf16[80,256]{1,0:T(8,128)(2,1)S(1)}, bf16[80,256]{1,0:T(8,128)(2,1)S(1)}, u32[]{:S(2)}, u32[]{:S(2)}) collective-permute-start(bf16[80,256]{1,0:T(8,128)(2,1)S(1)} %pad_maximum_fusion), channel_id=1, source_target_pairs={{0,28},{4,0},{8,4},{12,8},{16,12},{20,16},{24,20},{28,24},{1,29},{... | collective-permute-start | bytes 122888 | tf_op jit(solution)/shard_map/ppermute | solution.py:24
  12.1 6.7 %collective-permute-done.2 = s32[2,128]{1,0:T(2,128)S(1)} collective-permute-done((s32[2,128]{1,0:T(2,128)S(1)}, s32[2,128]{1,0:T(2,128)S(1)}, u32[]{:S(2)}, u32[]{:S(2)}) %collective-permute-start.2) | collective-permute-done | bytes 1056 | tf_op jit(solution)/shard_map/ppermute | solution.py:24
  18.8 1.6 %collective-permute-start.4 = (s32[4,128]{1,0:T(4,128)S(1)}, s32[4,128]{1,0:T(4,128)S(1)}, u32[]{:S(2)}, u32[]{:S(2)}) collective-permute-start(s32[4,128]{1,0:T(4,128)S(1)} %pad_add_fusion.rest_0_), channel_id=1, source_target_pairs={{0,2},{1,3},{2,0},{3,1},{4,6},{5,7},{6,4},{7,5},{8,10},{9,11},{10,... | collective-permute-start | bytes 6152 | tf_op jit(solution)/shard_map/ppermute | solution.py:29
  20.4 0.3 collective-permute-start.3
  20.7 0.7 broadcast_in_dim.20
  21.4 1.6 %copy-done = bf16[1024,1024]{1,0:T(8,128)(2,1)S(1)} copy-done((bf16[1024,1024]{1,0:T(8,128)(2,1)S(1)}, bf16[1024,1024]{1,0:T(8,128)(2,1)}, u32[]{:S(2)}) %copy-start) | copy-done | bytes 2097176
  22.9 0.9 %copy-done.1 = f32[64,1024]{1,0:T(8,128)S(1)} copy-done((f32[64,1024]{1,0:T(8,128)S(1)}, f32[64,1024]{1,0:T(8,128)}, u32[]{:S(2)}) %copy-start.1) | copy-done | bytes 262168
  23.9 1.7 %shard_map.64 = (bf16[4,256,1024]{2,1,0:T(8,128)(2,1)S(1)}, bf16[4,256,256]{2,1,0:T(8,128)(2,1)S(1)}, f32[4,72,256]{2,1,0:T(8,128)S(1)}) custom-call(bf16[1024,1024]{1,0:T(8,128)(2,1)S(1)} %copy-done, f32[1,1024]{1,0:T(1,128)S(1)} %bitcast.7, f32[64,1024]{1,0:T(8,128)S(1)} %copy-done.1), custom_call_target="tpu_custom_call" | custom-call | tf_op jit(solution)/shard_map/pallas_call | solution.py:267
  25.7 2.0 %shard_map.65 = (bf16[4,256,256]{2,1,0:T(8,128)(2,1)S(1)}, f32[16,256]{1,0:T(8,128)S(1)}, f32[72,256]{1,0:T(8,128)S(1)}, f32[72,256]{1,0:T(8,128)S(1)}, f32[72,2...) custom-call(bf16[4,256,1024]{2,1,0:T(8,128)(2,1)S(1)} %get-tuple-element.26.unit_ref, ...), custom_call_target="tpu_custom_call" | custom-call | tf_op jit(solution)/shard_map/pallas_call | solution.py:267
  28.0 1.4 %collective-permute-start.7 = (f32[72,256]{1,0:T(8,128)S(1)}, f32[72,256]{1,0:T(8,128)S(1)}, u32[]{:S(2)}, u32[]{:S(2)}) collective-permute-start(f32[72,256]{1,0:T(8,128)S(1)} %get-tuple-element.32), channel_id=1, source_target_pairs={{0,2},{1,3},{2,0},{3,1},{4,6},{5,7},{6,4},{7,5},{8,10},{9,11},{10,... | collective-permute-start | bytes 221192 | tf_op jit(solution)/shard_map/ppermute | solution.py:29
  29.4 0.3 collective-permute-start.8
  29.7 0.4 collective-permute-start.9
  30.0 2.6 %collective-permute-done.7.refs_2_ = f32[72,256]{1,0:T(8,128)S(1)} collective-permute-done((f32[72,256]{1,0:T(8,128)S(1)}, f32[72,256]{1,0:T(8,128)S(1)}, u32[]{:S(2)}, u32[]{:S(2)}) %collective-permute-start.7) | collective-permute-done | bytes 73760 | tf_op jit(solution)/shard_map/ppermute | solution.py:29
  32.6 1.2 %collective-permute-done.8.refs_3_ = f32[72,256]{1,0:T(8,128)S(1)} collective-permute-done((f32[72,256]{1,0:T(8,128)S(1)}, f32[72,256]{1,0:T(8,128)S(1)}, u32[]{:S(2)}, u32[]{:S(2)}) %collective-permute-start.8) | collective-permute-done | bytes 73760 | tf_op jit(solution)/shard_map/ppermute | solution.py:29
  33.8 3.9 %collective-permute-done.9.refs_4_ = f32[72,256]{1,0:T(8,128)S(1)} collective-permute-done((f32[72,256]{1,0:T(8,128)S(1)}, f32[72,256]{1,0:T(8,128)S(1)}, u32[]{:S(2)}, u32[]{:S(2)}) %collective-permute-start.9) | collective-permute-done | bytes 73760 | tf_op jit(solution)/shard_map/ppermute | solution.py:24
  37.8 0.8 collective-permute-start.13
  38.6 0.8 collective-permute-start.12
  39.4 0.3 collective-permute-start.11
  39.7 1.7 %collective-permute-start.10 = (f32[64,256]{1,0:T(8,128)S(1)}, f32[64,256]{1,0:T(8,128)S(1)}, u32[]{:S(2)}, u32[]{:S(2)}) collective-permute-start(f32[64,256]{1,0:T(8,128)S(1)} %get-tuple-element.35.rest_0_), channel_id=1, source_target_pairs={{0,28},{4,0},{8,4},{12,8},{16,12},{20,16},{24,20},{28,24},{1,29},{... | collective-permute-start | bytes 196616 | tf_op jit(solution)/shard_map/ppermute | solution.py:24
  41.5 0.7 collective-permute-done.13.rest_3_
  42.2 1.5 %collective-permute-done.12.rest_2_ = f32[64,256]{1,0:T(8,128)S(1)} collective-permute-done((f32[64,256]{1,0:T(8,128)S(1)}, f32[64,256]{1,0:T(8,128)S(1)}, u32[]{:S(2)}, u32[]{:S(2)}) %collective-permute-start.12) | collective-permute-done | bytes 65568 | tf_op jit(solution)/shard_map/ppermute | solution.py:29
  43.7 0.3 collective-permute-done.10.next_ref
  44.0 0.7 shard_map.67
  44.8 1.4 %collective-permute-start.19 = (f32[64,256]{1,0:T(8,128)S(1)}, f32[64,256]{1,0:T(8,128)S(1)}, u32[]{:S(2)}, u32[]{:S(2)}) collective-permute-start(f32[64,256]{1,0:T(8,128)S(1)} %get-tuple-element.40), channel_id=1, source_target_pairs={{0,2},{1,3},{2,0},{3,1},{4,6},{5,7},{6,4},{7,5},{8,10},{9,11},{10,... | collective-permute-start | bytes 196616 | tf_op jit(solution)/shard_map/ppermute | solution.py:29
  46.3 0.4 collective-permute-start.20
  46.7 2.8 %collective-permute-done.19.refs_2_ = f32[64,256]{1,0:T(8,128)S(1)} collective-permute-done((f32[64,256]{1,0:T(8,128)S(1)}, f32[64,256]{1,0:T(8,128)S(1)}, u32[]{:S(2)}, u32[]{:S(2)}) %collective-permute-start.19) | collective-permute-done | bytes 65568 | tf_op jit(solution)/shard_map/ppermute | solution.py:29
  49.5 1.0 %collective-permute-done.20.refs_3_ = f32[64,256]{1,0:T(8,128)S(1)} collective-permute-done((f32[64,256]{1,0:T(8,128)S(1)}, f32[64,256]{1,0:T(8,128)S(1)}, u32[]{:S(2)}, u32[]{:S(2)}) %collective-permute-start.20) | collective-permute-done | bytes 65568 | tf_op jit(solution)/shard_map/ppermute | solution.py:29
  50.5 3.2 %collective-permute-done.21.refs_4_ = f32[64,256]{1,0:T(8,128)S(1)} collective-permute-done((f32[64,256]{1,0:T(8,128)S(1)}, f32[64,256]{1,0:T(8,128)S(1)}, u32[]{:S(2)}, u32[]{:S(2)}) %collective-permute-start.21) | collective-permute-done | bytes 65568 | tf_op jit(solution)/shard_map/ppermute | solution.py:24
  53.8 0.6 collective-permute-start.24
  54.4 0.9 collective-permute-start.23
  55.3 0.4 collective-permute-start.22
  55.7 3.9 %collective-permute-done.14 = f32[64,64]{1,0:T(8,128)S(1)} collective-permute-done((f32[64,64]{1,0:T(8,128)S(1)}, f32[64,64]{1,0:T(8,128)S(1)}, u32[]{:S(2)}, u32[]{:S(2)}) %collective-permute-start.14) | collective-permute-done | bytes 16416 | tf_op jit(solution)/shard_map/ppermute | solution.py:29
  59.6 0.3 collective-permute-start.17
  59.9 5.6 %collective-permute-done.17.refs_3_ = f32[64,64]{1,0:T(8,128)S(1)} collective-permute-done((f32[64,64]{1,0:T(8,128)S(1)}, f32[64,64]{1,0:T(8,128)S(1)}, u32[]{:S(2)}, u32[]{:S(2)}) %collective-permute-start.17) | collective-permute-done | bytes 16416 | tf_op jit(solution)/shard_map/ppermute | solution.py:29
  65.6 3.9 %collective-permute-done.15.refs_1_ = f32[64,64]{1,0:T(8,128)S(1)} collective-permute-done((f32[64,64]{1,0:T(8,128)S(1)}, f32[64,64]{1,0:T(8,128)S(1)}, u32[]{:S(2)}, u32[]{:S(2)}) %collective-permute-start.15) | collective-permute-done | bytes 16416 | tf_op jit(solution)/shard_map/ppermute | solution.py:29
  69.5 6.3 %shard_map.69 = (f32[4,64,256]{2,1,0:T(8,128)S(1)}, f32[64,64]{1,0:T(8,128)S(1)}) custom-call(f32[64,64]{1,0:T(8,128)S(1)} %add.14.refs_0_, f32[64,64]{1,0:T(8,128)S(1)} %collective-permute-done.15.refs_1_, f32[64,64]{1,0:T(8,128)S(1)} %collective-permute-done.16.refs_2_, f32[64,64]{1,0:T(8,128)S(1)} %collective-permute-done.17.refs_3_, ...), custom_call_target="tpu_custom_call" | custom-call | tf_op jit(solution)/shard_map/pallas_call | solution.py:267
  75.9 3.9 %collective-permute-done.25 = f32[64,64]{1,0:T(8,128)S(1)} collective-permute-done((f32[64,64]{1,0:T(8,128)S(1)}, f32[64,64]{1,0:T(8,128)S(1)}, u32[]{:S(2)}, u32[]{:S(2)}) %collective-permute-start.25) | collective-permute-done | bytes 16416 | tf_op jit(solution)/shard_map/ppermute | solution.py:29
  79.9 1.4 %collective-permute-start.27 = (f32[64,64]{1,0:T(8,128)S(1)}, f32[64,64]{1,0:T(8,128)S(1)}, u32[]{:S(2)}, u32[]{:S(2)}) collective-permute-start(f32[64,64]{1,0:T(8,128)S(1)} %add.15.refs_0_), channel_id=1, source_target_pairs={{0,16},{4,20},{8,24},{12,28},{16,0},{20,4},{24,8},{28,12},{1,17},{... | collective-permute-start | bytes 49160 | tf_op jit(solution)/shard_map/ppermute | solution.py:29
  81.3 2.9 %collective-permute-start.26 = (f32[64,64]{1,0:T(8,128)S(1)}, f32[64,64]{1,0:T(8,128)S(1)}, u32[]{:S(2)}, u32[]{:S(2)}) collective-permute-start(f32[64,64]{1,0:T(8,128)S(1)} %add.15.refs_0_), channel_id=1, source_target_pairs={{0,8},{4,12},{8,0},{12,4},{16,24},{20,28},{24,16},{28,20},{1,9},{5... | collective-permute-start | bytes 49160 | tf_op jit(solution)/shard_map/ppermute | solution.py:29
  84.2 1.3 %collective-permute-done.28.refs_3_ = f32[64,64]{1,0:T(8,128)S(1)} collective-permute-done((f32[64,64]{1,0:T(8,128)S(1)}, f32[64,64]{1,0:T(8,128)S(1)}, u32[]{:S(2)}, u32[]{:S(2)}) %collective-permute-start.28) | collective-permute-done | bytes 16416 | tf_op jit(solution)/shard_map/ppermute | solution.py:29
  85.5 0.6 collective-permute-done.26.refs_1_
  86.1 6.5 %shard_map.70 = f32[64,1024]{1,0:T(8,128)} custom-call(f32[4,64,256]{2,1,0:T(8,128)S(1)} %get-tuple-element.43.smooth_ref, f32[64,64]{1,0:T(8,128)S(1)} %add.15.refs_0_, f32[64,64]{1,0:T(8,128)S(1)} %collective-permute-done.26.refs_1_, f32[64,64]{1,0:T(8,128)S(1)} %collective-permute-done.27.refs_2_, f32[64,64]{1,0:T(8,128)S(1)} %collective-permute-done.28.refs_3_), custom_call_target="tpu_custom_call" | custom-call | tf_op jit(solution)/shard_map/pallas_call | solution.py:267
  (33 shorter events, 0.6 us)
Async XLA Ops:
  1.1 24.6 %collective-permute-start = (bf16[256,1024]{1,0:T(8,128)(2,1)S(1)}, bf16[256,1024]{1,0:T(8,128)(2,1)S(1)}, u32[]{:S(2)}, u32[]{:S(2)}) collective-permute-start(bf16[256,1024]{1,0:T(8,128)(2,1)S(1)} %constant_dynamic-slice_fusion), channel_id=1, source_target_pairs={{0,28},{4,0},{8,4},{12,8},{16,12},{20,16},{24,20},{28,24},{1,29},{... | collective-permute-start | bytes 1572872 | tf_op jit(solution)/shard_map/ppermute | solution.py:24
  8.5 10.3 %collective-permute-start.2 = (s32[2,128]{1,0:T(2,128)S(1)}, s32[2,128]{1,0:T(2,128)S(1)}, u32[]{:S(2)}, u32[]{:S(2)}) collective-permute-start(s32[2,128]{1,0:T(2,128)S(1)} %pad.4), channel_id=1, source_target_pairs={{0,28},{4,0},{8,4},{12,8},{16,12},{20,16},{24,20},{28,24},{1,29},{... | collective-permute-start | bytes 3080 | tf_op jit(solution)/shard_map/ppermute | solution.py:24
  10.7 15.0 %collective-permute-start.1 = (bf16[80,256]{1,0:T(8,128)(2,1)S(1)}, bf16[80,256]{1,0:T(8,128)(2,1)S(1)}, u32[]{:S(2)}, u32[]{:S(2)}) collective-permute-start(bf16[80,256]{1,0:T(8,128)(2,1)S(1)} %pad_maximum_fusion), channel_id=1, source_target_pairs={{0,28},{4,0},{8,4},{12,8},{16,12},{20,16},{24,20},{28,24},{1,29},{... | collective-permute-start | bytes 122888 | tf_op jit(solution)/shard_map/ppermute | solution.py:24
  18.8 6.8 %collective-permute-start.5 = (s32[4,128]{1,0:T(4,128)S(1)}, s32[4,128]{1,0:T(4,128)S(1)}, u32[]{:S(2)}, u32[]{:S(2)}) collective-permute-start(s32[4,128]{1,0:T(4,128)S(1)} %pad_add_fusion.rest_0_), channel_id=1, source_target_pairs={{0,3},{1,2},{2,1},{3,0},{4,7},{5,6},{6,5},{7,4},{8,11},{9,10},{10,... | collective-permute-start | bytes 6152 | tf_op jit(solution)/shard_map/ppermute | solution.py:29
  18.8 6.8 %collective-permute-start.4 = (s32[4,128]{1,0:T(4,128)S(1)}, s32[4,128]{1,0:T(4,128)S(1)}, u32[]{:S(2)}, u32[]{:S(2)}) collective-permute-start(s32[4,128]{1,0:T(4,128)S(1)} %pad_add_fusion.rest_0_), channel_id=1, source_target_pairs={{0,2},{1,3},{2,0},{3,1},{4,6},{5,7},{6,4},{7,5},{8,10},{9,11},{10,... | collective-permute-start | bytes 6152 | tf_op jit(solution)/shard_map/ppermute | solution.py:29
  20.4 5.3 %collective-permute-start.3 = (s32[4,128]{1,0:T(4,128)S(1)}, s32[4,128]{1,0:T(4,128)S(1)}, u32[]{:S(2)}, u32[]{:S(2)}) collective-permute-start(s32[4,128]{1,0:T(4,128)S(1)} %pad_add_fusion.rest_0_), channel_id=1, source_target_pairs={{0,1},{1,0},{2,3},{3,2},{4,5},{5,4},{6,7},{7,6},{8,9},{9,8},{10,11... | collective-permute-start | bytes 6152 | tf_op jit(solution)/shard_map/ppermute | solution.py:29
  21.4 1.6 %copy-start = (bf16[1024,1024]{1,0:T(8,128)(2,1)S(1)}, bf16[1024,1024]{1,0:T(8,128)(2,1)}, u32[]{:S(2)}) copy-start(bf16[1024,1024]{1,0:T(8,128)(2,1)} %cells_ref.1) | copy-start | bytes 6291460
  22.9 0.9 %copy-start.1 = (f32[64,1024]{1,0:T(8,128)S(1)}, f32[64,1024]{1,0:T(8,128)}, u32[]{:S(2)}) copy-start(f32[64,1024]{1,0:T(8,128)} %start_ref.3) | copy-start | bytes 786436
  27.7 2.3 %collective-permute-start.6 = (f32[72,256]{1,0:T(8,128)S(1)}, f32[72,256]{1,0:T(8,128)S(1)}, u32[]{:S(2)}, u32[]{:S(2)}) collective-permute-start(f32[72,256]{1,0:T(8,128)S(1)} %get-tuple-element.31), channel_id=1, source_target_pairs={{0,1},{1,0},{2,3},{3,2},{4,5},{5,4},{6,7},{7,6},{8,9},{9,8},{10,11... | collective-permute-start | bytes 221192 | tf_op jit(solution)/shard_map/ppermute | solution.py:29
  28.0 4.6 %collective-permute-start.7 = (f32[72,256]{1,0:T(8,128)S(1)}, f32[72,256]{1,0:T(8,128)S(1)}, u32[]{:S(2)}, u32[]{:S(2)}) collective-permute-start(f32[72,256]{1,0:T(8,128)S(1)} %get-tuple-element.32), channel_id=1, source_target_pairs={{0,2},{1,3},{2,0},{3,1},{4,6},{5,7},{6,4},{7,5},{8,10},{9,11},{10,... | collective-permute-start | bytes 221192 | tf_op jit(solution)/shard_map/ppermute | solution.py:29
  29.4 4.5 %collective-permute-start.8 = (f32[72,256]{1,0:T(8,128)S(1)}, f32[72,256]{1,0:T(8,128)S(1)}, u32[]{:S(2)}, u32[]{:S(2)}) collective-permute-start(f32[72,256]{1,0:T(8,128)S(1)} %get-tuple-element.33), channel_id=1, source_target_pairs={{0,3},{1,2},{2,1},{3,0},{4,7},{5,6},{6,5},{7,4},{8,11},{9,10},{10,... | collective-permute-start | bytes 221192 | tf_op jit(solution)/shard_map/ppermute | solution.py:29
  29.7 8.1 %collective-permute-start.9 = (f32[72,256]{1,0:T(8,128)S(1)}, f32[72,256]{1,0:T(8,128)S(1)}, u32[]{:S(2)}, u32[]{:S(2)}) collective-permute-start(f32[72,256]{1,0:T(8,128)S(1)} %get-tuple-element.34), channel_id=1, source_target_pairs={{0,4},{4,8},{8,12},{12,16},{16,20},{20,24},{24,28},{28,0},{1,5},{5... | collective-permute-start | bytes 221192 | tf_op jit(solution)/shard_map/ppermute | solution.py:24
  37.8 4.4 %collective-permute-start.13 = (f32[64,256]{1,0:T(8,128)S(1)}, f32[64,256]{1,0:T(8,128)S(1)}, u32[]{:S(2)}, u32[]{:S(2)}) collective-permute-start(f32[64,256]{1,0:T(8,128)S(1)} %get-tuple-element.35.rest_0_), channel_id=1, source_target_pairs={{0,3},{1,2},{2,1},{3,0},{4,7},{5,6},{6,5},{7,4},{8,11},{9,10},{10,... | collective-permute-start | bytes 196616 | tf_op jit(solution)/shard_map/ppermute | solution.py:29
  38.6 5.1 %collective-permute-start.12 = (f32[64,256]{1,0:T(8,128)S(1)}, f32[64,256]{1,0:T(8,128)S(1)}, u32[]{:S(2)}, u32[]{:S(2)}) collective-permute-start(f32[64,256]{1,0:T(8,128)S(1)} %get-tuple-element.35.rest_0_), channel_id=1, source_target_pairs={{0,2},{1,3},{2,0},{3,1},{4,6},{5,7},{6,4},{7,5},{8,10},{9,11},{10,... | collective-permute-start | bytes 196616 | tf_op jit(solution)/shard_map/ppermute | solution.py:29
  39.4 4.3 %collective-permute-start.11 = (f32[64,256]{1,0:T(8,128)S(1)}, f32[64,256]{1,0:T(8,128)S(1)}, u32[]{:S(2)}, u32[]{:S(2)}) collective-permute-start(f32[64,256]{1,0:T(8,128)S(1)} %get-tuple-element.35.rest_0_), channel_id=1, source_target_pairs={{0,1},{1,0},{2,3},{3,2},{4,5},{5,4},{6,7},{7,6},{8,9},{9,8},{10,11... | collective-permute-start | bytes 196616 | tf_op jit(solution)/shard_map/ppermute | solution.py:29
  39.7 4.3 %collective-permute-start.10 = (f32[64,256]{1,0:T(8,128)S(1)}, f32[64,256]{1,0:T(8,128)S(1)}, u32[]{:S(2)}, u32[]{:S(2)}) collective-permute-start(f32[64,256]{1,0:T(8,128)S(1)} %get-tuple-element.35.rest_0_), channel_id=1, source_target_pairs={{0,28},{4,0},{8,4},{12,8},{16,12},{20,16},{24,20},{28,24},{1,29},{... | collective-permute-start | bytes 196616 | tf_op jit(solution)/shard_map/ppermute | solution.py:24
  44.8 1.9 %collective-permute-start.18 = (f32[64,256]{1,0:T(8,128)S(1)}, f32[64,256]{1,0:T(8,128)S(1)}, u32[]{:S(2)}, u32[]{:S(2)}) collective-permute-start(f32[64,256]{1,0:T(8,128)S(1)} %get-tuple-element.39), channel_id=1, source_target_pairs={{0,1},{1,0},{2,3},{3,2},{4,5},{5,4},{6,7},{7,6},{8,9},{9,8},{10,11... | collective-permute-start | bytes 196616 | tf_op jit(solution)/shard_map/ppermute | solution.py:29
  44.8 4.6 %collective-permute-start.19 = (f32[64,256]{1,0:T(8,128)S(1)}, f32[64,256]{1,0:T(8,128)S(1)}, u32[]{:S(2)}, u32[]{:S(2)}) collective-permute-start(f32[64,256]{1,0:T(8,128)S(1)} %get-tuple-element.40), channel_id=1, source_target_pairs={{0,2},{1,3},{2,0},{3,1},{4,6},{5,7},{6,4},{7,5},{8,10},{9,11},{10,... | collective-permute-start | bytes 196616 | tf_op jit(solution)/shard_map/ppermute | solution.py:29
  46.3 4.2 %collective-permute-start.20 = (f32[64,256]{1,0:T(8,128)S(1)}, f32[64,256]{1,0:T(8,128)S(1)}, u32[]{:S(2)}, u32[]{:S(2)}) collective-permute-start(f32[64,256]{1,0:T(8,128)S(1)} %get-tuple-element.41), channel_id=1, source_target_pairs={{0,3},{1,2},{2,1},{3,0},{4,7},{5,6},{6,5},{7,4},{8,11},{9,10},{10,... | collective-permute-start | bytes 196616 | tf_op jit(solution)/shard_map/ppermute | solution.py:29
  46.7 7.0 %collective-permute-start.21 = (f32[64,256]{1,0:T(8,128)S(1)}, f32[64,256]{1,0:T(8,128)S(1)}, u32[]{:S(2)}, u32[]{:S(2)}) collective-permute-start(f32[64,256]{1,0:T(8,128)S(1)} %get-tuple-element.42), channel_id=1, source_target_pairs={{0,4},{4,8},{8,12},{12,16},{16,20},{20,24},{24,28},{28,0},{1,5},{5... | collective-permute-start | bytes 196616 | tf_op jit(solution)/shard_map/ppermute | solution.py:24
  53.8 15.7 %collective-permute-start.24 = (f32[64,256]{1,0:T(8,128)S(1)}, f32[64,256]{1,0:T(8,128)S(1)}, u32[]{:S(2)}, u32[]{:S(2)}) collective-permute-start(f32[64,256]{1,0:T(8,128)S(1)} %shard_map.68.refs_4_), channel_id=1, source_target_pairs={{0,3},{1,2},{2,1},{3,0},{4,7},{5,6},{6,5},{7,4},{8,11},{9,10},{10,... | collective-permute-start | bytes 196616 | tf_op jit(solution)/shard_map/ppermute | solution.py:29
  54.4 15.1 %collective-permute-start.23 = (f32[64,256]{1,0:T(8,128)S(1)}, f32[64,256]{1,0:T(8,128)S(1)}, u32[]{:S(2)}, u32[]{:S(2)}) collective-permute-start(f32[64,256]{1,0:T(8,128)S(1)} %shard_map.68.refs_4_), channel_id=1, source_target_pairs={{0,2},{1,3},{2,0},{3,1},{4,6},{5,7},{6,4},{7,5},{8,10},{9,11},{10,... | collective-permute-start | bytes 196616 | tf_op jit(solution)/shard_map/ppermute | solution.py:29
  55.3 14.2 %collective-permute-start.22 = (f32[64,256]{1,0:T(8,128)S(1)}, f32[64,256]{1,0:T(8,128)S(1)}, u32[]{:S(2)}, u32[]{:S(2)}) collective-permute-start(f32[64,256]{1,0:T(8,128)S(1)} %shard_map.68.refs_4_), channel_id=1, source_target_pairs={{0,1},{1,0},{2,3},{3,2},{4,5},{5,4},{6,7},{7,6},{8,9},{9,8},{10,11... | collective-permute-start | bytes 196616 | tf_op jit(solution)/shard_map/ppermute | solution.py:29
  55.7 3.9 %collective-permute-start.14 = (f32[64,64]{1,0:T(8,128)S(1)}, f32[64,64]{1,0:T(8,128)S(1)}, u32[]{:S(2)}, u32[]{:S(2)}) collective-permute-start(f32[64,64]{1,0:T(8,128)S(1)} %get-tuple-element.36), channel_id=1, source_target_pairs={{0,4},{4,0},{8,12},{12,8},{16,20},{20,16},{24,28},{28,24},{1,5},{5... | collective-permute-start | bytes 49160 | tf_op jit(solution)/shard_map/ppermute | solution.py:29
  59.6 5.9 %collective-permute-start.17 = (f32[64,64]{1,0:T(8,128)S(1)}, f32[64,64]{1,0:T(8,128)S(1)}, u32[]{:S(2)}, u32[]{:S(2)}) collective-permute-start(f32[64,64]{1,0:T(8,128)S(1)} %add.14.refs_0_), channel_id=1, source_target_pairs={{0,24},{4,28},{8,16},{12,20},{16,8},{20,12},{24,0},{28,4},{1,25},{... | collective-permute-start | bytes 49160 | tf_op jit(solution)/shard_map/ppermute | solution.py:29
  59.9 5.7 %collective-permute-start.16 = (f32[64,64]{1,0:T(8,128)S(1)}, f32[64,64]{1,0:T(8,128)S(1)}, u32[]{:S(2)}, u32[]{:S(2)}) collective-permute-start(f32[64,64]{1,0:T(8,128)S(1)} %add.14.refs_0_), channel_id=1, source_target_pairs={{0,16},{4,20},{8,24},{12,28},{16,0},{20,4},{24,8},{28,12},{1,17},{... | collective-permute-start | bytes 49160 | tf_op jit(solution)/shard_map/ppermute | solution.py:29
  65.6 3.9 %collective-permute-start.15 = (f32[64,64]{1,0:T(8,128)S(1)}, f32[64,64]{1,0:T(8,128)S(1)}, u32[]{:S(2)}, u32[]{:S(2)}) collective-permute-start(f32[64,64]{1,0:T(8,128)S(1)} %add.14.refs_0_), channel_id=1, source_target_pairs={{0,8},{4,12},{8,0},{12,4},{16,24},{20,28},{24,16},{28,20},{1,9},{5... | collective-permute-start | bytes 49160 | tf_op jit(solution)/shard_map/ppermute | solution.py:29
  75.8 4.0 %collective-permute-start.25 = (f32[64,64]{1,0:T(8,128)S(1)}, f32[64,64]{1,0:T(8,128)S(1)}, u32[]{:S(2)}, u32[]{:S(2)}) collective-permute-start(f32[64,64]{1,0:T(8,128)S(1)} %get-tuple-element.44), channel_id=1, source_target_pairs={{0,4},{4,0},{8,12},{12,8},{16,20},{20,16},{24,28},{28,24},{1,5},{5... | collective-permute-start | bytes 49160 | tf_op jit(solution)/shard_map/ppermute | solution.py:29
  79.8 5.7 %collective-permute-start.28 = (f32[64,64]{1,0:T(8,128)S(1)}, f32[64,64]{1,0:T(8,128)S(1)}, u32[]{:S(2)}, u32[]{:S(2)}) collective-permute-start(f32[64,64]{1,0:T(8,128)S(1)} %add.15.refs_0_), channel_id=1, source_target_pairs={{0,24},{4,28},{8,16},{12,20},{16,8},{20,12},{24,0},{28,4},{1,25},{... | collective-permute-start | bytes 49160 | tf_op jit(solution)/shard_map/ppermute | solution.py:29
  79.9 5.6 %collective-permute-start.27 = (f32[64,64]{1,0:T(8,128)S(1)}, f32[64,64]{1,0:T(8,128)S(1)}, u32[]{:S(2)}, u32[]{:S(2)}) collective-permute-start(f32[64,64]{1,0:T(8,128)S(1)} %add.15.refs_0_), channel_id=1, source_target_pairs={{0,16},{4,20},{8,24},{12,28},{16,0},{20,4},{24,8},{28,12},{1,17},{... | collective-permute-start | bytes 49160 | tf_op jit(solution)/shard_map/ppermute | solution.py:29
  81.3 4.8 %collective-permute-start.26 = (f32[64,64]{1,0:T(8,128)S(1)}, f32[64,64]{1,0:T(8,128)S(1)}, u32[]{:S(2)}, u32[]{:S(2)}) collective-permute-start(f32[64,64]{1,0:T(8,128)S(1)} %add.15.refs_0_), channel_id=1, source_target_pairs={{0,8},{4,12},{8,0},{12,4},{16,24},{20,28},{24,16},{28,20},{1,9},{5... | collective-permute-start | bytes 49160 | tf_op jit(solution)/shard_map/ppermute | solution.py:29

commit v2 on v1

--- a/solution.py
+++ b/solution.py
@@ -87,27 +87,39 @@
 
 def inverse_factor(gram):
     size = gram.shape[0]
+    tile = 8
+    count = size // tile
     eye = jnp.where(diagonal(size), 1.0, 0.0).astype(f32)
     table = jnp.concatenate([gram, eye], axis=1)
-    tile = 8
-    parts = [table[g * tile : (g + 1) * tile] for g in range(size // tile)]
-    inner = lax.broadcasted_iota(jnp.int32, (tile, 1), 0)
-    scales = []
-    for k in range(size):
-        home, at = k // tile, k % tile
-        row = parts[home][at : at + 1]
-        pivot = row[:, k : k + 1]
-        scales.append(lax.rsqrt(pivot))
-        row_scaled = row / pivot
-        for g in range(home, size // tile):
-            column = parts[g][:, k : k + 1]
-            if g == home:
-                column = jnp.where(inner > at, column, 0.0)
-            parts[g] = parts[g] - column * row_scaled
+    parts = [table[g * tile : (g + 1) * tile] for g in range(count)]
+    shape = (tile, 2 * size)
+    place = lax.broadcasted_iota(jnp.int32, shape, 0)
+
+    def spread(piece):
+        return jnp.broadcast_to(piece, shape)
+
     out = []
-    for g in range(size // tile):
-        scale = jnp.concatenate(scales[g * tile : (g + 1) * tile], axis=0)
-        out.append(parts[g][:, size:] * scale)
+    for b in range(count):
+        first = b * tile
+        columns = [
+            [spread(parts[g][:, first + t : first + t + 1]) for g in range(b, count)]
+            for t in range(tile)
+        ]
+        home = parts[b]
+        scales = jnp.ones(shape, f32)
+        for t in range(tile):
+            scale = lax.rsqrt(spread(columns[t][0][t : t + 1]))
+            scales = jnp.where(place == t, scale, scales)
+            factor = [column * scale for column in columns[t]]
+            factor[0] = jnp.where(place > t, factor[0], 0.0)
+            for u in range(t + 1, tile):
+                ahead = spread(columns[u][0][t : t + 1]) * scale
+                columns[u] = [c - f * ahead for c, f in zip(columns[u], factor)]
+            row = spread(home[t : t + 1]) * scale
+            home = home - factor[0] * row
+            for g in range(b + 1, count):
+                parts[g] = parts[g] - factor[g - b] * row
+        out.append((home * scales)[:, size:])
     return jnp.concatenate(out, axis=0)
 
 
@@ -129,6 +141,30 @@
     return pl.ds(pl.multiple_of((lane ^ d) * BLOCK, BLOCK), BLOCK)
 
 
+def prep_kernel(lanes, mean_ref, start_ref, *refs):
+    lists, (side_ref, mask_ref) = refs[:lanes], refs[lanes:]
+    lane = lax.axis_index("cols")
+    group = lax.axis_index("rows")
+    blocks = lax.axis_size("rows") * lanes
+    size = start_ref.shape[0]
+    codes = jnp.concatenate([ref[0:1] * blocks + ref[1:2] for ref in lists], axis=0)
+
+    def live(row_block, col_block):
+        hit = jnp.where(codes == row_block * blocks + col_block, 1.0, 0.0)
+        hit = jnp.max(jnp.max(hit, axis=1, keepdims=True), axis=0, keepdims=True)
+        return jnp.broadcast_to(hit, (1, BLOCK))
+
+    mine = group * lanes + lane
+    rows = [group * lanes + (lane ^ d) for d in range(lanes)]
+    masks = [live(row, mine) for row in rows] + [live(row, mine + lanes) for row in rows]
+    mask_ref[...] = jnp.concatenate(masks, axis=0)
+    back = [live(mine, row - lanes) for row in rows]
+    means = mean_ref[:, block_of(lane, 0)]
+    pad = jnp.zeros((side_ref.shape[0] - size - lanes - 1, BLOCK), f32)
+    start = start_ref[:, block_of(lane, 0)]
+    side_ref[...] = jnp.concatenate([start, means, *back, pad], axis=0).astype(bf16)
+
+
 def own_kernel(lanes, cells_ref, mean_ref, start_ref, unit_ref, weight_ref, product_ref):
     lane = lax.axis_index("cols")
     for d in range(lanes):
@@ -147,57 +183,37 @@
         product_ref[d] = jnp.dot(left, weights, preferred_element_type=f32)[:rows]
 
 
-def next_kernel(
-    lanes,
-    columns,
-    unit_ref,
-    cells_ref,
-    side_ref,
-    mean_ref,
-    start_ref,
-    own_ref,
-    *rest,
-):
-    lists, (weight_ref, mask_ref, *product_refs, back_ref) = rest[:lanes], rest[lanes:]
+def next_kernel(lanes, *refs):
+    unit_ref, cells_ref, side_ref, mean_ref, start_ref, own_ref, mask_ref, *outs = refs
+    weight_ref, keep_ref, core_ref, back_ref = outs
     lane = lax.axis_index("cols")
-    group = lax.axis_index("rows")
-    blocks = lax.axis_size("rows") * lanes
-    size = columns
-    listed = jnp.concatenate([ref[...] for ref in lists], axis=0)
-    here = [listed[4 * p : 4 * p + 1] * blocks + listed[4 * p + 1 : 4 * p + 2] for p in range(lanes)]
-    after = [
-        listed[4 * p + 2 : 4 * p + 3] * blocks + listed[4 * p + 3 : 4 * p + 4] for p in range(lanes)
-    ]
-    here = jnp.concatenate(here, axis=0)
-    after = jnp.concatenate(after, axis=0)
-
-    def live(codes, row_block, col_block):
-        hit = jnp.where(codes == row_block * blocks + col_block, 1.0, 0.0)
-        return jnp.max(jnp.max(hit, axis=1, keepdims=True), axis=0, keepdims=True)
-
-    eye = diagonal(BLOCK)
+    size = start_ref.shape[0]
     col_unit = unit_rows(cells_ref[...])
-    col_mean = upright(side_ref[size : size + 1, :].astype(f32), eye)
+    after = side_ref[size:, :].astype(f32)
+    col_mean = upright(after[0:1], diagonal(BLOCK))
     left = with_ones(side_ref[:size, :])
     rows = own_ref.shape[1]
     back = jnp.zeros((rows, BLOCK), f32)
     for d in range(lanes):
-        row_block = group * lanes + (lane ^ d)
-        own_live = live(here, row_block, group * lanes + lane)
-        next_live = live(here, row_block, (group + 1) * lanes + lane)
-        back_live = live(after, (group + 1) * lanes + lane, row_block)
-        for at, value in ((0, own_live), (1, next_live), (2, back_live)):
-            mask_ref[at * lanes + d : at * lanes + d + 1, :] = jnp.broadcast_to(
-                value, (1, mask_ref.shape[1])
-            )
         weights = affinity(col_unit, unit_ref[d], col_mean, mean_ref[:, block_of(lane, d)])
         weights = weights.astype(bf16)
         weight_ref[d] = weights
         product = jnp.dot(left, weights, preferred_element_type=f32)[:rows]
-        product_refs[d][...] = own_live * own_ref[d] + next_live * product
+        own = mask_ref[d : d + 1, :] * own_ref[d]
+        halves(d, keep_ref, core_ref)[...] = own + mask_ref[lanes + d : lanes + d + 1, :] * product
         narrow = with_ones(start_ref[:, block_of(lane, d)].astype(bf16))
-        back = back + back_live * nt(narrow, weights)[:rows]
+        back = back + after[1 + d : 2 + d] * nt(narrow, weights)[:rows]
     back_ref[...] = back
+
+
+def halves(d, keep_ref, core_ref):
+    return (core_ref if d % 2 else keep_ref).at[d // 2]
+
+
+def pair_kernel(keep_ref, came_ref, own_ref, *away_refs):
+    own_ref[...] = keep_ref[0] + came_ref[0]
+    for m, away_ref in enumerate(away_refs):
+        away_ref[...] = keep_ref[m + 1] + came_ref[m + 1]
 
 
 def smooth_kernel(size, *refs):
@@ -210,22 +226,20 @@
     degree_ref[...] = jnp.broadcast_to(degree, degree_ref.shape)
 
 
-def sweep_kernel(lanes, total, own_ref, weight_ref, mask_ref, next_ref, *rest):
-    blocks, (*product_refs, back_ref, gram_ref) = rest[:lanes], rest[lanes:]
+def sweep_kernel(lanes, total, own_ref, weight_ref, mask_ref, side_ref, next_ref, *rest):
+    blocks, (keep_ref, core_ref, back_ref, gram_ref) = rest[:lanes], rest[lanes:]
     size = next_ref.shape[0]
     own_left = pieces(blocks[0][...])
     next_left = pieces(next_ref[...])
+    back_masks = side_ref[size:, :].astype(f32)
     back = jnp.zeros((size, BLOCK), f32)
-
-    def mask(at, d):
-        return mask_ref[at * lanes + d : at * lanes + d + 1, :]
-
     for d in range(lanes):
         own = joined(jnp.dot(own_left, own_ref[d], preferred_element_type=f32), size)
         after = joined(jnp.dot(next_left, weight_ref[d], preferred_element_type=f32), size)
-        product_refs[d][...] = mask(0, d) * own + mask(1, d) * after
+        own = mask_ref[d : d + 1, :] * own
+        halves(d, keep_ref, core_ref)[...] = own + mask_ref[lanes + d : lanes + d + 1, :] * after
         left = own_left if d == 0 else pieces(blocks[d][...])
-        back = back + mask(2, d) * joined(nt(left, weight_ref[d]), size)
+        back = back + back_masks[1 + d : 2 + d] * joined(nt(left, weight_ref[d]), size)
     back_ref[...] = back
     gram_ref[...] = gram_of([block[...] for block in blocks], total)
 
@@ -238,12 +252,17 @@
     smooth_ref[...] = total / degree_ref[0:1, :]
 
 
-def first_solve_kernel(lanes, total, *refs):
-    grams, blocks, smooth_ref, gram_ref = refs[: -lanes - 2], refs[-lanes - 2 : -2], refs[-2], refs[-1]
+def factor_kernel(*refs):
+    *grams, inverse_ref = refs
     gram = grams[0][...]
     for part in grams[1:]:
         gram = gram + part[...]
-    inverse = inverse_factor(gram)
+    inverse_ref[...] = inverse_factor(gram)
+
+
+def first_solve_kernel(lanes, total, inverse_ref, *refs):
+    blocks, (smooth_ref, gram_ref) = refs[:lanes], refs[lanes:]
+    inverse = inverse_ref[...]
     solved = []
     for d in range(lanes):
         value = times(inverse, blocks[d][...])
@@ -284,21 +303,20 @@
     assert rows_here == lanes * BLOCK and lanes & (lanes - 1) == 0 and groups & (groups - 1) == 0
     wide = size + 8
 
-    first = lane * BLOCK
-    next_cells = shift(lax.dynamic_slice_in_dim(embeddings, first, BLOCK, 0), -1)
+    next_cells = shift(lax.dynamic_slice_in_dim(embeddings, lane * BLOCK, BLOCK, 0), -1)
     live = jnp.arange(slots, dtype=jnp.int32) < pair_count[0, 0]
     mine = jnp.stack([jnp.where(live, pair_rows[0, 0], -1), jnp.where(live, pair_cols[0, 0], -1)])
     mine = jnp.pad(mine, ((0, 0), (0, 128 - slots)), constant_values=-1)
-    lists = lane_swaps(jnp.concatenate([mine, shift(mine, -1)], axis=0))
-    side = jnp.concatenate(
-        [
-            lax.dynamic_slice_in_dim(start_block, first, BLOCK, 1).astype(bf16),
-            jnp.broadcast_to(lax.dynamic_slice_in_dim(knn_mean, first, BLOCK, 0)[None], (16, BLOCK)),
-        ],
-        axis=0,
+    mean = knn_mean.astype(f32)[None, :]
+    side, masks = call(
+        functools.partial(prep_kernel, lanes),
+        [((size + 16, BLOCK), bf16), ((2 * lanes, BLOCK), f32)],
+        mean,
+        start_block,
+        *lane_swaps(mine),
     )
     next_side = shift(side, -1)
-    mean = knn_mean.astype(f32)[None, :]
+    mean, masks = lax.optimization_barrier((mean, masks))
 
     unit, own_weights, own_product = call(
         functools.partial(own_kernel, lanes),
@@ -311,57 +329,70 @@
         mean,
         start_block,
     )
-    next_weights, masks, *products, back = call(
-        functools.partial(next_kernel, lanes, size),
-        [((lanes, BLOCK, BLOCK), bf16), ((16, BLOCK), f32)] + [((wide, BLOCK), f32)] * (lanes + 1),
+    next_weights, keep, core, back = call(
+        functools.partial(next_kernel, lanes),
+        [((lanes, BLOCK, BLOCK), bf16)]
+        + [((lanes // 2, wide, BLOCK), f32)] * 2
+        + [((wide, BLOCK), f32)],
         unit,
         next_cells,
         next_side,
         mean,
         start_block,
         own_product,
-        *lists,
-    )
-
-    def scattered(products, back):
-        came = [swap(products[d], "cols", d) for d in range(1, lanes)]
-        return [products[0], *came, shift(back, 1)]
+        masks,
+    )
+
+    def scattered(keep, core, back):
+        back = shift(back, 1)
+        rows = keep.shape[1]
+        own, *away = call(
+            pair_kernel, [((rows, BLOCK), f32)] * (lanes // 2), keep, swap(core, "cols", 1)
+        )
+        return [own, *(swap(part, "cols", 2 * m + 2) for m, part in enumerate(away)), back]
 
     smooth, degree = call(
         functools.partial(smooth_kernel, size),
         [((size, BLOCK), f32), ((8, BLOCK), f32)],
-        *scattered(products, back),
-    )
-
-    *products, back, gram = call(
+        *scattered(keep, core, back),
+    )
+
+    keep, core, back, gram = call(
         functools.partial(sweep_kernel, lanes, total),
-        [((size, BLOCK), f32)] * (lanes + 1) + [((size, size), f32)],
+        [((lanes // 2, size, BLOCK), f32)] * 2 + [((size, BLOCK), f32), ((size, size), f32)],
         own_weights,
         next_weights,
         masks,
+        next_side,
         shift(smooth, -1),
         *lane_swaps(smooth),
     )
-    (smooth,) = call(resmooth_kernel, [((size, BLOCK), f32)], degree, *scattered(products, back))
-
-    def stages(gram):
-        parts = [gram]
-        for offsets in row_stages(groups):
-            whole = sum(parts[1:], parts[0])
-            parts = [whole] + [swap(whole, "rows", offset) for offset in offsets]
-        return parts
-
+
+    def stage(parts, offsets):
+        whole = sum(parts[1:], parts[0])
+        return [whole] + [swap(whole, "rows", offset) for offset in offsets]
+
+    first, *others = row_stages(groups)
+    grams = stage([gram], first)
+    products = scattered(keep, core, back)
+    if others:
+        whole, *products = lax.optimization_barrier((sum(grams[1:], grams[0]), *products))
+        grams = [whole] + [swap(whole, "rows", offset) for offset in others[0]]
+    (smooth,) = call(resmooth_kernel, [((size, BLOCK), f32)], degree, *products)
+    for offsets in others[1:]:
+        grams = stage(grams, offsets)
+    (inverse,) = call(factor_kernel, [((size, size), f32)], *grams)
     smooth, gram = call(
         functools.partial(first_solve_kernel, lanes, total),
         [((lanes, size, BLOCK), f32), ((size, size), f32)],
-        *stages(gram),
+        inverse,
         *lane_swaps(smooth),
     )
+    grams = [gram]
+    for offsets in row_stages(groups):
+        grams = stage(grams, offsets)
     (vector,) = call(
-        functools.partial(last_solve_kernel, lanes),
-        [((size, rows_here), f32)],
-        smooth,
-        *stages(gram),
+        functools.partial(last_solve_kernel, lanes), [((size, rows_here), f32)], smooth, *grams
     )
     return vector
 

time: 92.9 us -> 74.7 us (0.80)
  waiting for transfers between devices: 43.3 us -> 29.7 us
  Pallas kernels: 17.4 us -> 10.3 us
  starting transfers between devices: 24.5 us -> 27.6 us
    ppermute x6 -> x5, waiting for transfers between devices: 14.2 us -> 6.53 us  [shift(): lax.ppermute(cells, 'rows', [(i, (i + step) % count) for i in range(count)])]
    pallas_call x7 -> x11, Pallas kernels: 17.4 us -> 10.3 us  [call(): pl.pallas_call(body, out_shape=[jax.ShapeDtypeStruct(shape, kind) for sha...]
    ppermute x23 -> x21, waiting for transfers between devices: 29.1 us -> 23.1 us  [swap(): return lax.ppermute(cells, axis, [(i, i ^ offset) for i in range(count)])]
    ppermute x23 -> x21, starting transfers between devices: 14.3 us -> 17 us  [swap(): return lax.ppermute(cells, axis, [(i, i ^ offset) for i in range(count)])]
    unnamed x4 -> x8, local copies, waits for them, and re-layouts: 2.54 us -> 3.49 us
    ppermute x6 -> x5, starting transfers between devices: 10.2 us -> 10.6 us  [shift(): lax.ppermute(cells, 'rows', [(i, (i + step) % count) for i in range(count)])]
  transfers between devices with their start and end apart: 29 -> 26, of which waited for: 16 -> 15; matrix products, arithmetic and copies ran while one was open for 3% -> 2% of each run, Pallas kernels for 2% -> 5%
where the time goes in v2:
time: 74.7 us; the launch traced here: 74.4 us
  waiting for transfers between devices  29.7 us (40%)
  starting transfers between devices  27.6 us (37%)
  Pallas kernels  10.3 us (14%)
  local copies, waits for them, and re-layouts  4.62 us (6%)
  other arithmetic  1.38 us (2%)
  between operations  0.77 us (1%)
    ppermute x21, waiting for transfers between devices, swap(): return lax.ppermute(cells, axis, [(i, i ^ offset) for i in range(count)])  23.1 us
    ppermute x21, starting transfers between devices, swap(): return lax.ppermute(cells, axis, [(i, i ^ offset) for i in range(count)])  17 us
    ppermute x5, starting transfers between devices, shift(): lax.ppermute(cells, 'rows', [(i, (i + step) % count) for i in range(count)])  10.6 us
    pallas_call x11, Pallas kernels, call(): pl.pallas_call(body, out_shape=[jax.ShapeDtypeStruct(shape, kind) for sha...  10.3 us
    ppermute x5, waiting for transfers between devices, shift(): lax.ppermute(cells, 'rows', [(i, (i + step) % count) for i in range(count)])  6.53 us
    unnamed x8, local copies, waits for them, and re-layouts  3.49 us
  transfers between devices with their start and end apart: 26, of which 15 were waited for; matrix products, arithmetic and copies ran while one was open for 2% of the time, Pallas kernels for 5%

profile of v2, /device:TPU:0, one launch (start us, length us, event | category | flops | bytes accessed | tf_op | source)
XLA Modules:
  0.0 74.4 jit_solution(15035474552880038219)
XLA Ops:
  0.0 1.1 %constant_dynamic-slice_fusion = bf16[256,1024]{1,0:T(8,128)(2,1)S(1)} fusion(bf16[1024,1024]{1,0:T(8,128)(2,1)} %cells_ref.1, s32[]{:T(128)S(6)} %select_n.26), kind=kLoop, calls=%fused_computation.3 | loop fusion | bytes 1048580 | tf_op jit(solution)/shard_map/dynamic_slice | solution.py:306
  1.1 6.1 %collective-permute-start.3 = (bf16[256,1024]{1,0:T(8,128)(2,1)S(1)}, bf16[256,1024]{1,0:T(8,128)(2,1)S(1)}, u32[]{:S(2)}, u32[]{:S(2)}) collective-permute-start(bf16[256,1024]{1,0:T(8,128)(2,1)S(1)} %constant_dynamic-slice_fusion), channel_id=1, source_target_pairs={{0,28},{4,0},{8,4},{12,8},{16,12},{20,16},{24,20},{28,24},{1,29},{... | collective-permute-start | bytes 1572872 | tf_op jit(solution)/shard_map/ppermute | solution.py:24
  7.8 0.7 compare_select_fusion
  8.5 0.7 collective-permute-start.2
  9.3 0.9 %collective-permute-start.1 = (s32[2,128]{1,0:T(2,128)S(1)}, s32[2,128]{1,0:T(2,128)S(1)}, u32[]{:S(2)}, u32[]{:S(2)}) collective-permute-start(s32[2,128]{1,0:T(2,128)S(1)} %pad.4.refs_0_), channel_id=1, source_target_pairs={{0,2},{1,3},{2,0},{3,1},{4,6},{5,7},{6,4},{7,5},{8,10},{9,11},{10,... | collective-permute-start | bytes 3080 | tf_op jit(solution)/shard_map/ppermute | solution.py:29
  10.2 0.3 collective-permute-start
  10.5 0.7 broadcast_in_dim.13
  11.1 0.4 collective-permute-done.2.refs_3_
  11.6 1.2 %collective-permute-done.1.refs_2_ = s32[2,128]{1,0:T(2,128)S(1)} collective-permute-done((s32[2,128]{1,0:T(2,128)S(1)}, s32[2,128]{1,0:T(2,128)S(1)}, u32[]{:S(2)}, u32[]{:S(2)}) %collective-permute-start.1) | collective-permute-done | bytes 1056 | tf_op jit(solution)/shard_map/ppermute | solution.py:29
  12.8 0.9 %copy-done.1 = f32[64,1024]{1,0:T(8,128)S(1)} copy-done((f32[64,1024]{1,0:T(8,128)S(1)}, f32[64,1024]{1,0:T(8,128)}, u32[]{:S(2)}) %copy-start.1) | copy-done | bytes 262168
  13.8 0.1 shard_map.64
  13.9 0.6 collective-permute-start.4
  14.4 1.6 %copy-done = bf16[1024,1024]{1,0:T(8,128)(2,1)S(1)} copy-done((bf16[1024,1024]{1,0:T(8,128)(2,1)S(1)}, bf16[1024,1024]{1,0:T(8,128)(2,1)}, u32[]{:S(2)}) %copy-start) | copy-done | bytes 2097176
  16.0 0.9 %copy-done.2 = f32[64,1024]{1,0:T(8,128)S(1)} copy-done((f32[64,1024]{1,0:T(8,128)S(1)}, f32[64,1024]{1,0:T(8,128)}, u32[]{:S(2)}) %copy-start.2) | copy-done | bytes 262168
  17.0 1.7 %shard_map.65 = (bf16[4,256,1024]{2,1,0:T(8,128)(2,1)S(1)}, bf16[4,256,256]{2,1,0:T(8,128)(2,1)S(1)}, f32[4,72,256]{2,1,0:T(8,128)S(1)}) custom-call(bf16[1024,1024]{1,0:T(8,128)(2,1)S(1)} %copy-done, f32[1,1024]{1,0:T(1,128)S(1)} %bitcast.8, f32[64,1024]{1,0:T(8,128)S(1)} %copy-done.2), custom_call_target="tpu_custom_call" | custom-call | tf_op jit(solution)/shard_map/pallas_call | solution.py:286
  18.7 0.5 collective-permute-done.4.refs_2_.side_ref
  19.2 2.0 %shard_map.66 = (bf16[4,256,256]{2,1,0:T(8,128)(2,1)S(1)}, f32[2,72,256]{2,1,0:T(8,128)S(1)}, f32[2,72,256]{2,1,0:T(8,128)S(1)}, f32[72,256]{1,0:T(8,128)S(1)}) custom-call(bf16[4,256,1024]{2,1,0:T(8,128)(2,1)S(1)} %get-tuple-element.35.refs_0_, bf16[256,1024]{1,0:T(8,128)(2,1)S(1)} %collective-permute-done.3.refs_1_, ...), custom_call_target="tpu_custom_call" | custom-call | tf_op jit(solution)/shard_map/pallas_call | solution.py:286
  21.3 0.1 collective-permute-start.5
  21.4 1.1 %collective-permute-start.7 = (f32[72,256]{1,0:T(8,128)S(1)}, f32[72,256]{1,0:T(8,128)S(1)}, u32[]{:S(2)}, u32[]{:S(2)}) collective-permute-start(f32[72,256]{1,0:T(8,128)S(1)} %get-tuple-element.44), channel_id=1, source_target_pairs={{0,4},{4,8},{8,12},{12,16},{16,20},{20,24},{24,28},{28,0},{1,5},{5... | collective-permute-start | bytes 221192 | tf_op jit(solution)/shard_map/ppermute | solution.py:24
  22.5 0.3 collective-permute-done.5.came_ref
  22.8 1.6 %collective-permute-start.6 = (f32[72,256]{1,0:T(8,128)S(1)}, f32[72,256]{1,0:T(8,128)S(1)}, u32[]{:S(2)}, u32[]{:S(2)}) collective-permute-start(f32[72,256]{1,0:T(8,128)S(1)} %get-tuple-element.43), channel_id=1, source_target_pairs={{0,2},{1,3},{2,0},{3,1},{4,6},{5,7},{6,4},{7,5},{8,10},{9,11},{10,... | collective-permute-start | bytes 221192 | tf_op jit(solution)/shard_map/ppermute | solution.py:29
  24.3 5.2 %collective-permute-done.7.refs_2_ = f32[72,256]{1,0:T(8,128)S(1)} collective-permute-done((f32[72,256]{1,0:T(8,128)S(1)}, f32[72,256]{1,0:T(8,128)S(1)}, u32[]{:S(2)}, u32[]{:S(2)}) %collective-permute-start.7) | collective-permute-done | bytes 73760 | tf_op jit(solution)/shard_map/ppermute | solution.py:24
  29.5 1.0 %collective-permute-start.11 = (f32[64,256]{1,0:T(8,128)S(1)}, f32[64,256]{1,0:T(8,128)S(1)}, u32[]{:S(2)}, u32[]{:S(2)}) collective-permute-start(f32[64,256]{1,0:T(8,128)S(1)} %get-tuple-element.45.rest_0_), channel_id=1, source_target_pairs={{0,3},{1,2},{2,1},{3,0},{4,7},{5,6},{6,5},{7,4},{8,11},{9,10},{10,... | collective-permute-start | bytes 196616 | tf_op jit(solution)/shard_map/ppermute | solution.py:29
  30.5 0.6 collective-permute-start.10
  31.1 0.3 collective-permute-start.9
  31.4 2.9 %collective-permute-start.8 = (f32[64,256]{1,0:T(8,128)S(1)}, f32[64,256]{1,0:T(8,128)S(1)}, u32[]{:S(2)}, u32[]{:S(2)}) collective-permute-start(f32[64,256]{1,0:T(8,128)S(1)} %get-tuple-element.45.rest_0_), channel_id=1, source_target_pairs={{0,28},{4,0},{8,4},{12,8},{16,12},{20,16},{24,20},{28,24},{1,29},{... | collective-permute-start | bytes 196616 | tf_op jit(solution)/shard_map/ppermute | solution.py:24
  34.3 1.1 %collective-permute-done.10.rest_2_ = f32[64,256]{1,0:T(8,128)S(1)} collective-permute-done((f32[64,256]{1,0:T(8,128)S(1)}, f32[64,256]{1,0:T(8,128)S(1)}, u32[]{:S(2)}, u32[]{:S(2)}) %collective-permute-start.10) | collective-permute-done | bytes 65568 | tf_op jit(solution)/shard_map/ppermute | solution.py:29
  35.4 0.8 %collective-permute-done.8.next_ref = f32[64,256]{1,0:T(8,128)S(1)} collective-permute-done((f32[64,256]{1,0:T(8,128)S(1)}, f32[64,256]{1,0:T(8,128)S(1)}, u32[]{:S(2)}, u32[]{:S(2)}) %collective-permute-start.8) | collective-permute-done | bytes 65568 | tf_op jit(solution)/shard_map/ppermute | solution.py:24
  36.2 0.7 shard_map.69
  37.1 1.3 %collective-permute-done.13.came_ref = f32[2,64,256]{2,1,0:T(8,128)S(1)} collective-permute-done((f32[2,64,256]{2,1,0:T(8,128)S(1)}, f32[2,64,256]{2,1,0:T(8,128)S(1)}, u32[]{:S(2)}, u32[]{:S(2)}) %collective-permute-start.13) | collective-permute-done | bytes 131104 | tf_op jit(solution)/shard_map/ppermute | solution.py:29
  38.4 1.6 %collective-permute-start.14 = (f32[64,256]{1,0:T(8,128)S(1)}, f32[64,256]{1,0:T(8,128)S(1)}, u32[]{:S(2)}, u32[]{:S(2)}) collective-permute-start(f32[64,256]{1,0:T(8,128)S(1)} %get-tuple-element.50), channel_id=1, source_target_pairs={{0,2},{1,3},{2,0},{3,1},{4,6},{5,7},{6,4},{7,5},{8,10},{9,11},{10,... | collective-permute-start | bytes 196616 | tf_op jit(solution)/shard_map/ppermute | solution.py:29
  39.9 5.2 %collective-permute-done.12 = f32[64,64]{1,0:T(8,128)S(1)} collective-permute-done((f32[64,64]{1,0:T(8,128)S(1)}, f32[64,64]{1,0:T(8,128)S(1)}, u32[]{:S(2)}, u32[]{:S(2)}) %collective-permute-start.12) | collective-permute-done | bytes 16416 | tf_op jit(solution)/shard_map/ppermute | solution.py:29
  45.2 0.7 collective-permute-start.21
  45.9 0.6 collective-permute-start.20
  46.5 0.7 collective-permute-start.19
  47.2 3.0 %collective-permute-start.18 = (f32[64,64]{1,0:T(8,128)S(1)}, f32[64,64]{1,0:T(8,128)S(1)}, u32[]{:S(2)}, u32[]{:S(2)}) collective-permute-start(f32[64,64]{1,0:T(8,128)S(1)} %add.12.refs_0_), channel_id=1, source_target_pairs={{0,24},{4,28},{8,16},{12,20},{16,8},{20,12},{24,0},{28,4},{1,25},{... | collective-permute-start | bytes 49160 | tf_op jit(solution)/shard_map/ppermute | solution.py:29
  50.2 2.7 %collective-permute-done.18.refs_3_ = f32[64,64]{1,0:T(8,128)S(1)} collective-permute-done((f32[64,64]{1,0:T(8,128)S(1)}, f32[64,64]{1,0:T(8,128)S(1)}, u32[]{:S(2)}, u32[]{:S(2)}) %collective-permute-start.18) | collective-permute-done | bytes 16416 | tf_op jit(solution)/shard_map/ppermute | solution.py:29
  52.9 2.1 %collective-permute-done.17.refs_2_ = f32[64,64]{1,0:T(8,128)S(1)} collective-permute-done((f32[64,64]{1,0:T(8,128)S(1)}, f32[64,64]{1,0:T(8,128)S(1)}, u32[]{:S(2)}, u32[]{:S(2)}) %collective-permute-start.17) | collective-permute-done | bytes 16416 | tf_op jit(solution)/shard_map/ppermute | solution.py:29
  55.0 1.8 %collective-permute-done.16.refs_1_ = f32[64,64]{1,0:T(8,128)S(1)} collective-permute-done((f32[64,64]{1,0:T(8,128)S(1)}, f32[64,64]{1,0:T(8,128)S(1)}, u32[]{:S(2)}, u32[]{:S(2)}) %collective-permute-start.16) | collective-permute-done | bytes 16416 | tf_op jit(solution)/shard_map/ppermute | solution.py:29
  56.8 1.9 %shard_map.71.inverse_ref = f32[64,64]{1,0:T(8,128)S(1)} custom-call(f32[64,64]{1,0:T(8,128)S(1)} %add.12.refs_0_, f32[64,64]{1,0:T(8,128)S(1)} %collective-permute-done.16.refs_1_, f32[64,64]{1,0:T(8,128)S(1)} %collective-permute-done.17.refs_2_, f32[64,64]{1,0:T(8,128)S(1)} %collective-permute-done.18.refs_3_), custom_call_target="tpu_custom_call" | custom-call | tf_op jit(solution)/shard_map/pallas_call | solution.py:286
  58.7 0.8 %shard_map.73 = (f32[4,64,256]{2,1,0:T(8,128)S(1)}, f32[64,64]{1,0:T(8,128)S(1)}) custom-call(f32[64,64]{1,0:T(8,128)S(1)} %shard_map.71.inverse_ref, f32[64,256]{1,0:T(8,128)S(1)} %shard_map.72.refs_0_, f32[64,256]{1,0:T(8,128)S(1)} %collective-permute-done.19.refs_1_, f32[64,256]{1,0:T(8,128)S(1)} %collective-permute-done.20.refs_2_, ...), custom_call_target="tpu_custom_call" | custom-call | tf_op jit(solution)/shard_map/pallas_call | solution.py:286
  59.5 0.5 collective-permute-start.22
  60.1 3.4 %collective-permute-done.22 = f32[64,64]{1,0:T(8,128)S(1)} collective-permute-done((f32[64,64]{1,0:T(8,128)S(1)}, f32[64,64]{1,0:T(8,128)S(1)}, u32[]{:S(2)}, u32[]{:S(2)}) %collective-permute-start.22) | collective-permute-done | bytes 16416 | tf_op jit(solution)/shard_map/ppermute | solution.py:29
  63.5 3.1 %collective-permute-start.25 = (f32[64,64]{1,0:T(8,128)S(1)}, f32[64,64]{1,0:T(8,128)S(1)}, u32[]{:S(2)}, u32[]{:S(2)}) collective-permute-start(f32[64,64]{1,0:T(8,128)S(1)} %add.13.refs_0_), channel_id=1, source_target_pairs={{0,24},{4,28},{8,16},{12,20},{16,8},{20,12},{24,0},{28,4},{1,25},{... | collective-permute-start | bytes 49160 | tf_op jit(solution)/shard_map/ppermute | solution.py:29
  66.6 1.3 %collective-permute-start.23 = (f32[64,64]{1,0:T(8,128)S(1)}, f32[64,64]{1,0:T(8,128)S(1)}, u32[]{:S(2)}, u32[]{:S(2)}) collective-permute-start(f32[64,64]{1,0:T(8,128)S(1)} %add.13.refs_0_), channel_id=1, source_target_pairs={{0,8},{4,12},{8,0},{12,4},{16,24},{20,28},{24,16},{28,20},{1,9},{5... | collective-permute-start | bytes 49160 | tf_op jit(solution)/shard_map/ppermute | solution.py:29
  67.9 1.3 %collective-permute-done.25.refs_3_ = f32[64,64]{1,0:T(8,128)S(1)} collective-permute-done((f32[64,64]{1,0:T(8,128)S(1)}, f32[64,64]{1,0:T(8,128)S(1)}, u32[]{:S(2)}, u32[]{:S(2)}) %collective-permute-start.25) | collective-permute-done | bytes 16416 | tf_op jit(solution)/shard_map/ppermute | solution.py:29
  69.2 2.2 %collective-permute-done.24.refs_2_ = f32[64,64]{1,0:T(8,128)S(1)} collective-permute-done((f32[64,64]{1,0:T(8,128)S(1)}, f32[64,64]{1,0:T(8,128)S(1)}, u32[]{:S(2)}, u32[]{:S(2)}) %collective-permute-start.24) | collective-permute-done | bytes 16416 | tf_op jit(solution)/shard_map/ppermute | solution.py:29
  71.4 2.9 %shard_map.74 = f32[64,1024]{1,0:T(8,128)} custom-call(f32[4,64,256]{2,1,0:T(8,128)S(1)} %get-tuple-element.57.smooth_ref, f32[64,64]{1,0:T(8,128)S(1)} %add.13.refs_0_, f32[64,64]{1,0:T(8,128)S(1)} %collective-permute-done.23.refs_1_, f32[64,64]{1,0:T(8,128)S(1)} %collective-permute-done.24.refs_2_, f32[64,64]{1,0:T(8,128)S(1)} %collective-permute-done.25.refs_3_), custom_call_target="tpu_custom_call" | custom-call | tf_op jit(solution)/shard_map/pallas_call | solution.py:286
  (30 shorter events, 0.3 us)
Async XLA Ops:
  0.0 19.2 %copy-start.3 = (f32[64,1024]{1,0:T(8,128)S(1)}, f32[64,1024]{1,0:T(8,128)}, u32[]{:S(2)}) copy-start(f32[64,1024]{1,0:T(8,128)} %refs_4_.1) | copy-start | bytes 786436
  1.1 18.1 %collective-permute-start.3 = (bf16[256,1024]{1,0:T(8,128)(2,1)S(1)}, bf16[256,1024]{1,0:T(8,128)(2,1)S(1)}, u32[]{:S(2)}, u32[]{:S(2)}) collective-permute-start(bf16[256,1024]{1,0:T(8,128)(2,1)S(1)} %constant_dynamic-slice_fusion), channel_id=1, source_target_pairs={{0,28},{4,0},{8,4},{12,8},{16,12},{20,16},{24,20},{28,24},{1,29},{... | collective-permute-start | bytes 1572872 | tf_op jit(solution)/shard_map/ppermute | solution.py:24
  8.5 3.1 %collective-permute-start.2 = (s32[2,128]{1,0:T(2,128)S(1)}, s32[2,128]{1,0:T(2,128)S(1)}, u32[]{:S(2)}, u32[]{:S(2)}) collective-permute-start(s32[2,128]{1,0:T(2,128)S(1)} %pad.4.refs_0_), channel_id=1, source_target_pairs={{0,3},{1,2},{2,1},{3,0},{4,7},{5,6},{6,5},{7,4},{8,11},{9,10},{10,... | collective-permute-start | bytes 3080 | tf_op jit(solution)/shard_map/ppermute | solution.py:29
  9.3 3.6 %collective-permute-start.1 = (s32[2,128]{1,0:T(2,128)S(1)}, s32[2,128]{1,0:T(2,128)S(1)}, u32[]{:S(2)}, u32[]{:S(2)}) collective-permute-start(s32[2,128]{1,0:T(2,128)S(1)} %pad.4.refs_0_), channel_id=1, source_target_pairs={{0,2},{1,3},{2,0},{3,1},{4,6},{5,7},{6,4},{7,5},{8,10},{9,11},{10,... | collective-permute-start | bytes 3080 | tf_op jit(solution)/shard_map/ppermute | solution.py:29
  10.2 2.7 %collective-permute-start = (s32[2,128]{1,0:T(2,128)S(1)}, s32[2,128]{1,0:T(2,128)S(1)}, u32[]{:S(2)}, u32[]{:S(2)}) collective-permute-start(s32[2,128]{1,0:T(2,128)S(1)} %pad.4.refs_0_), channel_id=1, source_target_pairs={{0,1},{1,0},{2,3},{3,2},{4,5},{5,4},{6,7},{7,6},{8,9},{9,8},{10,11... | collective-permute-start | bytes 3080 | tf_op jit(solution)/shard_map/ppermute | solution.py:29
  12.8 1.0 %copy-start.1 = (f32[64,1024]{1,0:T(8,128)S(1)}, f32[64,1024]{1,0:T(8,128)}, u32[]{:S(2)}) copy-start(f32[64,1024]{1,0:T(8,128)} %refs_4_.1) | copy-start | bytes 786436
  13.9 5.4 %collective-permute-start.4 = (bf16[80,256]{1,0:T(8,128)(2,1)S(1)}, bf16[80,256]{1,0:T(8,128)(2,1)S(1)}, u32[]{:S(2)}, u32[]{:S(2)}) collective-permute-start(bf16[80,256]{1,0:T(8,128)(2,1)S(1)} %get-tuple-element.36), channel_id=1, source_target_pairs={{0,28},{4,0},{8,4},{12,8},{16,12},{20,16},{24,20},{28,24},{1,29},{... | collective-permute-start | bytes 122888 | tf_op jit(solution)/shard_map/ppermute | solution.py:24
  14.4 1.6 %copy-start = (bf16[1024,1024]{1,0:T(8,128)(2,1)S(1)}, bf16[1024,1024]{1,0:T(8,128)(2,1)}, u32[]{:S(2)}) copy-start(bf16[1024,1024]{1,0:T(8,128)(2,1)} %cells_ref.1) | copy-start | bytes 6291460
  16.0 0.9 %copy-start.2 = (f32[64,1024]{1,0:T(8,128)S(1)}, f32[64,1024]{1,0:T(8,128)}, u32[]{:S(2)}) copy-start(f32[64,1024]{1,0:T(8,128)} %refs_4_.1) | copy-start | bytes 786436
  21.3 1.4 %collective-permute-start.5 = (f32[2,72,256]{2,1,0:T(8,128)S(1)}, f32[2,72,256]{2,1,0:T(8,128)S(1)}, u32[]{:S(2)}, u32[]{:S(2)}) collective-permute-start(f32[2,72,256]{2,1,0:T(8,128)S(1)} %get-tuple-element.41), channel_id=1, source_target_pairs={{0,1},{1,0},{2,3},{3,2},{4,5},{5,4},{6,7},{7,6},{8,9},{9,8},{10,11... | collective-permute-start | bytes 442376 | tf_op jit(solution)/shard_map/ppermute | solution.py:29
  21.4 8.1 %collective-permute-start.7 = (f32[72,256]{1,0:T(8,128)S(1)}, f32[72,256]{1,0:T(8,128)S(1)}, u32[]{:S(2)}, u32[]{:S(2)}) collective-permute-start(f32[72,256]{1,0:T(8,128)S(1)} %get-tuple-element.44), channel_id=1, source_target_pairs={{0,4},{4,8},{8,12},{12,16},{16,20},{20,24},{24,28},{28,0},{1,5},{5... | collective-permute-start | bytes 221192 | tf_op jit(solution)/shard_map/ppermute | solution.py:24
  22.8 6.7 %collective-permute-start.6 = (f32[72,256]{1,0:T(8,128)S(1)}, f32[72,256]{1,0:T(8,128)S(1)}, u32[]{:S(2)}, u32[]{:S(2)}) collective-permute-start(f32[72,256]{1,0:T(8,128)S(1)} %get-tuple-element.43), channel_id=1, source_target_pairs={{0,2},{1,3},{2,0},{3,1},{4,6},{5,7},{6,4},{7,5},{8,10},{9,11},{10,... | collective-permute-start | bytes 221192 | tf_op jit(solution)/shard_map/ppermute | solution.py:29
  29.5 4.8 %collective-permute-start.11 = (f32[64,256]{1,0:T(8,128)S(1)}, f32[64,256]{1,0:T(8,128)S(1)}, u32[]{:S(2)}, u32[]{:S(2)}) collective-permute-start(f32[64,256]{1,0:T(8,128)S(1)} %get-tuple-element.45.rest_0_), channel_id=1, source_target_pairs={{0,3},{1,2},{2,1},{3,0},{4,7},{5,6},{6,5},{7,4},{8,11},{9,10},{10,... | collective-permute-start | bytes 196616 | tf_op jit(solution)/shard_map/ppermute | solution.py:29
  30.5 4.8 %collective-permute-start.10 = (f32[64,256]{1,0:T(8,128)S(1)}, f32[64,256]{1,0:T(8,128)S(1)}, u32[]{:S(2)}, u32[]{:S(2)}) collective-permute-start(f32[64,256]{1,0:T(8,128)S(1)} %get-tuple-element.45.rest_0_), channel_id=1, source_target_pairs={{0,2},{1,3},{2,0},{3,1},{4,6},{5,7},{6,4},{7,5},{8,10},{9,11},{10,... | collective-permute-start | bytes 196616 | tf_op jit(solution)/shard_map/ppermute | solution.py:29
  31.1 4.2 %collective-permute-start.9 = (f32[64,256]{1,0:T(8,128)S(1)}, f32[64,256]{1,0:T(8,128)S(1)}, u32[]{:S(2)}, u32[]{:S(2)}) collective-permute-start(f32[64,256]{1,0:T(8,128)S(1)} %get-tuple-element.45.rest_0_), channel_id=1, source_target_pairs={{0,1},{1,0},{2,3},{3,2},{4,5},{5,4},{6,7},{7,6},{8,9},{9,8},{10,11... | collective-permute-start | bytes 196616 | tf_op jit(solution)/shard_map/ppermute | solution.py:29
  31.4 4.8 %collective-permute-start.8 = (f32[64,256]{1,0:T(8,128)S(1)}, f32[64,256]{1,0:T(8,128)S(1)}, u32[]{:S(2)}, u32[]{:S(2)}) collective-permute-start(f32[64,256]{1,0:T(8,128)S(1)} %get-tuple-element.45.rest_0_), channel_id=1, source_target_pairs={{0,28},{4,0},{8,4},{12,8},{16,12},{20,16},{24,20},{28,24},{1,29},{... | collective-permute-start | bytes 196616 | tf_op jit(solution)/shard_map/ppermute | solution.py:24
  36.9 1.4 %collective-permute-start.13 = (f32[2,64,256]{2,1,0:T(8,128)S(1)}, f32[2,64,256]{2,1,0:T(8,128)S(1)}, u32[]{:S(2)}, u32[]{:S(2)}) collective-permute-start(f32[2,64,256]{2,1,0:T(8,128)S(1)} %get-tuple-element.48), channel_id=1, source_target_pairs={{0,1},{1,0},{2,3},{3,2},{4,5},{5,4},{6,7},{7,6},{8,9},{9,8},{10,11... | collective-permute-start | bytes 393224 | tf_op jit(solution)/shard_map/ppermute | solution.py:29
  37.0 8.2 %collective-permute-start.15 = (f32[64,256]{1,0:T(8,128)S(1)}, f32[64,256]{1,0:T(8,128)S(1)}, u32[]{:S(2)}, u32[]{:S(2)}) collective-permute-start(f32[64,256]{1,0:T(8,128)S(1)} %get-tuple-element.51), channel_id=1, source_target_pairs={{0,4},{4,8},{8,12},{12,16},{16,20},{20,24},{24,28},{28,0},{1,5},{5... | collective-permute-start | bytes 196616 | tf_op jit(solution)/shard_map/ppermute | solution.py:24
  38.4 6.8 %collective-permute-start.14 = (f32[64,256]{1,0:T(8,128)S(1)}, f32[64,256]{1,0:T(8,128)S(1)}, u32[]{:S(2)}, u32[]{:S(2)}) collective-permute-start(f32[64,256]{1,0:T(8,128)S(1)} %get-tuple-element.50), channel_id=1, source_target_pairs={{0,2},{1,3},{2,0},{3,1},{4,6},{5,7},{6,4},{7,5},{8,10},{9,11},{10,... | collective-permute-start | bytes 196616 | tf_op jit(solution)/shard_map/ppermute | solution.py:29
  39.9 5.2 %collective-permute-start.12 = (f32[64,64]{1,0:T(8,128)S(1)}, f32[64,64]{1,0:T(8,128)S(1)}, u32[]{:S(2)}, u32[]{:S(2)}) collective-permute-start(f32[64,64]{1,0:T(8,128)S(1)} %get-tuple-element.46), channel_id=1, source_target_pairs={{0,4},{4,0},{8,12},{12,8},{16,20},{20,16},{24,28},{28,24},{1,5},{5... | collective-permute-start | bytes 49160 | tf_op jit(solution)/shard_map/ppermute | solution.py:29
  45.2 13.4 %collective-permute-start.21 = (f32[64,256]{1,0:T(8,128)S(1)}, f32[64,256]{1,0:T(8,128)S(1)}, u32[]{:S(2)}, u32[]{:S(2)}) collective-permute-start(f32[64,256]{1,0:T(8,128)S(1)} %shard_map.72.refs_0_), channel_id=1, source_target_pairs={{0,3},{1,2},{2,1},{3,0},{4,7},{5,6},{6,5},{7,4},{8,11},{9,10},{10,... | collective-permute-start | bytes 196616 | tf_op jit(solution)/shard_map/ppermute | solution.py:29
  45.9 12.8 %collective-permute-start.20 = (f32[64,256]{1,0:T(8,128)S(1)}, f32[64,256]{1,0:T(8,128)S(1)}, u32[]{:S(2)}, u32[]{:S(2)}) collective-permute-start(f32[64,256]{1,0:T(8,128)S(1)} %shard_map.72.refs_0_), channel_id=1, source_target_pairs={{0,2},{1,3},{2,0},{3,1},{4,6},{5,7},{6,4},{7,5},{8,10},{9,11},{10,... | collective-permute-start | bytes 196616 | tf_op jit(solution)/shard_map/ppermute | solution.py:29
  46.5 12.2 %collective-permute-start.19 = (f32[64,256]{1,0:T(8,128)S(1)}, f32[64,256]{1,0:T(8,128)S(1)}, u32[]{:S(2)}, u32[]{:S(2)}) collective-permute-start(f32[64,256]{1,0:T(8,128)S(1)} %shard_map.72.refs_0_), channel_id=1, source_target_pairs={{0,1},{1,0},{2,3},{3,2},{4,5},{5,4},{6,7},{7,6},{8,9},{9,8},{10,11... | collective-permute-start | bytes 196616 | tf_op jit(solution)/shard_map/ppermute | solution.py:29
  47.2 5.7 %collective-permute-start.18 = (f32[64,64]{1,0:T(8,128)S(1)}, f32[64,64]{1,0:T(8,128)S(1)}, u32[]{:S(2)}, u32[]{:S(2)}) collective-permute-start(f32[64,64]{1,0:T(8,128)S(1)} %add.12.refs_0_), channel_id=1, source_target_pairs={{0,24},{4,28},{8,16},{12,20},{16,8},{20,12},{24,0},{28,4},{1,25},{... | collective-permute-start | bytes 49160 | tf_op jit(solution)/shard_map/ppermute | solution.py:29
  50.2 4.8 %collective-permute-start.17 = (f32[64,64]{1,0:T(8,128)S(1)}, f32[64,64]{1,0:T(8,128)S(1)}, u32[]{:S(2)}, u32[]{:S(2)}) collective-permute-start(f32[64,64]{1,0:T(8,128)S(1)} %add.12.refs_0_), channel_id=1, source_target_pairs={{0,16},{4,20},{8,24},{12,28},{16,0},{20,4},{24,8},{28,12},{1,17},{... | collective-permute-start | bytes 49160 | tf_op jit(solution)/shard_map/ppermute | solution.py:29
  52.9 3.9 %collective-permute-start.16 = (f32[64,64]{1,0:T(8,128)S(1)}, f32[64,64]{1,0:T(8,128)S(1)}, u32[]{:S(2)}, u32[]{:S(2)}) collective-permute-start(f32[64,64]{1,0:T(8,128)S(1)} %add.12.refs_0_), channel_id=1, source_target_pairs={{0,8},{4,12},{8,0},{12,4},{16,24},{20,28},{24,16},{28,20},{1,9},{5... | collective-permute-start | bytes 49160 | tf_op jit(solution)/shard_map/ppermute | solution.py:29
  59.5 4.0 %collective-permute-start.22 = (f32[64,64]{1,0:T(8,128)S(1)}, f32[64,64]{1,0:T(8,128)S(1)}, u32[]{:S(2)}, u32[]{:S(2)}) collective-permute-start(f32[64,64]{1,0:T(8,128)S(1)} %get-tuple-element.58), channel_id=1, source_target_pairs={{0,4},{4,0},{8,12},{12,8},{16,20},{20,16},{24,28},{28,24},{1,5},{5... | collective-permute-start | bytes 49160 | tf_op jit(solution)/shard_map/ppermute | solution.py:29
  63.5 5.7 %collective-permute-start.25 = (f32[64,64]{1,0:T(8,128)S(1)}, f32[64,64]{1,0:T(8,128)S(1)}, u32[]{:S(2)}, u32[]{:S(2)}) collective-permute-start(f32[64,64]{1,0:T(8,128)S(1)} %add.13.refs_0_), channel_id=1, source_target_pairs={{0,24},{4,28},{8,16},{12,20},{16,8},{20,12},{24,0},{28,4},{1,25},{... | collective-permute-start | bytes 49160 | tf_op jit(solution)/shard_map/ppermute | solution.py:29
  66.6 4.8 %collective-permute-start.24 = (f32[64,64]{1,0:T(8,128)S(1)}, f32[64,64]{1,0:T(8,128)S(1)}, u32[]{:S(2)}, u32[]{:S(2)}) collective-permute-start(f32[64,64]{1,0:T(8,128)S(1)} %add.13.refs_0_), channel_id=1, source_target_pairs={{0,16},{4,20},{8,24},{12,28},{16,0},{20,4},{24,8},{28,12},{1,17},{... | collective-permute-start | bytes 49160 | tf_op jit(solution)/shard_map/ppermute | solution.py:29
  66.6 4.8 %collective-permute-start.23 = (f32[64,64]{1,0:T(8,128)S(1)}, f32[64,64]{1,0:T(8,128)S(1)}, u32[]{:S(2)}, u32[]{:S(2)}) collective-permute-start(f32[64,64]{1,0:T(8,128)S(1)} %add.13.refs_0_), channel_id=1, source_target_pairs={{0,8},{4,12},{8,0},{12,4},{16,24},{20,28},{24,16},{28,20},{1,9},{5... | collective-permute-start | bytes 49160 | tf_op jit(solution)/shard_map/ppermute | solution.py:29

commit v3 on v2

--- a/solution.py
+++ b/solution.py
@@ -33,15 +33,32 @@
     return [cells] + [swap(cells, "cols", d) for d in range(1, lax.axis_size("cols"))]
 
 
-def row_stages(count):
-    bits = count.bit_length() - 1
-    stages = []
+def all_rows(cells):
+    bits = lax.axis_size("rows").bit_length() - 1
+    parts = [cells]
     low = 0
     while low < bits:
         wide = 1 if (bits - low) % 2 else 2
-        stages.append([m << low for m in range(1, 1 << wide)])
+        whole = sum(parts[1:], parts[0])
+        parts = [whole] + [swap(whole, "rows", m << low) for m in range(1, 1 << wide)]
         low += wide
-    return stages
+    return parts
+
+
+def shares(cells):
+    groups, lanes = lax.axis_size("rows"), lax.axis_size("cols")
+    if groups % lanes or groups // lanes > 4:
+        return [sum(all_rows(cells)) * (1.0 / lanes)]
+    each = groups // lanes
+    parts = []
+    for part in range(each):
+        pairs = [
+            (r * lanes + lane, (r ^ (lane * each + part)) * lanes + lane)
+            for r in range(groups)
+            for lane in range(lanes)
+        ]
+        parts.append(lax.ppermute(cells, ("rows", "cols"), pairs))
+    return parts
 
 
 def nt(left, right):
@@ -141,16 +158,19 @@
     return pl.ds(pl.multiple_of((lane ^ d) * BLOCK, BLOCK), BLOCK)
 
 
-def prep_kernel(lanes, mean_ref, start_ref, *refs):
-    lists, (side_ref, mask_ref) = refs[:lanes], refs[lanes:]
+def prep_kernel(lanes, knn_ref, start_ref, *refs):
+    lists, (side_ref, mask_ref, mean_ref, left_ref) = refs[:lanes], refs[lanes:]
     lane = lax.axis_index("cols")
     group = lax.axis_index("rows")
     blocks = lax.axis_size("rows") * lanes
     size = start_ref.shape[0]
-    codes = jnp.concatenate([ref[0:1] * blocks + ref[1:2] for ref in lists], axis=0)
+    stride = 4 * blocks
+    slot = lax.broadcasted_iota(jnp.int32, (1, lists[0].shape[1]), 1)
+    codes = [jnp.where(slot < ref[2:3], ref[0:1] * stride + ref[1:2], -stride) for ref in lists]
+    codes = jnp.concatenate(codes, axis=0)
 
     def live(row_block, col_block):
-        hit = jnp.where(codes == row_block * blocks + col_block, 1.0, 0.0)
+        hit = jnp.where(codes == row_block * stride + col_block, 1.0, 0.0)
         hit = jnp.max(jnp.max(hit, axis=1, keepdims=True), axis=0, keepdims=True)
         return jnp.broadcast_to(hit, (1, BLOCK))
 
@@ -159,23 +179,35 @@
     masks = [live(row, mine) for row in rows] + [live(row, mine + lanes) for row in rows]
     mask_ref[...] = jnp.concatenate(masks, axis=0)
     back = [live(mine, row - lanes) for row in rows]
+    knn = knn_ref[...].astype(f32)
+    mean_ref[...] = jnp.concatenate([knn[k : k + 1] for k in range(knn.shape[0])], axis=1)
     means = mean_ref[:, block_of(lane, 0)]
     pad = jnp.zeros((side_ref.shape[0] - size - lanes - 1, BLOCK), f32)
     start = start_ref[:, block_of(lane, 0)]
     side_ref[...] = jnp.concatenate([start, means, *back, pad], axis=0).astype(bf16)
-
-
-def own_kernel(lanes, cells_ref, mean_ref, start_ref, unit_ref, weight_ref, product_ref):
+    for d in range(lanes):
+        left_ref[d] = with_ones(start_ref[:, block_of(lane, d)].astype(bf16))
+
+
+def own_kernel(lanes, cells_ref, mean_ref, left_ref, unit_ref, weight_ref, product_ref, held, sems):
     lane = lax.axis_index("cols")
-    for d in range(lanes):
-        unit_ref[d] = unit_rows(cells_ref[block_of(lane, d), :])
+    copies = [
+        pltpu.make_async_copy(cells_ref.at[block_of(lane, d), :], held.at[d], sems.at[d])
+        for d in range(lanes)
+    ]
+    for copy in copies:
+        copy.start()
     eye = diagonal(BLOCK)
-    own = unit_ref[0]
     col_mean = upright(mean_ref[:, block_of(lane, 0)], eye)
-    left = with_ones(start_ref[:, block_of(lane, 0)].astype(bf16))
+    left = left_ref[0]
     rows = product_ref.shape[1]
     for d in range(lanes):
-        weights = affinity(own, unit_ref[d], col_mean, mean_ref[:, block_of(lane, d)])
+        copies[d].wait()
+        unit = unit_rows(held[d])
+        unit_ref[d] = unit
+        if d == 0:
+            own = unit
+        weights = affinity(own, unit, col_mean, mean_ref[:, block_of(lane, d)])
         if d == 0:
             weights = jnp.where(eye, 0.0, weights)
         weights = weights.astype(bf16)
@@ -184,10 +216,10 @@
 
 
 def next_kernel(lanes, *refs):
-    unit_ref, cells_ref, side_ref, mean_ref, start_ref, own_ref, mask_ref, *outs = refs
+    unit_ref, cells_ref, side_ref, mean_ref, left_ref, own_ref, mask_ref, *outs = refs
     weight_ref, keep_ref, core_ref, back_ref = outs
     lane = lax.axis_index("cols")
-    size = start_ref.shape[0]
+    size = left_ref.shape[1] - ONES
     col_unit = unit_rows(cells_ref[...])
     after = side_ref[size:, :].astype(f32)
     col_mean = upright(after[0:1], diagonal(BLOCK))
@@ -201,8 +233,7 @@
         product = jnp.dot(left, weights, preferred_element_type=f32)[:rows]
         own = mask_ref[d : d + 1, :] * own_ref[d]
         halves(d, keep_ref, core_ref)[...] = own + mask_ref[lanes + d : lanes + d + 1, :] * product
-        narrow = with_ones(start_ref[:, block_of(lane, d)].astype(bf16))
-        back = back + after[1 + d : 2 + d] * nt(narrow, weights)[:rows]
+        back = back + after[1 + d : 2 + d] * nt(left_ref[d], weights)[:rows]
     back_ref[...] = back
 
 
@@ -218,9 +249,7 @@
 
 def smooth_kernel(size, *refs):
     *parts, smooth_ref, degree_ref = refs
-    total = parts[0][...]
-    for part in parts[1:]:
-        total = total + part[...]
+    total = added(parts)
     degree = total[size : size + 1]
     smooth_ref[...] = total[:size] / degree
     degree_ref[...] = jnp.broadcast_to(degree, degree_ref.shape)
@@ -244,28 +273,42 @@
     gram_ref[...] = gram_of([block[...] for block in blocks], total)
 
 
-def resmooth_kernel(degree_ref, *refs):
-    *parts, smooth_ref = refs
-    total = parts[0][...]
-    for part in parts[1:]:
-        total = total + part[...]
-    smooth_ref[...] = total / degree_ref[0:1, :]
-
-
-def factor_kernel(*refs):
-    *grams, inverse_ref = refs
-    gram = grams[0][...]
-    for part in grams[1:]:
-        gram = gram + part[...]
-    inverse_ref[...] = inverse_factor(gram)
-
-
-def first_solve_kernel(lanes, total, inverse_ref, *refs):
-    blocks, (smooth_ref, gram_ref) = refs[:lanes], refs[lanes:]
-    inverse = inverse_ref[...]
+def packed(gram):
+    size = gram.shape[0]
+    wide = BLOCK // size
+    tall = size // wide
+    return jnp.concatenate([gram[k * tall : (k + 1) * tall] for k in range(wide)], axis=1)
+
+
+def unpacked(rows, size):
+    return jnp.concatenate(
+        [rows[:, k * size : (k + 1) * size] for k in range(BLOCK // size)], axis=0
+    )
+
+
+def added(refs):
+    total = refs[0][...]
+    for ref in refs[1:]:
+        total = total + ref[...]
+    return total
+
+
+def resmooth_kernel(terms, degree_ref, *refs):
+    parts, grams, out_ref = refs[:terms], refs[terms:-1], refs[-1]
+    out_ref[...] = jnp.concatenate(
+        [added(parts) / degree_ref[0:1, :], packed(added(grams))], axis=0
+    )
+
+
+def first_solve_kernel(size, total, *refs):
+    *blocks, smooth_ref, gram_ref = refs
+    gram = unpacked(blocks[0][size:], size)
+    for block in blocks[1:]:
+        gram = gram + unpacked(block[size:], size)
+    inverse = inverse_factor(gram)
     solved = []
-    for d in range(lanes):
-        value = times(inverse, blocks[d][...])
+    for d, block in enumerate(blocks):
+        value = times(inverse, block[:size])
         smooth_ref[d] = value
         solved.append(value)
     gram_ref[...] = gram_of(solved, total)
@@ -274,20 +317,20 @@
 def last_solve_kernel(lanes, smooth_ref, *refs):
     *grams, out_ref = refs
     lane = lax.axis_index("cols")
-    gram = grams[0][...]
-    for part in grams[1:]:
-        gram = gram + part[...]
-    inverse = inverse_factor(gram)
+    inverse = inverse_factor(added(grams))
     for d in range(lanes):
         out_ref[:, block_of(lane, d)] = times(inverse, smooth_ref[d])
 
 
-def call(body, outs, *args):
+def call(body, outs, *args, scratch=(), apart=()):
+    vmem = pl.BlockSpec(memory_space=pltpu.VMEM)
+    where = [pl.BlockSpec(memory_space=pl.ANY) if k in apart else vmem for k in range(len(args))]
     return pl.pallas_call(
         body,
         out_shape=[jax.ShapeDtypeStruct(shape, kind) for shape, kind in outs],
-        in_specs=[pl.BlockSpec(memory_space=pltpu.VMEM)] * len(args),
-        out_specs=[pl.BlockSpec(memory_space=pltpu.VMEM)] * len(outs),
+        in_specs=where,
+        out_specs=[vmem] * len(outs),
+        scratch_shapes=list(scratch),
         compiler_params=pltpu.CompilerParams(vmem_limit_bytes=40 * 1024 * 1024),
     )(*args)
 
@@ -304,19 +347,21 @@
     wide = size + 8
 
     next_cells = shift(lax.dynamic_slice_in_dim(embeddings, lane * BLOCK, BLOCK, 0), -1)
-    live = jnp.arange(slots, dtype=jnp.int32) < pair_count[0, 0]
-    mine = jnp.stack([jnp.where(live, pair_rows[0, 0], -1), jnp.where(live, pair_cols[0, 0], -1)])
-    mine = jnp.pad(mine, ((0, 0), (0, 128 - slots)), constant_values=-1)
-    mean = knn_mean.astype(f32)[None, :]
-    side, masks = call(
+    counts = jnp.broadcast_to(pair_count, (1, slots))
+    mine = jnp.concatenate([pair_rows[0], pair_cols[0], counts], axis=0)
+    side, masks, mean, left = call(
         functools.partial(prep_kernel, lanes),
-        [((size + 16, BLOCK), bf16), ((2 * lanes, BLOCK), f32)],
-        mean,
+        [
+            ((size + ONES, BLOCK), bf16),
+            ((2 * lanes, BLOCK), f32),
+            ((1, rows_here), f32),
+            ((lanes, size + ONES, BLOCK), bf16),
+        ],
+        knn_mean.reshape(rows_here // 128, 128),
         start_block,
         *lane_swaps(mine),
     )
     next_side = shift(side, -1)
-    mean, masks = lax.optimization_barrier((mean, masks))
 
     unit, own_weights, own_product = call(
         functools.partial(own_kernel, lanes),
@@ -327,7 +372,9 @@
         ],
         embeddings,
         mean,
-        start_block,
+        left,
+        scratch=[pltpu.VMEM((lanes, BLOCK, width), bf16), pltpu.SemaphoreType.DMA((lanes,))],
+        apart=(0,),
     )
     next_weights, keep, core, back = call(
         functools.partial(next_kernel, lanes),
@@ -338,7 +385,7 @@
         next_cells,
         next_side,
         mean,
-        start_block,
+        left,
         own_product,
         masks,
     )
@@ -368,31 +415,24 @@
         *lane_swaps(smooth),
     )
 
-    def stage(parts, offsets):
-        whole = sum(parts[1:], parts[0])
-        return [whole] + [swap(whole, "rows", offset) for offset in offsets]
-
-    first, *others = row_stages(groups)
-    grams = stage([gram], first)
     products = scattered(keep, core, back)
-    if others:
-        whole, *products = lax.optimization_barrier((sum(grams[1:], grams[0]), *products))
-        grams = [whole] + [swap(whole, "rows", offset) for offset in others[0]]
-    (smooth,) = call(resmooth_kernel, [((size, BLOCK), f32)], degree, *products)
-    for offsets in others[1:]:
-        grams = stage(grams, offsets)
-    (inverse,) = call(factor_kernel, [((size, size), f32)], *grams)
+    (block,) = call(
+        functools.partial(resmooth_kernel, len(products)),
+        [((size + size * size // BLOCK, BLOCK), f32)],
+        degree,
+        *products,
+        *shares(gram),
+    )
     smooth, gram = call(
-        functools.partial(first_solve_kernel, lanes, total),
+        functools.partial(first_solve_kernel, size, total),
         [((lanes, size, BLOCK), f32), ((size, size), f32)],
-        inverse,
-        *lane_swaps(smooth),
-    )
-    grams = [gram]
-    for offsets in row_stages(groups):
-        grams = stage(grams, offsets)
+        *lane_swaps(block),
+    )
     (vector,) = call(
-        functools.partial(last_solve_kernel, lanes), [((size, rows_here), f32)], smooth, *grams
+        functools.partial(last_solve_kernel, lanes),
+        [((size, rows_here), f32)],
+        smooth,
+        *all_rows(gram),
     )
     return vector
 

time: 74.7 us -> 72.3 us (0.968)
  waiting for transfers between devices: 29.7 us -> 24.5 us
  starting transfers between devices: 27.6 us -> 29.7 us
  Pallas kernels: 10.3 us -> 11.9 us
    ppermute x21 -> x17, waiting for transfers between devices: 23.1 us -> 14.1 us  [swap(): return lax.ppermute(cells, axis, [(i, i ^ offset) for i in range(count)])]
    ppermute x0 -> x2, waiting for transfers between devices: none -> 4.81 us  [shares(): parts.append(lax.ppermute(cells, ('rows', 'cols'), pairs))]
    pallas_call x11 -> x10, Pallas kernels: 10.3 us -> 11.9 us  [call(): pl.pallas_call(body, out_shape=[jax.ShapeDtypeStruct(shape, kind) for sha...]
    ppermute x5, waiting for transfers between devices: 6.53 us -> 5.6 us  [shift(): lax.ppermute(cells, 'rows', [(i, (i + step) % count) for i in range(count)])]
    ppermute x5, starting transfers between devices: 10.6 us -> 11.4 us  [shift(): lax.ppermute(cells, 'rows', [(i, (i + step) % count) for i in range(count)])]
    ppermute x21 -> x17, starting transfers between devices: 17 us -> 17.6 us  [swap(): return lax.ppermute(cells, axis, [(i, i ^ offset) for i in range(count)])]
    unnamed x8 -> x6, local copies, waits for them, and re-layouts: 3.49 us -> 3.22 us
  transfers between devices with their start and end apart: 26 -> 24, of which waited for: 15 -> 13; matrix products, arithmetic and copies ran while one was open for 2% -> 1% of each run, Pallas kernels for 5% -> 5%
where the time goes in v3:
time: 72.3 us; the launch traced here: 72 us
  starting transfers between devices  29.7 us (41%)
  waiting for transfers between devices  24.5 us (34%)
  Pallas kernels  11.9 us (16%)
  local copies, waits for them, and re-layouts  4.37 us (6%)
  between operations  0.77 us (1%)
  other arithmetic  0.75 us (1%)
    ppermute x17, starting transfers between devices, swap(): return lax.ppermute(cells, axis, [(i, i ^ offset) for i in range(count)])  17.6 us
    ppermute x17, waiting for transfers between devices, swap(): return lax.ppermute(cells, axis, [(i, i ^ offset) for i in range(count)])  14.1 us
    pallas_call x10, Pallas kernels, call(): pl.pallas_call(body, out_shape=[jax.ShapeDtypeStruct(shape, kind) for sha...  11.9 us
    ppermute x5, starting transfers between devices, shift(): lax.ppermute(cells, 'rows', [(i, (i + step) % count) for i in range(count)])  11.4 us
    ppermute x5, waiting for transfers between devices, shift(): lax.ppermute(cells, 'rows', [(i, (i + step) % count) for i in range(count)])  5.6 us
    ppermute x2, waiting for transfers between devices, shares(): parts.append(lax.ppermute(cells, ('rows', 'cols'), pairs))  4.81 us
    unnamed x6, local copies, waits for them, and re-layouts  3.22 us
  transfers between devices with their start and end apart: 24, of which 13 were waited for; matrix products, arithmetic and copies ran while one was open for 1% of the time, Pallas kernels for 5%

profile of v3, /device:TPU:0, one launch (start us, length us, event | category | flops | bytes accessed | tf_op | source)
XLA Modules:
  0.0 72.0 jit_solution(3870293525278592743)
XLA Ops:
  0.0 1.1 %constant_dynamic-slice_fusion = bf16[256,1024]{1,0:T(8,128)(2,1)S(1)} fusion(bf16[1024,1024]{1,0:T(8,128)(2,1)} %cells_ref.1, s32[]{:T(128)S(6)} %select_n.3), kind=kLoop, calls=%fused_computation.1 | loop fusion | bytes 1048580 | tf_op jit(solution)/shard_map/dynamic_slice | solution.py:349
  1.1 6.1 %collective-permute-start.3 = (bf16[256,1024]{1,0:T(8,128)(2,1)S(1)}, bf16[256,1024]{1,0:T(8,128)(2,1)S(1)}, u32[]{:S(2)}, u32[]{:S(2)}) collective-permute-start(bf16[256,1024]{1,0:T(8,128)(2,1)S(1)} %constant_dynamic-slice_fusion), channel_id=1, source_target_pairs={{0,28},{4,0},{8,4},{12,8},{16,12},{20,16},{24,20},{28,24},{1,29},{... | collective-permute-start | bytes 1572872 | tf_op jit(solution)/shard_map/ppermute | solution.py:24
  7.8 0.1 pad.2.clone
  7.9 0.7 %add_add_fusion.refs_0_ = s32[3,24]{1,0:T(4,128)S(1)} fusion(s32[1,24]{1,0:T(1,128)} %bitcast.8, s32[1,24]{1,0:T(1,128)} %bitcast.9, s32[3]{0:T(128)S(1)} %pad.2.clone), kind=kLoop, calls=%fused_computation | loop fusion | flops 144 | bytes 492 | tf_op jit(solution)/shard_map/concatenate | solution.py:351
  8.6 0.7 collective-permute-start.2
  9.3 0.9 %collective-permute-start.1 = (s32[3,24]{1,0:T(4,128)S(1)}, s32[3,24]{1,0:T(4,128)S(1)}, u32[]{:S(2)}, u32[]{:S(2)}) collective-permute-start(s32[3,24]{1,0:T(4,128)S(1)} %add_add_fusion.refs_0_), channel_id=1, source_target_pairs={{0,2},{1,3},{2,0},{3,1},{4,6},{5,7},{6,4},{7,5},{8,10},{9,11},{10,... | collective-permute-start | bytes 872 | tf_op jit(solution)/shard_map/ppermute | solution.py:29
  10.2 0.3 collective-permute-start
  10.5 1.1 %collective-permute-done.2.refs_3_ = s32[3,24]{1,0:T(4,128)S(1)} collective-permute-done((s32[3,24]{1,0:T(4,128)S(1)}, s32[3,24]{1,0:T(4,128)S(1)}, u32[]{:S(2)}, u32[]{:S(2)}) %collective-permute-start.2) | collective-permute-done | bytes 320 | tf_op jit(solution)/shard_map/ppermute | solution.py:29
  11.6 1.2 %collective-permute-done.1.refs_2_ = s32[3,24]{1,0:T(4,128)S(1)} collective-permute-done((s32[3,24]{1,0:T(4,128)S(1)}, s32[3,24]{1,0:T(4,128)S(1)}, u32[]{:S(2)}, u32[]{:S(2)}) %collective-permute-start.1) | collective-permute-done | bytes 320 | tf_op jit(solution)/shard_map/ppermute | solution.py:29
  12.9 0.9 %copy-done.1 = f32[64,1024]{1,0:T(8,128)S(1)} copy-done((f32[64,1024]{1,0:T(8,128)S(1)}, f32[64,1024]{1,0:T(8,128)}, u32[]{:S(2)}) %copy-start.1) | copy-done | bytes 262168
  13.8 0.7 copy-done.2
  14.5 0.1 shard_map.64
  14.6 0.6 collective-permute-start.4
  15.2 1.6 %copy-done = bf16[1024,1024]{1,0:T(8,128)(2,1)S(1)} copy-done((bf16[1024,1024]{1,0:T(8,128)(2,1)S(1)}, bf16[1024,1024]{1,0:T(8,128)(2,1)}, u32[]{:S(2)}) %copy-start) | copy-done | bytes 2097176
  16.7 3.2 %shard_map.65 = (bf16[4,256,1024]{2,1,0:T(8,128)(2,1)S(1)}, bf16[4,256,256]{2,1,0:T(8,128)(2,1)S(1)}, f32[4,72,256]{2,1,0:T(8,128)S(1)}) custom-call(bf16[1024,1024]{1,0:T(8,128)(2,1)S(1)} %copy-done, f32[1,1024]{1,0:T(1,128)S(1)} %get-tuple-element.28.mean_ref.refs_3_, bf16[4,80,256]{2,1,0:T(8,128)(2,1)S(1)} %get-tuple-element.29.left_ref.refs_4_), custom_call_target="tpu_custom_call" | custom-call | tf_op jit(solution)/shard_map/pallas_call | solution.py:328
  20.0 2.0 %shard_map.66 = (bf16[4,256,256]{2,1,0:T(8,128)(2,1)S(1)}, f32[2,72,256]{2,1,0:T(8,128)S(1)}, f32[2,72,256]{2,1,0:T(8,128)S(1)}, f32[72,256]{1,0:T(8,128)S(1)}) custom-call(bf16[4,256,1024]{2,1,0:T(8,128)(2,1)S(1)} %get-tuple-element.30.refs_0_, bf16[256,1024]{1,0:T(8,128)(2,1)S(1)} %collective-permute-done.3.refs_1_, ...), custom_call_target="tpu_custom_call" | custom-call | tf_op jit(solution)/shard_map/pallas_call | solution.py:328
  22.0 0.1 collective-permute-start.5
  22.1 1.6 %collective-permute-start.7 = (f32[72,256]{1,0:T(8,128)S(1)}, f32[72,256]{1,0:T(8,128)S(1)}, u32[]{:S(2)}, u32[]{:S(2)}) collective-permute-start(f32[72,256]{1,0:T(8,128)S(1)} %get-tuple-element.38), channel_id=1, source_target_pairs={{0,4},{4,8},{8,12},{12,16},{16,20},{20,24},{24,28},{28,0},{1,5},{5... | collective-permute-start | bytes 221192 | tf_op jit(solution)/shard_map/ppermute | solution.py:24
  23.7 1.0 %collective-permute-start.6 = (f32[72,256]{1,0:T(8,128)S(1)}, f32[72,256]{1,0:T(8,128)S(1)}, u32[]{:S(2)}, u32[]{:S(2)}) collective-permute-start(f32[72,256]{1,0:T(8,128)S(1)} %get-tuple-element.37), channel_id=1, source_target_pairs={{0,2},{1,3},{2,0},{3,1},{4,6},{5,7},{6,4},{7,5},{8,10},{9,11},{10,... | collective-permute-start | bytes 221192 | tf_op jit(solution)/shard_map/ppermute | solution.py:29
  24.7 4.8 %collective-permute-done.7.refs_2_ = f32[72,256]{1,0:T(8,128)S(1)} collective-permute-done((f32[72,256]{1,0:T(8,128)S(1)}, f32[72,256]{1,0:T(8,128)S(1)}, u32[]{:S(2)}, u32[]{:S(2)}) %collective-permute-start.7) | collective-permute-done | bytes 73760 | tf_op jit(solution)/shard_map/ppermute | solution.py:24
  29.5 1.0 %collective-permute-start.11 = (f32[64,256]{1,0:T(8,128)S(1)}, f32[64,256]{1,0:T(8,128)S(1)}, u32[]{:S(2)}, u32[]{:S(2)}) collective-permute-start(f32[64,256]{1,0:T(8,128)S(1)} %get-tuple-element.42.rest_0_), channel_id=1, source_target_pairs={{0,3},{1,2},{2,1},{3,0},{4,7},{5,6},{6,5},{7,4},{8,11},{9,10},{10,... | collective-permute-start | bytes 196616 | tf_op jit(solution)/shard_map/ppermute | solution.py:29
  30.5 0.6 collective-permute-start.10
  31.1 0.3 collective-permute-start.9
  31.4 2.8 %collective-permute-start.8 = (f32[64,256]{1,0:T(8,128)S(1)}, f32[64,256]{1,0:T(8,128)S(1)}, u32[]{:S(2)}, u32[]{:S(2)}) collective-permute-start(f32[64,256]{1,0:T(8,128)S(1)} %get-tuple-element.42.rest_0_), channel_id=1, source_target_pairs={{0,28},{4,0},{8,4},{12,8},{16,12},{20,16},{24,20},{28,24},{1,29},{... | collective-permute-start | bytes 196616 | tf_op jit(solution)/shard_map/ppermute | solution.py:24
  34.2 1.1 %collective-permute-done.10.rest_2_ = f32[64,256]{1,0:T(8,128)S(1)} collective-permute-done((f32[64,256]{1,0:T(8,128)S(1)}, f32[64,256]{1,0:T(8,128)S(1)}, u32[]{:S(2)}, u32[]{:S(2)}) %collective-permute-start.10) | collective-permute-done | bytes 65568 | tf_op jit(solution)/shard_map/ppermute | solution.py:29
  35.4 0.8 %collective-permute-done.8.next_ref = f32[64,256]{1,0:T(8,128)S(1)} collective-permute-done((f32[64,256]{1,0:T(8,128)S(1)}, f32[64,256]{1,0:T(8,128)S(1)}, u32[]{:S(2)}, u32[]{:S(2)}) %collective-permute-start.8) | collective-permute-done | bytes 65568 | tf_op jit(solution)/shard_map/ppermute | solution.py:24
  36.1 0.7 %shard_map.69 = (f32[2,64,256]{2,1,0:T(8,128)S(1)}, f32[2,64,256]{2,1,0:T(8,128)S(1)}, f32[64,256]{1,0:T(8,128)S(1)}, f32[64,64]{1,0:T(8,128)S(1)}) custom-call(bf16[4,256,256]{2,1,0:T(8,128)(2,1)S(1)} %get-tuple-element.40.own_ref, bf16[4,256,256]{2,1,0:T(8,128)(2,1)S(1)} %get-tuple-element.41.weight_ref, f32[8,256]{1,0:T(8,128)S(1)} %get-tuple-element.33.refs_6_.mask_ref, ...), custom_call_target="tpu_custom_call" | custom-call | tf_op jit(solution)/shard_map/pallas_call | solution.py:328
  36.9 0.1 collective-permute-start.12
  37.0 0.4 collective-permute-start.14
  37.4 0.9 %collective-permute-done.12.came_ref = f32[2,64,256]{2,1,0:T(8,128)S(1)} collective-permute-done((f32[2,64,256]{2,1,0:T(8,128)S(1)}, f32[2,64,256]{2,1,0:T(8,128)S(1)}, u32[]{:S(2)}, u32[]{:S(2)}) %collective-permute-start.12) | collective-permute-done | bytes 131104 | tf_op jit(solution)/shard_map/ppermute | solution.py:29
  38.3 1.6 %collective-permute-start.13 = (f32[64,256]{1,0:T(8,128)S(1)}, f32[64,256]{1,0:T(8,128)S(1)}, u32[]{:S(2)}, u32[]{:S(2)}) collective-permute-start(f32[64,256]{1,0:T(8,128)S(1)} %get-tuple-element.46), channel_id=1, source_target_pairs={{0,2},{1,3},{2,0},{3,1},{4,6},{5,7},{6,4},{7,5},{8,10},{9,11},{10,... | collective-permute-start | bytes 196616 | tf_op jit(solution)/shard_map/ppermute | solution.py:29
  39.9 0.7 collective-permute-start.15
  40.5 4.8 %collective-permute-done.16.refs_4_ = f32[64,64]{1,0:T(8,128)S(1)} collective-permute-done((f32[64,64]{1,0:T(8,128)S(1)}, f32[64,64]{1,0:T(8,128)S(1)}, u32[]{:S(2)}, u32[]{:S(2)}) %collective-permute-start.16) | collective-permute-done | bytes 16416 | tf_op jit(solution)/shard_map/ppermute | solution.py:60
  45.4 0.1 shard_map.71.refs_0_
  45.4 5.8 %collective-permute-start.19 = (f32[80,256]{1,0:T(8,128)S(1)}, f32[80,256]{1,0:T(8,128)S(1)}, u32[]{:S(2)}, u32[]{:S(2)}) collective-permute-start(f32[80,256]{1,0:T(8,128)S(1)} %shard_map.71.refs_0_), channel_id=1, source_target_pairs={{0,3},{1,2},{2,1},{3,0},{4,7},{5,6},{6,5},{7,4},{8,11},{9,10},{10,... | collective-permute-start | bytes 245768 | tf_op jit(solution)/shard_map/ppermute | solution.py:29
  51.2 0.2 collective-permute-start.17
  51.4 2.1 %collective-permute-done.19.refs_3_ = f32[80,256]{1,0:T(8,128)S(1)} collective-permute-done((f32[80,256]{1,0:T(8,128)S(1)}, f32[80,256]{1,0:T(8,128)S(1)}, u32[]{:S(2)}, u32[]{:S(2)}) %collective-permute-start.19) | collective-permute-done | bytes 81952 | tf_op jit(solution)/shard_map/ppermute | solution.py:29
  53.5 2.1 %collective-permute-done.18.refs_2_ = f32[80,256]{1,0:T(8,128)S(1)} collective-permute-done((f32[80,256]{1,0:T(8,128)S(1)}, f32[80,256]{1,0:T(8,128)S(1)}, u32[]{:S(2)}, u32[]{:S(2)}) %collective-permute-start.18) | collective-permute-done | bytes 81952 | tf_op jit(solution)/shard_map/ppermute | solution.py:29
  55.7 2.7 %shard_map.72 = (f32[4,64,256]{2,1,0:T(8,128)S(1)}, f32[64,64]{1,0:T(8,128)S(1)}) custom-call(f32[80,256]{1,0:T(8,128)S(1)} %shard_map.71.refs_0_, f32[80,256]{1,0:T(8,128)S(1)} %collective-permute-done.17.refs_1_, f32[80,256]{1,0:T(8,128)S(1)} %collective-permute-done.18.refs_2_, f32[80,256]{1,0:T(8,128)S(1)} %collective-permute-done.19.refs_3_), custom_call_target="tpu_custom_call" | custom-call | tf_op jit(solution)/shard_map/pallas_call | solution.py:328
  58.4 0.8 %collective-permute-start.20 = (f32[64,64]{1,0:T(8,128)S(1)}, f32[64,64]{1,0:T(8,128)S(1)}, u32[]{:S(2)}, u32[]{:S(2)}) collective-permute-start(f32[64,64]{1,0:T(8,128)S(1)} %get-tuple-element.50), channel_id=1, source_target_pairs={{0,4},{4,0},{8,12},{12,8},{16,20},{20,16},{24,28},{28,24},{1,5},{5... | collective-permute-start | bytes 49160 | tf_op jit(solution)/shard_map/ppermute | solution.py:29
  59.2 3.2 %collective-permute-done.20 = f32[64,64]{1,0:T(8,128)S(1)} collective-permute-done((f32[64,64]{1,0:T(8,128)S(1)}, f32[64,64]{1,0:T(8,128)S(1)}, u32[]{:S(2)}, u32[]{:S(2)}) %collective-permute-start.20) | collective-permute-done | bytes 16416 | tf_op jit(solution)/shard_map/ppermute | solution.py:29
  62.4 1.1 %collective-permute-start.23 = (f32[64,64]{1,0:T(8,128)S(1)}, f32[64,64]{1,0:T(8,128)S(1)}, u32[]{:S(2)}, u32[]{:S(2)}) collective-permute-start(f32[64,64]{1,0:T(8,128)S(1)} %add.7.refs_0_), channel_id=1, source_target_pairs={{0,24},{4,28},{8,16},{12,20},{16,8},{20,12},{24,0},{28,4},{1,25},{... | collective-permute-start | bytes 49160 | tf_op jit(solution)/shard_map/ppermute | solution.py:29
  63.5 1.4 %collective-permute-start.22 = (f32[64,64]{1,0:T(8,128)S(1)}, f32[64,64]{1,0:T(8,128)S(1)}, u32[]{:S(2)}, u32[]{:S(2)}) collective-permute-start(f32[64,64]{1,0:T(8,128)S(1)} %add.7.refs_0_), channel_id=1, source_target_pairs={{0,16},{4,20},{8,24},{12,28},{16,0},{20,4},{24,8},{28,12},{1,17},{... | collective-permute-start | bytes 49160 | tf_op jit(solution)/shard_map/ppermute | solution.py:29
  64.9 1.9 %collective-permute-start.21 = (f32[64,64]{1,0:T(8,128)S(1)}, f32[64,64]{1,0:T(8,128)S(1)}, u32[]{:S(2)}, u32[]{:S(2)}) collective-permute-start(f32[64,64]{1,0:T(8,128)S(1)} %add.7.refs_0_), channel_id=1, source_target_pairs={{0,8},{4,12},{8,0},{12,4},{16,24},{20,28},{24,16},{28,20},{1,9},{5... | collective-permute-start | bytes 49160 | tf_op jit(solution)/shard_map/ppermute | solution.py:29
  66.8 1.3 %collective-permute-done.23.refs_3_ = f32[64,64]{1,0:T(8,128)S(1)} collective-permute-done((f32[64,64]{1,0:T(8,128)S(1)}, f32[64,64]{1,0:T(8,128)S(1)}, u32[]{:S(2)}, u32[]{:S(2)}) %collective-permute-start.23) | collective-permute-done | bytes 16416 | tf_op jit(solution)/shard_map/ppermute | solution.py:29
  68.1 0.8 %collective-permute-done.22.refs_2_ = f32[64,64]{1,0:T(8,128)S(1)} collective-permute-done((f32[64,64]{1,0:T(8,128)S(1)}, f32[64,64]{1,0:T(8,128)S(1)}, u32[]{:S(2)}, u32[]{:S(2)}) %collective-permute-start.22) | collective-permute-done | bytes 16416 | tf_op jit(solution)/shard_map/ppermute | solution.py:29
  68.9 0.2 collective-permute-done.21.refs_1_
  69.1 2.9 %shard_map.73 = f32[64,1024]{1,0:T(8,128)} custom-call(f32[4,64,256]{2,1,0:T(8,128)S(1)} %get-tuple-element.49.smooth_ref, f32[64,64]{1,0:T(8,128)S(1)} %add.7.refs_0_, f32[64,64]{1,0:T(8,128)S(1)} %collective-permute-done.21.refs_1_, f32[64,64]{1,0:T(8,128)S(1)} %collective-permute-done.22.refs_2_, f32[64,64]{1,0:T(8,128)S(1)} %collective-permute-done.23.refs_3_), custom_call_target="tpu_custom_call" | custom-call | tf_op jit(solution)/shard_map/pallas_call | solution.py:328
  (20 shorter events, 0.1 us)
Async XLA Ops:
  1.1 18.9 %collective-permute-start.3 = (bf16[256,1024]{1,0:T(8,128)(2,1)S(1)}, bf16[256,1024]{1,0:T(8,128)(2,1)S(1)}, u32[]{:S(2)}, u32[]{:S(2)}) collective-permute-start(bf16[256,1024]{1,0:T(8,128)(2,1)S(1)} %constant_dynamic-slice_fusion), channel_id=1, source_target_pairs={{0,28},{4,0},{8,4},{12,8},{16,12},{20,16},{24,20},{28,24},{1,29},{... | collective-permute-start | bytes 1572872 | tf_op jit(solution)/shard_map/ppermute | solution.py:24
  8.6 3.0 %collective-permute-start.2 = (s32[3,24]{1,0:T(4,128)S(1)}, s32[3,24]{1,0:T(4,128)S(1)}, u32[]{:S(2)}, u32[]{:S(2)}) collective-permute-start(s32[3,24]{1,0:T(4,128)S(1)} %add_add_fusion.refs_0_), channel_id=1, source_target_pairs={{0,3},{1,2},{2,1},{3,0},{4,7},{5,6},{6,5},{7,4},{8,11},{9,10},{10,... | collective-permute-start | bytes 872 | tf_op jit(solution)/shard_map/ppermute | solution.py:29
  9.3 3.6 %collective-permute-start.1 = (s32[3,24]{1,0:T(4,128)S(1)}, s32[3,24]{1,0:T(4,128)S(1)}, u32[]{:S(2)}, u32[]{:S(2)}) collective-permute-start(s32[3,24]{1,0:T(4,128)S(1)} %add_add_fusion.refs_0_), channel_id=1, source_target_pairs={{0,2},{1,3},{2,0},{3,1},{4,6},{5,7},{6,4},{7,5},{8,10},{9,11},{10,... | collective-permute-start | bytes 872 | tf_op jit(solution)/shard_map/ppermute | solution.py:29
  10.2 2.7 %collective-permute-start = (s32[3,24]{1,0:T(4,128)S(1)}, s32[3,24]{1,0:T(4,128)S(1)}, u32[]{:S(2)}, u32[]{:S(2)}) collective-permute-start(s32[3,24]{1,0:T(4,128)S(1)} %add_add_fusion.refs_0_), channel_id=1, source_target_pairs={{0,1},{1,0},{2,3},{3,2},{4,5},{5,4},{6,7},{7,6},{8,9},{9,8},{10,11... | collective-permute-start | bytes 872 | tf_op jit(solution)/shard_map/ppermute | solution.py:29
  12.9 1.0 %copy-start.1 = (f32[64,1024]{1,0:T(8,128)S(1)}, f32[64,1024]{1,0:T(8,128)}, u32[]{:S(2)}) copy-start(f32[64,1024]{1,0:T(8,128)} %start_ref.1) | copy-start | bytes 786436
  13.8 0.7 copy-start.2
  14.6 5.4 %collective-permute-start.4 = (bf16[80,256]{1,0:T(8,128)(2,1)S(1)}, bf16[80,256]{1,0:T(8,128)(2,1)S(1)}, u32[]{:S(2)}, u32[]{:S(2)}) collective-permute-start(bf16[80,256]{1,0:T(8,128)(2,1)S(1)} %get-tuple-element.31), channel_id=1, source_target_pairs={{0,28},{4,0},{8,4},{12,8},{16,12},{20,16},{24,20},{28,24},{1,29},{... | collective-permute-start | bytes 122888 | tf_op jit(solution)/shard_map/ppermute | solution.py:24
  15.2 1.6 %copy-start = (bf16[1024,1024]{1,0:T(8,128)(2,1)S(1)}, bf16[1024,1024]{1,0:T(8,128)(2,1)}, u32[]{:S(2)}) copy-start(bf16[1024,1024]{1,0:T(8,128)(2,1)} %cells_ref.1) | copy-start | bytes 6291460
  22.0 1.7 %collective-permute-start.5 = (f32[2,72,256]{2,1,0:T(8,128)S(1)}, f32[2,72,256]{2,1,0:T(8,128)S(1)}, u32[]{:S(2)}, u32[]{:S(2)}) collective-permute-start(f32[2,72,256]{2,1,0:T(8,128)S(1)} %get-tuple-element.35), channel_id=1, source_target_pairs={{0,1},{1,0},{2,3},{3,2},{4,5},{5,4},{6,7},{7,6},{8,9},{9,8},{10,11... | collective-permute-start | bytes 442376 | tf_op jit(solution)/shard_map/ppermute | solution.py:29
  22.1 7.4 %collective-permute-start.7 = (f32[72,256]{1,0:T(8,128)S(1)}, f32[72,256]{1,0:T(8,128)S(1)}, u32[]{:S(2)}, u32[]{:S(2)}) collective-permute-start(f32[72,256]{1,0:T(8,128)S(1)} %get-tuple-element.38), channel_id=1, source_target_pairs={{0,4},{4,8},{8,12},{12,16},{16,20},{20,24},{24,28},{28,0},{1,5},{5... | collective-permute-start | bytes 221192 | tf_op jit(solution)/shard_map/ppermute | solution.py:24
  23.7 5.8 %collective-permute-start.6 = (f32[72,256]{1,0:T(8,128)S(1)}, f32[72,256]{1,0:T(8,128)S(1)}, u32[]{:S(2)}, u32[]{:S(2)}) collective-permute-start(f32[72,256]{1,0:T(8,128)S(1)} %get-tuple-element.37), channel_id=1, source_target_pairs={{0,2},{1,3},{2,0},{3,1},{4,6},{5,7},{6,4},{7,5},{8,10},{9,11},{10,... | collective-permute-start | bytes 221192 | tf_op jit(solution)/shard_map/ppermute | solution.py:29
  29.5 4.8 %collective-permute-start.11 = (f32[64,256]{1,0:T(8,128)S(1)}, f32[64,256]{1,0:T(8,128)S(1)}, u32[]{:S(2)}, u32[]{:S(2)}) collective-permute-start(f32[64,256]{1,0:T(8,128)S(1)} %get-tuple-element.42.rest_0_), channel_id=1, source_target_pairs={{0,3},{1,2},{2,1},{3,0},{4,7},{5,6},{6,5},{7,4},{8,11},{9,10},{10,... | collective-permute-start | bytes 196616 | tf_op jit(solution)/shard_map/ppermute | solution.py:29
  30.5 4.9 %collective-permute-start.10 = (f32[64,256]{1,0:T(8,128)S(1)}, f32[64,256]{1,0:T(8,128)S(1)}, u32[]{:S(2)}, u32[]{:S(2)}) collective-permute-start(f32[64,256]{1,0:T(8,128)S(1)} %get-tuple-element.42.rest_0_), channel_id=1, source_target_pairs={{0,2},{1,3},{2,0},{3,1},{4,6},{5,7},{6,4},{7,5},{8,10},{9,11},{10,... | collective-permute-start | bytes 196616 | tf_op jit(solution)/shard_map/ppermute | solution.py:29
  31.1 4.3 %collective-permute-start.9 = (f32[64,256]{1,0:T(8,128)S(1)}, f32[64,256]{1,0:T(8,128)S(1)}, u32[]{:S(2)}, u32[]{:S(2)}) collective-permute-start(f32[64,256]{1,0:T(8,128)S(1)} %get-tuple-element.42.rest_0_), channel_id=1, source_target_pairs={{0,1},{1,0},{2,3},{3,2},{4,5},{5,4},{6,7},{7,6},{8,9},{9,8},{10,11... | collective-permute-start | bytes 196616 | tf_op jit(solution)/shard_map/ppermute | solution.py:29
  31.4 4.7 %collective-permute-start.8 = (f32[64,256]{1,0:T(8,128)S(1)}, f32[64,256]{1,0:T(8,128)S(1)}, u32[]{:S(2)}, u32[]{:S(2)}) collective-permute-start(f32[64,256]{1,0:T(8,128)S(1)} %get-tuple-element.42.rest_0_), channel_id=1, source_target_pairs={{0,28},{4,0},{8,4},{12,8},{16,12},{20,16},{24,20},{28,24},{1,29},{... | collective-permute-start | bytes 196616 | tf_op jit(solution)/shard_map/ppermute | solution.py:24
  36.9 1.4 %collective-permute-start.12 = (f32[2,64,256]{2,1,0:T(8,128)S(1)}, f32[2,64,256]{2,1,0:T(8,128)S(1)}, u32[]{:S(2)}, u32[]{:S(2)}) collective-permute-start(f32[2,64,256]{2,1,0:T(8,128)S(1)} %get-tuple-element.44), channel_id=1, source_target_pairs={{0,1},{1,0},{2,3},{3,2},{4,5},{5,4},{6,7},{7,6},{8,9},{9,8},{10,11... | collective-permute-start | bytes 393224 | tf_op jit(solution)/shard_map/ppermute | solution.py:29
  37.0 8.4 %collective-permute-start.14 = (f32[64,256]{1,0:T(8,128)S(1)}, f32[64,256]{1,0:T(8,128)S(1)}, u32[]{:S(2)}, u32[]{:S(2)}) collective-permute-start(f32[64,256]{1,0:T(8,128)S(1)} %get-tuple-element.47), channel_id=1, source_target_pairs={{0,4},{4,8},{8,12},{12,16},{16,20},{20,24},{24,28},{28,0},{1,5},{5... | collective-permute-start | bytes 196616 | tf_op jit(solution)/shard_map/ppermute | solution.py:24
  38.3 7.0 %collective-permute-start.13 = (f32[64,256]{1,0:T(8,128)S(1)}, f32[64,256]{1,0:T(8,128)S(1)}, u32[]{:S(2)}, u32[]{:S(2)}) collective-permute-start(f32[64,256]{1,0:T(8,128)S(1)} %get-tuple-element.46), channel_id=1, source_target_pairs={{0,2},{1,3},{2,0},{3,1},{4,6},{5,7},{6,4},{7,5},{8,10},{9,11},{10,... | collective-permute-start | bytes 196616 | tf_op jit(solution)/shard_map/ppermute | solution.py:29
  39.9 5.5 %collective-permute-start.16 = (f32[64,64]{1,0:T(8,128)S(1)}, f32[64,64]{1,0:T(8,128)S(1)}, u32[]{:S(2)}, u32[]{:S(2)}) collective-permute-start(f32[64,64]{1,0:T(8,128)S(1)} %get-tuple-element.48), channel_id=1, source_target_pairs={{0,4},{1,13},{2,22},{3,31},{4,0},{5,9},{6,18},{7,27},{8,12},{9,5},... | collective-permute-start | bytes 49160 | tf_op jit(solution)/shard_map/ppermute | solution.py:60
  39.9 5.5 %collective-permute-start.15 = (f32[64,64]{1,0:T(8,128)S(1)}, f32[64,64]{1,0:T(8,128)S(1)}, u32[]{:S(2)}, u32[]{:S(2)}) collective-permute-start(f32[64,64]{1,0:T(8,128)S(1)} %get-tuple-element.48), channel_id=1, source_target_pairs={{0,0},{1,9},{2,18},{3,27},{4,4},{5,13},{6,22},{7,31},{8,8},{9,1},{... | collective-permute-start | bytes 49160 | tf_op jit(solution)/shard_map/ppermute | solution.py:60
  45.4 8.1 %collective-permute-start.19 = (f32[80,256]{1,0:T(8,128)S(1)}, f32[80,256]{1,0:T(8,128)S(1)}, u32[]{:S(2)}, u32[]{:S(2)}) collective-permute-start(f32[80,256]{1,0:T(8,128)S(1)} %shard_map.71.refs_0_), channel_id=1, source_target_pairs={{0,3},{1,2},{2,1},{3,0},{4,7},{5,6},{6,5},{7,4},{8,11},{9,10},{10,... | collective-permute-start | bytes 245768 | tf_op jit(solution)/shard_map/ppermute | solution.py:29
  51.2 4.4 %collective-permute-start.18 = (f32[80,256]{1,0:T(8,128)S(1)}, f32[80,256]{1,0:T(8,128)S(1)}, u32[]{:S(2)}, u32[]{:S(2)}) collective-permute-start(f32[80,256]{1,0:T(8,128)S(1)} %shard_map.71.refs_0_), channel_id=1, source_target_pairs={{0,2},{1,3},{2,0},{3,1},{4,6},{5,7},{6,4},{7,5},{8,10},{9,11},{10,... | collective-permute-start | bytes 245768 | tf_op jit(solution)/shard_map/ppermute | solution.py:29
  51.2 4.4 %collective-permute-start.17 = (f32[80,256]{1,0:T(8,128)S(1)}, f32[80,256]{1,0:T(8,128)S(1)}, u32[]{:S(2)}, u32[]{:S(2)}) collective-permute-start(f32[80,256]{1,0:T(8,128)S(1)} %shard_map.71.refs_0_), channel_id=1, source_target_pairs={{0,1},{1,0},{2,3},{3,2},{4,5},{5,4},{6,7},{7,6},{8,9},{9,8},{10,11... | collective-permute-start | bytes 245768 | tf_op jit(solution)/shard_map/ppermute | solution.py:29
  58.4 4.0 %collective-permute-start.20 = (f32[64,64]{1,0:T(8,128)S(1)}, f32[64,64]{1,0:T(8,128)S(1)}, u32[]{:S(2)}, u32[]{:S(2)}) collective-permute-start(f32[64,64]{1,0:T(8,128)S(1)} %get-tuple-element.50), channel_id=1, source_target_pairs={{0,4},{4,0},{8,12},{12,8},{16,20},{20,16},{24,28},{28,24},{1,5},{5... | collective-permute-start | bytes 49160 | tf_op jit(solution)/shard_map/ppermute | solution.py:29
  62.4 5.7 %collective-permute-start.23 = (f32[64,64]{1,0:T(8,128)S(1)}, f32[64,64]{1,0:T(8,128)S(1)}, u32[]{:S(2)}, u32[]{:S(2)}) collective-permute-start(f32[64,64]{1,0:T(8,128)S(1)} %add.7.refs_0_), channel_id=1, source_target_pairs={{0,24},{4,28},{8,16},{12,20},{16,8},{20,12},{24,0},{28,4},{1,25},{... | collective-permute-start | bytes 49160 | tf_op jit(solution)/shard_map/ppermute | solution.py:29
  63.5 5.4 %collective-permute-start.22 = (f32[64,64]{1,0:T(8,128)S(1)}, f32[64,64]{1,0:T(8,128)S(1)}, u32[]{:S(2)}, u32[]{:S(2)}) collective-permute-start(f32[64,64]{1,0:T(8,128)S(1)} %add.7.refs_0_), channel_id=1, source_target_pairs={{0,16},{4,20},{8,24},{12,28},{16,0},{20,4},{24,8},{28,12},{1,17},{... | collective-permute-start | bytes 49160 | tf_op jit(solution)/shard_map/ppermute | solution.py:29
  64.9 4.2 %collective-permute-start.21 = (f32[64,64]{1,0:T(8,128)S(1)}, f32[64,64]{1,0:T(8,128)S(1)}, u32[]{:S(2)}, u32[]{:S(2)}) collective-permute-start(f32[64,64]{1,0:T(8,128)S(1)} %add.7.refs_0_), channel_id=1, source_target_pairs={{0,8},{4,12},{8,0},{12,4},{16,24},{20,28},{24,16},{28,20},{1,9},{5... | collective-permute-start | bytes 49160 | tf_op jit(solution)/shard_map/ppermute | solution.py:29

commit v4 on v3

--- a/solution.py
+++ b/solution.py
@@ -42,22 +42,6 @@
         whole = sum(parts[1:], parts[0])
         parts = [whole] + [swap(whole, "rows", m << low) for m in range(1, 1 << wide)]
         low += wide
-    return parts
-
-
-def shares(cells):
-    groups, lanes = lax.axis_size("rows"), lax.axis_size("cols")
-    if groups % lanes or groups // lanes > 4:
-        return [sum(all_rows(cells)) * (1.0 / lanes)]
-    each = groups // lanes
-    parts = []
-    for part in range(each):
-        pairs = [
-            (r * lanes + lane, (r ^ (lane * each + part)) * lanes + lane)
-            for r in range(groups)
-            for lane in range(lanes)
-        ]
-        parts.append(lax.ppermute(cells, ("rows", "cols"), pairs))
     return parts
 
 
@@ -158,15 +142,25 @@
     return pl.ds(pl.multiple_of((lane ^ d) * BLOCK, BLOCK), BLOCK)
 
 
-def prep_kernel(lanes, knn_ref, start_ref, *refs):
-    lists, (side_ref, mask_ref, mean_ref, left_ref) = refs[:lanes], refs[lanes:]
+def vector_kernel(lanes, knn_ref, start_ref, mean_ref, left_ref):
+    lane = lax.axis_index("cols")
+    knn = knn_ref[...].astype(f32)
+    mean_ref[...] = jnp.concatenate([knn[k : k + 1] for k in range(knn.shape[0])], axis=1)
+    for d in range(lanes):
+        left_ref[d] = with_ones(start_ref[:, block_of(lane, d)].astype(bf16))
+
+
+def prep_kernel(lanes, mean_ref, left_ref, *refs):
+    lists, (side_ref, mask_ref) = refs[:lanes], refs[lanes:]
     lane = lax.axis_index("cols")
     group = lax.axis_index("rows")
     blocks = lax.axis_size("rows") * lanes
-    size = start_ref.shape[0]
+    size = left_ref.shape[1] - ONES
     stride = 4 * blocks
     slot = lax.broadcasted_iota(jnp.int32, (1, lists[0].shape[1]), 1)
-    codes = [jnp.where(slot < ref[2:3], ref[0:1] * stride + ref[1:2], -stride) for ref in lists]
+    codes = [
+        jnp.where(slot < ref[2:3, 0:1], ref[0:1] * stride + ref[1:2], -stride) for ref in lists
+    ]
     codes = jnp.concatenate(codes, axis=0)
 
     def live(row_block, col_block):
@@ -179,14 +173,10 @@
     masks = [live(row, mine) for row in rows] + [live(row, mine + lanes) for row in rows]
     mask_ref[...] = jnp.concatenate(masks, axis=0)
     back = [live(mine, row - lanes) for row in rows]
-    knn = knn_ref[...].astype(f32)
-    mean_ref[...] = jnp.concatenate([knn[k : k + 1] for k in range(knn.shape[0])], axis=1)
     means = mean_ref[:, block_of(lane, 0)]
-    pad = jnp.zeros((side_ref.shape[0] - size - lanes - 1, BLOCK), f32)
-    start = start_ref[:, block_of(lane, 0)]
-    side_ref[...] = jnp.concatenate([start, means, *back, pad], axis=0).astype(bf16)
-    for d in range(lanes):
-        left_ref[d] = with_ones(start_ref[:, block_of(lane, d)].astype(bf16))
+    pad = jnp.zeros((ONES - lanes - 1, BLOCK), f32)
+    after = jnp.concatenate([means, *back, pad], axis=0).astype(bf16)
+    side_ref[...] = jnp.concatenate([left_ref[0, :size, :], after], axis=0)
 
 
 def own_kernel(lanes, cells_ref, mean_ref, left_ref, unit_ref, weight_ref, product_ref, held, sems):
@@ -273,19 +263,6 @@
     gram_ref[...] = gram_of([block[...] for block in blocks], total)
 
 
-def packed(gram):
-    size = gram.shape[0]
-    wide = BLOCK // size
-    tall = size // wide
-    return jnp.concatenate([gram[k * tall : (k + 1) * tall] for k in range(wide)], axis=1)
-
-
-def unpacked(rows, size):
-    return jnp.concatenate(
-        [rows[:, k * size : (k + 1) * size] for k in range(BLOCK // size)], axis=0
-    )
-
-
 def added(refs):
     total = refs[0][...]
     for ref in refs[1:]:
@@ -293,38 +270,36 @@
     return total
 
 
-def resmooth_kernel(terms, degree_ref, *refs):
-    parts, grams, out_ref = refs[:terms], refs[terms:-1], refs[-1]
-    out_ref[...] = jnp.concatenate(
-        [added(parts) / degree_ref[0:1, :], packed(added(grams))], axis=0
-    )
-
-
-def first_solve_kernel(size, total, *refs):
-    *blocks, smooth_ref, gram_ref = refs
-    gram = unpacked(blocks[0][size:], size)
-    for block in blocks[1:]:
-        gram = gram + unpacked(block[size:], size)
-    inverse = inverse_factor(gram)
-    solved = []
-    for d, block in enumerate(blocks):
-        value = times(inverse, block[:size])
-        smooth_ref[d] = value
-        solved.append(value)
-    gram_ref[...] = gram_of(solved, total)
-
-
-def last_solve_kernel(lanes, smooth_ref, *refs):
-    *grams, out_ref = refs
-    lane = lax.axis_index("cols")
-    inverse = inverse_factor(added(grams))
+def resmooth_kernel(degree_ref, *refs):
+    *parts, smooth_ref = refs
+    smooth_ref[...] = added(parts) / degree_ref[0:1, :]
+
+
+def grams_kernel(total, first_ref, *refs):
+    *blocks, grams_ref = refs
+    second = gram_of([block[...] for block in blocks], total)
+    grams_ref[...] = jnp.concatenate([first_ref[...], second], axis=1)
+
+
+def solve_kernel(lanes, *refs):
+    blocks, grams, out_ref = refs[:lanes], refs[lanes:-1], refs[-1]
+    lane = lax.axis_index("cols")
+    size = out_ref.shape[0]
+    both = added(grams)
+    first = inverse_factor(both[:, :size])
+    solved = [times(first, block[...]) for block in blocks]
+    half = times(first, both[:, size:])
+    gram = lax.dot_general(
+        half, first, (((1,), (1,)), ((), ())), precision=HIGHEST, preferred_element_type=f32
+    )
+    second = inverse_factor(gram)
     for d in range(lanes):
-        out_ref[:, block_of(lane, d)] = times(inverse, smooth_ref[d])
+        out_ref[:, block_of(lane, d)] = times(second, solved[d])
 
 
 def call(body, outs, *args, scratch=(), apart=()):
     vmem = pl.BlockSpec(memory_space=pltpu.VMEM)
-    where = [pl.BlockSpec(memory_space=pl.ANY) if k in apart else vmem for k in range(len(args))]
+    where = [pl.BlockSpec(memory_space=pltpu.HBM) if k in apart else vmem for k in range(len(args))]
     return pl.pallas_call(
         body,
         out_shape=[jax.ShapeDtypeStruct(shape, kind) for shape, kind in outs],
@@ -347,18 +322,19 @@
     wide = size + 8
 
     next_cells = shift(lax.dynamic_slice_in_dim(embeddings, lane * BLOCK, BLOCK, 0), -1)
-    counts = jnp.broadcast_to(pair_count, (1, slots))
+    counts = jnp.pad(pair_count, ((0, 0), (0, slots - 1)))
     mine = jnp.concatenate([pair_rows[0], pair_cols[0], counts], axis=0)
-    side, masks, mean, left = call(
-        functools.partial(prep_kernel, lanes),
-        [
-            ((size + ONES, BLOCK), bf16),
-            ((2 * lanes, BLOCK), f32),
-            ((1, rows_here), f32),
-            ((lanes, size + ONES, BLOCK), bf16),
-        ],
+    mean, left = call(
+        functools.partial(vector_kernel, lanes),
+        [((1, rows_here), f32), ((lanes, size + ONES, BLOCK), bf16)],
         knn_mean.reshape(rows_here // 128, 128),
         start_block,
+    )
+    side, masks = call(
+        functools.partial(prep_kernel, lanes),
+        [((size + ONES, BLOCK), bf16), ((2 * lanes, BLOCK), f32)],
+        mean,
+        left,
         *lane_swaps(mine),
     )
     next_side = shift(side, -1)
@@ -416,23 +392,16 @@
     )
 
     products = scattered(keep, core, back)
-    (block,) = call(
-        functools.partial(resmooth_kernel, len(products)),
-        [((size + size * size // BLOCK, BLOCK), f32)],
-        degree,
-        *products,
-        *shares(gram),
-    )
-    smooth, gram = call(
-        functools.partial(first_solve_kernel, size, total),
-        [((lanes, size, BLOCK), f32), ((size, size), f32)],
-        *lane_swaps(block),
+    (smooth,) = call(resmooth_kernel, [((size, BLOCK), f32)], degree, *products)
+    blocks = lane_swaps(smooth)
+    (grams,) = call(
+        functools.partial(grams_kernel, total), [((size, 2 * size), f32)], gram, *blocks
     )
     (vector,) = call(
-        functools.partial(last_solve_kernel, lanes),
+        functools.partial(solve_kernel, lanes),
         [((size, rows_here), f32)],
-        smooth,
-        *all_rows(gram),
+        *blocks,
+        *all_rows(grams),
     )
     return vector
 

time: 72.3 us -> 67.7 us (0.936)
  starting transfers between devices: 29.7 us -> 23.7 us
  waiting for transfers between devices: 24.5 us -> 26 us
    ppermute x5, waiting for transfers between devices: 5.6 us -> 11.8 us  [shift(): lax.ppermute(cells, 'rows', [(i, (i + step) % count) for i in range(count)])]
    ppermute x2 -> x0, waiting for transfers between devices: 4.81 us -> none  [shares(): parts.append(lax.ppermute(cells, ('rows', 'cols'), pairs))]
    ppermute x17, starting transfers between devices: 17.6 us -> 13.5 us  [swap(): return lax.ppermute(cells, axis, [(i, i ^ offset) for i in range(count)])]
    ppermute x5, starting transfers between devices: 11.4 us -> 10.2 us  [shift(): lax.ppermute(cells, 'rows', [(i, (i + step) % count) for i in range(count)])]
    pallas_call x10 -> x11, Pallas kernels: 11.9 us -> 12 us  [call(): pl.pallas_call(body, out_shape=[jax.ShapeDtypeStruct(shape, kind) for sha...]
  transfers between devices with their start and end apart: 24 -> 22, of which waited for: 13 -> 13; matrix products, arithmetic and copies ran while one was open for 1% -> 1% of each run, Pallas kernels for 5% -> 5%
where the time goes in v4:
time: 67.7 us; the launch traced here: 67.5 us
  waiting for transfers between devices  26 us (38%)
  starting transfers between devices  23.7 us (35%)
  Pallas kernels  12 us (18%)
  local copies, waits for them, and re-layouts  4.3 us (6%)
  between operations  0.77 us (1%)
  other arithmetic  0.69 us (1%)
    ppermute x17, waiting for transfers between devices, swap(): return lax.ppermute(cells, axis, [(i, i ^ offset) for i in range(count)])  14.2 us
    ppermute x17, starting transfers between devices, swap(): return lax.ppermute(cells, axis, [(i, i ^ offset) for i in range(count)])  13.5 us
    pallas_call x11, Pallas kernels, call(): pl.pallas_call(body, out_shape=[jax.ShapeDtypeStruct(shape, kind) for sha...  12 us
    ppermute x5, waiting for transfers between devices, shift(): lax.ppermute(cells, 'rows', [(i, (i + step) % count) for i in range(count)])  11.8 us
    ppermute x5, starting transfers between devices, shift(): lax.ppermute(cells, 'rows', [(i, (i + step) % count) for i in range(count)])  10.2 us
    unnamed x6, local copies, waits for them, and re-layouts  3.22 us
  transfers between devices with their start and end apart: 22, of which 13 were waited for; matrix products, arithmetic and copies ran while one was open for 1% of the time, Pallas kernels for 5%

profile of v4, /device:TPU:0, one launch (start us, length us, event | category | flops | bytes accessed | tf_op | source)
XLA Modules:
  0.0 67.5 jit_solution(13262955941959240743)
XLA Ops:
  0.0 1.1 %constant_dynamic-slice_fusion = bf16[256,1024]{1,0:T(8,128)(2,1)S(1)} fusion(bf16[1024,1024]{1,0:T(8,128)(2,1)} %cells_ref.1, s32[]{:T(128)S(6)} %select_n.3), kind=kLoop, calls=%fused_computation.1 | loop fusion | bytes 1048580 | tf_op jit(solution)/shard_map/dynamic_slice | solution.py:324
  1.1 6.1 %collective-permute-start = (bf16[256,1024]{1,0:T(8,128)(2,1)S(1)}, bf16[256,1024]{1,0:T(8,128)(2,1)S(1)}, u32[]{:S(2)}, u32[]{:S(2)}) collective-permute-start(bf16[256,1024]{1,0:T(8,128)(2,1)S(1)} %constant_dynamic-slice_fusion), channel_id=1, source_target_pairs={{0,28},{4,0},{8,4},{12,8},{16,12},{20,16},{24,20},{28,24},{1,29},{... | collective-permute-start | bytes 1572872 | tf_op jit(solution)/shard_map/ppermute | solution.py:24
  7.8 0.7 %pad_add_fusion.refs_0_ = s32[3,24]{1,0:T(4,128)S(1)} fusion(s32[1,1]{1,0:T(1,128)S(6)} %copy.7, s32[1,24]{1,0:T(1,128)} %bitcast.4, s32[1,24]{1,0:T(1,128)} %bitcast.5), kind=kLoop, calls=%fused_computation | loop fusion | flops 144 | bytes 484 | tf_op jit(solution)/shard_map/concatenate | solution.py:326
  8.5 0.7 %collective-permute-start.3 = (s32[3,24]{1,0:T(4,128)S(1)}, s32[3,24]{1,0:T(4,128)S(1)}, u32[]{:S(2)}, u32[]{:S(2)}) collective-permute-start(s32[3,24]{1,0:T(4,128)S(1)} %pad_add_fusion.refs_0_), channel_id=1, source_target_pairs={{0,3},{1,2},{2,1},{3,0},{4,7},{5,6},{6,5},{7,4},{8,11},{9,10},{10,... | collective-permute-start | bytes 872 | tf_op jit(solution)/shard_map/ppermute | solution.py:29
  9.2 0.9 %collective-permute-start.2 = (s32[3,24]{1,0:T(4,128)S(1)}, s32[3,24]{1,0:T(4,128)S(1)}, u32[]{:S(2)}, u32[]{:S(2)}) collective-permute-start(s32[3,24]{1,0:T(4,128)S(1)} %pad_add_fusion.refs_0_), channel_id=1, source_target_pairs={{0,2},{1,3},{2,0},{3,1},{4,6},{5,7},{6,4},{7,5},{8,10},{9,11},{10,... | collective-permute-start | bytes 872 | tf_op jit(solution)/shard_map/ppermute | solution.py:29
  10.1 0.3 collective-permute-start.1
  10.4 0.9 %copy-done.1 = f32[64,1024]{1,0:T(8,128)S(1)} copy-done((f32[64,1024]{1,0:T(8,128)S(1)}, f32[64,1024]{1,0:T(8,128)}, u32[]{:S(2)}) %copy-start.1) | copy-done | bytes 262168
  11.3 0.7 %copy-done.2 = bf16[1024]{0:T(1024)(128)(2,1)S(1)} copy-done((bf16[1024]{0:T(1024)(128)(2,1)S(1)}, bf16[1024]{0:T(1024)(128)(2,1)}, u32[]{:S(2)}) %copy-start.2) | copy-done | bytes 2072
  12.0 0.0 collective-permute-done.3.refs_3_
  12.1 0.7 %collective-permute-done.2.refs_2_ = s32[3,24]{1,0:T(4,128)S(1)} collective-permute-done((s32[3,24]{1,0:T(4,128)S(1)}, s32[3,24]{1,0:T(4,128)S(1)}, u32[]{:S(2)}, u32[]{:S(2)}) %collective-permute-start.2) | collective-permute-done | bytes 320 | tf_op jit(solution)/shard_map/ppermute | solution.py:29
  12.8 0.0 collective-permute-done.1.refs_1_
  12.8 0.2 shard_map.66
  12.9 0.6 collective-permute-start.4
  13.5 1.6 %copy-done = bf16[1024,1024]{1,0:T(8,128)(2,1)S(1)} copy-done((bf16[1024,1024]{1,0:T(8,128)(2,1)S(1)}, bf16[1024,1024]{1,0:T(8,128)(2,1)}, u32[]{:S(2)}) %copy-start) | copy-done | bytes 2097176
  15.1 3.2 %shard_map.65 = (bf16[4,256,1024]{2,1,0:T(8,128)(2,1)S(1)}, bf16[4,256,256]{2,1,0:T(8,128)(2,1)S(1)}, f32[4,72,256]{2,1,0:T(8,128)S(1)}) custom-call(bf16[1024,1024]{1,0:T(8,128)(2,1)S(1)} %copy-done, f32[1,1024]{1,0:T(1,128)S(1)} %get-tuple-element.26.mean_ref.refs_3_, bf16[4,80,256]{2,1,0:T(8,128)(2,1)S(1)} %get-tuple-element.27.left_ref.refs_4_), custom_call_target="tpu_custom_call" | custom-call | tf_op jit(solution)/shard_map/pallas_call | solution.py:303
  18.3 0.9 %collective-permute-done.4.refs_2_.side_ref = bf16[80,256]{1,0:T(8,128)(2,1)S(1)} collective-permute-done((bf16[80,256]{1,0:T(8,128)(2,1)S(1)}, bf16[80,256]{1,0:T(8,128)(2,1)S(1)}, u32[]{:S(2)}, u32[]{:S(2)}) %collective-permute-start.4) | collective-permute-done | bytes 40992 | tf_op jit(solution)/shard_map/ppermute | solution.py:24
  19.2 0.0 collective-permute-done.refs_1_
  19.2 2.0 %shard_map.67 = (bf16[4,256,256]{2,1,0:T(8,128)(2,1)S(1)}, f32[2,72,256]{2,1,0:T(8,128)S(1)}, f32[2,72,256]{2,1,0:T(8,128)S(1)}, f32[72,256]{1,0:T(8,128)S(1)}) custom-call(bf16[4,256,1024]{2,1,0:T(8,128)(2,1)S(1)} %get-tuple-element.28.refs_0_, bf16[256,1024]{1,0:T(8,128)(2,1)S(1)} %collective-permute-done.refs_1_, ...), custom_call_target="tpu_custom_call" | custom-call | tf_op jit(solution)/shard_map/pallas_call | solution.py:303
  21.2 0.1 collective-permute-start.5
  21.3 0.7 %collective-permute-start.7 = (f32[72,256]{1,0:T(8,128)S(1)}, f32[72,256]{1,0:T(8,128)S(1)}, u32[]{:S(2)}, u32[]{:S(2)}) collective-permute-start(f32[72,256]{1,0:T(8,128)S(1)} %get-tuple-element.36), channel_id=1, source_target_pairs={{0,4},{4,8},{8,12},{12,16},{16,20},{20,24},{24,28},{28,0},{1,5},{5... | collective-permute-start | bytes 221192 | tf_op jit(solution)/shard_map/ppermute | solution.py:24
  22.0 0.7 collective-permute-done.5.came_ref
  22.7 1.6 %collective-permute-start.6 = (f32[72,256]{1,0:T(8,128)S(1)}, f32[72,256]{1,0:T(8,128)S(1)}, u32[]{:S(2)}, u32[]{:S(2)}) collective-permute-start(f32[72,256]{1,0:T(8,128)S(1)} %get-tuple-element.35), channel_id=1, source_target_pairs={{0,2},{1,3},{2,0},{3,1},{4,6},{5,7},{6,4},{7,5},{8,10},{9,11},{10,... | collective-permute-start | bytes 221192 | tf_op jit(solution)/shard_map/ppermute | solution.py:29
  24.3 5.2 %collective-permute-done.7.refs_2_ = f32[72,256]{1,0:T(8,128)S(1)} collective-permute-done((f32[72,256]{1,0:T(8,128)S(1)}, f32[72,256]{1,0:T(8,128)S(1)}, u32[]{:S(2)}, u32[]{:S(2)}) %collective-permute-start.7) | collective-permute-done | bytes 73760 | tf_op jit(solution)/shard_map/ppermute | solution.py:24
  29.4 1.0 %collective-permute-start.11 = (f32[64,256]{1,0:T(8,128)S(1)}, f32[64,256]{1,0:T(8,128)S(1)}, u32[]{:S(2)}, u32[]{:S(2)}) collective-permute-start(f32[64,256]{1,0:T(8,128)S(1)} %get-tuple-element.40.rest_0_), channel_id=1, source_target_pairs={{0,3},{1,2},{2,1},{3,0},{4,7},{5,6},{6,5},{7,4},{8,11},{9,10},{10,... | collective-permute-start | bytes 196616 | tf_op jit(solution)/shard_map/ppermute | solution.py:29
  30.5 0.6 collective-permute-start.10
  31.1 0.3 collective-permute-start.9
  31.4 2.9 %collective-permute-start.8 = (f32[64,256]{1,0:T(8,128)S(1)}, f32[64,256]{1,0:T(8,128)S(1)}, u32[]{:S(2)}, u32[]{:S(2)}) collective-permute-start(f32[64,256]{1,0:T(8,128)S(1)} %get-tuple-element.40.rest_0_), channel_id=1, source_target_pairs={{0,28},{4,0},{8,4},{12,8},{16,12},{20,16},{24,20},{28,24},{1,29},{... | collective-permute-start | bytes 196616 | tf_op jit(solution)/shard_map/ppermute | solution.py:24
  34.2 1.1 %collective-permute-done.10.rest_2_ = f32[64,256]{1,0:T(8,128)S(1)} collective-permute-done((f32[64,256]{1,0:T(8,128)S(1)}, f32[64,256]{1,0:T(8,128)S(1)}, u32[]{:S(2)}, u32[]{:S(2)}) %collective-permute-start.10) | collective-permute-done | bytes 65568 | tf_op jit(solution)/shard_map/ppermute | solution.py:29
  35.3 0.8 %collective-permute-done.8.next_ref = f32[64,256]{1,0:T(8,128)S(1)} collective-permute-done((f32[64,256]{1,0:T(8,128)S(1)}, f32[64,256]{1,0:T(8,128)S(1)}, u32[]{:S(2)}, u32[]{:S(2)}) %collective-permute-start.8) | collective-permute-done | bytes 65568 | tf_op jit(solution)/shard_map/ppermute | solution.py:24
  36.1 0.7 %shard_map.70 = (f32[2,64,256]{2,1,0:T(8,128)S(1)}, f32[2,64,256]{2,1,0:T(8,128)S(1)}, f32[64,256]{1,0:T(8,128)S(1)}, f32[64,64]{1,0:T(8,128)S(1)}) custom-call(bf16[4,256,256]{2,1,0:T(8,128)(2,1)S(1)} %get-tuple-element.38.own_ref, bf16[4,256,256]{2,1,0:T(8,128)(2,1)S(1)} %get-tuple-element.39.weight_ref, f32[8,256]{1,0:T(8,128)S(1)} %get-tuple-element.31.refs_6_.mask_ref, ...), custom_call_target="tpu_custom_call" | custom-call | tf_op jit(solution)/shard_map/pallas_call | solution.py:303
  36.9 0.1 collective-permute-start.12
  37.0 0.1 collective-permute-start.14
  37.0 1.3 %collective-permute-done.12.came_ref = f32[2,64,256]{2,1,0:T(8,128)S(1)} collective-permute-done((f32[2,64,256]{2,1,0:T(8,128)S(1)}, f32[2,64,256]{2,1,0:T(8,128)S(1)}, u32[]{:S(2)}, u32[]{:S(2)}) %collective-permute-start.12) | collective-permute-done | bytes 131104 | tf_op jit(solution)/shard_map/ppermute | solution.py:29
  38.3 1.6 %collective-permute-start.13 = (f32[64,256]{1,0:T(8,128)S(1)}, f32[64,256]{1,0:T(8,128)S(1)}, u32[]{:S(2)}, u32[]{:S(2)}) collective-permute-start(f32[64,256]{1,0:T(8,128)S(1)} %get-tuple-element.44), channel_id=1, source_target_pairs={{0,2},{1,3},{2,0},{3,1},{4,6},{5,7},{6,4},{7,5},{8,10},{9,11},{10,... | collective-permute-start | bytes 196616 | tf_op jit(solution)/shard_map/ppermute | solution.py:29
  39.9 4.9 %collective-permute-done.14.refs_2_ = f32[64,256]{1,0:T(8,128)S(1)} collective-permute-done((f32[64,256]{1,0:T(8,128)S(1)}, f32[64,256]{1,0:T(8,128)S(1)}, u32[]{:S(2)}, u32[]{:S(2)}) %collective-permute-start.14) | collective-permute-done | bytes 65568 | tf_op jit(solution)/shard_map/ppermute | solution.py:24
  44.8 1.0 %collective-permute-start.17 = (f32[64,256]{1,0:T(8,128)S(1)}, f32[64,256]{1,0:T(8,128)S(1)}, u32[]{:S(2)}, u32[]{:S(2)}) collective-permute-start(f32[64,256]{1,0:T(8,128)S(1)} %shard_map.72.refs_0_), channel_id=1, source_target_pairs={{0,3},{1,2},{2,1},{3,0},{4,7},{5,6},{6,5},{7,4},{8,11},{9,10},{10,... | collective-permute-start | bytes 196616 | tf_op jit(solution)/shard_map/ppermute | solution.py:29
  45.8 0.6 collective-permute-start.16
  46.4 0.3 collective-permute-start.15
  46.7 2.5 %collective-permute-done.17.refs_3_ = f32[64,256]{1,0:T(8,128)S(1)} collective-permute-done((f32[64,256]{1,0:T(8,128)S(1)}, f32[64,256]{1,0:T(8,128)S(1)}, u32[]{:S(2)}, u32[]{:S(2)}) %collective-permute-start.17) | collective-permute-done | bytes 65568 | tf_op jit(solution)/shard_map/ppermute | solution.py:29
  49.2 1.5 %collective-permute-done.16.refs_2_ = f32[64,256]{1,0:T(8,128)S(1)} collective-permute-done((f32[64,256]{1,0:T(8,128)S(1)}, f32[64,256]{1,0:T(8,128)S(1)}, u32[]{:S(2)}, u32[]{:S(2)}) %collective-permute-start.16) | collective-permute-done | bytes 65568 | tf_op jit(solution)/shard_map/ppermute | solution.py:29
  50.7 0.4 shard_map.73
  51.1 0.1 collective-permute-start.18
  51.2 3.9 %collective-permute-done.18 = f32[64,128]{1,0:T(8,128)S(1)} collective-permute-done((f32[64,128]{1,0:T(8,128)S(1)}, f32[64,128]{1,0:T(8,128)S(1)}, u32[]{:S(2)}, u32[]{:S(2)}) %collective-permute-start.18) | collective-permute-done | bytes 32800 | tf_op jit(solution)/shard_map/ppermute | solution.py:29
  55.1 2.2 %collective-permute-start.21 = (f32[64,128]{1,0:T(8,128)S(1)}, f32[64,128]{1,0:T(8,128)S(1)}, u32[]{:S(2)}, u32[]{:S(2)}) collective-permute-start(f32[64,128]{1,0:T(8,128)S(1)} %add.9.refs_4_), channel_id=1, source_target_pairs={{0,24},{4,28},{8,16},{12,20},{16,8},{20,12},{24,0},{28,4},{1,25},{... | collective-permute-start | bytes 98312 | tf_op jit(solution)/shard_map/ppermute | solution.py:29
  57.3 2.2 %collective-permute-start.19 = (f32[64,128]{1,0:T(8,128)S(1)}, f32[64,128]{1,0:T(8,128)S(1)}, u32[]{:S(2)}, u32[]{:S(2)}) collective-permute-start(f32[64,128]{1,0:T(8,128)S(1)} %add.9.refs_4_), channel_id=1, source_target_pairs={{0,8},{4,12},{8,0},{12,4},{16,24},{20,28},{24,16},{28,20},{1,9},{5... | collective-permute-start | bytes 98312 | tf_op jit(solution)/shard_map/ppermute | solution.py:29
  59.5 1.5 %collective-permute-done.21.refs_7_ = f32[64,128]{1,0:T(8,128)S(1)} collective-permute-done((f32[64,128]{1,0:T(8,128)S(1)}, f32[64,128]{1,0:T(8,128)S(1)}, u32[]{:S(2)}, u32[]{:S(2)}) %collective-permute-start.21) | collective-permute-done | bytes 32800 | tf_op jit(solution)/shard_map/ppermute | solution.py:29
  61.0 1.1 %collective-permute-done.20.refs_6_ = f32[64,128]{1,0:T(8,128)S(1)} collective-permute-done((f32[64,128]{1,0:T(8,128)S(1)}, f32[64,128]{1,0:T(8,128)S(1)}, u32[]{:S(2)}, u32[]{:S(2)}) %collective-permute-start.20) | collective-permute-done | bytes 32800 | tf_op jit(solution)/shard_map/ppermute | solution.py:29
  62.1 5.4 %shard_map.74 = f32[64,1024]{1,0:T(8,128)} custom-call(f32[64,256]{1,0:T(8,128)S(1)} %shard_map.72.refs_0_, f32[64,256]{1,0:T(8,128)S(1)} %collective-permute-done.15.refs_1_, f32[64,256]{1,0:T(8,128)S(1)} %collective-permute-done.16.refs_2_, f32[64,256]{1,0:T(8,128)S(1)} %collective-permute-done.17.refs_3_, f32[64,128]{1,0:T(8,128)S(1)} %add.9.refs_4_, ...), custom_call_target="tpu_custom_call" | custom-call | tf_op jit(solution)/shard_map/pallas_call | solution.py:303
  (16 shorter events, 0.1 us)
Async XLA Ops:
  1.1 18.1 %collective-permute-start = (bf16[256,1024]{1,0:T(8,128)(2,1)S(1)}, bf16[256,1024]{1,0:T(8,128)(2,1)S(1)}, u32[]{:S(2)}, u32[]{:S(2)}) collective-permute-start(bf16[256,1024]{1,0:T(8,128)(2,1)S(1)} %constant_dynamic-slice_fusion), channel_id=1, source_target_pairs={{0,28},{4,0},{8,4},{12,8},{16,12},{20,16},{24,20},{28,24},{1,29},{... | collective-permute-start | bytes 1572872 | tf_op jit(solution)/shard_map/ppermute | solution.py:24
  8.5 3.6 %collective-permute-start.3 = (s32[3,24]{1,0:T(4,128)S(1)}, s32[3,24]{1,0:T(4,128)S(1)}, u32[]{:S(2)}, u32[]{:S(2)}) collective-permute-start(s32[3,24]{1,0:T(4,128)S(1)} %pad_add_fusion.refs_0_), channel_id=1, source_target_pairs={{0,3},{1,2},{2,1},{3,0},{4,7},{5,6},{6,5},{7,4},{8,11},{9,10},{10,... | collective-permute-start | bytes 872 | tf_op jit(solution)/shard_map/ppermute | solution.py:29
  9.2 3.6 %collective-permute-start.2 = (s32[3,24]{1,0:T(4,128)S(1)}, s32[3,24]{1,0:T(4,128)S(1)}, u32[]{:S(2)}, u32[]{:S(2)}) collective-permute-start(s32[3,24]{1,0:T(4,128)S(1)} %pad_add_fusion.refs_0_), channel_id=1, source_target_pairs={{0,2},{1,3},{2,0},{3,1},{4,6},{5,7},{6,4},{7,5},{8,10},{9,11},{10,... | collective-permute-start | bytes 872 | tf_op jit(solution)/shard_map/ppermute | solution.py:29
  10.1 2.7 %collective-permute-start.1 = (s32[3,24]{1,0:T(4,128)S(1)}, s32[3,24]{1,0:T(4,128)S(1)}, u32[]{:S(2)}, u32[]{:S(2)}) collective-permute-start(s32[3,24]{1,0:T(4,128)S(1)} %pad_add_fusion.refs_0_), channel_id=1, source_target_pairs={{0,1},{1,0},{2,3},{3,2},{4,5},{5,4},{6,7},{7,6},{8,9},{9,8},{10,11... | collective-permute-start | bytes 872 | tf_op jit(solution)/shard_map/ppermute | solution.py:29
  10.4 0.9 %copy-start.1 = (f32[64,1024]{1,0:T(8,128)S(1)}, f32[64,1024]{1,0:T(8,128)}, u32[]{:S(2)}) copy-start(f32[64,1024]{1,0:T(8,128)} %start_ref.1) | copy-start | bytes 786436
  11.3 0.7 %copy-start.2 = (bf16[1024]{0:T(1024)(128)(2,1)S(1)}, bf16[1024]{0:T(1024)(128)(2,1)}, u32[]{:S(2)}) copy-start(bf16[1024]{0:T(1024)(128)(2,1)} %param.7) | copy-start | bytes 6148
  12.9 6.3 %collective-permute-start.4 = (bf16[80,256]{1,0:T(8,128)(2,1)S(1)}, bf16[80,256]{1,0:T(8,128)(2,1)S(1)}, u32[]{:S(2)}, u32[]{:S(2)}) collective-permute-start(bf16[80,256]{1,0:T(8,128)(2,1)S(1)} %get-tuple-element.29), channel_id=1, source_target_pairs={{0,28},{4,0},{8,4},{12,8},{16,12},{20,16},{24,20},{28,24},{1,29},{... | collective-permute-start | bytes 122888 | tf_op jit(solution)/shard_map/ppermute | solution.py:24
  13.5 1.6 %copy-start = (bf16[1024,1024]{1,0:T(8,128)(2,1)S(1)}, bf16[1024,1024]{1,0:T(8,128)(2,1)}, u32[]{:S(2)}) copy-start(bf16[1024,1024]{1,0:T(8,128)(2,1)} %cells_ref.1) | copy-start | bytes 6291460
  21.2 1.4 %collective-permute-start.5 = (f32[2,72,256]{2,1,0:T(8,128)S(1)}, f32[2,72,256]{2,1,0:T(8,128)S(1)}, u32[]{:S(2)}, u32[]{:S(2)}) collective-permute-start(f32[2,72,256]{2,1,0:T(8,128)S(1)} %get-tuple-element.33), channel_id=1, source_target_pairs={{0,1},{1,0},{2,3},{3,2},{4,5},{5,4},{6,7},{7,6},{8,9},{9,8},{10,11... | collective-permute-start | bytes 442376 | tf_op jit(solution)/shard_map/ppermute | solution.py:29
  21.3 8.1 %collective-permute-start.7 = (f32[72,256]{1,0:T(8,128)S(1)}, f32[72,256]{1,0:T(8,128)S(1)}, u32[]{:S(2)}, u32[]{:S(2)}) collective-permute-start(f32[72,256]{1,0:T(8,128)S(1)} %get-tuple-element.36), channel_id=1, source_target_pairs={{0,4},{4,8},{8,12},{12,16},{16,20},{20,24},{24,28},{28,0},{1,5},{5... | collective-permute-start | bytes 221192 | tf_op jit(solution)/shard_map/ppermute | solution.py:24
  22.7 6.7 %collective-permute-start.6 = (f32[72,256]{1,0:T(8,128)S(1)}, f32[72,256]{1,0:T(8,128)S(1)}, u32[]{:S(2)}, u32[]{:S(2)}) collective-permute-start(f32[72,256]{1,0:T(8,128)S(1)} %get-tuple-element.35), channel_id=1, source_target_pairs={{0,2},{1,3},{2,0},{3,1},{4,6},{5,7},{6,4},{7,5},{8,10},{9,11},{10,... | collective-permute-start | bytes 221192 | tf_op jit(solution)/shard_map/ppermute | solution.py:29
  29.4 4.8 %collective-permute-start.11 = (f32[64,256]{1,0:T(8,128)S(1)}, f32[64,256]{1,0:T(8,128)S(1)}, u32[]{:S(2)}, u32[]{:S(2)}) collective-permute-start(f32[64,256]{1,0:T(8,128)S(1)} %get-tuple-element.40.rest_0_), channel_id=1, source_target_pairs={{0,3},{1,2},{2,1},{3,0},{4,7},{5,6},{6,5},{7,4},{8,11},{9,10},{10,... | collective-permute-start | bytes 196616 | tf_op jit(solution)/shard_map/ppermute | solution.py:29
  30.5 4.8 %collective-permute-start.10 = (f32[64,256]{1,0:T(8,128)S(1)}, f32[64,256]{1,0:T(8,128)S(1)}, u32[]{:S(2)}, u32[]{:S(2)}) collective-permute-start(f32[64,256]{1,0:T(8,128)S(1)} %get-tuple-element.40.rest_0_), channel_id=1, source_target_pairs={{0,2},{1,3},{2,0},{3,1},{4,6},{5,7},{6,4},{7,5},{8,10},{9,11},{10,... | collective-permute-start | bytes 196616 | tf_op jit(solution)/shard_map/ppermute | solution.py:29
  31.1 4.2 %collective-permute-start.9 = (f32[64,256]{1,0:T(8,128)S(1)}, f32[64,256]{1,0:T(8,128)S(1)}, u32[]{:S(2)}, u32[]{:S(2)}) collective-permute-start(f32[64,256]{1,0:T(8,128)S(1)} %get-tuple-element.40.rest_0_), channel_id=1, source_target_pairs={{0,1},{1,0},{2,3},{3,2},{4,5},{5,4},{6,7},{7,6},{8,9},{9,8},{10,11... | collective-permute-start | bytes 196616 | tf_op jit(solution)/shard_map/ppermute | solution.py:29
  31.4 4.8 %collective-permute-start.8 = (f32[64,256]{1,0:T(8,128)S(1)}, f32[64,256]{1,0:T(8,128)S(1)}, u32[]{:S(2)}, u32[]{:S(2)}) collective-permute-start(f32[64,256]{1,0:T(8,128)S(1)} %get-tuple-element.40.rest_0_), channel_id=1, source_target_pairs={{0,28},{4,0},{8,4},{12,8},{16,12},{20,16},{24,20},{28,24},{1,29},{... | collective-permute-start | bytes 196616 | tf_op jit(solution)/shard_map/ppermute | solution.py:24
  36.9 1.4 %collective-permute-start.12 = (f32[2,64,256]{2,1,0:T(8,128)S(1)}, f32[2,64,256]{2,1,0:T(8,128)S(1)}, u32[]{:S(2)}, u32[]{:S(2)}) collective-permute-start(f32[2,64,256]{2,1,0:T(8,128)S(1)} %get-tuple-element.42), channel_id=1, source_target_pairs={{0,1},{1,0},{2,3},{3,2},{4,5},{5,4},{6,7},{7,6},{8,9},{9,8},{10,11... | collective-permute-start | bytes 393224 | tf_op jit(solution)/shard_map/ppermute | solution.py:29
  37.0 7.8 %collective-permute-start.14 = (f32[64,256]{1,0:T(8,128)S(1)}, f32[64,256]{1,0:T(8,128)S(1)}, u32[]{:S(2)}, u32[]{:S(2)}) collective-permute-start(f32[64,256]{1,0:T(8,128)S(1)} %get-tuple-element.45), channel_id=1, source_target_pairs={{0,4},{4,8},{8,12},{12,16},{16,20},{20,24},{24,28},{28,0},{1,5},{5... | collective-permute-start | bytes 196616 | tf_op jit(solution)/shard_map/ppermute | solution.py:24
  38.3 6.5 %collective-permute-start.13 = (f32[64,256]{1,0:T(8,128)S(1)}, f32[64,256]{1,0:T(8,128)S(1)}, u32[]{:S(2)}, u32[]{:S(2)}) collective-permute-start(f32[64,256]{1,0:T(8,128)S(1)} %get-tuple-element.44), channel_id=1, source_target_pairs={{0,2},{1,3},{2,0},{3,1},{4,6},{5,7},{6,4},{7,5},{8,10},{9,11},{10,... | collective-permute-start | bytes 196616 | tf_op jit(solution)/shard_map/ppermute | solution.py:29
  44.8 4.4 %collective-permute-start.17 = (f32[64,256]{1,0:T(8,128)S(1)}, f32[64,256]{1,0:T(8,128)S(1)}, u32[]{:S(2)}, u32[]{:S(2)}) collective-permute-start(f32[64,256]{1,0:T(8,128)S(1)} %shard_map.72.refs_0_), channel_id=1, source_target_pairs={{0,3},{1,2},{2,1},{3,0},{4,7},{5,6},{6,5},{7,4},{8,11},{9,10},{10,... | collective-permute-start | bytes 196616 | tf_op jit(solution)/shard_map/ppermute | solution.py:29
  45.8 4.8 %collective-permute-start.16 = (f32[64,256]{1,0:T(8,128)S(1)}, f32[64,256]{1,0:T(8,128)S(1)}, u32[]{:S(2)}, u32[]{:S(2)}) collective-permute-start(f32[64,256]{1,0:T(8,128)S(1)} %shard_map.72.refs_0_), channel_id=1, source_target_pairs={{0,2},{1,3},{2,0},{3,1},{4,6},{5,7},{6,4},{7,5},{8,10},{9,11},{10,... | collective-permute-start | bytes 196616 | tf_op jit(solution)/shard_map/ppermute | solution.py:29
  46.4 4.2 %collective-permute-start.15 = (f32[64,256]{1,0:T(8,128)S(1)}, f32[64,256]{1,0:T(8,128)S(1)}, u32[]{:S(2)}, u32[]{:S(2)}) collective-permute-start(f32[64,256]{1,0:T(8,128)S(1)} %shard_map.72.refs_0_), channel_id=1, source_target_pairs={{0,1},{1,0},{2,3},{3,2},{4,5},{5,4},{6,7},{7,6},{8,9},{9,8},{10,11... | collective-permute-start | bytes 196616 | tf_op jit(solution)/shard_map/ppermute | solution.py:29
  51.1 4.0 %collective-permute-start.18 = (f32[64,128]{1,0:T(8,128)S(1)}, f32[64,128]{1,0:T(8,128)S(1)}, u32[]{:S(2)}, u32[]{:S(2)}) collective-permute-start(f32[64,128]{1,0:T(8,128)S(1)} %shard_map.73), channel_id=1, source_target_pairs={{0,4},{4,0},{8,12},{12,8},{16,20},{20,16},{24,28},{28,24},{1,5},{5... | collective-permute-start | bytes 98312 | tf_op jit(solution)/shard_map/ppermute | solution.py:29
  55.1 5.9 %collective-permute-start.21 = (f32[64,128]{1,0:T(8,128)S(1)}, f32[64,128]{1,0:T(8,128)S(1)}, u32[]{:S(2)}, u32[]{:S(2)}) collective-permute-start(f32[64,128]{1,0:T(8,128)S(1)} %add.9.refs_4_), channel_id=1, source_target_pairs={{0,24},{4,28},{8,16},{12,20},{16,8},{20,12},{24,0},{28,4},{1,25},{... | collective-permute-start | bytes 98312 | tf_op jit(solution)/shard_map/ppermute | solution.py:29
  57.3 4.8 %collective-permute-start.20 = (f32[64,128]{1,0:T(8,128)S(1)}, f32[64,128]{1,0:T(8,128)S(1)}, u32[]{:S(2)}, u32[]{:S(2)}) collective-permute-start(f32[64,128]{1,0:T(8,128)S(1)} %add.9.refs_4_), channel_id=1, source_target_pairs={{0,16},{4,20},{8,24},{12,28},{16,0},{20,4},{24,8},{28,12},{1,17},{... | collective-permute-start | bytes 98312 | tf_op jit(solution)/shard_map/ppermute | solution.py:29
  57.3 4.8 %collective-permute-start.19 = (f32[64,128]{1,0:T(8,128)S(1)}, f32[64,128]{1,0:T(8,128)S(1)}, u32[]{:S(2)}, u32[]{:S(2)}) collective-permute-start(f32[64,128]{1,0:T(8,128)S(1)} %add.9.refs_4_), channel_id=1, source_target_pairs={{0,8},{4,12},{8,0},{12,4},{16,24},{20,28},{24,16},{28,20},{1,9},{5... | collective-permute-start | bytes 98312 | tf_op jit(solution)/shard_map/ppermute | solution.py:29

commit v5 on v4

--- a/solution.py
+++ b/solution.py
@@ -19,9 +19,10 @@
 bf16 = jnp.bfloat16
 
 
-def shift(cells, step):
+def shift(cells, step, around=True):
     count = lax.axis_size("rows")
-    return lax.ppermute(cells, "rows", [(i, (i + step) % count) for i in range(count)])
+    pairs = [(i, (i + step) % count) for i in range(count) if around or 0 <= i + step < count]
+    return lax.ppermute(cells, "rows", pairs)
 
 
 def swap(cells, axis, offset):
@@ -31,6 +32,13 @@
 
 def lane_swaps(cells):
     return [cells] + [swap(cells, "cols", d) for d in range(1, lax.axis_size("cols"))]
+
+
+def lane_gather(cells):
+    lanes = lax.axis_size("cols")
+    even = [cells] + [swap(cells, "cols", d) for d in range(2, lanes, 2)]
+    odd = [swap(part, "cols", 1) for part in even]
+    return [part for pair in zip(even, odd) for part in pair]
 
 
 def all_rows(cells):
@@ -96,32 +104,33 @@
     shape = (tile, 2 * size)
     place = lax.broadcasted_iota(jnp.int32, shape, 0)
 
-    def spread(piece):
+    def wide(piece):
         return jnp.broadcast_to(piece, shape)
 
-    out = []
-    for b in range(count):
-        first = b * tile
-        columns = [
-            [spread(parts[g][:, first + t : first + t + 1]) for g in range(b, count)]
+    def spread(b):
+        if b >= count:
+            return []
+        return [
+            {g: wide(parts[g][:, b * tile + t : b * tile + t + 1]) for g in range(b, count)}
             for t in range(tile)
         ]
-        home = parts[b]
-        scales = jnp.ones(shape, f32)
+
+    scales = [jnp.ones(shape, f32) for _ in range(count)]
+    columns = spread(0) + spread(1)
+    for b in range(count):
         for t in range(tile):
-            scale = lax.rsqrt(spread(columns[t][0][t : t + 1]))
-            scales = jnp.where(place == t, scale, scales)
-            factor = [column * scale for column in columns[t]]
-            factor[0] = jnp.where(place > t, factor[0], 0.0)
-            for u in range(t + 1, tile):
-                ahead = spread(columns[u][0][t : t + 1]) * scale
-                columns[u] = [c - f * ahead for c, f in zip(columns[u], factor)]
-            row = spread(home[t : t + 1]) * scale
-            home = home - factor[0] * row
-            for g in range(b + 1, count):
-                parts[g] = parts[g] - factor[g - b] * row
-        out.append((home * scales)[:, size:])
-    return jnp.concatenate(out, axis=0)
+            scale = lax.rsqrt(wide(columns[t][b][t : t + 1]))
+            scales[b] = jnp.where(place == t, scale, scales[b])
+            factor = {g: column * scale for g, column in columns[t].items()}
+            for u in range(t + 1, len(columns)):
+                ahead = wide(columns[t][b + u // tile][u % tile : u % tile + 1]) * scale
+                columns[u] = {g: c - factor[g] * ahead for g, c in columns[u].items()}
+            factor[b] = jnp.where(place > t, factor[b], 0.0)
+            row = wide(parts[b][t : t + 1]) * scale
+            for g in range(b, count):
+                parts[g] = parts[g] - factor[g] * row
+        columns = columns[tile:] + spread(b + 2)
+    return jnp.concatenate([(p * s)[:, size:] for p, s in zip(parts, scales)], axis=0)
 
 
 def times(left, right):
@@ -179,21 +188,14 @@
     side_ref[...] = jnp.concatenate([left_ref[0, :size, :], after], axis=0)
 
 
-def own_kernel(lanes, cells_ref, mean_ref, left_ref, unit_ref, weight_ref, product_ref, held, sems):
-    lane = lax.axis_index("cols")
-    copies = [
-        pltpu.make_async_copy(cells_ref.at[block_of(lane, d), :], held.at[d], sems.at[d])
-        for d in range(lanes)
-    ]
-    for copy in copies:
-        copy.start()
+def own_kernel(lanes, cells_ref, mean_ref, left_ref, unit_ref, weight_ref, product_ref):
+    lane = lax.axis_index("cols")
     eye = diagonal(BLOCK)
     col_mean = upright(mean_ref[:, block_of(lane, 0)], eye)
     left = left_ref[0]
     rows = product_ref.shape[1]
     for d in range(lanes):
-        copies[d].wait()
-        unit = unit_rows(held[d])
+        unit = unit_rows(cells_ref[block_of(lane, d), :])
         unit_ref[d] = unit
         if d == 0:
             own = unit
@@ -297,15 +299,13 @@
         out_ref[:, block_of(lane, d)] = times(second, solved[d])
 
 
-def call(body, outs, *args, scratch=(), apart=()):
+def call(body, outs, *args):
     vmem = pl.BlockSpec(memory_space=pltpu.VMEM)
-    where = [pl.BlockSpec(memory_space=pltpu.HBM) if k in apart else vmem for k in range(len(args))]
     return pl.pallas_call(
         body,
         out_shape=[jax.ShapeDtypeStruct(shape, kind) for shape, kind in outs],
-        in_specs=where,
+        in_specs=[vmem] * len(args),
         out_specs=[vmem] * len(outs),
-        scratch_shapes=list(scratch),
         compiler_params=pltpu.CompilerParams(vmem_limit_bytes=40 * 1024 * 1024),
     )(*args)
 
@@ -321,7 +321,7 @@
     assert rows_here == lanes * BLOCK and lanes & (lanes - 1) == 0 and groups & (groups - 1) == 0
     wide = size + 8
 
-    next_cells = shift(lax.dynamic_slice_in_dim(embeddings, lane * BLOCK, BLOCK, 0), -1)
+    next_cells = shift(lax.dynamic_slice_in_dim(embeddings, lane * BLOCK, BLOCK, 0), -1, around=False)
     counts = jnp.pad(pair_count, ((0, 0), (0, slots - 1)))
     mine = jnp.concatenate([pair_rows[0], pair_cols[0], counts], axis=0)
     mean, left = call(
@@ -349,8 +349,6 @@
         embeddings,
         mean,
         left,
-        scratch=[pltpu.VMEM((lanes, BLOCK, width), bf16), pltpu.SemaphoreType.DMA((lanes,))],
-        apart=(0,),
     )
     next_weights, keep, core, back = call(
         functools.partial(next_kernel, lanes),
@@ -388,12 +386,12 @@
         masks,
         next_side,
         shift(smooth, -1),
-        *lane_swaps(smooth),
+        *lane_gather(smooth),
     )
 
     products = scattered(keep, core, back)
     (smooth,) = call(resmooth_kernel, [((size, BLOCK), f32)], degree, *products)
-    blocks = lane_swaps(smooth)
+    blocks = lane_gather(smooth)
     (grams,) = call(
         functools.partial(grams_kernel, total), [((size, 2 * size), f32)], gram, *blocks
     )

time: 67.7 us -> 64.5 us (0.953)
  waiting for transfers between devices: 26 us -> 23 us
  Pallas kernels: 12 us -> 9.8 us
  starting transfers between devices: 23.7 us -> 25.7 us
    ppermute x5, starting transfers between devices: 10.2 us -> 13 us  [shift(): return lax.ppermute(cells, 'rows', pairs)]
    pallas_call x11, Pallas kernels: 12 us -> 9.8 us  [call(): pl.pallas_call(body, out_shape=[jax.ShapeDtypeStruct(shape, kind) for sha...]
    ppermute x5, waiting for transfers between devices: 11.8 us -> 9.92 us  [shift(): return lax.ppermute(cells, 'rows', pairs)]
    ppermute x17, waiting for transfers between devices: 14.2 us -> 13.1 us  [swap(): return lax.ppermute(cells, axis, [(i, i ^ offset) for i in range(count)])]
    ppermute x17, starting transfers between devices: 13.5 us -> 12.7 us  [swap(): return lax.ppermute(cells, axis, [(i, i ^ offset) for i in range(count)])]
  transfers between devices with their start and end apart: 22 -> 22, of which waited for: 13 -> 10; matrix products, arithmetic and copies ran while one was open for 1% -> 1% of each run, Pallas kernels for 5% -> 3%
where the time goes in v5:
time: 64.5 us; the launch traced here: 64.2 us
  starting transfers between devices  25.7 us (40%)
  waiting for transfers between devices  23 us (36%)
  Pallas kernels  9.8 us (15%)
  local copies, waits for them, and re-layouts  4.3 us (7%)
  between operations  0.77 us (1%)
  other arithmetic  0.69 us (1%)
    ppermute x17, waiting for transfers between devices, swap(): return lax.ppermute(cells, axis, [(i, i ^ offset) for i in range(count)])  13.1 us
    ppermute x5, starting transfers between devices, shift(): return lax.ppermute(cells, 'rows', pairs)  13 us
    ppermute x17, starting transfers between devices, swap(): return lax.ppermute(cells, axis, [(i, i ^ offset) for i in range(count)])  12.7 us
    ppermute x5, waiting for transfers between devices, shift(): return lax.ppermute(cells, 'rows', pairs)  9.92 us
    pallas_call x11, Pallas kernels, call(): pl.pallas_call(body, out_shape=[jax.ShapeDtypeStruct(shape, kind) for sha...  9.8 us
    unnamed x6, local copies, waits for them, and re-layouts  3.22 us
  transfers between devices with their start and end apart: 22, of which 10 were waited for; matrix products, arithmetic and copies ran while one was open for 1% of the time, Pallas kernels for 3%

profile of v5, /device:TPU:0, one launch (start us, length us, event | category | flops | bytes accessed | tf_op | source)
XLA Modules:
  0.0 64.2 jit_solution(4084135117215876085)
XLA Ops:
  0.0 1.1 %constant_dynamic-slice_fusion = bf16[256,1024]{1,0:T(8,128)(2,1)S(1)} fusion(bf16[1024,1024]{1,0:T(8,128)(2,1)} %cells_ref.1, s32[]{:T(128)S(6)} %select_n.3), kind=kLoop, calls=%fused_computation.1 | loop fusion | bytes 1048580 | tf_op jit(solution)/shard_map/dynamic_slice | solution.py:324
  1.1 1.3 %collective-permute-start = (bf16[256,1024]{1,0:T(8,128)(2,1)S(1)}, bf16[256,1024]{1,0:T(8,128)(2,1)S(1)}, u32[]{:S(2)}, u32[]{:S(2)}) collective-permute-start(bf16[256,1024]{1,0:T(8,128)(2,1)S(1)} %constant_dynamic-slice_fusion), channel_id=1, source_target_pairs={{4,0},{8,4},{12,8},{16,12},{20,16},{24,20},{28,24},{5,1},{9,5},{13... | collective-permute-start | bytes 1572872 | tf_op jit(solution)/shard_map/ppermute | solution.py:25
  3.0 0.7 %pad_add_fusion.refs_0_ = s32[3,24]{1,0:T(4,128)S(1)} fusion(s32[1,1]{1,0:T(1,128)S(6)} %copy.7, s32[1,24]{1,0:T(1,128)} %bitcast.4, s32[1,24]{1,0:T(1,128)} %bitcast.5), kind=kLoop, calls=%fused_computation | loop fusion | flops 144 | bytes 484 | tf_op jit(solution)/shard_map/concatenate | solution.py:326
  3.7 2.4 %collective-permute-start.3 = (s32[3,24]{1,0:T(4,128)S(1)}, s32[3,24]{1,0:T(4,128)S(1)}, u32[]{:S(2)}, u32[]{:S(2)}) collective-permute-start(s32[3,24]{1,0:T(4,128)S(1)} %pad_add_fusion.refs_0_), channel_id=1, source_target_pairs={{0,3},{1,2},{2,1},{3,0},{4,7},{5,6},{6,5},{7,4},{8,11},{9,10},{10,... | collective-permute-start | bytes 872 | tf_op jit(solution)/shard_map/ppermute | solution.py:30
  6.1 0.6 collective-permute-start.2
  6.8 0.0 collective-permute-start.1
  6.8 0.9 %copy-done.1 = f32[64,1024]{1,0:T(8,128)S(1)} copy-done((f32[64,1024]{1,0:T(8,128)S(1)}, f32[64,1024]{1,0:T(8,128)}, u32[]{:S(2)}) %copy-start.1) | copy-done | bytes 262168
  7.8 0.7 %copy-done.2 = bf16[1024]{0:T(1024)(128)(2,1)S(1)} copy-done((bf16[1024]{0:T(1024)(128)(2,1)S(1)}, bf16[1024]{0:T(1024)(128)(2,1)}, u32[]{:S(2)}) %copy-start.2) | copy-done | bytes 2072
  8.5 1.2 %collective-permute-done.2.refs_2_ = s32[3,24]{1,0:T(4,128)S(1)} collective-permute-done((s32[3,24]{1,0:T(4,128)S(1)}, s32[3,24]{1,0:T(4,128)S(1)}, u32[]{:S(2)}, u32[]{:S(2)}) %collective-permute-start.2) | collective-permute-done | bytes 320 | tf_op jit(solution)/shard_map/ppermute | solution.py:30
  9.7 0.0 collective-permute-done.1.refs_1_
  9.7 0.2 shard_map.66
  9.9 5.5 %collective-permute-start.4 = (bf16[80,256]{1,0:T(8,128)(2,1)S(1)}, bf16[80,256]{1,0:T(8,128)(2,1)S(1)}, u32[]{:S(2)}, u32[]{:S(2)}) collective-permute-start(bf16[80,256]{1,0:T(8,128)(2,1)S(1)} %get-tuple-element.29), channel_id=1, source_target_pairs={{0,28},{4,0},{8,4},{12,8},{16,12},{20,16},{24,20},{28,24},{1,29},{... | collective-permute-start | bytes 122888 | tf_op jit(solution)/shard_map/ppermute | solution.py:25
  15.4 1.6 %copy-done = bf16[1024,1024]{1,0:T(8,128)(2,1)S(1)} copy-done((bf16[1024,1024]{1,0:T(8,128)(2,1)S(1)}, bf16[1024,1024]{1,0:T(8,128)(2,1)}, u32[]{:S(2)}) %copy-start) | copy-done | bytes 2097176
  17.0 1.8 %shard_map.65 = (bf16[4,256,1024]{2,1,0:T(8,128)(2,1)S(1)}, bf16[4,256,256]{2,1,0:T(8,128)(2,1)S(1)}, f32[4,72,256]{2,1,0:T(8,128)S(1)}) custom-call(bf16[1024,1024]{1,0:T(8,128)(2,1)S(1)} %copy-done, f32[1,1024]{1,0:T(1,128)S(1)} %get-tuple-element.26.mean_ref.refs_3_, bf16[4,80,256]{2,1,0:T(8,128)(2,1)S(1)} %get-tuple-element.27.left_ref.refs_4_), custom_call_target="tpu_custom_call" | custom-call | tf_op jit(solution)/shard_map/pallas_call | solution.py:304
  18.8 0.0 collective-permute-done.4.refs_2_.side_ref
  18.8 2.0 %shard_map.67 = (bf16[4,256,256]{2,1,0:T(8,128)(2,1)S(1)}, f32[2,72,256]{2,1,0:T(8,128)S(1)}, f32[2,72,256]{2,1,0:T(8,128)S(1)}, f32[72,256]{1,0:T(8,128)S(1)}) custom-call(bf16[4,256,1024]{2,1,0:T(8,128)(2,1)S(1)} %get-tuple-element.28.refs_0_, bf16[256,1024]{1,0:T(8,128)(2,1)S(1)} %collective-permute-done.refs_1_, ...), custom_call_target="tpu_custom_call" | custom-call | tf_op jit(solution)/shard_map/pallas_call | solution.py:304
  20.9 0.1 collective-permute-start.5
  21.0 2.6 %collective-permute-start.7 = (f32[72,256]{1,0:T(8,128)S(1)}, f32[72,256]{1,0:T(8,128)S(1)}, u32[]{:S(2)}, u32[]{:S(2)}) collective-permute-start(f32[72,256]{1,0:T(8,128)S(1)} %get-tuple-element.36), channel_id=1, source_target_pairs={{0,4},{4,8},{8,12},{12,16},{16,20},{20,24},{24,28},{28,0},{1,5},{5... | collective-permute-start | bytes 221192 | tf_op jit(solution)/shard_map/ppermute | solution.py:25
  23.6 0.0 collective-permute-done.5.came_ref
  23.6 1.6 %collective-permute-start.6 = (f32[72,256]{1,0:T(8,128)S(1)}, f32[72,256]{1,0:T(8,128)S(1)}, u32[]{:S(2)}, u32[]{:S(2)}) collective-permute-start(f32[72,256]{1,0:T(8,128)S(1)} %get-tuple-element.35), channel_id=1, source_target_pairs={{0,2},{1,3},{2,0},{3,1},{4,6},{5,7},{6,4},{7,5},{8,10},{9,11},{10,... | collective-permute-start | bytes 221192 | tf_op jit(solution)/shard_map/ppermute | solution.py:30
  25.1 3.2 %collective-permute-done.7.refs_2_ = f32[72,256]{1,0:T(8,128)S(1)} collective-permute-done((f32[72,256]{1,0:T(8,128)S(1)}, f32[72,256]{1,0:T(8,128)S(1)}, u32[]{:S(2)}, u32[]{:S(2)}) %collective-permute-start.7) | collective-permute-done | bytes 73760 | tf_op jit(solution)/shard_map/ppermute | solution.py:25
  28.3 0.0 collective-permute-done.6.refs_1_
  28.3 1.7 %collective-permute-start.10 = (f32[64,256]{1,0:T(8,128)S(1)}, f32[64,256]{1,0:T(8,128)S(1)}, u32[]{:S(2)}, u32[]{:S(2)}) collective-permute-start(f32[64,256]{1,0:T(8,128)S(1)} %get-tuple-element.40.rest_0_), channel_id=1, source_target_pairs={{0,2},{1,3},{2,0},{3,1},{4,6},{5,7},{6,4},{7,5},{8,10},{9,11},{10,... | collective-permute-start | bytes 196616 | tf_op jit(solution)/shard_map/ppermute | solution.py:30
  30.0 0.0 collective-permute-start.9
  30.0 1.8 %collective-permute-start.8 = (f32[64,256]{1,0:T(8,128)S(1)}, f32[64,256]{1,0:T(8,128)S(1)}, u32[]{:S(2)}, u32[]{:S(2)}) collective-permute-start(f32[64,256]{1,0:T(8,128)S(1)} %get-tuple-element.40.rest_0_), channel_id=1, source_target_pairs={{0,28},{4,0},{8,4},{12,8},{16,12},{20,16},{24,20},{28,24},{1,29},{... | collective-permute-start | bytes 196616 | tf_op jit(solution)/shard_map/ppermute | solution.py:25
  31.9 0.8 %collective-permute-done.10.rest_2_ = f32[64,256]{1,0:T(8,128)S(1)} collective-permute-done((f32[64,256]{1,0:T(8,128)S(1)}, f32[64,256]{1,0:T(8,128)S(1)}, u32[]{:S(2)}, u32[]{:S(2)}) %collective-permute-start.10) | collective-permute-done | bytes 65568 | tf_op jit(solution)/shard_map/ppermute | solution.py:30
  32.7 0.0 collective-permute-start.11
  32.7 0.0 collective-permute-done.9.rest_1_
  32.7 1.9 %collective-permute-done.8.next_ref = f32[64,256]{1,0:T(8,128)S(1)} collective-permute-done((f32[64,256]{1,0:T(8,128)S(1)}, f32[64,256]{1,0:T(8,128)S(1)}, u32[]{:S(2)}, u32[]{:S(2)}) %collective-permute-start.8) | collective-permute-done | bytes 65568 | tf_op jit(solution)/shard_map/ppermute | solution.py:25
  34.5 0.7 %shard_map.70 = (f32[2,64,256]{2,1,0:T(8,128)S(1)}, f32[2,64,256]{2,1,0:T(8,128)S(1)}, f32[64,256]{1,0:T(8,128)S(1)}, f32[64,64]{1,0:T(8,128)S(1)}) custom-call(bf16[4,256,256]{2,1,0:T(8,128)(2,1)S(1)} %get-tuple-element.38.own_ref, bf16[4,256,256]{2,1,0:T(8,128)(2,1)S(1)} %get-tuple-element.39.weight_ref, f32[8,256]{1,0:T(8,128)S(1)} %get-tuple-element.31.refs_6_.mask_ref, ...), custom_call_target="tpu_custom_call" | custom-call | tf_op jit(solution)/shard_map/pallas_call | solution.py:304
  35.3 0.1 collective-permute-start.12
  35.4 1.8 %collective-permute-start.14 = (f32[64,256]{1,0:T(8,128)S(1)}, f32[64,256]{1,0:T(8,128)S(1)}, u32[]{:S(2)}, u32[]{:S(2)}) collective-permute-start(f32[64,256]{1,0:T(8,128)S(1)} %get-tuple-element.45), channel_id=1, source_target_pairs={{0,4},{4,8},{8,12},{12,16},{16,20},{20,24},{24,28},{28,0},{1,5},{5... | collective-permute-start | bytes 196616 | tf_op jit(solution)/shard_map/ppermute | solution.py:25
  37.2 0.6 collective-permute-start.13
  37.8 4.9 %collective-permute-done.14.refs_2_ = f32[64,256]{1,0:T(8,128)S(1)} collective-permute-done((f32[64,256]{1,0:T(8,128)S(1)}, f32[64,256]{1,0:T(8,128)S(1)}, u32[]{:S(2)}, u32[]{:S(2)}) %collective-permute-start.14) | collective-permute-done | bytes 65568 | tf_op jit(solution)/shard_map/ppermute | solution.py:25
  42.7 0.0 collective-permute-done.13.refs_1_
  42.7 1.0 %collective-permute-start.16 = (f32[64,256]{1,0:T(8,128)S(1)}, f32[64,256]{1,0:T(8,128)S(1)}, u32[]{:S(2)}, u32[]{:S(2)}) collective-permute-start(f32[64,256]{1,0:T(8,128)S(1)} %shard_map.72.refs_0_), channel_id=1, source_target_pairs={{0,2},{1,3},{2,0},{3,1},{4,6},{5,7},{6,4},{7,5},{8,10},{9,11},{10,... | collective-permute-start | bytes 196616 | tf_op jit(solution)/shard_map/ppermute | solution.py:30
  43.7 0.0 collective-permute-start.15
  43.7 3.4 %collective-permute-done.16.refs_2_ = f32[64,256]{1,0:T(8,128)S(1)} collective-permute-done((f32[64,256]{1,0:T(8,128)S(1)}, f32[64,256]{1,0:T(8,128)S(1)}, u32[]{:S(2)}, u32[]{:S(2)}) %collective-permute-start.16) | collective-permute-done | bytes 65568 | tf_op jit(solution)/shard_map/ppermute | solution.py:30
  47.0 1.2 %collective-permute-done.17.refs_3_ = f32[64,256]{1,0:T(8,128)S(1)} collective-permute-done((f32[64,256]{1,0:T(8,128)S(1)}, f32[64,256]{1,0:T(8,128)S(1)}, u32[]{:S(2)}, u32[]{:S(2)}) %collective-permute-start.17) | collective-permute-done | bytes 65568 | tf_op jit(solution)/shard_map/ppermute | solution.py:30
  48.3 0.4 shard_map.73
  48.7 0.2 collective-permute-start.18
  48.9 3.8 %collective-permute-done.18 = f32[64,128]{1,0:T(8,128)S(1)} collective-permute-done((f32[64,128]{1,0:T(8,128)S(1)}, f32[64,128]{1,0:T(8,128)S(1)}, u32[]{:S(2)}, u32[]{:S(2)}) %collective-permute-start.18) | collective-permute-done | bytes 32800 | tf_op jit(solution)/shard_map/ppermute | solution.py:30
  52.7 2.2 %collective-permute-start.21 = (f32[64,128]{1,0:T(8,128)S(1)}, f32[64,128]{1,0:T(8,128)S(1)}, u32[]{:S(2)}, u32[]{:S(2)}) collective-permute-start(f32[64,128]{1,0:T(8,128)S(1)} %add.9.refs_4_), channel_id=1, source_target_pairs={{0,24},{4,28},{8,16},{12,20},{16,8},{20,12},{24,0},{28,4},{1,25},{... | collective-permute-start | bytes 98312 | tf_op jit(solution)/shard_map/ppermute | solution.py:30
  54.9 0.0 collective-permute-start.20
  54.9 2.2 %collective-permute-start.19 = (f32[64,128]{1,0:T(8,128)S(1)}, f32[64,128]{1,0:T(8,128)S(1)}, u32[]{:S(2)}, u32[]{:S(2)}) collective-permute-start(f32[64,128]{1,0:T(8,128)S(1)} %add.9.refs_4_), channel_id=1, source_target_pairs={{0,8},{4,12},{8,0},{12,4},{16,24},{20,28},{24,16},{28,20},{1,9},{5... | collective-permute-start | bytes 98312 | tf_op jit(solution)/shard_map/ppermute | solution.py:30
  57.1 1.4 %collective-permute-done.21.refs_7_ = f32[64,128]{1,0:T(8,128)S(1)} collective-permute-done((f32[64,128]{1,0:T(8,128)S(1)}, f32[64,128]{1,0:T(8,128)S(1)}, u32[]{:S(2)}, u32[]{:S(2)}) %collective-permute-start.21) | collective-permute-done | bytes 32800 | tf_op jit(solution)/shard_map/ppermute | solution.py:30
  58.5 1.2 %collective-permute-done.20.refs_6_ = f32[64,128]{1,0:T(8,128)S(1)} collective-permute-done((f32[64,128]{1,0:T(8,128)S(1)}, f32[64,128]{1,0:T(8,128)S(1)}, u32[]{:S(2)}, u32[]{:S(2)}) %collective-permute-start.20) | collective-permute-done | bytes 32800 | tf_op jit(solution)/shard_map/ppermute | solution.py:30
  59.7 4.5 %shard_map.74 = f32[64,1024]{1,0:T(8,128)} custom-call(f32[64,256]{1,0:T(8,128)S(1)} %shard_map.72.refs_0_, f32[64,256]{1,0:T(8,128)S(1)} %collective-permute-done.15.refs_1_, f32[64,256]{1,0:T(8,128)S(1)} %collective-permute-done.16.refs_2_, f32[64,256]{1,0:T(8,128)S(1)} %collective-permute-done.17.refs_3_, f32[64,128]{1,0:T(8,128)S(1)} %add.9.refs_4_, ...), custom_call_target="tpu_custom_call" | custom-call | tf_op jit(solution)/shard_map/pallas_call | solution.py:304
  (16 shorter events, 0.1 us)
Async XLA Ops:
  1.1 17.7 %collective-permute-start = (bf16[256,1024]{1,0:T(8,128)(2,1)S(1)}, bf16[256,1024]{1,0:T(8,128)(2,1)S(1)}, u32[]{:S(2)}, u32[]{:S(2)}) collective-permute-start(bf16[256,1024]{1,0:T(8,128)(2,1)S(1)} %constant_dynamic-slice_fusion), channel_id=1, source_target_pairs={{4,0},{8,4},{12,8},{16,12},{20,16},{24,20},{28,24},{5,1},{9,5},{13... | collective-permute-start | bytes 1572872 | tf_op jit(solution)/shard_map/ppermute | solution.py:25
  3.7 4.8 %collective-permute-start.3 = (s32[3,24]{1,0:T(4,128)S(1)}, s32[3,24]{1,0:T(4,128)S(1)}, u32[]{:S(2)}, u32[]{:S(2)}) collective-permute-start(s32[3,24]{1,0:T(4,128)S(1)} %pad_add_fusion.refs_0_), channel_id=1, source_target_pairs={{0,3},{1,2},{2,1},{3,0},{4,7},{5,6},{6,5},{7,4},{8,11},{9,10},{10,... | collective-permute-start | bytes 872 | tf_op jit(solution)/shard_map/ppermute | solution.py:30
  6.1 3.6 %collective-permute-start.2 = (s32[3,24]{1,0:T(4,128)S(1)}, s32[3,24]{1,0:T(4,128)S(1)}, u32[]{:S(2)}, u32[]{:S(2)}) collective-permute-start(s32[3,24]{1,0:T(4,128)S(1)} %pad_add_fusion.refs_0_), channel_id=1, source_target_pairs={{0,2},{1,3},{2,0},{3,1},{4,6},{5,7},{6,4},{7,5},{8,10},{9,11},{10,... | collective-permute-start | bytes 872 | tf_op jit(solution)/shard_map/ppermute | solution.py:30
  6.8 2.9 %collective-permute-start.1 = (s32[3,24]{1,0:T(4,128)S(1)}, s32[3,24]{1,0:T(4,128)S(1)}, u32[]{:S(2)}, u32[]{:S(2)}) collective-permute-start(s32[3,24]{1,0:T(4,128)S(1)} %pad_add_fusion.refs_0_), channel_id=1, source_target_pairs={{0,1},{1,0},{2,3},{3,2},{4,5},{5,4},{6,7},{7,6},{8,9},{9,8},{10,11... | collective-permute-start | bytes 872 | tf_op jit(solution)/shard_map/ppermute | solution.py:30
  6.8 0.9 %copy-start.1 = (f32[64,1024]{1,0:T(8,128)S(1)}, f32[64,1024]{1,0:T(8,128)}, u32[]{:S(2)}) copy-start(f32[64,1024]{1,0:T(8,128)} %start_ref.1) | copy-start | bytes 786436
  7.8 0.7 %copy-start.2 = (bf16[1024]{0:T(1024)(128)(2,1)S(1)}, bf16[1024]{0:T(1024)(128)(2,1)}, u32[]{:S(2)}) copy-start(bf16[1024]{0:T(1024)(128)(2,1)} %param.7) | copy-start | bytes 6148
  9.9 8.9 %collective-permute-start.4 = (bf16[80,256]{1,0:T(8,128)(2,1)S(1)}, bf16[80,256]{1,0:T(8,128)(2,1)S(1)}, u32[]{:S(2)}, u32[]{:S(2)}) collective-permute-start(bf16[80,256]{1,0:T(8,128)(2,1)S(1)} %get-tuple-element.29), channel_id=1, source_target_pairs={{0,28},{4,0},{8,4},{12,8},{16,12},{20,16},{24,20},{28,24},{1,29},{... | collective-permute-start | bytes 122888 | tf_op jit(solution)/shard_map/ppermute | solution.py:25
  15.4 1.6 %copy-start = (bf16[1024,1024]{1,0:T(8,128)(2,1)S(1)}, bf16[1024,1024]{1,0:T(8,128)(2,1)}, u32[]{:S(2)}) copy-start(bf16[1024,1024]{1,0:T(8,128)(2,1)} %cells_ref.1) | copy-start | bytes 6291460
  20.9 2.7 %collective-permute-start.5 = (f32[2,72,256]{2,1,0:T(8,128)S(1)}, f32[2,72,256]{2,1,0:T(8,128)S(1)}, u32[]{:S(2)}, u32[]{:S(2)}) collective-permute-start(f32[2,72,256]{2,1,0:T(8,128)S(1)} %get-tuple-element.33), channel_id=1, source_target_pairs={{0,1},{1,0},{2,3},{3,2},{4,5},{5,4},{6,7},{7,6},{8,9},{9,8},{10,11... | collective-permute-start | bytes 442376 | tf_op jit(solution)/shard_map/ppermute | solution.py:30
  21.0 7.4 %collective-permute-start.7 = (f32[72,256]{1,0:T(8,128)S(1)}, f32[72,256]{1,0:T(8,128)S(1)}, u32[]{:S(2)}, u32[]{:S(2)}) collective-permute-start(f32[72,256]{1,0:T(8,128)S(1)} %get-tuple-element.36), channel_id=1, source_target_pairs={{0,4},{4,8},{8,12},{12,16},{16,20},{20,24},{24,28},{28,0},{1,5},{5... | collective-permute-start | bytes 221192 | tf_op jit(solution)/shard_map/ppermute | solution.py:25
  23.6 4.7 %collective-permute-start.6 = (f32[72,256]{1,0:T(8,128)S(1)}, f32[72,256]{1,0:T(8,128)S(1)}, u32[]{:S(2)}, u32[]{:S(2)}) collective-permute-start(f32[72,256]{1,0:T(8,128)S(1)} %get-tuple-element.35), channel_id=1, source_target_pairs={{0,2},{1,3},{2,0},{3,1},{4,6},{5,7},{6,4},{7,5},{8,10},{9,11},{10,... | collective-permute-start | bytes 221192 | tf_op jit(solution)/shard_map/ppermute | solution.py:30
  28.3 4.3 %collective-permute-start.10 = (f32[64,256]{1,0:T(8,128)S(1)}, f32[64,256]{1,0:T(8,128)S(1)}, u32[]{:S(2)}, u32[]{:S(2)}) collective-permute-start(f32[64,256]{1,0:T(8,128)S(1)} %get-tuple-element.40.rest_0_), channel_id=1, source_target_pairs={{0,2},{1,3},{2,0},{3,1},{4,6},{5,7},{6,4},{7,5},{8,10},{9,11},{10,... | collective-permute-start | bytes 196616 | tf_op jit(solution)/shard_map/ppermute | solution.py:30
  30.0 2.7 %collective-permute-start.9 = (f32[64,256]{1,0:T(8,128)S(1)}, f32[64,256]{1,0:T(8,128)S(1)}, u32[]{:S(2)}, u32[]{:S(2)}) collective-permute-start(f32[64,256]{1,0:T(8,128)S(1)} %get-tuple-element.40.rest_0_), channel_id=1, source_target_pairs={{0,1},{1,0},{2,3},{3,2},{4,5},{5,4},{6,7},{7,6},{8,9},{9,8},{10,11... | collective-permute-start | bytes 196616 | tf_op jit(solution)/shard_map/ppermute | solution.py:30
  30.0 4.5 %collective-permute-start.8 = (f32[64,256]{1,0:T(8,128)S(1)}, f32[64,256]{1,0:T(8,128)S(1)}, u32[]{:S(2)}, u32[]{:S(2)}) collective-permute-start(f32[64,256]{1,0:T(8,128)S(1)} %get-tuple-element.40.rest_0_), channel_id=1, source_target_pairs={{0,28},{4,0},{8,4},{12,8},{16,12},{20,16},{24,20},{28,24},{1,29},{... | collective-permute-start | bytes 196616 | tf_op jit(solution)/shard_map/ppermute | solution.py:25
  32.7 1.9 %collective-permute-start.11 = (f32[64,256]{1,0:T(8,128)S(1)}, f32[64,256]{1,0:T(8,128)S(1)}, u32[]{:S(2)}, u32[]{:S(2)}) collective-permute-start(f32[64,256]{1,0:T(8,128)S(1)} %collective-permute-done.10.rest_2_), channel_id=1, source_target_pairs={{0,1},{1,0},{2,3},{3,2},{4,5},{5,4},{6,7},{7,6},{8,9},{9,8},{10,11... | collective-permute-start | bytes 196616 | tf_op jit(solution)/shard_map/ppermute | solution.py:30
  35.3 1.9 %collective-permute-start.12 = (f32[2,64,256]{2,1,0:T(8,128)S(1)}, f32[2,64,256]{2,1,0:T(8,128)S(1)}, u32[]{:S(2)}, u32[]{:S(2)}) collective-permute-start(f32[2,64,256]{2,1,0:T(8,128)S(1)} %get-tuple-element.42), channel_id=1, source_target_pairs={{0,1},{1,0},{2,3},{3,2},{4,5},{5,4},{6,7},{7,6},{8,9},{9,8},{10,11... | collective-permute-start | bytes 393224 | tf_op jit(solution)/shard_map/ppermute | solution.py:30
  35.4 7.3 %collective-permute-start.14 = (f32[64,256]{1,0:T(8,128)S(1)}, f32[64,256]{1,0:T(8,128)S(1)}, u32[]{:S(2)}, u32[]{:S(2)}) collective-permute-start(f32[64,256]{1,0:T(8,128)S(1)} %get-tuple-element.45), channel_id=1, source_target_pairs={{0,4},{4,8},{8,12},{12,16},{16,20},{20,24},{24,28},{28,0},{1,5},{5... | collective-permute-start | bytes 196616 | tf_op jit(solution)/shard_map/ppermute | solution.py:25
  37.2 5.5 %collective-permute-start.13 = (f32[64,256]{1,0:T(8,128)S(1)}, f32[64,256]{1,0:T(8,128)S(1)}, u32[]{:S(2)}, u32[]{:S(2)}) collective-permute-start(f32[64,256]{1,0:T(8,128)S(1)} %get-tuple-element.44), channel_id=1, source_target_pairs={{0,2},{1,3},{2,0},{3,1},{4,6},{5,7},{6,4},{7,5},{8,10},{9,11},{10,... | collective-permute-start | bytes 196616 | tf_op jit(solution)/shard_map/ppermute | solution.py:30
  42.7 4.3 %collective-permute-start.16 = (f32[64,256]{1,0:T(8,128)S(1)}, f32[64,256]{1,0:T(8,128)S(1)}, u32[]{:S(2)}, u32[]{:S(2)}) collective-permute-start(f32[64,256]{1,0:T(8,128)S(1)} %shard_map.72.refs_0_), channel_id=1, source_target_pairs={{0,2},{1,3},{2,0},{3,1},{4,6},{5,7},{6,4},{7,5},{8,10},{9,11},{10,... | collective-permute-start | bytes 196616 | tf_op jit(solution)/shard_map/ppermute | solution.py:30
  43.7 3.4 %collective-permute-start.15 = (f32[64,256]{1,0:T(8,128)S(1)}, f32[64,256]{1,0:T(8,128)S(1)}, u32[]{:S(2)}, u32[]{:S(2)}) collective-permute-start(f32[64,256]{1,0:T(8,128)S(1)} %shard_map.72.refs_0_), channel_id=1, source_target_pairs={{0,1},{1,0},{2,3},{3,2},{4,5},{5,4},{6,7},{7,6},{8,9},{9,8},{10,11... | collective-permute-start | bytes 196616 | tf_op jit(solution)/shard_map/ppermute | solution.py:30
  47.0 1.3 %collective-permute-start.17 = (f32[64,256]{1,0:T(8,128)S(1)}, f32[64,256]{1,0:T(8,128)S(1)}, u32[]{:S(2)}, u32[]{:S(2)}) collective-permute-start(f32[64,256]{1,0:T(8,128)S(1)} %collective-permute-done.16.refs_2_), channel_id=1, source_target_pairs={{0,1},{1,0},{2,3},{3,2},{4,5},{5,4},{6,7},{7,6},{8,9},{9,8},{10,11... | collective-permute-start | bytes 196616 | tf_op jit(solution)/shard_map/ppermute | solution.py:30
  48.7 4.0 %collective-permute-start.18 = (f32[64,128]{1,0:T(8,128)S(1)}, f32[64,128]{1,0:T(8,128)S(1)}, u32[]{:S(2)}, u32[]{:S(2)}) collective-permute-start(f32[64,128]{1,0:T(8,128)S(1)} %shard_map.73), channel_id=1, source_target_pairs={{0,4},{4,0},{8,12},{12,8},{16,20},{20,16},{24,28},{28,24},{1,5},{5... | collective-permute-start | bytes 98312 | tf_op jit(solution)/shard_map/ppermute | solution.py:30
  52.7 5.8 %collective-permute-start.21 = (f32[64,128]{1,0:T(8,128)S(1)}, f32[64,128]{1,0:T(8,128)S(1)}, u32[]{:S(2)}, u32[]{:S(2)}) collective-permute-start(f32[64,128]{1,0:T(8,128)S(1)} %add.9.refs_4_), channel_id=1, source_target_pairs={{0,24},{4,28},{8,16},{12,20},{16,8},{20,12},{24,0},{28,4},{1,25},{... | collective-permute-start | bytes 98312 | tf_op jit(solution)/shard_map/ppermute | solution.py:30
  54.9 4.8 %collective-permute-start.20 = (f32[64,128]{1,0:T(8,128)S(1)}, f32[64,128]{1,0:T(8,128)S(1)}, u32[]{:S(2)}, u32[]{:S(2)}) collective-permute-start(f32[64,128]{1,0:T(8,128)S(1)} %add.9.refs_4_), channel_id=1, source_target_pairs={{0,16},{4,20},{8,24},{12,28},{16,0},{20,4},{24,8},{28,12},{1,17},{... | collective-permute-start | bytes 98312 | tf_op jit(solution)/shard_map/ppermute | solution.py:30
  54.9 4.8 %collective-permute-start.19 = (f32[64,128]{1,0:T(8,128)S(1)}, f32[64,128]{1,0:T(8,128)S(1)}, u32[]{:S(2)}, u32[]{:S(2)}) collective-permute-start(f32[64,128]{1,0:T(8,128)S(1)} %add.9.refs_4_), channel_id=1, source_target_pairs={{0,8},{4,12},{8,0},{12,4},{16,24},{20,28},{24,16},{28,20},{1,9},{5... | collective-permute-start | bytes 98312 | tf_op jit(solution)/shard_map/ppermute | solution.py:30

commit v6 on v5

--- a/solution.py
+++ b/solution.py
@@ -32,13 +32,6 @@
 
 def lane_swaps(cells):
     return [cells] + [swap(cells, "cols", d) for d in range(1, lax.axis_size("cols"))]
-
-
-def lane_gather(cells):
-    lanes = lax.axis_size("cols")
-    even = [cells] + [swap(cells, "cols", d) for d in range(2, lanes, 2)]
-    odd = [swap(part, "cols", 1) for part in even]
-    return [part for pair in zip(even, odd) for part in pair]
 
 
 def all_rows(cells):
@@ -48,7 +41,7 @@
     while low < bits:
         wide = 1 if (bits - low) % 2 else 2
         whole = sum(parts[1:], parts[0])
-        parts = [whole] + [swap(whole, "rows", m << low) for m in range(1, 1 << wide)]
+        parts = [whole] + [swap(whole, "rows", m << low) for m in range((1 << wide) - 1, 0, -1)]
         low += wide
     return parts
 
@@ -76,6 +69,10 @@
 def affinity(col_unit, row_unit, col_mean, row_mean):
     scores = nt(col_unit, row_unit)
     return jnp.exp((2.0 * sharpness) * scores / (col_mean + row_mean))
+
+
+def weighted(scores, col_mean, row_mean):
+    return jnp.exp((2.0 * sharpness) * scores / (col_mean + row_mean)).astype(bf16)
 
 
 def with_ones(narrow):
@@ -96,7 +93,7 @@
 
 def inverse_factor(gram):
     size = gram.shape[0]
-    tile = 8
+    tile, step = 8, 4
     count = size // tile
     eye = jnp.where(diagonal(size), 1.0, 0.0).astype(f32)
     table = jnp.concatenate([gram, eye], axis=1)
@@ -107,29 +104,29 @@
     def wide(piece):
         return jnp.broadcast_to(piece, shape)
 
-    def spread(b):
-        if b >= count:
-            return []
+    def spread(first):
         return [
-            {g: wide(parts[g][:, b * tile + t : b * tile + t + 1]) for g in range(b, count)}
-            for t in range(tile)
+            {g: wide(parts[g][:, k : k + 1]) for g in range(k // tile, count)}
+            for k in range(first, min(first + step, size))
         ]
 
     scales = [jnp.ones(shape, f32) for _ in range(count)]
-    columns = spread(0) + spread(1)
-    for b in range(count):
-        for t in range(tile):
-            scale = lax.rsqrt(wide(columns[t][b][t : t + 1]))
-            scales[b] = jnp.where(place == t, scale, scales[b])
+    columns = spread(0) + spread(step)
+    for first in range(0, size, step):
+        for t in range(step):
+            b, at = (first + t) // tile, (first + t) % tile
+            scale = lax.rsqrt(wide(columns[t][b][at : at + 1]))
+            scales[b] = jnp.where(place == at, scale, scales[b])
             factor = {g: column * scale for g, column in columns[t].items()}
             for u in range(t + 1, len(columns)):
-                ahead = wide(columns[t][b + u // tile][u % tile : u % tile + 1]) * scale
+                g, r = (first + u) // tile, (first + u) % tile
+                ahead = wide(columns[t][g][r : r + 1]) * scale
                 columns[u] = {g: c - factor[g] * ahead for g, c in columns[u].items()}
-            factor[b] = jnp.where(place > t, factor[b], 0.0)
-            row = wide(parts[b][t : t + 1]) * scale
+            factor[b] = jnp.where(place > at, factor[b], 0.0)
+            row = wide(parts[b][at : at + 1]) * scale
             for g in range(b, count):
                 parts[g] = parts[g] - factor[g] * row
-        columns = columns[tile:] + spread(b + 2)
+        columns = columns[step:] + spread(first + 2 * step)
     return jnp.concatenate([(p * s)[:, size:] for p, s in zip(parts, scales)], axis=0)
 
 
@@ -179,9 +176,9 @@
 
     mine = group * lanes + lane
     rows = [group * lanes + (lane ^ d) for d in range(lanes)]
-    masks = [live(row, mine) for row in rows] + [live(row, mine + lanes) for row in rows]
+    masks = [live(row, mine) for row in rows] + [live(row, mine - lanes) for row in rows]
     mask_ref[...] = jnp.concatenate(masks, axis=0)
-    back = [live(mine, row - lanes) for row in rows]
+    back = [live(mine, row + lanes) for row in rows]
     means = mean_ref[:, block_of(lane, 0)]
     pad = jnp.zeros((ONES - lanes - 1, BLOCK), f32)
     after = jnp.concatenate([means, *back, pad], axis=0).astype(bf16)
@@ -207,62 +204,34 @@
         product_ref[d] = jnp.dot(left, weights, preferred_element_type=f32)[:rows]
 
 
+def scores_kernel(lanes, unit_ref, cells_ref, scores_ref):
+    col_unit = unit_rows(cells_ref[...])
+    for d in range(lanes):
+        scores_ref[d] = nt(col_unit, unit_ref[d])
+
+
 def next_kernel(lanes, *refs):
-    unit_ref, cells_ref, side_ref, mean_ref, left_ref, own_ref, mask_ref, *outs = refs
-    weight_ref, keep_ref, core_ref, back_ref = outs
+    scores_ref, side_ref, mean_ref, left_ref, own_ref, mask_ref, *outs = refs
+    weight_ref, keep_ref, *core_refs, back_ref = outs
     lane = lax.axis_index("cols")
     size = left_ref.shape[1] - ONES
-    col_unit = unit_rows(cells_ref[...])
     after = side_ref[size:, :].astype(f32)
     col_mean = upright(after[0:1], diagonal(BLOCK))
     left = with_ones(side_ref[:size, :])
     rows = own_ref.shape[1]
     back = jnp.zeros((rows, BLOCK), f32)
     for d in range(lanes):
-        weights = affinity(col_unit, unit_ref[d], col_mean, mean_ref[:, block_of(lane, d)])
-        weights = weights.astype(bf16)
+        weights = weighted(scores_ref[d], col_mean, mean_ref[:, block_of(lane, d)])
         weight_ref[d] = weights
         product = jnp.dot(left, weights, preferred_element_type=f32)[:rows]
         own = mask_ref[d : d + 1, :] * own_ref[d]
-        halves(d, keep_ref, core_ref)[...] = own + mask_ref[lanes + d : lanes + d + 1, :] * product
+        halves(d, keep_ref, core_refs)[...] = own + mask_ref[lanes + d : lanes + d + 1, :] * product
         back = back + after[1 + d : 2 + d] * nt(left_ref[d], weights)[:rows]
     back_ref[...] = back
 
 
-def halves(d, keep_ref, core_ref):
-    return (core_ref if d % 2 else keep_ref).at[d // 2]
-
-
-def pair_kernel(keep_ref, came_ref, own_ref, *away_refs):
-    own_ref[...] = keep_ref[0] + came_ref[0]
-    for m, away_ref in enumerate(away_refs):
-        away_ref[...] = keep_ref[m + 1] + came_ref[m + 1]
-
-
-def smooth_kernel(size, *refs):
-    *parts, smooth_ref, degree_ref = refs
-    total = added(parts)
-    degree = total[size : size + 1]
-    smooth_ref[...] = total[:size] / degree
-    degree_ref[...] = jnp.broadcast_to(degree, degree_ref.shape)
-
-
-def sweep_kernel(lanes, total, own_ref, weight_ref, mask_ref, side_ref, next_ref, *rest):
-    blocks, (keep_ref, core_ref, back_ref, gram_ref) = rest[:lanes], rest[lanes:]
-    size = next_ref.shape[0]
-    own_left = pieces(blocks[0][...])
-    next_left = pieces(next_ref[...])
-    back_masks = side_ref[size:, :].astype(f32)
-    back = jnp.zeros((size, BLOCK), f32)
-    for d in range(lanes):
-        own = joined(jnp.dot(own_left, own_ref[d], preferred_element_type=f32), size)
-        after = joined(jnp.dot(next_left, weight_ref[d], preferred_element_type=f32), size)
-        own = mask_ref[d : d + 1, :] * own
-        halves(d, keep_ref, core_ref)[...] = own + mask_ref[lanes + d : lanes + d + 1, :] * after
-        left = own_left if d == 0 else pieces(blocks[d][...])
-        back = back + back_masks[1 + d : 2 + d] * joined(nt(left, weight_ref[d]), size)
-    back_ref[...] = back
-    gram_ref[...] = gram_of([block[...] for block in blocks], total)
+def halves(d, keep_ref, core_refs):
+    return core_refs[d // 2] if d % 2 else keep_ref.at[d // 2]
 
 
 def added(refs):
@@ -272,24 +241,79 @@
     return total
 
 
-def resmooth_kernel(degree_ref, *refs):
-    *parts, smooth_ref = refs
-    smooth_ref[...] = added(parts) / degree_ref[0:1, :]
-
-
-def grams_kernel(total, first_ref, *refs):
-    *blocks, grams_ref = refs
-    second = gram_of([block[...] for block in blocks], total)
+def chip_kernel(keep_ref, back_ref, *refs):
+    *came_refs, out_ref = refs
+    rows = out_ref.shape[1]
+    for m, came_ref in enumerate(came_refs):
+        total = keep_ref[m] + came_ref[...]
+        out_ref[m] = total + back_ref[:rows] if m == 0 else total
+
+
+def pair_kernel(keep_ref, *refs):
+    *came_refs, own_ref, away_ref = refs
+    own_ref[...] = keep_ref[0] + came_refs[0][...]
+    away_ref[...] = keep_ref[1] + came_refs[1][...]
+
+
+def smooth_kernel(size, *refs):
+    *parts, lead_ref, out_ref, wide_ref = refs
+    total = added(parts)
+    degree = total[size : size + 1]
+    smooth = total[:size] / degree
+    lead_ref[...] = smooth
+    out_ref[:size] = smooth
+    out_ref[size:] = jnp.broadcast_to(degree, (out_ref.shape[0] - size, BLOCK))
+    wide_ref[:size] = smooth
+    wide_ref[size:] = jnp.zeros((wide_ref.shape[0] - size, BLOCK), f32)
+
+
+def back_kernel(lanes, total, weight_ref, side_ref, *refs):
+    *block_refs, back_ref, gram_ref = refs
+    size = gram_ref.shape[0]
+    blocks = [ref[:size] for ref in block_refs]
+    masks = side_ref[size:, :].astype(f32)
+    back = jnp.zeros((size, BLOCK), f32)
+    for d in range(lanes):
+        left = pieces(blocks[d])
+        back = back + masks[1 + d : 2 + d] * joined(nt(left, weight_ref[d]), size)
+    back_ref[:size] = back
+    back_ref[size:] = jnp.zeros((back_ref.shape[0] - size, BLOCK), f32)
+    gram_ref[...] = gram_of(blocks, total)
+
+
+def ordered(here_ref, there_ref):
+    return [ref[m] for m in range(here_ref.shape[0]) for ref in (here_ref, there_ref)]
+
+
+def forward_kernel(lanes, own_ref, weight_ref, mask_ref, lead_ref, next_ref, keep_ref, *core_refs):
+    size = lead_ref.shape[0]
+    own_left = pieces(lead_ref[...])
+    next_left = pieces(next_ref[:size])
+    for d in range(lanes):
+        own = joined(jnp.dot(own_left, own_ref[d], preferred_element_type=f32), size)
+        after = joined(jnp.dot(next_left, weight_ref[d], preferred_element_type=f32), size)
+        own = mask_ref[d : d + 1, :] * own
+        halves(d, keep_ref, core_refs)[...] = own + mask_ref[lanes + d : lanes + d + 1, :] * after
+
+
+def resmooth_kernel(own_ref, came_ref, block_ref, across_ref, out_ref):
+    size = out_ref.shape[1]
+    for m, ref in enumerate((block_ref, across_ref)):
+        out_ref[m] = (own_ref[m] + came_ref[1 - m]) / ref[size : size + 1]
+
+
+def grams_kernel(total, first_ref, here_ref, there_ref, grams_ref):
+    second = gram_of(ordered(here_ref, there_ref), total)
     grams_ref[...] = jnp.concatenate([first_ref[...], second], axis=1)
 
 
-def solve_kernel(lanes, *refs):
-    blocks, grams, out_ref = refs[:lanes], refs[lanes:-1], refs[-1]
+def solve_kernel(lanes, here_ref, there_ref, *refs):
+    *grams, out_ref = refs
     lane = lax.axis_index("cols")
     size = out_ref.shape[0]
     both = added(grams)
     first = inverse_factor(both[:, :size])
-    solved = [times(first, block[...]) for block in blocks]
+    solved = [times(first, block) for block in ordered(here_ref, there_ref)]
     half = times(first, both[:, size:])
     gram = lax.dot_general(
         half, first, (((1,), (1,)), ((), ())), precision=HIGHEST, preferred_element_type=f32
@@ -318,10 +342,10 @@
     lane = lax.axis_index("cols")
     groups = lax.axis_size("rows")
     total = rows_here * groups
-    assert rows_here == lanes * BLOCK and lanes & (lanes - 1) == 0 and groups & (groups - 1) == 0
+    assert rows_here == lanes * BLOCK and lanes == 4 and groups & (groups - 1) == 0
     wide = size + 8
 
-    next_cells = shift(lax.dynamic_slice_in_dim(embeddings, lane * BLOCK, BLOCK, 0), -1, around=False)
+    next_cells = shift(lax.dynamic_slice_in_dim(embeddings, lane * BLOCK, BLOCK, 0), 1)
     counts = jnp.pad(pair_count, ((0, 0), (0, slots - 1)))
     mine = jnp.concatenate([pair_rows[0], pair_cols[0], counts], axis=0)
     mean, left = call(
@@ -337,7 +361,7 @@
         left,
         *lane_swaps(mine),
     )
-    next_side = shift(side, -1)
+    next_side = shift(side, 1)
 
     unit, own_weights, own_product = call(
         functools.partial(own_kernel, lanes),
@@ -350,13 +374,14 @@
         mean,
         left,
     )
-    next_weights, keep, core, back = call(
+    (scores,) = call(
+        functools.partial(scores_kernel, lanes), [((lanes, BLOCK, BLOCK), f32)], unit, next_cells
+    )
+    next_weights, keep, *core, back = call(
         functools.partial(next_kernel, lanes),
-        [((lanes, BLOCK, BLOCK), bf16)]
-        + [((lanes // 2, wide, BLOCK), f32)] * 2
-        + [((wide, BLOCK), f32)],
-        unit,
-        next_cells,
+        [((lanes, BLOCK, BLOCK), bf16), ((lanes // 2, wide, BLOCK), f32)]
+        + [((wide, BLOCK), f32)] * (lanes // 2 + 1),
+        scores,
         next_side,
         mean,
         left,
@@ -364,41 +389,57 @@
         masks,
     )
 
-    def scattered(keep, core, back):
-        back = shift(back, 1)
-        rows = keep.shape[1]
-        own, *away = call(
-            pair_kernel, [((rows, BLOCK), f32)] * (lanes // 2), keep, swap(core, "cols", 1)
-        )
-        return [own, *(swap(part, "cols", 2 * m + 2) for m, part in enumerate(away)), back]
-
-    smooth, degree = call(
+    came = [swap(part, "cols", 1) for part in core]
+    own, away = call(pair_kernel, [((wide, BLOCK), f32)] * 2, keep, *came)
+    lead, smooth, wider = call(
         functools.partial(smooth_kernel, size),
-        [((size, BLOCK), f32), ((8, BLOCK), f32)],
-        *scattered(keep, core, back),
-    )
-
-    keep, core, back, gram = call(
-        functools.partial(sweep_kernel, lanes, total),
-        [((lanes // 2, size, BLOCK), f32)] * 2 + [((size, BLOCK), f32), ((size, size), f32)],
+        [((size, BLOCK), f32), ((wide, BLOCK), f32), ((wide + 8, BLOCK), f32)],
+        own,
+        swap(away, "cols", 2),
+        shift(back, -1),
+    )
+
+    after = shift(wider, 1)
+    across = swap(smooth, "cols", 2)
+    back, gram = call(
+        functools.partial(back_kernel, lanes, total),
+        [((wide, BLOCK), f32), ((size, size), f32)],
+        next_weights,
+        next_side,
+        lead,
+        swap(lead, "cols", 1),
+        across,
+        swap(across, "cols", 1),
+    )
+    masks, gram = lax.optimization_barrier((masks, gram))
+    keep, *core = call(
+        functools.partial(forward_kernel, lanes),
+        [((lanes // 2, size, BLOCK), f32)] + [((size, BLOCK), f32)] * (lanes // 2),
         own_weights,
         next_weights,
         masks,
-        next_side,
-        shift(smooth, -1),
-        *lane_gather(smooth),
-    )
-
-    products = scattered(keep, core, back)
-    (smooth,) = call(resmooth_kernel, [((size, BLOCK), f32)], degree, *products)
-    blocks = lane_gather(smooth)
+        lead,
+        after,
+    )
+    came = [swap(part, "cols", 1) for part in core]
+    (both,) = call(chip_kernel, [(keep.shape, f32)], keep, shift(back, -1, around=False), *came)
+    (here,) = call(
+        resmooth_kernel,
+        [((lanes // 2, size, BLOCK), f32)],
+        both,
+        swap(both, "cols", 2),
+        smooth,
+        across,
+    )
+    there = swap(here, "cols", 1)
     (grams,) = call(
-        functools.partial(grams_kernel, total), [((size, 2 * size), f32)], gram, *blocks
+        functools.partial(grams_kernel, total), [((size, 2 * size), f32)], gram, here, there
     )
     (vector,) = call(
         functools.partial(solve_kernel, lanes),
         [((size, rows_here), f32)],
-        *blocks,
+        here,
+        there,
         *all_rows(grams),
     )
     return vector

time: 64.5 us -> 62.4 us (0.967)
  starting transfers between devices: 25.7 us -> 21.8 us
  waiting for transfers between devices: 23 us -> 25.6 us
  Pallas kernels: 9.8 us -> 8.99 us
    ppermute x5, starting transfers between devices: 13 us -> 7.92 us  [shift(): return lax.ppermute(cells, 'rows', pairs)]
    ppermute x17, waiting for transfers between devices: 13.1 us -> 17 us  [swap(): return lax.ppermute(cells, axis, [(i, i ^ offset) for i in range(count)])]
    ppermute x5, waiting for transfers between devices: 9.92 us -> 8.56 us  [shift(): return lax.ppermute(cells, 'rows', pairs)]
    ppermute x17, starting transfers between devices: 12.7 us -> 13.9 us  [swap(): return lax.ppermute(cells, axis, [(i, i ^ offset) for i in range(count)])]
    pallas_call x11 -> x13, Pallas kernels: 9.8 us -> 8.99 us  [call(): pl.pallas_call(body, out_shape=[jax.ShapeDtypeStruct(shape, kind) for sha...]
  transfers between devices with their start and end apart: 22 -> 22, of which waited for: 10 -> 17; matrix products, arithmetic and copies ran while one was open for 1% -> 1% of each run, Pallas kernels for 3% -> 6%
where the time goes in v6:
time: 62.4 us; the launch traced here: 62.2 us
  waiting for transfers between devices  25.6 us (41%)
  starting transfers between devices  21.8 us (35%)
  Pallas kernels  8.99 us (14%)
  local copies, waits for them, and re-layouts  4.3 us (7%)
  between operations  0.79 us (1%)
  other arithmetic  0.69 us (1%)
    ppermute x17, waiting for transfers between devices, swap(): return lax.ppermute(cells, axis, [(i, i ^ offset) for i in range(count)])  17 us
    ppermute x17, starting transfers between devices, swap(): return lax.ppermute(cells, axis, [(i, i ^ offset) for i in range(count)])  13.9 us
    pallas_call x13, Pallas kernels, call(): pl.pallas_call(body, out_shape=[jax.ShapeDtypeStruct(shape, kind) for sha...  8.99 us
    ppermute x5, waiting for transfers between devices, shift(): return lax.ppermute(cells, 'rows', pairs)  8.56 us
    ppermute x5, starting transfers between devices, shift(): return lax.ppermute(cells, 'rows', pairs)  7.92 us
    unnamed x6, local copies, waits for them, and re-layouts  3.22 us
  transfers between devices with their start and end apart: 22, of which 17 were waited for; matrix products, arithmetic and copies ran while one was open for 1% of the time, Pallas kernels for 6%

profile of v6, /device:TPU:0, one launch (start us, length us, event | category | flops | bytes accessed | tf_op | source)
XLA Modules:
  0.0 62.2 jit_solution(11603148390898656618)
XLA Ops:
  0.0 1.1 %constant_dynamic-slice_fusion = bf16[256,1024]{1,0:T(8,128)(2,1)S(1)} fusion(bf16[1024,1024]{1,0:T(8,128)(2,1)} %cells_ref.1, s32[]{:T(128)S(6)} %select_n.3), kind=kLoop, calls=%fused_computation.1 | loop fusion | bytes 1048580 | tf_op jit(solution)/shard_map/dynamic_slice | solution.py:348
  1.1 3.0 %collective-permute-start = (bf16[256,1024]{1,0:T(8,128)(2,1)S(1)}, bf16[256,1024]{1,0:T(8,128)(2,1)S(1)}, u32[]{:S(2)}, u32[]{:S(2)}) collective-permute-start(bf16[256,1024]{1,0:T(8,128)(2,1)S(1)} %constant_dynamic-slice_fusion), channel_id=1, source_target_pairs={{0,4},{4,8},{8,12},{12,16},{16,20},{20,24},{24,28},{28,0},{1,5},{5... | collective-permute-start | bytes 1572872 | tf_op jit(solution)/shard_map/ppermute | solution.py:25
  4.8 0.7 %pad_add_fusion.refs_0_ = s32[3,24]{1,0:T(4,128)S(1)} fusion(s32[1,1]{1,0:T(1,128)S(6)} %copy.7, s32[1,24]{1,0:T(1,128)} %bitcast.4, s32[1,24]{1,0:T(1,128)} %bitcast.5), kind=kLoop, calls=%fused_computation | loop fusion | flops 144 | bytes 484 | tf_op jit(solution)/shard_map/concatenate | solution.py:350
  5.5 1.6 %collective-permute-start.2 = (s32[3,24]{1,0:T(4,128)S(1)}, s32[3,24]{1,0:T(4,128)S(1)}, u32[]{:S(2)}, u32[]{:S(2)}) collective-permute-start(s32[3,24]{1,0:T(4,128)S(1)} %pad_add_fusion.refs_0_), channel_id=1, source_target_pairs={{0,2},{1,3},{2,0},{3,1},{4,6},{5,7},{6,4},{7,5},{8,10},{9,11},{10,... | collective-permute-start | bytes 872 | tf_op jit(solution)/shard_map/ppermute | solution.py:30
  7.1 0.3 collective-permute-start.3
  7.4 0.9 %copy-done.1 = f32[64,1024]{1,0:T(8,128)S(1)} copy-done((f32[64,1024]{1,0:T(8,128)S(1)}, f32[64,1024]{1,0:T(8,128)}, u32[]{:S(2)}) %copy-start.1) | copy-done | bytes 262168
  8.3 0.7 %copy-done.2 = bf16[1024]{0:T(1024)(128)(2,1)S(1)} copy-done((bf16[1024]{0:T(1024)(128)(2,1)S(1)}, bf16[1024]{0:T(1024)(128)(2,1)}, u32[]{:S(2)}) %copy-start.2) | copy-done | bytes 2072
  9.0 0.1 collective-permute-done.2.refs_2_
  9.1 0.9 %collective-permute-done.3.refs_3_ = s32[3,24]{1,0:T(4,128)S(1)} collective-permute-done((s32[3,24]{1,0:T(4,128)S(1)}, s32[3,24]{1,0:T(4,128)S(1)}, u32[]{:S(2)}, u32[]{:S(2)}) %collective-permute-start.3) | collective-permute-done | bytes 320 | tf_op jit(solution)/shard_map/ppermute | solution.py:30
  10.1 0.2 shard_map.67
  10.2 1.6 %collective-permute-start.4 = (bf16[80,256]{1,0:T(8,128)(2,1)S(1)}, bf16[80,256]{1,0:T(8,128)(2,1)S(1)}, u32[]{:S(2)}, u32[]{:S(2)}) collective-permute-start(bf16[80,256]{1,0:T(8,128)(2,1)S(1)} %get-tuple-element.33), channel_id=1, source_target_pairs={{0,4},{4,8},{8,12},{12,16},{16,20},{20,24},{24,28},{28,0},{1,5},{5... | collective-permute-start | bytes 122888 | tf_op jit(solution)/shard_map/ppermute | solution.py:25
  11.8 1.6 %copy-done = bf16[1024,1024]{1,0:T(8,128)(2,1)S(1)} copy-done((bf16[1024,1024]{1,0:T(8,128)(2,1)S(1)}, bf16[1024,1024]{1,0:T(8,128)(2,1)}, u32[]{:S(2)}) %copy-start) | copy-done | bytes 2097176
  13.4 1.8 %shard_map.65 = (bf16[4,256,1024]{2,1,0:T(8,128)(2,1)S(1)}, bf16[4,256,256]{2,1,0:T(8,128)(2,1)S(1)}, f32[4,72,256]{2,1,0:T(8,128)S(1)}) custom-call(bf16[1024,1024]{1,0:T(8,128)(2,1)S(1)} %copy-done, f32[1,1024]{1,0:T(1,128)S(1)} %get-tuple-element.29.mean_ref.refs_2_, bf16[4,80,256]{2,1,0:T(8,128)(2,1)S(1)} %get-tuple-element.30.left_ref.refs_3_), custom_call_target="tpu_custom_call" | custom-call | tf_op jit(solution)/shard_map/pallas_call | solution.py:328
  15.2 4.3 %collective-permute-done.cells_ref = bf16[256,1024]{1,0:T(8,128)(2,1)S(1)} collective-permute-done((bf16[256,1024]{1,0:T(8,128)(2,1)S(1)}, bf16[256,1024]{1,0:T(8,128)(2,1)S(1)}, u32[]{:S(2)}, u32[]{:S(2)}) %collective-permute-start) | collective-permute-done | bytes 524320 | tf_op jit(solution)/shard_map/ppermute | solution.py:25
  19.5 0.8 %shard_map.66.refs_0_ = f32[4,256,256]{2,1,0:T(8,128)S(1)} custom-call(bf16[4,256,1024]{2,1,0:T(8,128)(2,1)S(1)} %get-tuple-element.32.unit_ref, bf16[256,1024]{1,0:T(8,128)(2,1)S(1)} %collective-permute-done.cells_ref), custom_call_target="tpu_custom_call" | custom-call | tf_op jit(solution)/shard_map/pallas_call | solution.py:328
  20.3 0.7 %shard_map.68 = (bf16[4,256,256]{2,1,0:T(8,128)(2,1)S(1)}, f32[2,72,256]{2,1,0:T(8,128)S(1)}, f32[72,256]{1,0:T(8,128)S(1)}, f32[72,256]{1,0:T(8,128)S(1)}, f32[72,256]{1,0:T(8,128)S(1)}) custom-call(f32[4,256,256]{2,1,0:T(8,128)S(1)} %shard_map.66.refs_0_, bf16[80,256]{1,0:T(8,128)(2,1)S(1)} %collective-permute-done.4.refs_1_.side_ref, ...), custom_call_target="tpu_custom_call" | custom-call | tf_op jit(solution)/shard_map/pallas_call | solution.py:328
  21.1 0.5 collective-permute-start.6
  21.6 1.7 %collective-permute-start.8 = (f32[72,256]{1,0:T(8,128)S(1)}, f32[72,256]{1,0:T(8,128)S(1)}, u32[]{:S(2)}, u32[]{:S(2)}) collective-permute-start(f32[72,256]{1,0:T(8,128)S(1)} %get-tuple-element.42), channel_id=1, source_target_pairs={{0,28},{4,0},{8,4},{12,8},{16,12},{20,16},{24,20},{28,24},{1,29},{... | collective-permute-start | bytes 221192 | tf_op jit(solution)/shard_map/ppermute | solution.py:25
  23.4 1.5 %collective-permute-start.7 = (f32[72,256]{1,0:T(8,128)S(1)}, f32[72,256]{1,0:T(8,128)S(1)}, u32[]{:S(2)}, u32[]{:S(2)}) collective-permute-start(f32[72,256]{1,0:T(8,128)S(1)} %get-tuple-element.41), channel_id=1, source_target_pairs={{0,2},{1,3},{2,0},{3,1},{4,6},{5,7},{6,4},{7,5},{8,10},{9,11},{10,... | collective-permute-start | bytes 221192 | tf_op jit(solution)/shard_map/ppermute | solution.py:30
  24.9 1.0 %collective-permute-done.8.refs_2_ = f32[72,256]{1,0:T(8,128)S(1)} collective-permute-done((f32[72,256]{1,0:T(8,128)S(1)}, f32[72,256]{1,0:T(8,128)S(1)}, u32[]{:S(2)}, u32[]{:S(2)}) %collective-permute-start.8) | collective-permute-done | bytes 73760 | tf_op jit(solution)/shard_map/ppermute | solution.py:25
  25.9 1.8 %collective-permute-done.7.refs_1_ = f32[72,256]{1,0:T(8,128)S(1)} collective-permute-done((f32[72,256]{1,0:T(8,128)S(1)}, f32[72,256]{1,0:T(8,128)S(1)}, u32[]{:S(2)}, u32[]{:S(2)}) %collective-permute-start.7) | collective-permute-done | bytes 73760 | tf_op jit(solution)/shard_map/ppermute | solution.py:30
  27.8 1.5 %collective-permute-start.10 = (f32[72,256]{1,0:T(8,128)S(1)}, f32[72,256]{1,0:T(8,128)S(1)}, u32[]{:S(2)}, u32[]{:S(2)}) collective-permute-start(f32[72,256]{1,0:T(8,128)S(1)} %get-tuple-element.44.block_ref), channel_id=1, source_target_pairs={{0,2},{1,3},{2,0},{3,1},{4,6},{5,7},{6,4},{7,5},{8,10},{9,11},{10,... | collective-permute-start | bytes 221192 | tf_op jit(solution)/shard_map/ppermute | solution.py:30
  29.4 0.3 collective-permute-start.12
  29.7 2.6 %collective-permute-done.10.refs_2_.across_ref = f32[72,256]{1,0:T(8,128)S(1)} collective-permute-done((f32[72,256]{1,0:T(8,128)S(1)}, f32[72,256]{1,0:T(8,128)S(1)}, u32[]{:S(2)}, u32[]{:S(2)}) %collective-permute-start.10) | collective-permute-done | bytes 73760 | tf_op jit(solution)/shard_map/ppermute | solution.py:30
  32.2 0.5 collective-permute-start.9
  32.8 0.9 %collective-permute-done.9.refs_1_ = f32[64,256]{1,0:T(8,128)S(1)} collective-permute-done((f32[64,256]{1,0:T(8,128)S(1)}, f32[64,256]{1,0:T(8,128)S(1)}, u32[]{:S(2)}, u32[]{:S(2)}) %collective-permute-start.9) | collective-permute-done | bytes 65568 | tf_op jit(solution)/shard_map/ppermute | solution.py:30
  33.7 0.5 shard_map.71
  34.2 1.3 %collective-permute-start.13 = (f32[72,256]{1,0:T(8,128)S(1)}, f32[72,256]{1,0:T(8,128)S(1)}, u32[]{:S(2)}, u32[]{:S(2)}) collective-permute-start(f32[72,256]{1,0:T(8,128)S(1)} %get-tuple-element.49), channel_id=1, source_target_pairs={{4,0},{8,4},{12,8},{16,12},{20,16},{24,20},{28,24},{5,1},{9,5},{13... | collective-permute-start | bytes 221192 | tf_op jit(solution)/shard_map/ppermute | solution.py:25
  35.5 1.0 %collective-permute-done.12.next_ref = f32[80,256]{1,0:T(8,128)S(1)} collective-permute-done((f32[80,256]{1,0:T(8,128)S(1)}, f32[80,256]{1,0:T(8,128)S(1)}, u32[]{:S(2)}, u32[]{:S(2)}) %collective-permute-start.12) | collective-permute-done | bytes 81952 | tf_op jit(solution)/shard_map/ppermute | solution.py:25
  36.5 0.4 shard_map.72
  36.9 0.1 collective-permute-start.14
  37.0 0.5 collective-permute-start.15
  37.5 0.7 %collective-permute-done.14.refs_0_ = f32[64,256]{1,0:T(8,128)S(1)} collective-permute-done((f32[64,256]{1,0:T(8,128)S(1)}, f32[64,256]{1,0:T(8,128)S(1)}, u32[]{:S(2)}, u32[]{:S(2)}) %collective-permute-start.14) | collective-permute-done | bytes 65568 | tf_op jit(solution)/shard_map/ppermute | solution.py:30
  38.2 0.2 collective-permute-done.15.refs_1_
  38.4 2.2 %collective-permute-done.13.back_ref = f32[72,256]{1,0:T(8,128)S(1)} collective-permute-done((f32[72,256]{1,0:T(8,128)S(1)}, f32[72,256]{1,0:T(8,128)S(1)}, u32[]{:S(2)}, u32[]{:S(2)}) %collective-permute-start.13) | collective-permute-done | bytes 73760 | tf_op jit(solution)/shard_map/ppermute | solution.py:25
  40.6 1.5 %collective-permute-start.16 = (f32[2,64,256]{2,1,0:T(8,128)S(1)}, f32[2,64,256]{2,1,0:T(8,128)S(1)}, u32[]{:S(2)}, u32[]{:S(2)}) collective-permute-start(f32[2,64,256]{2,1,0:T(8,128)S(1)} %shard_map.73.own_ref), channel_id=1, source_target_pairs={{0,2},{1,3},{2,0},{3,1},{4,6},{5,7},{6,4},{7,5},{8,10},{9,11},{10,... | collective-permute-start | bytes 393224 | tf_op jit(solution)/shard_map/ppermute | solution.py:30
  42.2 3.5 %collective-permute-done.16.came_ref = f32[2,64,256]{2,1,0:T(8,128)S(1)} collective-permute-done((f32[2,64,256]{2,1,0:T(8,128)S(1)}, f32[2,64,256]{2,1,0:T(8,128)S(1)}, u32[]{:S(2)}, u32[]{:S(2)}) %collective-permute-start.16) | collective-permute-done | bytes 131104 | tf_op jit(solution)/shard_map/ppermute | solution.py:30
  45.7 0.1 collective-permute-start.17
  45.8 1.3 %collective-permute-done.17.there_ref = f32[2,64,256]{2,1,0:T(8,128)S(1)} collective-permute-done((f32[2,64,256]{2,1,0:T(8,128)S(1)}, f32[2,64,256]{2,1,0:T(8,128)S(1)}, u32[]{:S(2)}, u32[]{:S(2)}) %collective-permute-start.17) | collective-permute-done | bytes 131104 | tf_op jit(solution)/shard_map/ppermute | solution.py:30
  47.1 0.4 shard_map.75
  47.5 1.2 %collective-permute-start.18 = (f32[64,128]{1,0:T(8,128)S(1)}, f32[64,128]{1,0:T(8,128)S(1)}, u32[]{:S(2)}, u32[]{:S(2)}) collective-permute-start(f32[64,128]{1,0:T(8,128)S(1)} %shard_map.75), channel_id=1, source_target_pairs={{0,4},{4,0},{8,12},{12,8},{16,20},{20,16},{24,28},{28,24},{1,5},{5... | collective-permute-start | bytes 98312 | tf_op jit(solution)/shard_map/ppermute | solution.py:30
  48.8 2.7 %collective-permute-done.18 = f32[64,128]{1,0:T(8,128)S(1)} collective-permute-done((f32[64,128]{1,0:T(8,128)S(1)}, f32[64,128]{1,0:T(8,128)S(1)}, u32[]{:S(2)}, u32[]{:S(2)}) %collective-permute-start.18) | collective-permute-done | bytes 32800 | tf_op jit(solution)/shard_map/ppermute | solution.py:30
  51.5 1.0 %collective-permute-start.19 = (f32[64,128]{1,0:T(8,128)S(1)}, f32[64,128]{1,0:T(8,128)S(1)}, u32[]{:S(2)}, u32[]{:S(2)}) collective-permute-start(f32[64,128]{1,0:T(8,128)S(1)} %add.9.refs_0_), channel_id=1, source_target_pairs={{0,24},{4,28},{8,16},{12,20},{16,8},{20,12},{24,0},{28,4},{1,25},{... | collective-permute-start | bytes 98312 | tf_op jit(solution)/shard_map/ppermute | solution.py:30
  52.5 0.4 collective-permute-start.20
  52.9 3.0 %collective-permute-start.21 = (f32[64,128]{1,0:T(8,128)S(1)}, f32[64,128]{1,0:T(8,128)S(1)}, u32[]{:S(2)}, u32[]{:S(2)}) collective-permute-start(f32[64,128]{1,0:T(8,128)S(1)} %add.9.refs_0_), channel_id=1, source_target_pairs={{0,8},{4,12},{8,0},{12,4},{16,24},{20,28},{24,16},{28,20},{1,9},{5... | collective-permute-start | bytes 98312 | tf_op jit(solution)/shard_map/ppermute | solution.py:30
  55.9 1.3 %collective-permute-done.19.refs_1_ = f32[64,128]{1,0:T(8,128)S(1)} collective-permute-done((f32[64,128]{1,0:T(8,128)S(1)}, f32[64,128]{1,0:T(8,128)S(1)}, u32[]{:S(2)}, u32[]{:S(2)}) %collective-permute-start.19) | collective-permute-done | bytes 32800 | tf_op jit(solution)/shard_map/ppermute | solution.py:30
  57.2 0.8 %collective-permute-done.20.refs_2_ = f32[64,128]{1,0:T(8,128)S(1)} collective-permute-done((f32[64,128]{1,0:T(8,128)S(1)}, f32[64,128]{1,0:T(8,128)S(1)}, u32[]{:S(2)}, u32[]{:S(2)}) %collective-permute-start.20) | collective-permute-done | bytes 32800 | tf_op jit(solution)/shard_map/ppermute | solution.py:30
  58.1 4.1 %shard_map.76 = f32[64,1024]{1,0:T(8,128)} custom-call(f32[2,64,256]{2,1,0:T(8,128)S(1)} %shard_map.74.here_ref, f32[2,64,256]{2,1,0:T(8,128)S(1)} %collective-permute-done.17.there_ref, f32[64,128]{1,0:T(8,128)S(1)} %add.9.refs_0_, f32[64,128]{1,0:T(8,128)S(1)} %collective-permute-done.19.refs_1_, f32[64,128]{1,0:T(8,128)S(1)} %collective-permute-done.20.refs_2_, ...), custom_call_target="tpu_custom_call" | custom-call | tf_op jit(solution)/shard_map/pallas_call | solution.py:328
  (18 shorter events, 0.3 us)
Async XLA Ops:
  1.1 18.4 %collective-permute-start = (bf16[256,1024]{1,0:T(8,128)(2,1)S(1)}, bf16[256,1024]{1,0:T(8,128)(2,1)S(1)}, u32[]{:S(2)}, u32[]{:S(2)}) collective-permute-start(bf16[256,1024]{1,0:T(8,128)(2,1)S(1)} %constant_dynamic-slice_fusion), channel_id=1, source_target_pairs={{0,4},{4,8},{8,12},{12,16},{16,20},{20,24},{24,28},{28,0},{1,5},{5... | collective-permute-start | bytes 1572872 | tf_op jit(solution)/shard_map/ppermute | solution.py:25
  5.4 3.6 %collective-permute-start.1 = (s32[3,24]{1,0:T(4,128)S(1)}, s32[3,24]{1,0:T(4,128)S(1)}, u32[]{:S(2)}, u32[]{:S(2)}) collective-permute-start(s32[3,24]{1,0:T(4,128)S(1)} %pad_add_fusion.refs_0_), channel_id=1, source_target_pairs={{0,1},{1,0},{2,3},{3,2},{4,5},{5,4},{6,7},{7,6},{8,9},{9,8},{10,11... | collective-permute-start | bytes 872 | tf_op jit(solution)/shard_map/ppermute | solution.py:30
  5.5 3.7 %collective-permute-start.2 = (s32[3,24]{1,0:T(4,128)S(1)}, s32[3,24]{1,0:T(4,128)S(1)}, u32[]{:S(2)}, u32[]{:S(2)}) collective-permute-start(s32[3,24]{1,0:T(4,128)S(1)} %pad_add_fusion.refs_0_), channel_id=1, source_target_pairs={{0,2},{1,3},{2,0},{3,1},{4,6},{5,7},{6,4},{7,5},{8,10},{9,11},{10,... | collective-permute-start | bytes 872 | tf_op jit(solution)/shard_map/ppermute | solution.py:30
  7.1 3.0 %collective-permute-start.3 = (s32[3,24]{1,0:T(4,128)S(1)}, s32[3,24]{1,0:T(4,128)S(1)}, u32[]{:S(2)}, u32[]{:S(2)}) collective-permute-start(s32[3,24]{1,0:T(4,128)S(1)} %pad_add_fusion.refs_0_), channel_id=1, source_target_pairs={{0,3},{1,2},{2,1},{3,0},{4,7},{5,6},{6,5},{7,4},{8,11},{9,10},{10,... | collective-permute-start | bytes 872 | tf_op jit(solution)/shard_map/ppermute | solution.py:30
  7.4 0.9 %copy-start.1 = (f32[64,1024]{1,0:T(8,128)S(1)}, f32[64,1024]{1,0:T(8,128)}, u32[]{:S(2)}) copy-start(f32[64,1024]{1,0:T(8,128)} %start_ref.1) | copy-start | bytes 786436
  8.3 0.7 %copy-start.2 = (bf16[1024]{0:T(1024)(128)(2,1)S(1)}, bf16[1024]{0:T(1024)(128)(2,1)}, u32[]{:S(2)}) copy-start(bf16[1024]{0:T(1024)(128)(2,1)} %param.7) | copy-start | bytes 6148
  10.2 10.1 %collective-permute-start.4 = (bf16[80,256]{1,0:T(8,128)(2,1)S(1)}, bf16[80,256]{1,0:T(8,128)(2,1)S(1)}, u32[]{:S(2)}, u32[]{:S(2)}) collective-permute-start(bf16[80,256]{1,0:T(8,128)(2,1)S(1)} %get-tuple-element.33), channel_id=1, source_target_pairs={{0,4},{4,8},{8,12},{12,16},{16,20},{20,24},{24,28},{28,0},{1,5},{5... | collective-permute-start | bytes 122888 | tf_op jit(solution)/shard_map/ppermute | solution.py:25
  11.8 1.6 %copy-start = (bf16[1024,1024]{1,0:T(8,128)(2,1)S(1)}, bf16[1024,1024]{1,0:T(8,128)(2,1)}, u32[]{:S(2)}) copy-start(bf16[1024,1024]{1,0:T(8,128)(2,1)} %cells_ref.1) | copy-start | bytes 6291460
  21.0 2.3 %collective-permute-start.5 = (f32[72,256]{1,0:T(8,128)S(1)}, f32[72,256]{1,0:T(8,128)S(1)}, u32[]{:S(2)}, u32[]{:S(2)}) collective-permute-start(f32[72,256]{1,0:T(8,128)S(1)} %get-tuple-element.38), channel_id=1, source_target_pairs={{0,1},{1,0},{2,3},{3,2},{4,5},{5,4},{6,7},{7,6},{8,9},{9,8},{10,11... | collective-permute-start | bytes 221192 | tf_op jit(solution)/shard_map/ppermute | solution.py:30
  21.1 2.3 %collective-permute-start.6 = (f32[72,256]{1,0:T(8,128)S(1)}, f32[72,256]{1,0:T(8,128)S(1)}, u32[]{:S(2)}, u32[]{:S(2)}) collective-permute-start(f32[72,256]{1,0:T(8,128)S(1)} %get-tuple-element.39), channel_id=1, source_target_pairs={{0,1},{1,0},{2,3},{3,2},{4,5},{5,4},{6,7},{7,6},{8,9},{9,8},{10,11... | collective-permute-start | bytes 221192 | tf_op jit(solution)/shard_map/ppermute | solution.py:30
  21.6 4.4 %collective-permute-start.8 = (f32[72,256]{1,0:T(8,128)S(1)}, f32[72,256]{1,0:T(8,128)S(1)}, u32[]{:S(2)}, u32[]{:S(2)}) collective-permute-start(f32[72,256]{1,0:T(8,128)S(1)} %get-tuple-element.42), channel_id=1, source_target_pairs={{0,28},{4,0},{8,4},{12,8},{16,12},{20,16},{24,20},{28,24},{1,29},{... | collective-permute-start | bytes 221192 | tf_op jit(solution)/shard_map/ppermute | solution.py:25
  23.4 4.4 %collective-permute-start.7 = (f32[72,256]{1,0:T(8,128)S(1)}, f32[72,256]{1,0:T(8,128)S(1)}, u32[]{:S(2)}, u32[]{:S(2)}) collective-permute-start(f32[72,256]{1,0:T(8,128)S(1)} %get-tuple-element.41), channel_id=1, source_target_pairs={{0,2},{1,3},{2,0},{3,1},{4,6},{5,7},{6,4},{7,5},{8,10},{9,11},{10,... | collective-permute-start | bytes 221192 | tf_op jit(solution)/shard_map/ppermute | solution.py:30
  27.8 4.4 %collective-permute-start.10 = (f32[72,256]{1,0:T(8,128)S(1)}, f32[72,256]{1,0:T(8,128)S(1)}, u32[]{:S(2)}, u32[]{:S(2)}) collective-permute-start(f32[72,256]{1,0:T(8,128)S(1)} %get-tuple-element.44.block_ref), channel_id=1, source_target_pairs={{0,2},{1,3},{2,0},{3,1},{4,6},{5,7},{6,4},{7,5},{8,10},{9,11},{10,... | collective-permute-start | bytes 221192 | tf_op jit(solution)/shard_map/ppermute | solution.py:30
  29.4 7.1 %collective-permute-start.12 = (f32[80,256]{1,0:T(8,128)S(1)}, f32[80,256]{1,0:T(8,128)S(1)}, u32[]{:S(2)}, u32[]{:S(2)}) collective-permute-start(f32[80,256]{1,0:T(8,128)S(1)} %get-tuple-element.47), channel_id=1, source_target_pairs={{0,4},{4,8},{8,12},{12,16},{16,20},{20,24},{24,28},{28,0},{1,5},{5... | collective-permute-start | bytes 245768 | tf_op jit(solution)/shard_map/ppermute | solution.py:25
  32.2 1.4 %collective-permute-start.11 = (f32[72,256]{1,0:T(8,128)S(1)}, f32[72,256]{1,0:T(8,128)S(1)}, u32[]{:S(2)}, u32[]{:S(2)}) collective-permute-start(f32[72,256]{1,0:T(8,128)S(1)} %collective-permute-done.10.refs_2_.across_ref), channel_id=1, source_target_pairs={{0,1},{1,0},{2,3},{3,2},{4,5},{5,4},{6,7},{7,6},{8,9},{9,8},{10,11... | collective-permute-start | bytes 221192 | tf_op jit(solution)/shard_map/ppermute | solution.py:30
  32.2 1.4 %collective-permute-start.9 = (f32[64,256]{1,0:T(8,128)S(1)}, f32[64,256]{1,0:T(8,128)S(1)}, u32[]{:S(2)}, u32[]{:S(2)}) collective-permute-start(f32[64,256]{1,0:T(8,128)S(1)} %get-tuple-element.43.refs_0_.lead_ref), channel_id=1, source_target_pairs={{0,1},{1,0},{2,3},{3,2},{4,5},{5,4},{6,7},{7,6},{8,9},{9,8},{10,11... | collective-permute-start | bytes 196616 | tf_op jit(solution)/shard_map/ppermute | solution.py:30
  34.2 6.4 %collective-permute-start.13 = (f32[72,256]{1,0:T(8,128)S(1)}, f32[72,256]{1,0:T(8,128)S(1)}, u32[]{:S(2)}, u32[]{:S(2)}) collective-permute-start(f32[72,256]{1,0:T(8,128)S(1)} %get-tuple-element.49), channel_id=1, source_target_pairs={{4,0},{8,4},{12,8},{16,12},{20,16},{24,20},{28,24},{5,1},{9,5},{13... | collective-permute-start | bytes 221192 | tf_op jit(solution)/shard_map/ppermute | solution.py:25
  36.9 1.3 %collective-permute-start.14 = (f32[64,256]{1,0:T(8,128)S(1)}, f32[64,256]{1,0:T(8,128)S(1)}, u32[]{:S(2)}, u32[]{:S(2)}) collective-permute-start(f32[64,256]{1,0:T(8,128)S(1)} %get-tuple-element.50), channel_id=1, source_target_pairs={{0,1},{1,0},{2,3},{3,2},{4,5},{5,4},{6,7},{7,6},{8,9},{9,8},{10,11... | collective-permute-start | bytes 196616 | tf_op jit(solution)/shard_map/ppermute | solution.py:30
  37.0 1.4 %collective-permute-start.15 = (f32[64,256]{1,0:T(8,128)S(1)}, f32[64,256]{1,0:T(8,128)S(1)}, u32[]{:S(2)}, u32[]{:S(2)}) collective-permute-start(f32[64,256]{1,0:T(8,128)S(1)} %get-tuple-element.51), channel_id=1, source_target_pairs={{0,1},{1,0},{2,3},{3,2},{4,5},{5,4},{6,7},{7,6},{8,9},{9,8},{10,11... | collective-permute-start | bytes 196616 | tf_op jit(solution)/shard_map/ppermute | solution.py:30
  40.6 5.0 %collective-permute-start.16 = (f32[2,64,256]{2,1,0:T(8,128)S(1)}, f32[2,64,256]{2,1,0:T(8,128)S(1)}, u32[]{:S(2)}, u32[]{:S(2)}) collective-permute-start(f32[2,64,256]{2,1,0:T(8,128)S(1)} %shard_map.73.own_ref), channel_id=1, source_target_pairs={{0,2},{1,3},{2,0},{3,1},{4,6},{5,7},{6,4},{7,5},{8,10},{9,11},{10,... | collective-permute-start | bytes 393224 | tf_op jit(solution)/shard_map/ppermute | solution.py:30
  45.7 1.4 %collective-permute-start.17 = (f32[2,64,256]{2,1,0:T(8,128)S(1)}, f32[2,64,256]{2,1,0:T(8,128)S(1)}, u32[]{:S(2)}, u32[]{:S(2)}) collective-permute-start(f32[2,64,256]{2,1,0:T(8,128)S(1)} %shard_map.74.here_ref), channel_id=1, source_target_pairs={{0,1},{1,0},{2,3},{3,2},{4,5},{5,4},{6,7},{7,6},{8,9},{9,8},{10,11... | collective-permute-start | bytes 393224 | tf_op jit(solution)/shard_map/ppermute | solution.py:30
  47.5 4.0 %collective-permute-start.18 = (f32[64,128]{1,0:T(8,128)S(1)}, f32[64,128]{1,0:T(8,128)S(1)}, u32[]{:S(2)}, u32[]{:S(2)}) collective-permute-start(f32[64,128]{1,0:T(8,128)S(1)} %shard_map.75), channel_id=1, source_target_pairs={{0,4},{4,0},{8,12},{12,8},{16,20},{20,16},{24,28},{28,24},{1,5},{5... | collective-permute-start | bytes 98312 | tf_op jit(solution)/shard_map/ppermute | solution.py:30
  51.5 5.7 %collective-permute-start.19 = (f32[64,128]{1,0:T(8,128)S(1)}, f32[64,128]{1,0:T(8,128)S(1)}, u32[]{:S(2)}, u32[]{:S(2)}) collective-permute-start(f32[64,128]{1,0:T(8,128)S(1)} %add.9.refs_0_), channel_id=1, source_target_pairs={{0,24},{4,28},{8,16},{12,20},{16,8},{20,12},{24,0},{28,4},{1,25},{... | collective-permute-start | bytes 98312 | tf_op jit(solution)/shard_map/ppermute | solution.py:30
  52.5 5.5 %collective-permute-start.20 = (f32[64,128]{1,0:T(8,128)S(1)}, f32[64,128]{1,0:T(8,128)S(1)}, u32[]{:S(2)}, u32[]{:S(2)}) collective-permute-start(f32[64,128]{1,0:T(8,128)S(1)} %add.9.refs_0_), channel_id=1, source_target_pairs={{0,16},{4,20},{8,24},{12,28},{16,0},{20,4},{24,8},{28,12},{1,17},{... | collective-permute-start | bytes 98312 | tf_op jit(solution)/shard_map/ppermute | solution.py:30
  52.9 5.2 %collective-permute-start.21 = (f32[64,128]{1,0:T(8,128)S(1)}, f32[64,128]{1,0:T(8,128)S(1)}, u32[]{:S(2)}, u32[]{:S(2)}) collective-permute-start(f32[64,128]{1,0:T(8,128)S(1)} %add.9.refs_0_), channel_id=1, source_target_pairs={{0,8},{4,12},{8,0},{12,4},{16,24},{20,28},{24,16},{28,20},{1,9},{5... | collective-permute-start | bytes 98312 | tf_op jit(solution)/shard_map/ppermute | solution.py:30

commit v7 on v6

--- a/solution.py
+++ b/solution.py
@@ -34,16 +34,14 @@
     return [cells] + [swap(cells, "cols", d) for d in range(1, lax.axis_size("cols"))]
 
 
-def all_rows(cells):
-    bits = lax.axis_size("rows").bit_length() - 1
-    parts = [cells]
-    low = 0
-    while low < bits:
-        wide = 1 if (bits - low) % 2 else 2
-        whole = sum(parts[1:], parts[0])
-        parts = [whole] + [swap(whole, "rows", m << low) for m in range((1 << wide) - 1, 0, -1)]
-        low += wide
-    return parts
+def both_swap(cells, row_offset, lane_offset):
+    groups, lanes = lax.axis_size("rows"), lax.axis_size("cols")
+    pairs = [
+        (r * lanes + lane, (r ^ row_offset) * lanes + (lane ^ lane_offset))
+        for r in range(groups)
+        for lane in range(lanes)
+    ]
+    return lax.ppermute(cells, ("rows", "cols"), pairs)
 
 
 def nt(left, right):
@@ -278,7 +276,7 @@
         back = back + masks[1 + d : 2 + d] * joined(nt(left, weight_ref[d]), size)
     back_ref[:size] = back
     back_ref[size:] = jnp.zeros((back_ref.shape[0] - size, BLOCK), f32)
-    gram_ref[...] = gram_of(blocks, total)
+    gram_ref[...] = gram_of(blocks[::2], total)
 
 
 def ordered(here_ref, there_ref):
@@ -296,22 +294,39 @@
         halves(d, keep_ref, core_refs)[...] = own + mask_ref[lanes + d : lanes + d + 1, :] * after
 
 
-def resmooth_kernel(own_ref, came_ref, block_ref, across_ref, out_ref):
+def resmooth_kernel(total, first_ref, own_ref, came_ref, block_ref, across_ref, out_ref, *grams_refs):
     size = out_ref.shape[1]
+    blocks = []
     for m, ref in enumerate((block_ref, across_ref)):
-        out_ref[m] = (own_ref[m] + came_ref[1 - m]) / ref[size : size + 1]
-
-
-def grams_kernel(total, first_ref, here_ref, there_ref, grams_ref):
-    second = gram_of(ordered(here_ref, there_ref), total)
-    grams_ref[...] = jnp.concatenate([first_ref[...], second], axis=1)
+        blocks.append((own_ref[m] + came_ref[1 - m]) / ref[size : size + 1])
+        out_ref[m] = blocks[m]
+    spread_out(jnp.concatenate([first_ref[...], gram_of(blocks, total)], axis=1), grams_refs)
+
+
+def spread_out(value, refs):
+    rows = value.shape[0]
+    for ref in refs:
+        ref[:rows] = value
+        if ref.shape[0] > rows:
+            ref[rows:] = jnp.zeros((ref.shape[0] - rows, ref.shape[1]), f32)
+
+
+def sum_kernel(count, *refs):
+    parts, outs = refs[:count], refs[count:]
+    rows = outs[0].shape[0]
+    total = parts[0][:rows]
+    for part in parts[1:]:
+        total = total + part[:rows]
+    spread_out(total, outs)
 
 
 def solve_kernel(lanes, here_ref, there_ref, *refs):
     *grams, out_ref = refs
     lane = lax.axis_index("cols")
     size = out_ref.shape[0]
-    both = added(grams)
+    both = grams[0][:size]
+    for part in grams[1:]:
+        both = both + part[:size]
     first = inverse_factor(both[:, :size])
     solved = [times(first, block) for block in ordered(here_ref, there_ref)]
     half = times(first, both[:, size:])
@@ -423,24 +438,34 @@
     )
     came = [swap(part, "cols", 1) for part in core]
     (both,) = call(chip_kernel, [(keep.shape, f32)], keep, shift(back, -1, around=False), *came)
-    (here,) = call(
-        resmooth_kernel,
-        [((lanes // 2, size, BLOCK), f32)],
+    tall = [((size + 8 * k, 2 * size), f32) for k in range(3)]
+    here, *grams = call(
+        functools.partial(resmooth_kernel, total),
+        [((lanes // 2, size, BLOCK), f32), *tall],
+        gram,
         both,
         swap(both, "cols", 2),
         smooth,
         across,
     )
-    there = swap(here, "cols", 1)
-    (grams,) = call(
-        functools.partial(grams_kernel, total), [((size, 2 * size), f32)], gram, here, there
-    )
+
+    bits = groups.bit_length() - 1
+    low = bits % 2
+    parts = [grams[0], swap(grams[0], "cols", 1)]
+    if low:
+        parts += [swap(grams[1], "rows", 1), both_swap(grams[2], 1, 1)]
+    while low < bits:
+        grams = call(functools.partial(sum_kernel, len(parts)), tall, *parts)
+        if low < 2:
+            here, grams = lax.optimization_barrier((here, grams))
+        parts = [grams[0]] + [swap(grams[m - 1], "rows", m << low) for m in (1, 2, 3)]
+        low += 2
     (vector,) = call(
         functools.partial(solve_kernel, lanes),
         [((size, rows_here), f32)],
         here,
-        there,
-        *all_rows(grams),
+        swap(here, "cols", 1),
+        *parts,
     )
     return vector
 

time: 62.4 us -> 61.9 us (level)
  waiting for transfers between devices: 25.6 us -> 24.4 us
  starting transfers between devices: 21.8 us -> 22.6 us
    ppermute x17 -> x18, waiting for transfers between devices: 17 us -> 15.5 us  [swap(): return lax.ppermute(cells, axis, [(i, i ^ offset) for i in range(count)])]
    ppermute x17 -> x18, starting transfers between devices: 13.9 us -> 14.6 us  [swap(): return lax.ppermute(cells, axis, [(i, i ^ offset) for i in range(count)])]
  transfers between devices with their start and end apart: 22 -> 24, of which waited for: 17 -> 15; matrix products, arithmetic and copies ran while one was open for 1% -> 1% of each run, Pallas kernels for 6% -> 6%
where the time goes in v7:
time: 61.9 us; the launch traced here: 61.6 us
  waiting for transfers between devices  24.4 us (39%)
  starting transfers between devices  22.6 us (37%)
  Pallas kernels  8.85 us (14%)
  local copies, waits for them, and re-layouts  4.3 us (7%)
  between operations  0.77 us (1%)
  other arithmetic  0.68 us (1%)
    ppermute x18, waiting for transfers between devices, swap(): return lax.ppermute(cells, axis, [(i, i ^ offset) for i in range(count)])  15.5 us
    ppermute x18, starting transfers between devices, swap(): return lax.ppermute(cells, axis, [(i, i ^ offset) for i in range(count)])  14.6 us
    ppermute x5, waiting for transfers between devices, shift(): return lax.ppermute(cells, 'rows', pairs)  8.9 us
    pallas_call x13, Pallas kernels, call(): pl.pallas_call(body, out_shape=[jax.ShapeDtypeStruct(shape, kind) for sha...  8.85 us
    ppermute x5, starting transfers between devices, shift(): return lax.ppermute(cells, 'rows', pairs)  7.92 us
    unnamed x6, local copies, waits for them, and re-layouts  3.22 us
  transfers between devices with their start and end apart: 24, of which 15 were waited for; matrix products, arithmetic and copies ran while one was open for 1% of the time, Pallas kernels for 6%

profile of v7, /device:TPU:0, one launch (start us, length us, event | category | flops | bytes accessed | tf_op | source)
XLA Modules:
  0.0 61.6 jit_solution(15802547377469773300)
XLA Ops:
  0.0 1.1 %constant_dynamic-slice_fusion = bf16[256,1024]{1,0:T(8,128)(2,1)S(1)} fusion(bf16[1024,1024]{1,0:T(8,128)(2,1)} %cells_ref.1, s32[]{:T(128)S(6)} %select_n.3), kind=kLoop, calls=%fused_computation.1 | loop fusion | bytes 1048580 | tf_op jit(solution)/shard_map/dynamic_slice | solution.py:363
  1.1 3.0 %collective-permute-start.3 = (bf16[256,1024]{1,0:T(8,128)(2,1)S(1)}, bf16[256,1024]{1,0:T(8,128)(2,1)S(1)}, u32[]{:S(2)}, u32[]{:S(2)}) collective-permute-start(bf16[256,1024]{1,0:T(8,128)(2,1)S(1)} %constant_dynamic-slice_fusion), channel_id=1, source_target_pairs={{0,4},{4,8},{8,12},{12,16},{16,20},{20,24},{24,28},{28,0},{1,5},{5... | collective-permute-start | bytes 1572872 | tf_op jit(solution)/shard_map/ppermute | solution.py:25
  4.8 0.7 %pad_add_fusion.refs_0_ = s32[3,24]{1,0:T(4,128)S(1)} fusion(s32[1,1]{1,0:T(1,128)S(6)} %copy.7, s32[1,24]{1,0:T(1,128)} %bitcast.4, s32[1,24]{1,0:T(1,128)} %bitcast.5), kind=kLoop, calls=%fused_computation | loop fusion | flops 144 | bytes 484 | tf_op jit(solution)/shard_map/concatenate | solution.py:365
  5.4 0.7 %collective-permute-start.2 = (s32[3,24]{1,0:T(4,128)S(1)}, s32[3,24]{1,0:T(4,128)S(1)}, u32[]{:S(2)}, u32[]{:S(2)}) collective-permute-start(s32[3,24]{1,0:T(4,128)S(1)} %pad_add_fusion.refs_0_), channel_id=1, source_target_pairs={{0,3},{1,2},{2,1},{3,0},{4,7},{5,6},{6,5},{7,4},{8,11},{9,10},{10,... | collective-permute-start | bytes 872 | tf_op jit(solution)/shard_map/ppermute | solution.py:30
  6.1 0.9 %collective-permute-start.1 = (s32[3,24]{1,0:T(4,128)S(1)}, s32[3,24]{1,0:T(4,128)S(1)}, u32[]{:S(2)}, u32[]{:S(2)}) collective-permute-start(s32[3,24]{1,0:T(4,128)S(1)} %pad_add_fusion.refs_0_), channel_id=1, source_target_pairs={{0,2},{1,3},{2,0},{3,1},{4,6},{5,7},{6,4},{7,5},{8,10},{9,11},{10,... | collective-permute-start | bytes 872 | tf_op jit(solution)/shard_map/ppermute | solution.py:30
  7.1 0.3 collective-permute-start
  7.3 0.9 %copy-done.1 = f32[64,1024]{1,0:T(8,128)S(1)} copy-done((f32[64,1024]{1,0:T(8,128)S(1)}, f32[64,1024]{1,0:T(8,128)}, u32[]{:S(2)}) %copy-start.1) | copy-done | bytes 262168
  8.3 0.7 %copy-done.2 = bf16[1024]{0:T(1024)(128)(2,1)S(1)} copy-done((bf16[1024]{0:T(1024)(128)(2,1)S(1)}, bf16[1024]{0:T(1024)(128)(2,1)}, u32[]{:S(2)}) %copy-start.2) | copy-done | bytes 2072
  9.0 0.7 %collective-permute-done.1.refs_2_ = s32[3,24]{1,0:T(4,128)S(1)} collective-permute-done((s32[3,24]{1,0:T(4,128)S(1)}, s32[3,24]{1,0:T(4,128)S(1)}, u32[]{:S(2)}, u32[]{:S(2)}) %collective-permute-start.1) | collective-permute-done | bytes 320 | tf_op jit(solution)/shard_map/ppermute | solution.py:30
  9.7 0.2 shard_map.65
  9.9 1.6 %collective-permute-start.4 = (bf16[80,256]{1,0:T(8,128)(2,1)S(1)}, bf16[80,256]{1,0:T(8,128)(2,1)S(1)}, u32[]{:S(2)}, u32[]{:S(2)}) collective-permute-start(bf16[80,256]{1,0:T(8,128)(2,1)S(1)} %get-tuple-element.44), channel_id=1, source_target_pairs={{0,4},{4,8},{8,12},{12,16},{16,20},{20,24},{24,28},{28,0},{1,5},{5... | collective-permute-start | bytes 122888 | tf_op jit(solution)/shard_map/ppermute | solution.py:25
  11.5 1.6 %copy-done = bf16[1024,1024]{1,0:T(8,128)(2,1)S(1)} copy-done((bf16[1024,1024]{1,0:T(8,128)(2,1)S(1)}, bf16[1024,1024]{1,0:T(8,128)(2,1)}, u32[]{:S(2)}) %copy-start) | copy-done | bytes 2097176
  13.1 1.8 %shard_map.66 = (bf16[4,256,1024]{2,1,0:T(8,128)(2,1)S(1)}, bf16[4,256,256]{2,1,0:T(8,128)(2,1)S(1)}, f32[4,72,256]{2,1,0:T(8,128)S(1)}) custom-call(bf16[1024,1024]{1,0:T(8,128)(2,1)S(1)} %copy-done, f32[1,1024]{1,0:T(1,128)S(1)} %get-tuple-element.40.mean_ref.refs_2_, bf16[4,80,256]{2,1,0:T(8,128)(2,1)S(1)} %get-tuple-element.41.left_ref.refs_3_), custom_call_target="tpu_custom_call" | custom-call | tf_op jit(solution)/shard_map/pallas_call | solution.py:343
  14.9 4.6 %collective-permute-done.3.cells_ref = bf16[256,1024]{1,0:T(8,128)(2,1)S(1)} collective-permute-done((bf16[256,1024]{1,0:T(8,128)(2,1)S(1)}, bf16[256,1024]{1,0:T(8,128)(2,1)S(1)}, u32[]{:S(2)}, u32[]{:S(2)}) %collective-permute-start.3) | collective-permute-done | bytes 524320 | tf_op jit(solution)/shard_map/ppermute | solution.py:25
  19.5 0.8 %shard_map.67.refs_0_ = f32[4,256,256]{2,1,0:T(8,128)S(1)} custom-call(bf16[4,256,1024]{2,1,0:T(8,128)(2,1)S(1)} %get-tuple-element.43.unit_ref, bf16[256,1024]{1,0:T(8,128)(2,1)S(1)} %collective-permute-done.3.cells_ref), custom_call_target="tpu_custom_call" | custom-call | tf_op jit(solution)/shard_map/pallas_call | solution.py:343
  20.3 0.7 %shard_map.68 = (bf16[4,256,256]{2,1,0:T(8,128)(2,1)S(1)}, f32[2,72,256]{2,1,0:T(8,128)S(1)}, f32[72,256]{1,0:T(8,128)S(1)}, f32[72,256]{1,0:T(8,128)S(1)}, f32[72,256]{1,0:T(8,128)S(1)}) custom-call(f32[4,256,256]{2,1,0:T(8,128)S(1)} %shard_map.67.refs_0_, bf16[80,256]{1,0:T(8,128)(2,1)S(1)} %collective-permute-done.4.refs_1_.side_ref, ...), custom_call_target="tpu_custom_call" | custom-call | tf_op jit(solution)/shard_map/pallas_call | solution.py:343
  21.1 0.5 collective-permute-start.6
  21.6 1.7 %collective-permute-start.8 = (f32[72,256]{1,0:T(8,128)S(1)}, f32[72,256]{1,0:T(8,128)S(1)}, u32[]{:S(2)}, u32[]{:S(2)}) collective-permute-start(f32[72,256]{1,0:T(8,128)S(1)} %get-tuple-element.52), channel_id=1, source_target_pairs={{0,28},{4,0},{8,4},{12,8},{16,12},{20,16},{24,20},{28,24},{1,29},{... | collective-permute-start | bytes 221192 | tf_op jit(solution)/shard_map/ppermute | solution.py:25
  23.4 1.5 %collective-permute-start.7 = (f32[72,256]{1,0:T(8,128)S(1)}, f32[72,256]{1,0:T(8,128)S(1)}, u32[]{:S(2)}, u32[]{:S(2)}) collective-permute-start(f32[72,256]{1,0:T(8,128)S(1)} %get-tuple-element.51), channel_id=1, source_target_pairs={{0,2},{1,3},{2,0},{3,1},{4,6},{5,7},{6,4},{7,5},{8,10},{9,11},{10,... | collective-permute-start | bytes 221192 | tf_op jit(solution)/shard_map/ppermute | solution.py:30
  24.9 1.0 %collective-permute-done.8.refs_2_ = f32[72,256]{1,0:T(8,128)S(1)} collective-permute-done((f32[72,256]{1,0:T(8,128)S(1)}, f32[72,256]{1,0:T(8,128)S(1)}, u32[]{:S(2)}, u32[]{:S(2)}) %collective-permute-start.8) | collective-permute-done | bytes 73760 | tf_op jit(solution)/shard_map/ppermute | solution.py:25
  25.9 1.8 %collective-permute-done.7.refs_1_ = f32[72,256]{1,0:T(8,128)S(1)} collective-permute-done((f32[72,256]{1,0:T(8,128)S(1)}, f32[72,256]{1,0:T(8,128)S(1)}, u32[]{:S(2)}, u32[]{:S(2)}) %collective-permute-start.7) | collective-permute-done | bytes 73760 | tf_op jit(solution)/shard_map/ppermute | solution.py:30
  27.8 1.5 %collective-permute-start.10 = (f32[72,256]{1,0:T(8,128)S(1)}, f32[72,256]{1,0:T(8,128)S(1)}, u32[]{:S(2)}, u32[]{:S(2)}) collective-permute-start(f32[72,256]{1,0:T(8,128)S(1)} %get-tuple-element.54.block_ref), channel_id=1, source_target_pairs={{0,2},{1,3},{2,0},{3,1},{4,6},{5,7},{6,4},{7,5},{8,10},{9,11},{10,... | collective-permute-start | bytes 221192 | tf_op jit(solution)/shard_map/ppermute | solution.py:30
  29.4 0.3 collective-permute-start.12
  29.7 2.6 %collective-permute-done.10.refs_2_.across_ref = f32[72,256]{1,0:T(8,128)S(1)} collective-permute-done((f32[72,256]{1,0:T(8,128)S(1)}, f32[72,256]{1,0:T(8,128)S(1)}, u32[]{:S(2)}, u32[]{:S(2)}) %collective-permute-start.10) | collective-permute-done | bytes 73760 | tf_op jit(solution)/shard_map/ppermute | solution.py:30
  32.2 0.5 collective-permute-start.9
  32.8 0.9 %collective-permute-done.9.refs_1_ = f32[64,256]{1,0:T(8,128)S(1)} collective-permute-done((f32[64,256]{1,0:T(8,128)S(1)}, f32[64,256]{1,0:T(8,128)S(1)}, u32[]{:S(2)}, u32[]{:S(2)}) %collective-permute-start.9) | collective-permute-done | bytes 65568 | tf_op jit(solution)/shard_map/ppermute | solution.py:30
  33.7 0.4 shard_map.71
  34.1 1.3 %collective-permute-start.13 = (f32[72,256]{1,0:T(8,128)S(1)}, f32[72,256]{1,0:T(8,128)S(1)}, u32[]{:S(2)}, u32[]{:S(2)}) collective-permute-start(f32[72,256]{1,0:T(8,128)S(1)} %get-tuple-element.61), channel_id=1, source_target_pairs={{4,0},{8,4},{12,8},{16,12},{20,16},{24,20},{28,24},{5,1},{9,5},{13... | collective-permute-start | bytes 221192 | tf_op jit(solution)/shard_map/ppermute | solution.py:25
  35.4 1.1 %collective-permute-done.12.next_ref = f32[80,256]{1,0:T(8,128)S(1)} collective-permute-done((f32[80,256]{1,0:T(8,128)S(1)}, f32[80,256]{1,0:T(8,128)S(1)}, u32[]{:S(2)}, u32[]{:S(2)}) %collective-permute-start.12) | collective-permute-done | bytes 81952 | tf_op jit(solution)/shard_map/ppermute | solution.py:25
  36.5 0.4 shard_map.72
  37.0 0.5 collective-permute-start.15
  37.5 0.7 %collective-permute-done.14.refs_0_ = f32[64,256]{1,0:T(8,128)S(1)} collective-permute-done((f32[64,256]{1,0:T(8,128)S(1)}, f32[64,256]{1,0:T(8,128)S(1)}, u32[]{:S(2)}, u32[]{:S(2)}) %collective-permute-start.14) | collective-permute-done | bytes 65568 | tf_op jit(solution)/shard_map/ppermute | solution.py:30
  38.2 0.2 collective-permute-done.15.refs_1_
  38.4 2.1 %collective-permute-done.13.back_ref = f32[72,256]{1,0:T(8,128)S(1)} collective-permute-done((f32[72,256]{1,0:T(8,128)S(1)}, f32[72,256]{1,0:T(8,128)S(1)}, u32[]{:S(2)}, u32[]{:S(2)}) %collective-permute-start.13) | collective-permute-done | bytes 73760 | tf_op jit(solution)/shard_map/ppermute | solution.py:25
  40.5 1.5 %collective-permute-start.16 = (f32[2,64,256]{2,1,0:T(8,128)S(1)}, f32[2,64,256]{2,1,0:T(8,128)S(1)}, u32[]{:S(2)}, u32[]{:S(2)}) collective-permute-start(f32[2,64,256]{2,1,0:T(8,128)S(1)} %shard_map.73.own_ref), channel_id=1, source_target_pairs={{0,2},{1,3},{2,0},{3,1},{4,6},{5,7},{6,4},{7,5},{8,10},{9,11},{10,... | collective-permute-start | bytes 393224 | tf_op jit(solution)/shard_map/ppermute | solution.py:30
  42.1 3.5 %collective-permute-done.16.came_ref = f32[2,64,256]{2,1,0:T(8,128)S(1)} collective-permute-done((f32[2,64,256]{2,1,0:T(8,128)S(1)}, f32[2,64,256]{2,1,0:T(8,128)S(1)}, u32[]{:S(2)}, u32[]{:S(2)}) %collective-permute-start.16) | collective-permute-done | bytes 131104 | tf_op jit(solution)/shard_map/ppermute | solution.py:30
  45.6 0.3 shard_map.74
  46.0 1.2 %collective-permute-start.18 = (f32[72,128]{1,0:T(8,128)S(1)}, f32[72,128]{1,0:T(8,128)S(1)}, u32[]{:S(2)}, u32[]{:S(2)}) collective-permute-start(f32[72,128]{1,0:T(8,128)S(1)} %get-tuple-element.66), channel_id=1, source_target_pairs={{0,4},{4,0},{8,12},{12,8},{16,20},{20,16},{24,28},{28,24},{1,5},{5... | collective-permute-start | bytes 110600 | tf_op jit(solution)/shard_map/ppermute | solution.py:30
  47.2 0.6 collective-permute-start.17
  47.8 0.9 %collective-permute-done.17.refs_1_ = f32[64,128]{1,0:T(8,128)S(1)} collective-permute-done((f32[64,128]{1,0:T(8,128)S(1)}, f32[64,128]{1,0:T(8,128)S(1)}, u32[]{:S(2)}, u32[]{:S(2)}) %collective-permute-start.17) | collective-permute-done | bytes 32800 | tf_op jit(solution)/shard_map/ppermute | solution.py:30
  48.7 1.5 %collective-permute-done.18.refs_2_ = f32[72,128]{1,0:T(8,128)S(1)} collective-permute-done((f32[72,128]{1,0:T(8,128)S(1)}, f32[72,128]{1,0:T(8,128)S(1)}, u32[]{:S(2)}, u32[]{:S(2)}) %collective-permute-start.18) | collective-permute-done | bytes 36896 | tf_op jit(solution)/shard_map/ppermute | solution.py:30
  50.2 0.2 collective-permute-start.20
  50.4 1.0 %collective-permute-start.23 = (f32[80,128]{1,0:T(8,128)S(1)}, f32[80,128]{1,0:T(8,128)S(1)}, u32[]{:S(2)}, u32[]{:S(2)}) collective-permute-start(f32[80,128]{1,0:T(8,128)S(1)} %get-tuple-element.74), channel_id=1, source_target_pairs={{0,24},{4,28},{8,16},{12,20},{16,8},{20,12},{24,0},{28,4},{1,25},{... | collective-permute-start | bytes 122888 | tf_op jit(solution)/shard_map/ppermute | solution.py:30
  51.4 0.6 collective-permute-start.22
  52.0 2.8 %collective-permute-start.21 = (f32[64,128]{1,0:T(8,128)S(1)}, f32[64,128]{1,0:T(8,128)S(1)}, u32[]{:S(2)}, u32[]{:S(2)}) collective-permute-start(f32[64,128]{1,0:T(8,128)S(1)} %get-tuple-element.72.refs_0_), channel_id=1, source_target_pairs={{0,8},{4,12},{8,0},{12,4},{16,24},{20,28},{24,16},{28,20},{1,9},{5... | collective-permute-start | bytes 98312 | tf_op jit(solution)/shard_map/ppermute | solution.py:30
  54.8 2.4 %collective-permute-done.21.refs_1_ = f32[64,128]{1,0:T(8,128)S(1)} collective-permute-done((f32[64,128]{1,0:T(8,128)S(1)}, f32[64,128]{1,0:T(8,128)S(1)}, u32[]{:S(2)}, u32[]{:S(2)}) %collective-permute-start.21) | collective-permute-done | bytes 32800 | tf_op jit(solution)/shard_map/ppermute | solution.py:30
  57.2 0.3 collective-permute-done.22.refs_2_
  57.5 4.1 %shard_map.76 = f32[64,1024]{1,0:T(8,128)} custom-call(f32[2,64,256]{2,1,0:T(8,128)S(1)} %get-tuple-element.71.here_ref, f32[2,64,256]{2,1,0:T(8,128)S(1)} %collective-permute-done.20.there_ref, f32[64,128]{1,0:T(8,128)S(1)} %get-tuple-element.72.refs_0_, f32[64,128]{1,0:T(8,128)S(1)} %collective-permute-done.21.refs_1_, ...), custom_call_target="tpu_custom_call" | custom-call | tf_op jit(solution)/shard_map/pallas_call | solution.py:343
  (21 shorter events, 0.4 us)
Async XLA Ops:
  1.1 18.4 %collective-permute-start.3 = (bf16[256,1024]{1,0:T(8,128)(2,1)S(1)}, bf16[256,1024]{1,0:T(8,128)(2,1)S(1)}, u32[]{:S(2)}, u32[]{:S(2)}) collective-permute-start(bf16[256,1024]{1,0:T(8,128)(2,1)S(1)} %constant_dynamic-slice_fusion), channel_id=1, source_target_pairs={{0,4},{4,8},{8,12},{12,16},{16,20},{20,24},{24,28},{28,0},{1,5},{5... | collective-permute-start | bytes 1572872 | tf_op jit(solution)/shard_map/ppermute | solution.py:25
  5.4 3.6 %collective-permute-start.2 = (s32[3,24]{1,0:T(4,128)S(1)}, s32[3,24]{1,0:T(4,128)S(1)}, u32[]{:S(2)}, u32[]{:S(2)}) collective-permute-start(s32[3,24]{1,0:T(4,128)S(1)} %pad_add_fusion.refs_0_), channel_id=1, source_target_pairs={{0,3},{1,2},{2,1},{3,0},{4,7},{5,6},{6,5},{7,4},{8,11},{9,10},{10,... | collective-permute-start | bytes 872 | tf_op jit(solution)/shard_map/ppermute | solution.py:30
  6.1 3.6 %collective-permute-start.1 = (s32[3,24]{1,0:T(4,128)S(1)}, s32[3,24]{1,0:T(4,128)S(1)}, u32[]{:S(2)}, u32[]{:S(2)}) collective-permute-start(s32[3,24]{1,0:T(4,128)S(1)} %pad_add_fusion.refs_0_), channel_id=1, source_target_pairs={{0,2},{1,3},{2,0},{3,1},{4,6},{5,7},{6,4},{7,5},{8,10},{9,11},{10,... | collective-permute-start | bytes 872 | tf_op jit(solution)/shard_map/ppermute | solution.py:30
  7.1 2.7 %collective-permute-start = (s32[3,24]{1,0:T(4,128)S(1)}, s32[3,24]{1,0:T(4,128)S(1)}, u32[]{:S(2)}, u32[]{:S(2)}) collective-permute-start(s32[3,24]{1,0:T(4,128)S(1)} %pad_add_fusion.refs_0_), channel_id=1, source_target_pairs={{0,1},{1,0},{2,3},{3,2},{4,5},{5,4},{6,7},{7,6},{8,9},{9,8},{10,11... | collective-permute-start | bytes 872 | tf_op jit(solution)/shard_map/ppermute | solution.py:30
  7.3 0.9 %copy-start.1 = (f32[64,1024]{1,0:T(8,128)S(1)}, f32[64,1024]{1,0:T(8,128)}, u32[]{:S(2)}) copy-start(f32[64,1024]{1,0:T(8,128)} %start_ref.1) | copy-start | bytes 786436
  8.3 0.7 %copy-start.2 = (bf16[1024]{0:T(1024)(128)(2,1)S(1)}, bf16[1024]{0:T(1024)(128)(2,1)}, u32[]{:S(2)}) copy-start(bf16[1024]{0:T(1024)(128)(2,1)} %param.7) | copy-start | bytes 6148
  9.9 10.4 %collective-permute-start.4 = (bf16[80,256]{1,0:T(8,128)(2,1)S(1)}, bf16[80,256]{1,0:T(8,128)(2,1)S(1)}, u32[]{:S(2)}, u32[]{:S(2)}) collective-permute-start(bf16[80,256]{1,0:T(8,128)(2,1)S(1)} %get-tuple-element.44), channel_id=1, source_target_pairs={{0,4},{4,8},{8,12},{12,16},{16,20},{20,24},{24,28},{28,0},{1,5},{5... | collective-permute-start | bytes 122888 | tf_op jit(solution)/shard_map/ppermute | solution.py:25
  11.5 1.6 %copy-start = (bf16[1024,1024]{1,0:T(8,128)(2,1)S(1)}, bf16[1024,1024]{1,0:T(8,128)(2,1)}, u32[]{:S(2)}) copy-start(bf16[1024,1024]{1,0:T(8,128)(2,1)} %cells_ref.1) | copy-start | bytes 6291460
  21.0 2.3 %collective-permute-start.5 = (f32[72,256]{1,0:T(8,128)S(1)}, f32[72,256]{1,0:T(8,128)S(1)}, u32[]{:S(2)}, u32[]{:S(2)}) collective-permute-start(f32[72,256]{1,0:T(8,128)S(1)} %get-tuple-element.48), channel_id=1, source_target_pairs={{0,1},{1,0},{2,3},{3,2},{4,5},{5,4},{6,7},{7,6},{8,9},{9,8},{10,11... | collective-permute-start | bytes 221192 | tf_op jit(solution)/shard_map/ppermute | solution.py:30
  21.1 2.3 %collective-permute-start.6 = (f32[72,256]{1,0:T(8,128)S(1)}, f32[72,256]{1,0:T(8,128)S(1)}, u32[]{:S(2)}, u32[]{:S(2)}) collective-permute-start(f32[72,256]{1,0:T(8,128)S(1)} %get-tuple-element.49), channel_id=1, source_target_pairs={{0,1},{1,0},{2,3},{3,2},{4,5},{5,4},{6,7},{7,6},{8,9},{9,8},{10,11... | collective-permute-start | bytes 221192 | tf_op jit(solution)/shard_map/ppermute | solution.py:30
  21.6 4.4 %collective-permute-start.8 = (f32[72,256]{1,0:T(8,128)S(1)}, f32[72,256]{1,0:T(8,128)S(1)}, u32[]{:S(2)}, u32[]{:S(2)}) collective-permute-start(f32[72,256]{1,0:T(8,128)S(1)} %get-tuple-element.52), channel_id=1, source_target_pairs={{0,28},{4,0},{8,4},{12,8},{16,12},{20,16},{24,20},{28,24},{1,29},{... | collective-permute-start | bytes 221192 | tf_op jit(solution)/shard_map/ppermute | solution.py:25
  23.4 4.4 %collective-permute-start.7 = (f32[72,256]{1,0:T(8,128)S(1)}, f32[72,256]{1,0:T(8,128)S(1)}, u32[]{:S(2)}, u32[]{:S(2)}) collective-permute-start(f32[72,256]{1,0:T(8,128)S(1)} %get-tuple-element.51), channel_id=1, source_target_pairs={{0,2},{1,3},{2,0},{3,1},{4,6},{5,7},{6,4},{7,5},{8,10},{9,11},{10,... | collective-permute-start | bytes 221192 | tf_op jit(solution)/shard_map/ppermute | solution.py:30
  27.8 4.4 %collective-permute-start.10 = (f32[72,256]{1,0:T(8,128)S(1)}, f32[72,256]{1,0:T(8,128)S(1)}, u32[]{:S(2)}, u32[]{:S(2)}) collective-permute-start(f32[72,256]{1,0:T(8,128)S(1)} %get-tuple-element.54.block_ref), channel_id=1, source_target_pairs={{0,2},{1,3},{2,0},{3,1},{4,6},{5,7},{6,4},{7,5},{8,10},{9,11},{10,... | collective-permute-start | bytes 221192 | tf_op jit(solution)/shard_map/ppermute | solution.py:30
  29.4 7.1 %collective-permute-start.12 = (f32[80,256]{1,0:T(8,128)S(1)}, f32[80,256]{1,0:T(8,128)S(1)}, u32[]{:S(2)}, u32[]{:S(2)}) collective-permute-start(f32[80,256]{1,0:T(8,128)S(1)} %get-tuple-element.59), channel_id=1, source_target_pairs={{0,4},{4,8},{8,12},{12,16},{16,20},{20,24},{24,28},{28,0},{1,5},{5... | collective-permute-start | bytes 245768 | tf_op jit(solution)/shard_map/ppermute | solution.py:25
  32.2 1.4 %collective-permute-start.11 = (f32[72,256]{1,0:T(8,128)S(1)}, f32[72,256]{1,0:T(8,128)S(1)}, u32[]{:S(2)}, u32[]{:S(2)}) collective-permute-start(f32[72,256]{1,0:T(8,128)S(1)} %collective-permute-done.10.refs_2_.across_ref), channel_id=1, source_target_pairs={{0,1},{1,0},{2,3},{3,2},{4,5},{5,4},{6,7},{7,6},{8,9},{9,8},{10,11... | collective-permute-start | bytes 221192 | tf_op jit(solution)/shard_map/ppermute | solution.py:30
  32.2 1.4 %collective-permute-start.9 = (f32[64,256]{1,0:T(8,128)S(1)}, f32[64,256]{1,0:T(8,128)S(1)}, u32[]{:S(2)}, u32[]{:S(2)}) collective-permute-start(f32[64,256]{1,0:T(8,128)S(1)} %get-tuple-element.53.refs_0_.lead_ref), channel_id=1, source_target_pairs={{0,1},{1,0},{2,3},{3,2},{4,5},{5,4},{6,7},{7,6},{8,9},{9,8},{10,11... | collective-permute-start | bytes 196616 | tf_op jit(solution)/shard_map/ppermute | solution.py:30
  34.1 6.4 %collective-permute-start.13 = (f32[72,256]{1,0:T(8,128)S(1)}, f32[72,256]{1,0:T(8,128)S(1)}, u32[]{:S(2)}, u32[]{:S(2)}) collective-permute-start(f32[72,256]{1,0:T(8,128)S(1)} %get-tuple-element.61), channel_id=1, source_target_pairs={{4,0},{8,4},{12,8},{16,12},{20,16},{24,20},{28,24},{5,1},{9,5},{13... | collective-permute-start | bytes 221192 | tf_op jit(solution)/shard_map/ppermute | solution.py:25
  36.9 1.3 %collective-permute-start.14 = (f32[64,256]{1,0:T(8,128)S(1)}, f32[64,256]{1,0:T(8,128)S(1)}, u32[]{:S(2)}, u32[]{:S(2)}) collective-permute-start(f32[64,256]{1,0:T(8,128)S(1)} %get-tuple-element.62), channel_id=1, source_target_pairs={{0,1},{1,0},{2,3},{3,2},{4,5},{5,4},{6,7},{7,6},{8,9},{9,8},{10,11... | collective-permute-start | bytes 196616 | tf_op jit(solution)/shard_map/ppermute | solution.py:30
  37.0 1.4 %collective-permute-start.15 = (f32[64,256]{1,0:T(8,128)S(1)}, f32[64,256]{1,0:T(8,128)S(1)}, u32[]{:S(2)}, u32[]{:S(2)}) collective-permute-start(f32[64,256]{1,0:T(8,128)S(1)} %get-tuple-element.63), channel_id=1, source_target_pairs={{0,1},{1,0},{2,3},{3,2},{4,5},{5,4},{6,7},{7,6},{8,9},{9,8},{10,11... | collective-permute-start | bytes 196616 | tf_op jit(solution)/shard_map/ppermute | solution.py:30
  40.5 5.0 %collective-permute-start.16 = (f32[2,64,256]{2,1,0:T(8,128)S(1)}, f32[2,64,256]{2,1,0:T(8,128)S(1)}, u32[]{:S(2)}, u32[]{:S(2)}) collective-permute-start(f32[2,64,256]{2,1,0:T(8,128)S(1)} %shard_map.73.own_ref), channel_id=1, source_target_pairs={{0,2},{1,3},{2,0},{3,1},{4,6},{5,7},{6,4},{7,5},{8,10},{9,11},{10,... | collective-permute-start | bytes 393224 | tf_op jit(solution)/shard_map/ppermute | solution.py:30
  45.9 4.3 %collective-permute-start.19 = (f32[80,128]{1,0:T(8,128)S(1)}, f32[80,128]{1,0:T(8,128)S(1)}, u32[]{:S(2)}, u32[]{:S(2)}) collective-permute-start(f32[80,128]{1,0:T(8,128)S(1)} %get-tuple-element.67), channel_id=1, source_target_pairs={{0,5},{1,4},{2,7},{3,6},{4,1},{5,0},{6,3},{7,2},{8,13},{9,12},{10,... | collective-permute-start | bytes 122888 | tf_op jit(solution)/shard_map/ppermute | solution.py:44
  46.0 4.2 %collective-permute-start.18 = (f32[72,128]{1,0:T(8,128)S(1)}, f32[72,128]{1,0:T(8,128)S(1)}, u32[]{:S(2)}, u32[]{:S(2)}) collective-permute-start(f32[72,128]{1,0:T(8,128)S(1)} %get-tuple-element.66), channel_id=1, source_target_pairs={{0,4},{4,0},{8,12},{12,8},{16,20},{20,16},{24,28},{28,24},{1,5},{5... | collective-permute-start | bytes 110600 | tf_op jit(solution)/shard_map/ppermute | solution.py:30
  47.2 1.5 %collective-permute-start.17 = (f32[64,128]{1,0:T(8,128)S(1)}, f32[64,128]{1,0:T(8,128)S(1)}, u32[]{:S(2)}, u32[]{:S(2)}) collective-permute-start(f32[64,128]{1,0:T(8,128)S(1)} %get-tuple-element.65.refs_0_), channel_id=1, source_target_pairs={{0,1},{1,0},{2,3},{3,2},{4,5},{5,4},{6,7},{7,6},{8,9},{9,8},{10,11... | collective-permute-start | bytes 98312 | tf_op jit(solution)/shard_map/ppermute | solution.py:30
  50.2 7.3 %collective-permute-start.20 = (f32[2,64,256]{2,1,0:T(8,128)S(1)}, f32[2,64,256]{2,1,0:T(8,128)S(1)}, u32[]{:S(2)}, u32[]{:S(2)}) collective-permute-start(f32[2,64,256]{2,1,0:T(8,128)S(1)} %get-tuple-element.71.here_ref), channel_id=1, source_target_pairs={{0,1},{1,0},{2,3},{3,2},{4,5},{5,4},{6,7},{7,6},{8,9},{9,8},{10,11... | collective-permute-start | bytes 393224 | tf_op jit(solution)/shard_map/ppermute | solution.py:30
  50.4 7.1 %collective-permute-start.23 = (f32[80,128]{1,0:T(8,128)S(1)}, f32[80,128]{1,0:T(8,128)S(1)}, u32[]{:S(2)}, u32[]{:S(2)}) collective-permute-start(f32[80,128]{1,0:T(8,128)S(1)} %get-tuple-element.74), channel_id=1, source_target_pairs={{0,24},{4,28},{8,16},{12,20},{16,8},{20,12},{24,0},{28,4},{1,25},{... | collective-permute-start | bytes 122888 | tf_op jit(solution)/shard_map/ppermute | solution.py:30
  51.4 6.1 %collective-permute-start.22 = (f32[72,128]{1,0:T(8,128)S(1)}, f32[72,128]{1,0:T(8,128)S(1)}, u32[]{:S(2)}, u32[]{:S(2)}) collective-permute-start(f32[72,128]{1,0:T(8,128)S(1)} %get-tuple-element.73), channel_id=1, source_target_pairs={{0,16},{4,20},{8,24},{12,28},{16,0},{20,4},{24,8},{28,12},{1,17},{... | collective-permute-start | bytes 110600 | tf_op jit(solution)/shard_map/ppermute | solution.py:30
  52.0 5.2 %collective-permute-start.21 = (f32[64,128]{1,0:T(8,128)S(1)}, f32[64,128]{1,0:T(8,128)S(1)}, u32[]{:S(2)}, u32[]{:S(2)}) collective-permute-start(f32[64,128]{1,0:T(8,128)S(1)} %get-tuple-element.72.refs_0_), channel_id=1, source_target_pairs={{0,8},{4,12},{8,0},{12,4},{16,24},{20,28},{24,16},{28,20},{1,9},{5... | collective-permute-start | bytes 98312 | tf_op jit(solution)/shard_map/ppermute | solution.py:30

commit v8 on v7

--- a/solution.py
+++ b/solution.py
@@ -300,7 +300,34 @@
     for m, ref in enumerate((block_ref, across_ref)):
         blocks.append((own_ref[m] + came_ref[1 - m]) / ref[size : size + 1])
         out_ref[m] = blocks[m]
-    spread_out(jnp.concatenate([first_ref[...], gram_of(blocks, total)], axis=1), grams_refs)
+    spread_out(packed(first_ref[...], gram_of(blocks, total)), grams_refs)
+
+
+def places(size):
+    shape = (size, size)
+    return lax.broadcasted_iota(jnp.int32, shape, 0), lax.broadcasted_iota(jnp.int32, shape, 1)
+
+
+def packed(first, second):
+    size = first.shape[0]
+    row, column = places(size)
+    mixed = jnp.where(row >= column, first, second)
+    middle = size // 2
+    edge = jnp.sum(jnp.where(row == column, second, 0.0), axis=0, keepdims=True)
+    edge = jnp.broadcast_to(jnp.concatenate([edge, edge], axis=1), (8, 2 * size))
+    return jnp.concatenate(
+        [jnp.concatenate([mixed[:middle], mixed[middle:]], axis=1), edge], axis=0
+    )
+
+
+def unpacked(rows, size):
+    row, column = places(size)
+    middle = size // 2
+    mixed = jnp.concatenate([rows[:middle, :size], rows[:middle, size:]], axis=0)
+    flipped = mixed.T
+    first = jnp.where(row >= column, mixed, flipped)
+    second = jnp.where(row < column, mixed, flipped)
+    return first, jnp.where(row == column, rows[middle : middle + 1, :size], second)
 
 
 def spread_out(value, refs):
@@ -324,12 +351,14 @@
     *grams, out_ref = refs
     lane = lax.axis_index("cols")
     size = out_ref.shape[0]
-    both = grams[0][:size]
+    rows = grams[0].shape[0]
+    both = grams[0][...]
     for part in grams[1:]:
-        both = both + part[:size]
-    first = inverse_factor(both[:, :size])
+        both = both + part[:rows]
+    one, two = unpacked(both, size)
+    first = inverse_factor(one)
     solved = [times(first, block) for block in ordered(here_ref, there_ref)]
-    half = times(first, both[:, size:])
+    half = times(first, two)
     gram = lax.dot_general(
         half, first, (((1,), (1,)), ((), ())), precision=HIGHEST, preferred_element_type=f32
     )
@@ -438,7 +467,7 @@
     )
     came = [swap(part, "cols", 1) for part in core]
     (both,) = call(chip_kernel, [(keep.shape, f32)], keep, shift(back, -1, around=False), *came)
-    tall = [((size + 8 * k, 2 * size), f32) for k in range(3)]
+    tall = [((size // 2 + 8 + 8 * k, 2 * size), f32) for k in range(3)]
     here, *grams = call(
         functools.partial(resmooth_kernel, total),
         [((lanes // 2, size, BLOCK), f32), *tall],

time: 61.9 us -> 60.9 us (0.984)
  waiting for transfers between devices: 24.4 us -> 23.3 us
    ppermute x18, waiting for transfers between devices: 15.5 us -> 14.4 us  [swap(): return lax.ppermute(cells, axis, [(i, i ^ offset) for i in range(count)])]
  transfers between devices with their start and end apart: 24 -> 24, of which waited for: 15 -> 14; matrix products, arithmetic and copies ran while one was open for 1% -> 1% of each run, Pallas kernels for 6% -> 6%
where the time goes in v8:
time: 60.9 us; the launch traced here: 60.6 us
  waiting for transfers between devices  23.3 us (38%)
  starting transfers between devices  22.6 us (37%)
  Pallas kernels  8.91 us (15%)
  local copies, waits for them, and re-layouts  4.3 us (7%)
  between operations  0.77 us (1%)
  other arithmetic  0.68 us (1%)
    ppermute x18, starting transfers between devices, swap(): return lax.ppermute(cells, axis, [(i, i ^ offset) for i in range(count)])  14.6 us
    ppermute x18, waiting for transfers between devices, swap(): return lax.ppermute(cells, axis, [(i, i ^ offset) for i in range(count)])  14.4 us
    pallas_call x13, Pallas kernels, call(): pl.pallas_call(body, out_shape=[jax.ShapeDtypeStruct(shape, kind) for sha...  8.91 us
    ppermute x5, waiting for transfers between devices, shift(): return lax.ppermute(cells, 'rows', pairs)  8.9 us
    ppermute x5, starting transfers between devices, shift(): return lax.ppermute(cells, 'rows', pairs)  7.92 us
    unnamed x6, local copies, waits for them, and re-layouts  3.22 us
  transfers between devices with their start and end apart: 24, of which 14 were waited for; matrix products, arithmetic and copies ran while one was open for 1% of the time, Pallas kernels for 6%

profile of v8, /device:TPU:0, one launch (start us, length us, event | category | flops | bytes accessed | tf_op | source)
XLA Modules:
  0.0 60.6 jit_solution(742181254134069110)
XLA Ops:
  0.0 1.1 %constant_dynamic-slice_fusion = bf16[256,1024]{1,0:T(8,128)(2,1)S(1)} fusion(bf16[1024,1024]{1,0:T(8,128)(2,1)} %cells_ref.1, s32[]{:T(128)S(6)} %select_n.3), kind=kLoop, calls=%fused_computation.1 | loop fusion | bytes 1048580 | tf_op jit(solution)/shard_map/dynamic_slice | solution.py:392
  1.1 3.0 %collective-permute-start.3 = (bf16[256,1024]{1,0:T(8,128)(2,1)S(1)}, bf16[256,1024]{1,0:T(8,128)(2,1)S(1)}, u32[]{:S(2)}, u32[]{:S(2)}) collective-permute-start(bf16[256,1024]{1,0:T(8,128)(2,1)S(1)} %constant_dynamic-slice_fusion), channel_id=1, source_target_pairs={{0,4},{4,8},{8,12},{12,16},{16,20},{20,24},{24,28},{28,0},{1,5},{5... | collective-permute-start | bytes 1572872 | tf_op jit(solution)/shard_map/ppermute | solution.py:25
  4.8 0.7 %pad_add_fusion.refs_0_ = s32[3,24]{1,0:T(4,128)S(1)} fusion(s32[1,1]{1,0:T(1,128)S(6)} %copy.7, s32[1,24]{1,0:T(1,128)} %bitcast.4, s32[1,24]{1,0:T(1,128)} %bitcast.5), kind=kLoop, calls=%fused_computation | loop fusion | flops 144 | bytes 484 | tf_op jit(solution)/shard_map/concatenate | solution.py:394
  5.4 0.7 %collective-permute-start.2 = (s32[3,24]{1,0:T(4,128)S(1)}, s32[3,24]{1,0:T(4,128)S(1)}, u32[]{:S(2)}, u32[]{:S(2)}) collective-permute-start(s32[3,24]{1,0:T(4,128)S(1)} %pad_add_fusion.refs_0_), channel_id=1, source_target_pairs={{0,3},{1,2},{2,1},{3,0},{4,7},{5,6},{6,5},{7,4},{8,11},{9,10},{10,... | collective-permute-start | bytes 872 | tf_op jit(solution)/shard_map/ppermute | solution.py:30
  6.1 0.9 %collective-permute-start.1 = (s32[3,24]{1,0:T(4,128)S(1)}, s32[3,24]{1,0:T(4,128)S(1)}, u32[]{:S(2)}, u32[]{:S(2)}) collective-permute-start(s32[3,24]{1,0:T(4,128)S(1)} %pad_add_fusion.refs_0_), channel_id=1, source_target_pairs={{0,2},{1,3},{2,0},{3,1},{4,6},{5,7},{6,4},{7,5},{8,10},{9,11},{10,... | collective-permute-start | bytes 872 | tf_op jit(solution)/shard_map/ppermute | solution.py:30
  7.1 0.3 collective-permute-start
  7.3 0.9 %copy-done.1 = f32[64,1024]{1,0:T(8,128)S(1)} copy-done((f32[64,1024]{1,0:T(8,128)S(1)}, f32[64,1024]{1,0:T(8,128)}, u32[]{:S(2)}) %copy-start.1) | copy-done | bytes 262168
  8.3 0.7 %copy-done.2 = bf16[1024]{0:T(1024)(128)(2,1)S(1)} copy-done((bf16[1024]{0:T(1024)(128)(2,1)S(1)}, bf16[1024]{0:T(1024)(128)(2,1)}, u32[]{:S(2)}) %copy-start.2) | copy-done | bytes 2072
  9.0 0.7 %collective-permute-done.1.refs_2_ = s32[3,24]{1,0:T(4,128)S(1)} collective-permute-done((s32[3,24]{1,0:T(4,128)S(1)}, s32[3,24]{1,0:T(4,128)S(1)}, u32[]{:S(2)}, u32[]{:S(2)}) %collective-permute-start.1) | collective-permute-done | bytes 320 | tf_op jit(solution)/shard_map/ppermute | solution.py:30
  9.7 0.2 shard_map.65
  9.9 1.6 %collective-permute-start.4 = (bf16[80,256]{1,0:T(8,128)(2,1)S(1)}, bf16[80,256]{1,0:T(8,128)(2,1)S(1)}, u32[]{:S(2)}, u32[]{:S(2)}) collective-permute-start(bf16[80,256]{1,0:T(8,128)(2,1)S(1)} %get-tuple-element.44), channel_id=1, source_target_pairs={{0,4},{4,8},{8,12},{12,16},{16,20},{20,24},{24,28},{28,0},{1,5},{5... | collective-permute-start | bytes 122888 | tf_op jit(solution)/shard_map/ppermute | solution.py:25
  11.5 1.6 %copy-done = bf16[1024,1024]{1,0:T(8,128)(2,1)S(1)} copy-done((bf16[1024,1024]{1,0:T(8,128)(2,1)S(1)}, bf16[1024,1024]{1,0:T(8,128)(2,1)}, u32[]{:S(2)}) %copy-start) | copy-done | bytes 2097176
  13.1 1.8 %shard_map.66 = (bf16[4,256,1024]{2,1,0:T(8,128)(2,1)S(1)}, bf16[4,256,256]{2,1,0:T(8,128)(2,1)S(1)}, f32[4,72,256]{2,1,0:T(8,128)S(1)}) custom-call(bf16[1024,1024]{1,0:T(8,128)(2,1)S(1)} %copy-done, f32[1,1024]{1,0:T(1,128)S(1)} %get-tuple-element.40.mean_ref.refs_2_, bf16[4,80,256]{2,1,0:T(8,128)(2,1)S(1)} %get-tuple-element.41.left_ref.refs_3_), custom_call_target="tpu_custom_call" | custom-call | tf_op jit(solution)/shard_map/pallas_call | solution.py:372
  14.9 4.6 %collective-permute-done.3.cells_ref = bf16[256,1024]{1,0:T(8,128)(2,1)S(1)} collective-permute-done((bf16[256,1024]{1,0:T(8,128)(2,1)S(1)}, bf16[256,1024]{1,0:T(8,128)(2,1)S(1)}, u32[]{:S(2)}, u32[]{:S(2)}) %collective-permute-start.3) | collective-permute-done | bytes 524320 | tf_op jit(solution)/shard_map/ppermute | solution.py:25
  19.5 0.8 %shard_map.67.refs_0_ = f32[4,256,256]{2,1,0:T(8,128)S(1)} custom-call(bf16[4,256,1024]{2,1,0:T(8,128)(2,1)S(1)} %get-tuple-element.43.unit_ref, bf16[256,1024]{1,0:T(8,128)(2,1)S(1)} %collective-permute-done.3.cells_ref), custom_call_target="tpu_custom_call" | custom-call | tf_op jit(solution)/shard_map/pallas_call | solution.py:372
  20.3 0.7 %shard_map.68 = (bf16[4,256,256]{2,1,0:T(8,128)(2,1)S(1)}, f32[2,72,256]{2,1,0:T(8,128)S(1)}, f32[72,256]{1,0:T(8,128)S(1)}, f32[72,256]{1,0:T(8,128)S(1)}, f32[72,256]{1,0:T(8,128)S(1)}) custom-call(f32[4,256,256]{2,1,0:T(8,128)S(1)} %shard_map.67.refs_0_, bf16[80,256]{1,0:T(8,128)(2,1)S(1)} %collective-permute-done.4.refs_1_.side_ref, ...), custom_call_target="tpu_custom_call" | custom-call | tf_op jit(solution)/shard_map/pallas_call | solution.py:372
  21.1 0.5 collective-permute-start.6
  21.6 1.7 %collective-permute-start.8 = (f32[72,256]{1,0:T(8,128)S(1)}, f32[72,256]{1,0:T(8,128)S(1)}, u32[]{:S(2)}, u32[]{:S(2)}) collective-permute-start(f32[72,256]{1,0:T(8,128)S(1)} %get-tuple-element.52), channel_id=1, source_target_pairs={{0,28},{4,0},{8,4},{12,8},{16,12},{20,16},{24,20},{28,24},{1,29},{... | collective-permute-start | bytes 221192 | tf_op jit(solution)/shard_map/ppermute | solution.py:25
  23.4 1.5 %collective-permute-start.7 = (f32[72,256]{1,0:T(8,128)S(1)}, f32[72,256]{1,0:T(8,128)S(1)}, u32[]{:S(2)}, u32[]{:S(2)}) collective-permute-start(f32[72,256]{1,0:T(8,128)S(1)} %get-tuple-element.51), channel_id=1, source_target_pairs={{0,2},{1,3},{2,0},{3,1},{4,6},{5,7},{6,4},{7,5},{8,10},{9,11},{10,... | collective-permute-start | bytes 221192 | tf_op jit(solution)/shard_map/ppermute | solution.py:30
  24.9 1.0 %collective-permute-done.8.refs_2_ = f32[72,256]{1,0:T(8,128)S(1)} collective-permute-done((f32[72,256]{1,0:T(8,128)S(1)}, f32[72,256]{1,0:T(8,128)S(1)}, u32[]{:S(2)}, u32[]{:S(2)}) %collective-permute-start.8) | collective-permute-done | bytes 73760 | tf_op jit(solution)/shard_map/ppermute | solution.py:25
  25.9 1.8 %collective-permute-done.7.refs_1_ = f32[72,256]{1,0:T(8,128)S(1)} collective-permute-done((f32[72,256]{1,0:T(8,128)S(1)}, f32[72,256]{1,0:T(8,128)S(1)}, u32[]{:S(2)}, u32[]{:S(2)}) %collective-permute-start.7) | collective-permute-done | bytes 73760 | tf_op jit(solution)/shard_map/ppermute | solution.py:30
  27.8 1.5 %collective-permute-start.10 = (f32[72,256]{1,0:T(8,128)S(1)}, f32[72,256]{1,0:T(8,128)S(1)}, u32[]{:S(2)}, u32[]{:S(2)}) collective-permute-start(f32[72,256]{1,0:T(8,128)S(1)} %get-tuple-element.54.block_ref), channel_id=1, source_target_pairs={{0,2},{1,3},{2,0},{3,1},{4,6},{5,7},{6,4},{7,5},{8,10},{9,11},{10,... | collective-permute-start | bytes 221192 | tf_op jit(solution)/shard_map/ppermute | solution.py:30
  29.4 0.3 collective-permute-start.12
  29.7 2.6 %collective-permute-done.10.refs_2_.across_ref = f32[72,256]{1,0:T(8,128)S(1)} collective-permute-done((f32[72,256]{1,0:T(8,128)S(1)}, f32[72,256]{1,0:T(8,128)S(1)}, u32[]{:S(2)}, u32[]{:S(2)}) %collective-permute-start.10) | collective-permute-done | bytes 73760 | tf_op jit(solution)/shard_map/ppermute | solution.py:30
  32.2 0.5 collective-permute-start.9
  32.8 0.9 %collective-permute-done.9.refs_1_ = f32[64,256]{1,0:T(8,128)S(1)} collective-permute-done((f32[64,256]{1,0:T(8,128)S(1)}, f32[64,256]{1,0:T(8,128)S(1)}, u32[]{:S(2)}, u32[]{:S(2)}) %collective-permute-start.9) | collective-permute-done | bytes 65568 | tf_op jit(solution)/shard_map/ppermute | solution.py:30
  33.7 0.4 shard_map.71
  34.1 1.3 %collective-permute-start.13 = (f32[72,256]{1,0:T(8,128)S(1)}, f32[72,256]{1,0:T(8,128)S(1)}, u32[]{:S(2)}, u32[]{:S(2)}) collective-permute-start(f32[72,256]{1,0:T(8,128)S(1)} %get-tuple-element.61), channel_id=1, source_target_pairs={{4,0},{8,4},{12,8},{16,12},{20,16},{24,20},{28,24},{5,1},{9,5},{13... | collective-permute-start | bytes 221192 | tf_op jit(solution)/shard_map/ppermute | solution.py:25
  35.4 1.1 %collective-permute-done.12.next_ref = f32[80,256]{1,0:T(8,128)S(1)} collective-permute-done((f32[80,256]{1,0:T(8,128)S(1)}, f32[80,256]{1,0:T(8,128)S(1)}, u32[]{:S(2)}, u32[]{:S(2)}) %collective-permute-start.12) | collective-permute-done | bytes 81952 | tf_op jit(solution)/shard_map/ppermute | solution.py:25
  36.5 0.4 shard_map.72
  37.0 0.5 collective-permute-start.15
  37.5 0.7 %collective-permute-done.14.refs_0_ = f32[64,256]{1,0:T(8,128)S(1)} collective-permute-done((f32[64,256]{1,0:T(8,128)S(1)}, f32[64,256]{1,0:T(8,128)S(1)}, u32[]{:S(2)}, u32[]{:S(2)}) %collective-permute-start.14) | collective-permute-done | bytes 65568 | tf_op jit(solution)/shard_map/ppermute | solution.py:30
  38.2 0.2 collective-permute-done.15.refs_1_
  38.4 2.1 %collective-permute-done.13.back_ref = f32[72,256]{1,0:T(8,128)S(1)} collective-permute-done((f32[72,256]{1,0:T(8,128)S(1)}, f32[72,256]{1,0:T(8,128)S(1)}, u32[]{:S(2)}, u32[]{:S(2)}) %collective-permute-start.13) | collective-permute-done | bytes 73760 | tf_op jit(solution)/shard_map/ppermute | solution.py:25
  40.5 1.5 %collective-permute-start.16 = (f32[2,64,256]{2,1,0:T(8,128)S(1)}, f32[2,64,256]{2,1,0:T(8,128)S(1)}, u32[]{:S(2)}, u32[]{:S(2)}) collective-permute-start(f32[2,64,256]{2,1,0:T(8,128)S(1)} %shard_map.73.own_ref), channel_id=1, source_target_pairs={{0,2},{1,3},{2,0},{3,1},{4,6},{5,7},{6,4},{7,5},{8,10},{9,11},{10,... | collective-permute-start | bytes 393224 | tf_op jit(solution)/shard_map/ppermute | solution.py:30
  42.1 3.5 %collective-permute-done.16.came_ref = f32[2,64,256]{2,1,0:T(8,128)S(1)} collective-permute-done((f32[2,64,256]{2,1,0:T(8,128)S(1)}, f32[2,64,256]{2,1,0:T(8,128)S(1)}, u32[]{:S(2)}, u32[]{:S(2)}) %collective-permute-start.16) | collective-permute-done | bytes 131104 | tf_op jit(solution)/shard_map/ppermute | solution.py:30
  45.6 0.4 shard_map.74
  45.9 0.1 collective-permute-start.19
  46.0 1.2 %collective-permute-start.18 = (f32[48,128]{1,0:T(8,128)S(1)}, f32[48,128]{1,0:T(8,128)S(1)}, u32[]{:S(2)}, u32[]{:S(2)}) collective-permute-start(f32[48,128]{1,0:T(8,128)S(1)} %get-tuple-element.66), channel_id=1, source_target_pairs={{0,4},{4,0},{8,12},{12,8},{16,20},{20,16},{24,28},{28,24},{1,5},{5... | collective-permute-start | bytes 73736 | tf_op jit(solution)/shard_map/ppermute | solution.py:30
  47.2 0.6 %collective-permute-start.17 = (f32[40,128]{1,0:T(8,128)S(1)}, f32[40,128]{1,0:T(8,128)S(1)}, u32[]{:S(2)}, u32[]{:S(2)}) collective-permute-start(f32[40,128]{1,0:T(8,128)S(1)} %get-tuple-element.65.refs_0_), channel_id=1, source_target_pairs={{0,1},{1,0},{2,3},{3,2},{4,5},{5,4},{6,7},{7,6},{8,9},{9,8},{10,11... | collective-permute-start | bytes 61448 | tf_op jit(solution)/shard_map/ppermute | solution.py:30
  47.9 0.8 %collective-permute-done.17.refs_1_ = f32[40,128]{1,0:T(8,128)S(1)} collective-permute-done((f32[40,128]{1,0:T(8,128)S(1)}, f32[40,128]{1,0:T(8,128)S(1)}, u32[]{:S(2)}, u32[]{:S(2)}) %collective-permute-start.17) | collective-permute-done | bytes 20512 | tf_op jit(solution)/shard_map/ppermute | solution.py:30
  48.7 1.2 %collective-permute-done.18.refs_2_ = f32[48,128]{1,0:T(8,128)S(1)} collective-permute-done((f32[48,128]{1,0:T(8,128)S(1)}, f32[48,128]{1,0:T(8,128)S(1)}, u32[]{:S(2)}, u32[]{:S(2)}) %collective-permute-start.18) | collective-permute-done | bytes 24608 | tf_op jit(solution)/shard_map/ppermute | solution.py:30
  49.9 0.2 collective-permute-start.20
  50.1 0.9 %collective-permute-start.23 = (f32[56,128]{1,0:T(8,128)S(1)}, f32[56,128]{1,0:T(8,128)S(1)}, u32[]{:S(2)}, u32[]{:S(2)}) collective-permute-start(f32[56,128]{1,0:T(8,128)S(1)} %get-tuple-element.74), channel_id=1, source_target_pairs={{0,24},{4,28},{8,16},{12,20},{16,8},{20,12},{24,0},{28,4},{1,25},{... | collective-permute-start | bytes 86024 | tf_op jit(solution)/shard_map/ppermute | solution.py:30
  51.1 0.6 %collective-permute-start.22 = (f32[48,128]{1,0:T(8,128)S(1)}, f32[48,128]{1,0:T(8,128)S(1)}, u32[]{:S(2)}, u32[]{:S(2)}) collective-permute-start(f32[48,128]{1,0:T(8,128)S(1)} %get-tuple-element.73), channel_id=1, source_target_pairs={{0,16},{4,20},{8,24},{12,28},{16,0},{20,4},{24,8},{28,12},{1,17},{... | collective-permute-start | bytes 73736 | tf_op jit(solution)/shard_map/ppermute | solution.py:30
  51.7 2.8 %collective-permute-start.21 = (f32[40,128]{1,0:T(8,128)S(1)}, f32[40,128]{1,0:T(8,128)S(1)}, u32[]{:S(2)}, u32[]{:S(2)}) collective-permute-start(f32[40,128]{1,0:T(8,128)S(1)} %get-tuple-element.72.refs_0_), channel_id=1, source_target_pairs={{0,8},{4,12},{8,0},{12,4},{16,24},{20,28},{24,16},{28,20},{1,9},{5... | collective-permute-start | bytes 61448 | tf_op jit(solution)/shard_map/ppermute | solution.py:30
  54.5 1.9 %collective-permute-done.21.refs_1_ = f32[40,128]{1,0:T(8,128)S(1)} collective-permute-done((f32[40,128]{1,0:T(8,128)S(1)}, f32[40,128]{1,0:T(8,128)S(1)}, u32[]{:S(2)}, u32[]{:S(2)}) %collective-permute-start.21) | collective-permute-done | bytes 20512 | tf_op jit(solution)/shard_map/ppermute | solution.py:30
  56.5 4.1 %shard_map.76 = f32[64,1024]{1,0:T(8,128)} custom-call(f32[2,64,256]{2,1,0:T(8,128)S(1)} %get-tuple-element.71.here_ref, f32[2,64,256]{2,1,0:T(8,128)S(1)} %collective-permute-done.20.there_ref, f32[40,128]{1,0:T(8,128)S(1)} %get-tuple-element.72.refs_0_, f32[40,128]{1,0:T(8,128)S(1)} %collective-permute-done.21.refs_1_, ...), custom_call_target="tpu_custom_call" | custom-call | tf_op jit(solution)/shard_map/pallas_call | solution.py:372
  (21 shorter events, 0.3 us)
Async XLA Ops:
  1.1 18.4 %collective-permute-start.3 = (bf16[256,1024]{1,0:T(8,128)(2,1)S(1)}, bf16[256,1024]{1,0:T(8,128)(2,1)S(1)}, u32[]{:S(2)}, u32[]{:S(2)}) collective-permute-start(bf16[256,1024]{1,0:T(8,128)(2,1)S(1)} %constant_dynamic-slice_fusion), channel_id=1, source_target_pairs={{0,4},{4,8},{8,12},{12,16},{16,20},{20,24},{24,28},{28,0},{1,5},{5... | collective-permute-start | bytes 1572872 | tf_op jit(solution)/shard_map/ppermute | solution.py:25
  5.4 3.6 %collective-permute-start.2 = (s32[3,24]{1,0:T(4,128)S(1)}, s32[3,24]{1,0:T(4,128)S(1)}, u32[]{:S(2)}, u32[]{:S(2)}) collective-permute-start(s32[3,24]{1,0:T(4,128)S(1)} %pad_add_fusion.refs_0_), channel_id=1, source_target_pairs={{0,3},{1,2},{2,1},{3,0},{4,7},{5,6},{6,5},{7,4},{8,11},{9,10},{10,... | collective-permute-start | bytes 872 | tf_op jit(solution)/shard_map/ppermute | solution.py:30
  6.1 3.6 %collective-permute-start.1 = (s32[3,24]{1,0:T(4,128)S(1)}, s32[3,24]{1,0:T(4,128)S(1)}, u32[]{:S(2)}, u32[]{:S(2)}) collective-permute-start(s32[3,24]{1,0:T(4,128)S(1)} %pad_add_fusion.refs_0_), channel_id=1, source_target_pairs={{0,2},{1,3},{2,0},{3,1},{4,6},{5,7},{6,4},{7,5},{8,10},{9,11},{10,... | collective-permute-start | bytes 872 | tf_op jit(solution)/shard_map/ppermute | solution.py:30
  7.1 2.7 %collective-permute-start = (s32[3,24]{1,0:T(4,128)S(1)}, s32[3,24]{1,0:T(4,128)S(1)}, u32[]{:S(2)}, u32[]{:S(2)}) collective-permute-start(s32[3,24]{1,0:T(4,128)S(1)} %pad_add_fusion.refs_0_), channel_id=1, source_target_pairs={{0,1},{1,0},{2,3},{3,2},{4,5},{5,4},{6,7},{7,6},{8,9},{9,8},{10,11... | collective-permute-start | bytes 872 | tf_op jit(solution)/shard_map/ppermute | solution.py:30
  7.3 0.9 %copy-start.1 = (f32[64,1024]{1,0:T(8,128)S(1)}, f32[64,1024]{1,0:T(8,128)}, u32[]{:S(2)}) copy-start(f32[64,1024]{1,0:T(8,128)} %start_ref.1) | copy-start | bytes 786436
  8.3 0.7 %copy-start.2 = (bf16[1024]{0:T(1024)(128)(2,1)S(1)}, bf16[1024]{0:T(1024)(128)(2,1)}, u32[]{:S(2)}) copy-start(bf16[1024]{0:T(1024)(128)(2,1)} %param.7) | copy-start | bytes 6148
  9.9 10.4 %collective-permute-start.4 = (bf16[80,256]{1,0:T(8,128)(2,1)S(1)}, bf16[80,256]{1,0:T(8,128)(2,1)S(1)}, u32[]{:S(2)}, u32[]{:S(2)}) collective-permute-start(bf16[80,256]{1,0:T(8,128)(2,1)S(1)} %get-tuple-element.44), channel_id=1, source_target_pairs={{0,4},{4,8},{8,12},{12,16},{16,20},{20,24},{24,28},{28,0},{1,5},{5... | collective-permute-start | bytes 122888 | tf_op jit(solution)/shard_map/ppermute | solution.py:25
  11.5 1.6 %copy-start = (bf16[1024,1024]{1,0:T(8,128)(2,1)S(1)}, bf16[1024,1024]{1,0:T(8,128)(2,1)}, u32[]{:S(2)}) copy-start(bf16[1024,1024]{1,0:T(8,128)(2,1)} %cells_ref.1) | copy-start | bytes 6291460
  21.0 2.3 %collective-permute-start.5 = (f32[72,256]{1,0:T(8,128)S(1)}, f32[72,256]{1,0:T(8,128)S(1)}, u32[]{:S(2)}, u32[]{:S(2)}) collective-permute-start(f32[72,256]{1,0:T(8,128)S(1)} %get-tuple-element.48), channel_id=1, source_target_pairs={{0,1},{1,0},{2,3},{3,2},{4,5},{5,4},{6,7},{7,6},{8,9},{9,8},{10,11... | collective-permute-start | bytes 221192 | tf_op jit(solution)/shard_map/ppermute | solution.py:30
  21.1 2.3 %collective-permute-start.6 = (f32[72,256]{1,0:T(8,128)S(1)}, f32[72,256]{1,0:T(8,128)S(1)}, u32[]{:S(2)}, u32[]{:S(2)}) collective-permute-start(f32[72,256]{1,0:T(8,128)S(1)} %get-tuple-element.49), channel_id=1, source_target_pairs={{0,1},{1,0},{2,3},{3,2},{4,5},{5,4},{6,7},{7,6},{8,9},{9,8},{10,11... | collective-permute-start | bytes 221192 | tf_op jit(solution)/shard_map/ppermute | solution.py:30
  21.6 4.4 %collective-permute-start.8 = (f32[72,256]{1,0:T(8,128)S(1)}, f32[72,256]{1,0:T(8,128)S(1)}, u32[]{:S(2)}, u32[]{:S(2)}) collective-permute-start(f32[72,256]{1,0:T(8,128)S(1)} %get-tuple-element.52), channel_id=1, source_target_pairs={{0,28},{4,0},{8,4},{12,8},{16,12},{20,16},{24,20},{28,24},{1,29},{... | collective-permute-start | bytes 221192 | tf_op jit(solution)/shard_map/ppermute | solution.py:25
  23.4 4.4 %collective-permute-start.7 = (f32[72,256]{1,0:T(8,128)S(1)}, f32[72,256]{1,0:T(8,128)S(1)}, u32[]{:S(2)}, u32[]{:S(2)}) collective-permute-start(f32[72,256]{1,0:T(8,128)S(1)} %get-tuple-element.51), channel_id=1, source_target_pairs={{0,2},{1,3},{2,0},{3,1},{4,6},{5,7},{6,4},{7,5},{8,10},{9,11},{10,... | collective-permute-start | bytes 221192 | tf_op jit(solution)/shard_map/ppermute | solution.py:30
  27.8 4.4 %collective-permute-start.10 = (f32[72,256]{1,0:T(8,128)S(1)}, f32[72,256]{1,0:T(8,128)S(1)}, u32[]{:S(2)}, u32[]{:S(2)}) collective-permute-start(f32[72,256]{1,0:T(8,128)S(1)} %get-tuple-element.54.block_ref), channel_id=1, source_target_pairs={{0,2},{1,3},{2,0},{3,1},{4,6},{5,7},{6,4},{7,5},{8,10},{9,11},{10,... | collective-permute-start | bytes 221192 | tf_op jit(solution)/shard_map/ppermute | solution.py:30
  29.4 7.1 %collective-permute-start.12 = (f32[80,256]{1,0:T(8,128)S(1)}, f32[80,256]{1,0:T(8,128)S(1)}, u32[]{:S(2)}, u32[]{:S(2)}) collective-permute-start(f32[80,256]{1,0:T(8,128)S(1)} %get-tuple-element.59), channel_id=1, source_target_pairs={{0,4},{4,8},{8,12},{12,16},{16,20},{20,24},{24,28},{28,0},{1,5},{5... | collective-permute-start | bytes 245768 | tf_op jit(solution)/shard_map/ppermute | solution.py:25
  32.2 1.4 %collective-permute-start.11 = (f32[72,256]{1,0:T(8,128)S(1)}, f32[72,256]{1,0:T(8,128)S(1)}, u32[]{:S(2)}, u32[]{:S(2)}) collective-permute-start(f32[72,256]{1,0:T(8,128)S(1)} %collective-permute-done.10.refs_2_.across_ref), channel_id=1, source_target_pairs={{0,1},{1,0},{2,3},{3,2},{4,5},{5,4},{6,7},{7,6},{8,9},{9,8},{10,11... | collective-permute-start | bytes 221192 | tf_op jit(solution)/shard_map/ppermute | solution.py:30
  32.2 1.4 %collective-permute-start.9 = (f32[64,256]{1,0:T(8,128)S(1)}, f32[64,256]{1,0:T(8,128)S(1)}, u32[]{:S(2)}, u32[]{:S(2)}) collective-permute-start(f32[64,256]{1,0:T(8,128)S(1)} %get-tuple-element.53.refs_0_.lead_ref), channel_id=1, source_target_pairs={{0,1},{1,0},{2,3},{3,2},{4,5},{5,4},{6,7},{7,6},{8,9},{9,8},{10,11... | collective-permute-start | bytes 196616 | tf_op jit(solution)/shard_map/ppermute | solution.py:30
  34.1 6.4 %collective-permute-start.13 = (f32[72,256]{1,0:T(8,128)S(1)}, f32[72,256]{1,0:T(8,128)S(1)}, u32[]{:S(2)}, u32[]{:S(2)}) collective-permute-start(f32[72,256]{1,0:T(8,128)S(1)} %get-tuple-element.61), channel_id=1, source_target_pairs={{4,0},{8,4},{12,8},{16,12},{20,16},{24,20},{28,24},{5,1},{9,5},{13... | collective-permute-start | bytes 221192 | tf_op jit(solution)/shard_map/ppermute | solution.py:25
  36.9 1.3 %collective-permute-start.14 = (f32[64,256]{1,0:T(8,128)S(1)}, f32[64,256]{1,0:T(8,128)S(1)}, u32[]{:S(2)}, u32[]{:S(2)}) collective-permute-start(f32[64,256]{1,0:T(8,128)S(1)} %get-tuple-element.62), channel_id=1, source_target_pairs={{0,1},{1,0},{2,3},{3,2},{4,5},{5,4},{6,7},{7,6},{8,9},{9,8},{10,11... | collective-permute-start | bytes 196616 | tf_op jit(solution)/shard_map/ppermute | solution.py:30
  37.0 1.4 %collective-permute-start.15 = (f32[64,256]{1,0:T(8,128)S(1)}, f32[64,256]{1,0:T(8,128)S(1)}, u32[]{:S(2)}, u32[]{:S(2)}) collective-permute-start(f32[64,256]{1,0:T(8,128)S(1)} %get-tuple-element.63), channel_id=1, source_target_pairs={{0,1},{1,0},{2,3},{3,2},{4,5},{5,4},{6,7},{7,6},{8,9},{9,8},{10,11... | collective-permute-start | bytes 196616 | tf_op jit(solution)/shard_map/ppermute | solution.py:30
  40.5 5.0 %collective-permute-start.16 = (f32[2,64,256]{2,1,0:T(8,128)S(1)}, f32[2,64,256]{2,1,0:T(8,128)S(1)}, u32[]{:S(2)}, u32[]{:S(2)}) collective-permute-start(f32[2,64,256]{2,1,0:T(8,128)S(1)} %shard_map.73.own_ref), channel_id=1, source_target_pairs={{0,2},{1,3},{2,0},{3,1},{4,6},{5,7},{6,4},{7,5},{8,10},{9,11},{10,... | collective-permute-start | bytes 393224 | tf_op jit(solution)/shard_map/ppermute | solution.py:30
  45.9 4.0 %collective-permute-start.19 = (f32[56,128]{1,0:T(8,128)S(1)}, f32[56,128]{1,0:T(8,128)S(1)}, u32[]{:S(2)}, u32[]{:S(2)}) collective-permute-start(f32[56,128]{1,0:T(8,128)S(1)} %get-tuple-element.67), channel_id=1, source_target_pairs={{0,5},{1,4},{2,7},{3,6},{4,1},{5,0},{6,3},{7,2},{8,13},{9,12},{10,... | collective-permute-start | bytes 86024 | tf_op jit(solution)/shard_map/ppermute | solution.py:44
  46.0 3.9 %collective-permute-start.18 = (f32[48,128]{1,0:T(8,128)S(1)}, f32[48,128]{1,0:T(8,128)S(1)}, u32[]{:S(2)}, u32[]{:S(2)}) collective-permute-start(f32[48,128]{1,0:T(8,128)S(1)} %get-tuple-element.66), channel_id=1, source_target_pairs={{0,4},{4,0},{8,12},{12,8},{16,20},{20,16},{24,28},{28,24},{1,5},{5... | collective-permute-start | bytes 73736 | tf_op jit(solution)/shard_map/ppermute | solution.py:30
  47.2 1.5 %collective-permute-start.17 = (f32[40,128]{1,0:T(8,128)S(1)}, f32[40,128]{1,0:T(8,128)S(1)}, u32[]{:S(2)}, u32[]{:S(2)}) collective-permute-start(f32[40,128]{1,0:T(8,128)S(1)} %get-tuple-element.65.refs_0_), channel_id=1, source_target_pairs={{0,1},{1,0},{2,3},{3,2},{4,5},{5,4},{6,7},{7,6},{8,9},{9,8},{10,11... | collective-permute-start | bytes 61448 | tf_op jit(solution)/shard_map/ppermute | solution.py:30
  49.9 6.6 %collective-permute-start.20 = (f32[2,64,256]{2,1,0:T(8,128)S(1)}, f32[2,64,256]{2,1,0:T(8,128)S(1)}, u32[]{:S(2)}, u32[]{:S(2)}) collective-permute-start(f32[2,64,256]{2,1,0:T(8,128)S(1)} %get-tuple-element.71.here_ref), channel_id=1, source_target_pairs={{0,1},{1,0},{2,3},{3,2},{4,5},{5,4},{6,7},{7,6},{8,9},{9,8},{10,11... | collective-permute-start | bytes 393224 | tf_op jit(solution)/shard_map/ppermute | solution.py:30
  50.1 6.4 %collective-permute-start.23 = (f32[56,128]{1,0:T(8,128)S(1)}, f32[56,128]{1,0:T(8,128)S(1)}, u32[]{:S(2)}, u32[]{:S(2)}) collective-permute-start(f32[56,128]{1,0:T(8,128)S(1)} %get-tuple-element.74), channel_id=1, source_target_pairs={{0,24},{4,28},{8,16},{12,20},{16,8},{20,12},{24,0},{28,4},{1,25},{... | collective-permute-start | bytes 86024 | tf_op jit(solution)/shard_map/ppermute | solution.py:30
  51.1 5.4 %collective-permute-start.22 = (f32[48,128]{1,0:T(8,128)S(1)}, f32[48,128]{1,0:T(8,128)S(1)}, u32[]{:S(2)}, u32[]{:S(2)}) collective-permute-start(f32[48,128]{1,0:T(8,128)S(1)} %get-tuple-element.73), channel_id=1, source_target_pairs={{0,16},{4,20},{8,24},{12,28},{16,0},{20,4},{24,8},{28,12},{1,17},{... | collective-permute-start | bytes 73736 | tf_op jit(solution)/shard_map/ppermute | solution.py:30
  51.7 4.8 %collective-permute-start.21 = (f32[40,128]{1,0:T(8,128)S(1)}, f32[40,128]{1,0:T(8,128)S(1)}, u32[]{:S(2)}, u32[]{:S(2)}) collective-permute-start(f32[40,128]{1,0:T(8,128)S(1)} %get-tuple-element.72.refs_0_), channel_id=1, source_target_pairs={{0,8},{4,12},{8,0},{12,4},{16,24},{20,28},{24,16},{28,20},{1,9},{5... | collective-permute-start | bytes 61448 | tf_op jit(solution)/shard_map/ppermute | solution.py:30

commit v9 on v8

--- a/solution.py
+++ b/solution.py
@@ -79,14 +79,11 @@
 
 def pieces(values):
     first = values.astype(bf16)
-    rest = values - first.astype(f32)
-    second = rest.astype(bf16)
-    third = (rest - second.astype(f32)).astype(bf16)
-    return jnp.concatenate([first, second, third], axis=0)
+    return jnp.concatenate([first, (values - first.astype(f32)).astype(bf16)], axis=0)
 
 
 def joined(product, size):
-    return product[:size] + (product[size : 2 * size] + product[2 * size :])
+    return product[:size] + product[size:]
 
 
 def inverse_factor(gram):
@@ -161,11 +158,7 @@
     blocks = lax.axis_size("rows") * lanes
     size = left_ref.shape[1] - ONES
     stride = 4 * blocks
-    slot = lax.broadcasted_iota(jnp.int32, (1, lists[0].shape[1]), 1)
-    codes = [
-        jnp.where(slot < ref[2:3, 0:1], ref[0:1] * stride + ref[1:2], -stride) for ref in lists
-    ]
-    codes = jnp.concatenate(codes, axis=0)
+    codes = jnp.concatenate([ref[0:1] * stride + ref[1:2] for ref in lists], axis=0)
 
     def live(row_block, col_block):
         hit = jnp.where(codes == row_block * stride + col_block, 1.0, 0.0)
@@ -381,7 +374,6 @@
 def local(embeddings, knn_mean, pair_rows, pair_cols, pair_count, start_block):
     rows_here, width = embeddings.shape
     size = start_block.shape[0]
-    slots = pair_rows.shape[2]
     lanes = lax.axis_size("cols")
     lane = lax.axis_index("cols")
     groups = lax.axis_size("rows")
@@ -390,8 +382,7 @@
     wide = size + 8
 
     next_cells = shift(lax.dynamic_slice_in_dim(embeddings, lane * BLOCK, BLOCK, 0), 1)
-    counts = jnp.pad(pair_count, ((0, 0), (0, slots - 1)))
-    mine = jnp.concatenate([pair_rows[0], pair_cols[0], counts], axis=0)
+    mine = jnp.concatenate([pair_rows[0], pair_cols[0]], axis=0)
     mean, left = call(
         functools.partial(vector_kernel, lanes),
         [((1, rows_here), f32), ((lanes, size + ONES, BLOCK), bf16)],

time: 60.9 us -> 60.9 us (level)
  waiting for transfers between devices: 23.3 us -> 24.2 us
  between operations: 0.77 us -> 0.12 us
    ppermute x5, waiting for transfers between devices: 8.9 us -> 9.77 us  [shift(): return lax.ppermute(cells, 'rows', pairs)]
where the time goes in v9:
time: 60.9 us; the launch traced here: 60.6 us
  waiting for transfers between devices  24.2 us (40%)
  starting transfers between devices  22.6 us (37%)
  Pallas kernels  8.76 us (14%)
  local copies, waits for them, and re-layouts  4.3 us (7%)
  other arithmetic  0.68 us (1%)
    ppermute x18, starting transfers between devices, swap(): return lax.ppermute(cells, axis, [(i, i ^ offset) for i in range(count)])  14.6 us
    ppermute x18, waiting for transfers between devices, swap(): return lax.ppermute(cells, axis, [(i, i ^ offset) for i in range(count)])  14.4 us
    ppermute x5, waiting for transfers between devices, shift(): return lax.ppermute(cells, 'rows', pairs)  9.77 us
    pallas_call x13, Pallas kernels, call(): pl.pallas_call(body, out_shape=[jax.ShapeDtypeStruct(shape, kind) for sha...  8.76 us
    ppermute x5, starting transfers between devices, shift(): return lax.ppermute(cells, 'rows', pairs)  7.92 us
    unnamed x6, local copies, waits for them, and re-layouts  3.22 us
  transfers between devices with their start and end apart: 24, of which 14 were waited for; matrix products, arithmetic and copies ran while one was open for 1% of the time, Pallas kernels for 6%

profile of v9, /device:TPU:0, one launch (start us, length us, event | category | flops | bytes accessed | tf_op | source)
XLA Modules:
  0.0 60.6 jit_solution(9246883732948051120)
XLA Ops:
  0.0 1.1 %constant_dynamic-slice_fusion = bf16[256,1024]{1,0:T(8,128)(2,1)S(1)} fusion(bf16[1024,1024]{1,0:T(8,128)(2,1)} %cells_ref.1, s32[]{:T(128)S(6)} %select_n.3), kind=kLoop, calls=%fused_computation.1 | loop fusion | bytes 1048580 | tf_op jit(solution)/shard_map/dynamic_slice | solution.py:384
  1.1 3.0 %collective-permute-start.3 = (bf16[256,1024]{1,0:T(8,128)(2,1)S(1)}, bf16[256,1024]{1,0:T(8,128)(2,1)S(1)}, u32[]{:S(2)}, u32[]{:S(2)}) collective-permute-start(bf16[256,1024]{1,0:T(8,128)(2,1)S(1)} %constant_dynamic-slice_fusion), channel_id=1, source_target_pairs={{0,4},{4,8},{8,12},{12,16},{16,20},{20,24},{24,28},{28,0},{1,5},{5... | collective-permute-start | bytes 1572872 | tf_op jit(solution)/shard_map/ppermute | solution.py:25
  4.1 0.7 %pad_add_fusion.refs_0_ = s32[2,24]{1,0:T(2,128)S(1)} fusion(s32[1,24]{1,0:T(1,128)} %bitcast.4, s32[1,24]{1,0:T(1,128)} %bitcast.5), kind=kLoop, calls=%fused_computation | loop fusion | flops 48 | bytes 384 | tf_op jit(solution)/shard_map/concatenate | solution.py:385
  4.8 0.7 %collective-permute-start.2 = (s32[2,24]{1,0:T(2,128)S(1)}, s32[2,24]{1,0:T(2,128)S(1)}, u32[]{:S(2)}, u32[]{:S(2)}) collective-permute-start(s32[2,24]{1,0:T(2,128)S(1)} %pad_add_fusion.refs_0_), channel_id=1, source_target_pairs={{0,3},{1,2},{2,1},{3,0},{4,7},{5,6},{6,5},{7,4},{8,11},{9,10},{10,... | collective-permute-start | bytes 584 | tf_op jit(solution)/shard_map/ppermute | solution.py:30
  5.4 0.9 %collective-permute-start.1 = (s32[2,24]{1,0:T(2,128)S(1)}, s32[2,24]{1,0:T(2,128)S(1)}, u32[]{:S(2)}, u32[]{:S(2)}) collective-permute-start(s32[2,24]{1,0:T(2,128)S(1)} %pad_add_fusion.refs_0_), channel_id=1, source_target_pairs={{0,2},{1,3},{2,0},{3,1},{4,6},{5,7},{6,4},{7,5},{8,10},{9,11},{10,... | collective-permute-start | bytes 584 | tf_op jit(solution)/shard_map/ppermute | solution.py:30
  6.3 0.3 collective-permute-start
  6.6 0.9 %copy-done.1 = f32[64,1024]{1,0:T(8,128)S(1)} copy-done((f32[64,1024]{1,0:T(8,128)S(1)}, f32[64,1024]{1,0:T(8,128)}, u32[]{:S(2)}) %copy-start.1) | copy-done | bytes 262168
  7.6 0.7 %copy-done.2 = bf16[1024]{0:T(1024)(128)(2,1)S(1)} copy-done((bf16[1024]{0:T(1024)(128)(2,1)S(1)}, bf16[1024]{0:T(1024)(128)(2,1)}, u32[]{:S(2)}) %copy-start.2) | copy-done | bytes 2072
  8.3 0.7 %collective-permute-done.1.refs_2_ = s32[2,24]{1,0:T(2,128)S(1)} collective-permute-done((s32[2,24]{1,0:T(2,128)S(1)}, s32[2,24]{1,0:T(2,128)S(1)}, u32[]{:S(2)}, u32[]{:S(2)}) %collective-permute-start.1) | collective-permute-done | bytes 224 | tf_op jit(solution)/shard_map/ppermute | solution.py:30
  9.0 0.1 shard_map.56
  9.1 1.6 %collective-permute-start.4 = (bf16[80,256]{1,0:T(8,128)(2,1)S(1)}, bf16[80,256]{1,0:T(8,128)(2,1)S(1)}, u32[]{:S(2)}, u32[]{:S(2)}) collective-permute-start(bf16[80,256]{1,0:T(8,128)(2,1)S(1)} %get-tuple-element.44), channel_id=1, source_target_pairs={{0,4},{4,8},{8,12},{12,16},{16,20},{20,24},{24,28},{28,0},{1,5},{5... | collective-permute-start | bytes 122888 | tf_op jit(solution)/shard_map/ppermute | solution.py:25
  10.7 1.6 %copy-done = bf16[1024,1024]{1,0:T(8,128)(2,1)S(1)} copy-done((bf16[1024,1024]{1,0:T(8,128)(2,1)S(1)}, bf16[1024,1024]{1,0:T(8,128)(2,1)}, u32[]{:S(2)}) %copy-start) | copy-done | bytes 2097176
  12.3 1.8 %shard_map.57 = (bf16[4,256,1024]{2,1,0:T(8,128)(2,1)S(1)}, bf16[4,256,256]{2,1,0:T(8,128)(2,1)S(1)}, f32[4,72,256]{2,1,0:T(8,128)S(1)}) custom-call(bf16[1024,1024]{1,0:T(8,128)(2,1)S(1)} %copy-done, f32[1,1024]{1,0:T(1,128)S(1)} %get-tuple-element.40.mean_ref.refs_2_, bf16[4,80,256]{2,1,0:T(8,128)(2,1)S(1)} %get-tuple-element.41.left_ref.refs_3_), custom_call_target="tpu_custom_call" | custom-call | tf_op jit(solution)/shard_map/pallas_call | solution.py:365
  14.1 5.4 %collective-permute-done.3.cells_ref = bf16[256,1024]{1,0:T(8,128)(2,1)S(1)} collective-permute-done((bf16[256,1024]{1,0:T(8,128)(2,1)S(1)}, bf16[256,1024]{1,0:T(8,128)(2,1)S(1)}, u32[]{:S(2)}, u32[]{:S(2)}) %collective-permute-start.3) | collective-permute-done | bytes 524320 | tf_op jit(solution)/shard_map/ppermute | solution.py:25
  19.5 0.8 %shard_map.58.refs_0_ = f32[4,256,256]{2,1,0:T(8,128)S(1)} custom-call(bf16[4,256,1024]{2,1,0:T(8,128)(2,1)S(1)} %get-tuple-element.43.unit_ref, bf16[256,1024]{1,0:T(8,128)(2,1)S(1)} %collective-permute-done.3.cells_ref), custom_call_target="tpu_custom_call" | custom-call | tf_op jit(solution)/shard_map/pallas_call | solution.py:365
  20.3 0.7 %shard_map.59 = (bf16[4,256,256]{2,1,0:T(8,128)(2,1)S(1)}, f32[2,72,256]{2,1,0:T(8,128)S(1)}, f32[72,256]{1,0:T(8,128)S(1)}, f32[72,256]{1,0:T(8,128)S(1)}, f32[72,256]{1,0:T(8,128)S(1)}) custom-call(f32[4,256,256]{2,1,0:T(8,128)S(1)} %shard_map.58.refs_0_, bf16[80,256]{1,0:T(8,128)(2,1)S(1)} %collective-permute-done.4.refs_1_.side_ref, ...), custom_call_target="tpu_custom_call" | custom-call | tf_op jit(solution)/shard_map/pallas_call | solution.py:365
  21.1 0.5 collective-permute-start.6
  21.6 1.7 %collective-permute-start.8 = (f32[72,256]{1,0:T(8,128)S(1)}, f32[72,256]{1,0:T(8,128)S(1)}, u32[]{:S(2)}, u32[]{:S(2)}) collective-permute-start(f32[72,256]{1,0:T(8,128)S(1)} %get-tuple-element.52), channel_id=1, source_target_pairs={{0,28},{4,0},{8,4},{12,8},{16,12},{20,16},{24,20},{28,24},{1,29},{... | collective-permute-start | bytes 221192 | tf_op jit(solution)/shard_map/ppermute | solution.py:25
  23.4 1.5 %collective-permute-start.7 = (f32[72,256]{1,0:T(8,128)S(1)}, f32[72,256]{1,0:T(8,128)S(1)}, u32[]{:S(2)}, u32[]{:S(2)}) collective-permute-start(f32[72,256]{1,0:T(8,128)S(1)} %get-tuple-element.51), channel_id=1, source_target_pairs={{0,2},{1,3},{2,0},{3,1},{4,6},{5,7},{6,4},{7,5},{8,10},{9,11},{10,... | collective-permute-start | bytes 221192 | tf_op jit(solution)/shard_map/ppermute | solution.py:30
  24.9 1.0 %collective-permute-done.8.refs_2_ = f32[72,256]{1,0:T(8,128)S(1)} collective-permute-done((f32[72,256]{1,0:T(8,128)S(1)}, f32[72,256]{1,0:T(8,128)S(1)}, u32[]{:S(2)}, u32[]{:S(2)}) %collective-permute-start.8) | collective-permute-done | bytes 73760 | tf_op jit(solution)/shard_map/ppermute | solution.py:25
  25.9 1.8 %collective-permute-done.7.refs_1_ = f32[72,256]{1,0:T(8,128)S(1)} collective-permute-done((f32[72,256]{1,0:T(8,128)S(1)}, f32[72,256]{1,0:T(8,128)S(1)}, u32[]{:S(2)}, u32[]{:S(2)}) %collective-permute-start.7) | collective-permute-done | bytes 73760 | tf_op jit(solution)/shard_map/ppermute | solution.py:30
  27.8 1.5 %collective-permute-start.10 = (f32[72,256]{1,0:T(8,128)S(1)}, f32[72,256]{1,0:T(8,128)S(1)}, u32[]{:S(2)}, u32[]{:S(2)}) collective-permute-start(f32[72,256]{1,0:T(8,128)S(1)} %get-tuple-element.54.block_ref), channel_id=1, source_target_pairs={{0,2},{1,3},{2,0},{3,1},{4,6},{5,7},{6,4},{7,5},{8,10},{9,11},{10,... | collective-permute-start | bytes 221192 | tf_op jit(solution)/shard_map/ppermute | solution.py:30
  29.4 0.3 collective-permute-start.12
  29.7 2.6 %collective-permute-done.10.refs_2_.across_ref = f32[72,256]{1,0:T(8,128)S(1)} collective-permute-done((f32[72,256]{1,0:T(8,128)S(1)}, f32[72,256]{1,0:T(8,128)S(1)}, u32[]{:S(2)}, u32[]{:S(2)}) %collective-permute-start.10) | collective-permute-done | bytes 73760 | tf_op jit(solution)/shard_map/ppermute | solution.py:30
  32.2 0.5 collective-permute-start.9
  32.8 0.9 %collective-permute-done.9.refs_1_ = f32[64,256]{1,0:T(8,128)S(1)} collective-permute-done((f32[64,256]{1,0:T(8,128)S(1)}, f32[64,256]{1,0:T(8,128)S(1)}, u32[]{:S(2)}, u32[]{:S(2)}) %collective-permute-start.9) | collective-permute-done | bytes 65568 | tf_op jit(solution)/shard_map/ppermute | solution.py:30
  33.7 0.4 shard_map.62
  34.1 1.3 %collective-permute-start.13 = (f32[72,256]{1,0:T(8,128)S(1)}, f32[72,256]{1,0:T(8,128)S(1)}, u32[]{:S(2)}, u32[]{:S(2)}) collective-permute-start(f32[72,256]{1,0:T(8,128)S(1)} %get-tuple-element.61), channel_id=1, source_target_pairs={{4,0},{8,4},{12,8},{16,12},{20,16},{24,20},{28,24},{5,1},{9,5},{13... | collective-permute-start | bytes 221192 | tf_op jit(solution)/shard_map/ppermute | solution.py:25
  35.4 1.1 %collective-permute-done.12.next_ref = f32[80,256]{1,0:T(8,128)S(1)} collective-permute-done((f32[80,256]{1,0:T(8,128)S(1)}, f32[80,256]{1,0:T(8,128)S(1)}, u32[]{:S(2)}, u32[]{:S(2)}) %collective-permute-start.12) | collective-permute-done | bytes 81952 | tf_op jit(solution)/shard_map/ppermute | solution.py:25
  36.5 0.3 shard_map.63
  36.8 0.1 collective-permute-start.14
  36.9 0.5 collective-permute-start.15
  37.4 0.7 %collective-permute-done.14.refs_0_ = f32[64,256]{1,0:T(8,128)S(1)} collective-permute-done((f32[64,256]{1,0:T(8,128)S(1)}, f32[64,256]{1,0:T(8,128)S(1)}, u32[]{:S(2)}, u32[]{:S(2)}) %collective-permute-start.14) | collective-permute-done | bytes 65568 | tf_op jit(solution)/shard_map/ppermute | solution.py:30
  38.1 0.2 collective-permute-done.15.refs_1_
  38.3 2.2 %collective-permute-done.13.back_ref = f32[72,256]{1,0:T(8,128)S(1)} collective-permute-done((f32[72,256]{1,0:T(8,128)S(1)}, f32[72,256]{1,0:T(8,128)S(1)}, u32[]{:S(2)}, u32[]{:S(2)}) %collective-permute-start.13) | collective-permute-done | bytes 73760 | tf_op jit(solution)/shard_map/ppermute | solution.py:25
  40.5 1.5 %collective-permute-start.16 = (f32[2,64,256]{2,1,0:T(8,128)S(1)}, f32[2,64,256]{2,1,0:T(8,128)S(1)}, u32[]{:S(2)}, u32[]{:S(2)}) collective-permute-start(f32[2,64,256]{2,1,0:T(8,128)S(1)} %shard_map.64.own_ref), channel_id=1, source_target_pairs={{0,2},{1,3},{2,0},{3,1},{4,6},{5,7},{6,4},{7,5},{8,10},{9,11},{10,... | collective-permute-start | bytes 393224 | tf_op jit(solution)/shard_map/ppermute | solution.py:30
  42.1 3.5 %collective-permute-done.16.came_ref = f32[2,64,256]{2,1,0:T(8,128)S(1)} collective-permute-done((f32[2,64,256]{2,1,0:T(8,128)S(1)}, f32[2,64,256]{2,1,0:T(8,128)S(1)}, u32[]{:S(2)}, u32[]{:S(2)}) %collective-permute-start.16) | collective-permute-done | bytes 131104 | tf_op jit(solution)/shard_map/ppermute | solution.py:30
  45.5 0.4 shard_map.65
  46.0 1.2 %collective-permute-start.18 = (f32[48,128]{1,0:T(8,128)S(1)}, f32[48,128]{1,0:T(8,128)S(1)}, u32[]{:S(2)}, u32[]{:S(2)}) collective-permute-start(f32[48,128]{1,0:T(8,128)S(1)} %get-tuple-element.66), channel_id=1, source_target_pairs={{0,4},{4,0},{8,12},{12,8},{16,20},{20,16},{24,28},{28,24},{1,5},{5... | collective-permute-start | bytes 73736 | tf_op jit(solution)/shard_map/ppermute | solution.py:30
  47.2 0.6 collective-permute-start.17
  47.8 0.8 %collective-permute-done.17.refs_1_ = f32[40,128]{1,0:T(8,128)S(1)} collective-permute-done((f32[40,128]{1,0:T(8,128)S(1)}, f32[40,128]{1,0:T(8,128)S(1)}, u32[]{:S(2)}, u32[]{:S(2)}) %collective-permute-start.17) | collective-permute-done | bytes 20512 | tf_op jit(solution)/shard_map/ppermute | solution.py:30
  48.7 1.2 %collective-permute-done.18.refs_2_ = f32[48,128]{1,0:T(8,128)S(1)} collective-permute-done((f32[48,128]{1,0:T(8,128)S(1)}, f32[48,128]{1,0:T(8,128)S(1)}, u32[]{:S(2)}, u32[]{:S(2)}) %collective-permute-start.18) | collective-permute-done | bytes 24608 | tf_op jit(solution)/shard_map/ppermute | solution.py:30
  49.9 0.2 collective-permute-start.20
  50.1 1.0 %collective-permute-start.23 = (f32[56,128]{1,0:T(8,128)S(1)}, f32[56,128]{1,0:T(8,128)S(1)}, u32[]{:S(2)}, u32[]{:S(2)}) collective-permute-start(f32[56,128]{1,0:T(8,128)S(1)} %get-tuple-element.74), channel_id=1, source_target_pairs={{0,24},{4,28},{8,16},{12,20},{16,8},{20,12},{24,0},{28,4},{1,25},{... | collective-permute-start | bytes 86024 | tf_op jit(solution)/shard_map/ppermute | solution.py:30
  51.0 0.5 collective-permute-start.22
  51.6 2.9 %collective-permute-start.21 = (f32[40,128]{1,0:T(8,128)S(1)}, f32[40,128]{1,0:T(8,128)S(1)}, u32[]{:S(2)}, u32[]{:S(2)}) collective-permute-start(f32[40,128]{1,0:T(8,128)S(1)} %get-tuple-element.72.refs_0_), channel_id=1, source_target_pairs={{0,8},{4,12},{8,0},{12,4},{16,24},{20,28},{24,16},{28,20},{1,9},{5... | collective-permute-start | bytes 61448 | tf_op jit(solution)/shard_map/ppermute | solution.py:30
  54.5 2.0 %collective-permute-done.21.refs_1_ = f32[40,128]{1,0:T(8,128)S(1)} collective-permute-done((f32[40,128]{1,0:T(8,128)S(1)}, f32[40,128]{1,0:T(8,128)S(1)}, u32[]{:S(2)}, u32[]{:S(2)}) %collective-permute-start.21) | collective-permute-done | bytes 20512 | tf_op jit(solution)/shard_map/ppermute | solution.py:30
  56.5 4.2 %shard_map.67 = f32[64,1024]{1,0:T(8,128)} custom-call(f32[2,64,256]{2,1,0:T(8,128)S(1)} %get-tuple-element.71.here_ref, f32[2,64,256]{2,1,0:T(8,128)S(1)} %collective-permute-done.20.there_ref, f32[40,128]{1,0:T(8,128)S(1)} %get-tuple-element.72.refs_0_, f32[40,128]{1,0:T(8,128)S(1)} %collective-permute-done.21.refs_1_, ...), custom_call_target="tpu_custom_call" | custom-call | tf_op jit(solution)/shard_map/pallas_call | solution.py:365
  (21 shorter events, 0.3 us)
Async XLA Ops:
  1.1 18.4 %collective-permute-start.3 = (bf16[256,1024]{1,0:T(8,128)(2,1)S(1)}, bf16[256,1024]{1,0:T(8,128)(2,1)S(1)}, u32[]{:S(2)}, u32[]{:S(2)}) collective-permute-start(bf16[256,1024]{1,0:T(8,128)(2,1)S(1)} %constant_dynamic-slice_fusion), channel_id=1, source_target_pairs={{0,4},{4,8},{8,12},{12,16},{16,20},{20,24},{24,28},{28,0},{1,5},{5... | collective-permute-start | bytes 1572872 | tf_op jit(solution)/shard_map/ppermute | solution.py:25
  4.8 3.5 %collective-permute-start.2 = (s32[2,24]{1,0:T(2,128)S(1)}, s32[2,24]{1,0:T(2,128)S(1)}, u32[]{:S(2)}, u32[]{:S(2)}) collective-permute-start(s32[2,24]{1,0:T(2,128)S(1)} %pad_add_fusion.refs_0_), channel_id=1, source_target_pairs={{0,3},{1,2},{2,1},{3,0},{4,7},{5,6},{6,5},{7,4},{8,11},{9,10},{10,... | collective-permute-start | bytes 584 | tf_op jit(solution)/shard_map/ppermute | solution.py:30
  5.4 3.6 %collective-permute-start.1 = (s32[2,24]{1,0:T(2,128)S(1)}, s32[2,24]{1,0:T(2,128)S(1)}, u32[]{:S(2)}, u32[]{:S(2)}) collective-permute-start(s32[2,24]{1,0:T(2,128)S(1)} %pad_add_fusion.refs_0_), channel_id=1, source_target_pairs={{0,2},{1,3},{2,0},{3,1},{4,6},{5,7},{6,4},{7,5},{8,10},{9,11},{10,... | collective-permute-start | bytes 584 | tf_op jit(solution)/shard_map/ppermute | solution.py:30
  6.3 2.7 %collective-permute-start = (s32[2,24]{1,0:T(2,128)S(1)}, s32[2,24]{1,0:T(2,128)S(1)}, u32[]{:S(2)}, u32[]{:S(2)}) collective-permute-start(s32[2,24]{1,0:T(2,128)S(1)} %pad_add_fusion.refs_0_), channel_id=1, source_target_pairs={{0,1},{1,0},{2,3},{3,2},{4,5},{5,4},{6,7},{7,6},{8,9},{9,8},{10,11... | collective-permute-start | bytes 584 | tf_op jit(solution)/shard_map/ppermute | solution.py:30
  6.6 0.9 %copy-start.1 = (f32[64,1024]{1,0:T(8,128)S(1)}, f32[64,1024]{1,0:T(8,128)}, u32[]{:S(2)}) copy-start(f32[64,1024]{1,0:T(8,128)} %start_ref.1) | copy-start | bytes 786436
  7.6 0.7 %copy-start.2 = (bf16[1024]{0:T(1024)(128)(2,1)S(1)}, bf16[1024]{0:T(1024)(128)(2,1)}, u32[]{:S(2)}) copy-start(bf16[1024]{0:T(1024)(128)(2,1)} %param.7) | copy-start | bytes 6148
  9.1 11.2 %collective-permute-start.4 = (bf16[80,256]{1,0:T(8,128)(2,1)S(1)}, bf16[80,256]{1,0:T(8,128)(2,1)S(1)}, u32[]{:S(2)}, u32[]{:S(2)}) collective-permute-start(bf16[80,256]{1,0:T(8,128)(2,1)S(1)} %get-tuple-element.44), channel_id=1, source_target_pairs={{0,4},{4,8},{8,12},{12,16},{16,20},{20,24},{24,28},{28,0},{1,5},{5... | collective-permute-start | bytes 122888 | tf_op jit(solution)/shard_map/ppermute | solution.py:25
  10.7 1.6 %copy-start = (bf16[1024,1024]{1,0:T(8,128)(2,1)S(1)}, bf16[1024,1024]{1,0:T(8,128)(2,1)}, u32[]{:S(2)}) copy-start(bf16[1024,1024]{1,0:T(8,128)(2,1)} %cells_ref.1) | copy-start | bytes 6291460
  21.0 2.3 %collective-permute-start.5 = (f32[72,256]{1,0:T(8,128)S(1)}, f32[72,256]{1,0:T(8,128)S(1)}, u32[]{:S(2)}, u32[]{:S(2)}) collective-permute-start(f32[72,256]{1,0:T(8,128)S(1)} %get-tuple-element.48), channel_id=1, source_target_pairs={{0,1},{1,0},{2,3},{3,2},{4,5},{5,4},{6,7},{7,6},{8,9},{9,8},{10,11... | collective-permute-start | bytes 221192 | tf_op jit(solution)/shard_map/ppermute | solution.py:30
  21.1 2.3 %collective-permute-start.6 = (f32[72,256]{1,0:T(8,128)S(1)}, f32[72,256]{1,0:T(8,128)S(1)}, u32[]{:S(2)}, u32[]{:S(2)}) collective-permute-start(f32[72,256]{1,0:T(8,128)S(1)} %get-tuple-element.49), channel_id=1, source_target_pairs={{0,1},{1,0},{2,3},{3,2},{4,5},{5,4},{6,7},{7,6},{8,9},{9,8},{10,11... | collective-permute-start | bytes 221192 | tf_op jit(solution)/shard_map/ppermute | solution.py:30
  21.6 4.4 %collective-permute-start.8 = (f32[72,256]{1,0:T(8,128)S(1)}, f32[72,256]{1,0:T(8,128)S(1)}, u32[]{:S(2)}, u32[]{:S(2)}) collective-permute-start(f32[72,256]{1,0:T(8,128)S(1)} %get-tuple-element.52), channel_id=1, source_target_pairs={{0,28},{4,0},{8,4},{12,8},{16,12},{20,16},{24,20},{28,24},{1,29},{... | collective-permute-start | bytes 221192 | tf_op jit(solution)/shard_map/ppermute | solution.py:25
  23.4 4.4 %collective-permute-start.7 = (f32[72,256]{1,0:T(8,128)S(1)}, f32[72,256]{1,0:T(8,128)S(1)}, u32[]{:S(2)}, u32[]{:S(2)}) collective-permute-start(f32[72,256]{1,0:T(8,128)S(1)} %get-tuple-element.51), channel_id=1, source_target_pairs={{0,2},{1,3},{2,0},{3,1},{4,6},{5,7},{6,4},{7,5},{8,10},{9,11},{10,... | collective-permute-start | bytes 221192 | tf_op jit(solution)/shard_map/ppermute | solution.py:30
  27.8 4.4 %collective-permute-start.10 = (f32[72,256]{1,0:T(8,128)S(1)}, f32[72,256]{1,0:T(8,128)S(1)}, u32[]{:S(2)}, u32[]{:S(2)}) collective-permute-start(f32[72,256]{1,0:T(8,128)S(1)} %get-tuple-element.54.block_ref), channel_id=1, source_target_pairs={{0,2},{1,3},{2,0},{3,1},{4,6},{5,7},{6,4},{7,5},{8,10},{9,11},{10,... | collective-permute-start | bytes 221192 | tf_op jit(solution)/shard_map/ppermute | solution.py:30
  29.4 7.1 %collective-permute-start.12 = (f32[80,256]{1,0:T(8,128)S(1)}, f32[80,256]{1,0:T(8,128)S(1)}, u32[]{:S(2)}, u32[]{:S(2)}) collective-permute-start(f32[80,256]{1,0:T(8,128)S(1)} %get-tuple-element.59), channel_id=1, source_target_pairs={{0,4},{4,8},{8,12},{12,16},{16,20},{20,24},{24,28},{28,0},{1,5},{5... | collective-permute-start | bytes 245768 | tf_op jit(solution)/shard_map/ppermute | solution.py:25
  32.2 1.4 %collective-permute-start.11 = (f32[72,256]{1,0:T(8,128)S(1)}, f32[72,256]{1,0:T(8,128)S(1)}, u32[]{:S(2)}, u32[]{:S(2)}) collective-permute-start(f32[72,256]{1,0:T(8,128)S(1)} %collective-permute-done.10.refs_2_.across_ref), channel_id=1, source_target_pairs={{0,1},{1,0},{2,3},{3,2},{4,5},{5,4},{6,7},{7,6},{8,9},{9,8},{10,11... | collective-permute-start | bytes 221192 | tf_op jit(solution)/shard_map/ppermute | solution.py:30
  32.2 1.4 %collective-permute-start.9 = (f32[64,256]{1,0:T(8,128)S(1)}, f32[64,256]{1,0:T(8,128)S(1)}, u32[]{:S(2)}, u32[]{:S(2)}) collective-permute-start(f32[64,256]{1,0:T(8,128)S(1)} %get-tuple-element.53.refs_0_.lead_ref), channel_id=1, source_target_pairs={{0,1},{1,0},{2,3},{3,2},{4,5},{5,4},{6,7},{7,6},{8,9},{9,8},{10,11... | collective-permute-start | bytes 196616 | tf_op jit(solution)/shard_map/ppermute | solution.py:30
  34.1 6.4 %collective-permute-start.13 = (f32[72,256]{1,0:T(8,128)S(1)}, f32[72,256]{1,0:T(8,128)S(1)}, u32[]{:S(2)}, u32[]{:S(2)}) collective-permute-start(f32[72,256]{1,0:T(8,128)S(1)} %get-tuple-element.61), channel_id=1, source_target_pairs={{4,0},{8,4},{12,8},{16,12},{20,16},{24,20},{28,24},{5,1},{9,5},{13... | collective-permute-start | bytes 221192 | tf_op jit(solution)/shard_map/ppermute | solution.py:25
  36.8 1.3 %collective-permute-start.14 = (f32[64,256]{1,0:T(8,128)S(1)}, f32[64,256]{1,0:T(8,128)S(1)}, u32[]{:S(2)}, u32[]{:S(2)}) collective-permute-start(f32[64,256]{1,0:T(8,128)S(1)} %get-tuple-element.62), channel_id=1, source_target_pairs={{0,1},{1,0},{2,3},{3,2},{4,5},{5,4},{6,7},{7,6},{8,9},{9,8},{10,11... | collective-permute-start | bytes 196616 | tf_op jit(solution)/shard_map/ppermute | solution.py:30
  36.9 1.4 %collective-permute-start.15 = (f32[64,256]{1,0:T(8,128)S(1)}, f32[64,256]{1,0:T(8,128)S(1)}, u32[]{:S(2)}, u32[]{:S(2)}) collective-permute-start(f32[64,256]{1,0:T(8,128)S(1)} %get-tuple-element.63), channel_id=1, source_target_pairs={{0,1},{1,0},{2,3},{3,2},{4,5},{5,4},{6,7},{7,6},{8,9},{9,8},{10,11... | collective-permute-start | bytes 196616 | tf_op jit(solution)/shard_map/ppermute | solution.py:30
  40.5 5.0 %collective-permute-start.16 = (f32[2,64,256]{2,1,0:T(8,128)S(1)}, f32[2,64,256]{2,1,0:T(8,128)S(1)}, u32[]{:S(2)}, u32[]{:S(2)}) collective-permute-start(f32[2,64,256]{2,1,0:T(8,128)S(1)} %shard_map.64.own_ref), channel_id=1, source_target_pairs={{0,2},{1,3},{2,0},{3,1},{4,6},{5,7},{6,4},{7,5},{8,10},{9,11},{10,... | collective-permute-start | bytes 393224 | tf_op jit(solution)/shard_map/ppermute | solution.py:30
  45.9 4.0 %collective-permute-start.19 = (f32[56,128]{1,0:T(8,128)S(1)}, f32[56,128]{1,0:T(8,128)S(1)}, u32[]{:S(2)}, u32[]{:S(2)}) collective-permute-start(f32[56,128]{1,0:T(8,128)S(1)} %get-tuple-element.67), channel_id=1, source_target_pairs={{0,5},{1,4},{2,7},{3,6},{4,1},{5,0},{6,3},{7,2},{8,13},{9,12},{10,... | collective-permute-start | bytes 86024 | tf_op jit(solution)/shard_map/ppermute | solution.py:44
  46.0 3.9 %collective-permute-start.18 = (f32[48,128]{1,0:T(8,128)S(1)}, f32[48,128]{1,0:T(8,128)S(1)}, u32[]{:S(2)}, u32[]{:S(2)}) collective-permute-start(f32[48,128]{1,0:T(8,128)S(1)} %get-tuple-element.66), channel_id=1, source_target_pairs={{0,4},{4,0},{8,12},{12,8},{16,20},{20,16},{24,28},{28,24},{1,5},{5... | collective-permute-start | bytes 73736 | tf_op jit(solution)/shard_map/ppermute | solution.py:30
  47.2 1.4 %collective-permute-start.17 = (f32[40,128]{1,0:T(8,128)S(1)}, f32[40,128]{1,0:T(8,128)S(1)}, u32[]{:S(2)}, u32[]{:S(2)}) collective-permute-start(f32[40,128]{1,0:T(8,128)S(1)} %get-tuple-element.65.refs_0_), channel_id=1, source_target_pairs={{0,1},{1,0},{2,3},{3,2},{4,5},{5,4},{6,7},{7,6},{8,9},{9,8},{10,11... | collective-permute-start | bytes 61448 | tf_op jit(solution)/shard_map/ppermute | solution.py:30
  49.9 6.6 %collective-permute-start.20 = (f32[2,64,256]{2,1,0:T(8,128)S(1)}, f32[2,64,256]{2,1,0:T(8,128)S(1)}, u32[]{:S(2)}, u32[]{:S(2)}) collective-permute-start(f32[2,64,256]{2,1,0:T(8,128)S(1)} %get-tuple-element.71.here_ref), channel_id=1, source_target_pairs={{0,1},{1,0},{2,3},{3,2},{4,5},{5,4},{6,7},{7,6},{8,9},{9,8},{10,11... | collective-permute-start | bytes 393224 | tf_op jit(solution)/shard_map/ppermute | solution.py:30
  50.1 6.4 %collective-permute-start.23 = (f32[56,128]{1,0:T(8,128)S(1)}, f32[56,128]{1,0:T(8,128)S(1)}, u32[]{:S(2)}, u32[]{:S(2)}) collective-permute-start(f32[56,128]{1,0:T(8,128)S(1)} %get-tuple-element.74), channel_id=1, source_target_pairs={{0,24},{4,28},{8,16},{12,20},{16,8},{20,12},{24,0},{28,4},{1,25},{... | collective-permute-start | bytes 86024 | tf_op jit(solution)/shard_map/ppermute | solution.py:30
  51.0 5.4 %collective-permute-start.22 = (f32[48,128]{1,0:T(8,128)S(1)}, f32[48,128]{1,0:T(8,128)S(1)}, u32[]{:S(2)}, u32[]{:S(2)}) collective-permute-start(f32[48,128]{1,0:T(8,128)S(1)} %get-tuple-element.73), channel_id=1, source_target_pairs={{0,16},{4,20},{8,24},{12,28},{16,0},{20,4},{24,8},{28,12},{1,17},{... | collective-permute-start | bytes 73736 | tf_op jit(solution)/shard_map/ppermute | solution.py:30
  51.6 4.9 %collective-permute-start.21 = (f32[40,128]{1,0:T(8,128)S(1)}, f32[40,128]{1,0:T(8,128)S(1)}, u32[]{:S(2)}, u32[]{:S(2)}) collective-permute-start(f32[40,128]{1,0:T(8,128)S(1)} %get-tuple-element.72.refs_0_), channel_id=1, source_target_pairs={{0,8},{4,12},{8,0},{12,4},{16,24},{20,28},{24,16},{28,20},{1,9},{5... | collective-permute-start | bytes 61448 | tf_op jit(solution)/shard_map/ppermute | solution.py:30

commit v10 on v9

--- a/solution.py
+++ b/solution.py
@@ -458,7 +458,7 @@
     )
     came = [swap(part, "cols", 1) for part in core]
     (both,) = call(chip_kernel, [(keep.shape, f32)], keep, shift(back, -1, around=False), *came)
-    tall = [((size // 2 + 8 + 8 * k, 2 * size), f32) for k in range(3)]
+    tall = [((size // 2 + 8 + 8 * k, 2 * size), f32) for k in range(2)]
     here, *grams = call(
         functools.partial(resmooth_kernel, total),
         [((lanes // 2, size, BLOCK), f32), *tall],
@@ -473,12 +473,12 @@
     low = bits % 2
     parts = [grams[0], swap(grams[0], "cols", 1)]
     if low:
-        parts += [swap(grams[1], "rows", 1), both_swap(grams[2], 1, 1)]
+        parts += [swap(grams[0], "rows", 1), both_swap(grams[1], 1, 1)]
     while low < bits:
         grams = call(functools.partial(sum_kernel, len(parts)), tall, *parts)
         if low < 2:
             here, grams = lax.optimization_barrier((here, grams))
-        parts = [grams[0]] + [swap(grams[m - 1], "rows", m << low) for m in (1, 2, 3)]
+        parts = [grams[0]] + [swap(grams[m // 3], "rows", m << low) for m in (1, 2, 3)]
         low += 2
     (vector,) = call(
         functools.partial(solve_kernel, lanes),

time: 60.9 us -> 60.7 us (level)
  no operation moved by 1% of the time
where the time goes in v10:
time: 60.7 us; the launch traced here: 60.4 us
  waiting for transfers between devices  24.1 us (40%)
  starting transfers between devices  22.5 us (37%)
  Pallas kernels  8.75 us (14%)
  local copies, waits for them, and re-layouts  4.3 us (7%)
  other arithmetic  0.68 us (1%)
    ppermute x18, starting transfers between devices, swap(): return lax.ppermute(cells, axis, [(i, i ^ offset) for i in range(count)])  14.6 us
    ppermute x18, waiting for transfers between devices, swap(): return lax.ppermute(cells, axis, [(i, i ^ offset) for i in range(count)])  14.3 us
    ppermute x5, waiting for transfers between devices, shift(): return lax.ppermute(cells, 'rows', pairs)  9.77 us
    pallas_call x13, Pallas kernels, call(): pl.pallas_call(body, out_shape=[jax.ShapeDtypeStruct(shape, kind) for sha...  8.75 us
    ppermute x5, starting transfers between devices, shift(): return lax.ppermute(cells, 'rows', pairs)  7.92 us
    unnamed x6, local copies, waits for them, and re-layouts  3.22 us
  transfers between devices with their start and end apart: 24, of which 14 were waited for; matrix products, arithmetic and copies ran while one was open for 1% of the time, Pallas kernels for 6%

profile of v10, /device:TPU:0, one launch (start us, length us, event | category | flops | bytes accessed | tf_op | source)
XLA Modules:
  0.0 60.4 jit_solution(12200481727550658958)
XLA Ops:
  0.0 1.1 %constant_dynamic-slice_fusion = bf16[256,1024]{1,0:T(8,128)(2,1)S(1)} fusion(bf16[1024,1024]{1,0:T(8,128)(2,1)} %cells_ref.1, s32[]{:T(128)S(6)} %select_n.3), kind=kLoop, calls=%fused_computation.1 | loop fusion | bytes 1048580 | tf_op jit(solution)/shard_map/dynamic_slice | solution.py:384
  1.1 3.0 %collective-permute-start.3 = (bf16[256,1024]{1,0:T(8,128)(2,1)S(1)}, bf16[256,1024]{1,0:T(8,128)(2,1)S(1)}, u32[]{:S(2)}, u32[]{:S(2)}) collective-permute-start(bf16[256,1024]{1,0:T(8,128)(2,1)S(1)} %constant_dynamic-slice_fusion), channel_id=1, source_target_pairs={{0,4},{4,8},{8,12},{12,16},{16,20},{20,24},{24,28},{28,0},{1,5},{5... | collective-permute-start | bytes 1572872 | tf_op jit(solution)/shard_map/ppermute | solution.py:25
  4.1 0.7 %pad_add_fusion.refs_0_ = s32[2,24]{1,0:T(2,128)S(1)} fusion(s32[1,24]{1,0:T(1,128)} %bitcast.4, s32[1,24]{1,0:T(1,128)} %bitcast.5), kind=kLoop, calls=%fused_computation | loop fusion | flops 48 | bytes 384 | tf_op jit(solution)/shard_map/concatenate | solution.py:385
  4.8 0.7 %collective-permute-start.2 = (s32[2,24]{1,0:T(2,128)S(1)}, s32[2,24]{1,0:T(2,128)S(1)}, u32[]{:S(2)}, u32[]{:S(2)}) collective-permute-start(s32[2,24]{1,0:T(2,128)S(1)} %pad_add_fusion.refs_0_), channel_id=1, source_target_pairs={{0,3},{1,2},{2,1},{3,0},{4,7},{5,6},{6,5},{7,4},{8,11},{9,10},{10,... | collective-permute-start | bytes 584 | tf_op jit(solution)/shard_map/ppermute | solution.py:30
  5.4 0.9 %collective-permute-start.1 = (s32[2,24]{1,0:T(2,128)S(1)}, s32[2,24]{1,0:T(2,128)S(1)}, u32[]{:S(2)}, u32[]{:S(2)}) collective-permute-start(s32[2,24]{1,0:T(2,128)S(1)} %pad_add_fusion.refs_0_), channel_id=1, source_target_pairs={{0,2},{1,3},{2,0},{3,1},{4,6},{5,7},{6,4},{7,5},{8,10},{9,11},{10,... | collective-permute-start | bytes 584 | tf_op jit(solution)/shard_map/ppermute | solution.py:30
  6.3 0.3 collective-permute-start
  6.6 0.9 %copy-done.1 = f32[64,1024]{1,0:T(8,128)S(1)} copy-done((f32[64,1024]{1,0:T(8,128)S(1)}, f32[64,1024]{1,0:T(8,128)}, u32[]{:S(2)}) %copy-start.1) | copy-done | bytes 262168
  7.6 0.7 %copy-done.2 = bf16[1024]{0:T(1024)(128)(2,1)S(1)} copy-done((bf16[1024]{0:T(1024)(128)(2,1)S(1)}, bf16[1024]{0:T(1024)(128)(2,1)}, u32[]{:S(2)}) %copy-start.2) | copy-done | bytes 2072
  8.3 0.7 %collective-permute-done.1.refs_2_ = s32[2,24]{1,0:T(2,128)S(1)} collective-permute-done((s32[2,24]{1,0:T(2,128)S(1)}, s32[2,24]{1,0:T(2,128)S(1)}, u32[]{:S(2)}, u32[]{:S(2)}) %collective-permute-start.1) | collective-permute-done | bytes 224 | tf_op jit(solution)/shard_map/ppermute | solution.py:30
  9.0 0.1 shard_map.56
  9.1 1.6 %collective-permute-start.4 = (bf16[80,256]{1,0:T(8,128)(2,1)S(1)}, bf16[80,256]{1,0:T(8,128)(2,1)S(1)}, u32[]{:S(2)}, u32[]{:S(2)}) collective-permute-start(bf16[80,256]{1,0:T(8,128)(2,1)S(1)} %get-tuple-element.41), channel_id=1, source_target_pairs={{0,4},{4,8},{8,12},{12,16},{16,20},{20,24},{24,28},{28,0},{1,5},{5... | collective-permute-start | bytes 122888 | tf_op jit(solution)/shard_map/ppermute | solution.py:25
  10.7 1.6 %copy-done = bf16[1024,1024]{1,0:T(8,128)(2,1)S(1)} copy-done((bf16[1024,1024]{1,0:T(8,128)(2,1)S(1)}, bf16[1024,1024]{1,0:T(8,128)(2,1)}, u32[]{:S(2)}) %copy-start) | copy-done | bytes 2097176
  12.3 1.8 %shard_map.57 = (bf16[4,256,1024]{2,1,0:T(8,128)(2,1)S(1)}, bf16[4,256,256]{2,1,0:T(8,128)(2,1)S(1)}, f32[4,72,256]{2,1,0:T(8,128)S(1)}) custom-call(bf16[1024,1024]{1,0:T(8,128)(2,1)S(1)} %copy-done, f32[1,1024]{1,0:T(1,128)S(1)} %get-tuple-element.37.mean_ref.refs_2_, bf16[4,80,256]{2,1,0:T(8,128)(2,1)S(1)} %get-tuple-element.38.left_ref.refs_3_), custom_call_target="tpu_custom_call" | custom-call | tf_op jit(solution)/shard_map/pallas_call | solution.py:365
  14.1 5.4 %collective-permute-done.3.cells_ref = bf16[256,1024]{1,0:T(8,128)(2,1)S(1)} collective-permute-done((bf16[256,1024]{1,0:T(8,128)(2,1)S(1)}, bf16[256,1024]{1,0:T(8,128)(2,1)S(1)}, u32[]{:S(2)}, u32[]{:S(2)}) %collective-permute-start.3) | collective-permute-done | bytes 524320 | tf_op jit(solution)/shard_map/ppermute | solution.py:25
  19.5 0.8 %shard_map.58.refs_0_ = f32[4,256,256]{2,1,0:T(8,128)S(1)} custom-call(bf16[4,256,1024]{2,1,0:T(8,128)(2,1)S(1)} %get-tuple-element.40.unit_ref, bf16[256,1024]{1,0:T(8,128)(2,1)S(1)} %collective-permute-done.3.cells_ref), custom_call_target="tpu_custom_call" | custom-call | tf_op jit(solution)/shard_map/pallas_call | solution.py:365
  20.3 0.7 %shard_map.59 = (bf16[4,256,256]{2,1,0:T(8,128)(2,1)S(1)}, f32[2,72,256]{2,1,0:T(8,128)S(1)}, f32[72,256]{1,0:T(8,128)S(1)}, f32[72,256]{1,0:T(8,128)S(1)}, f32[72,256]{1,0:T(8,128)S(1)}) custom-call(f32[4,256,256]{2,1,0:T(8,128)S(1)} %shard_map.58.refs_0_, bf16[80,256]{1,0:T(8,128)(2,1)S(1)} %collective-permute-done.4.refs_1_.side_ref, ...), custom_call_target="tpu_custom_call" | custom-call | tf_op jit(solution)/shard_map/pallas_call | solution.py:365
  21.1 0.5 collective-permute-start.6
  21.6 1.7 %collective-permute-start.8 = (f32[72,256]{1,0:T(8,128)S(1)}, f32[72,256]{1,0:T(8,128)S(1)}, u32[]{:S(2)}, u32[]{:S(2)}) collective-permute-start(f32[72,256]{1,0:T(8,128)S(1)} %get-tuple-element.49), channel_id=1, source_target_pairs={{0,28},{4,0},{8,4},{12,8},{16,12},{20,16},{24,20},{28,24},{1,29},{... | collective-permute-start | bytes 221192 | tf_op jit(solution)/shard_map/ppermute | solution.py:25
  23.4 1.5 %collective-permute-start.7 = (f32[72,256]{1,0:T(8,128)S(1)}, f32[72,256]{1,0:T(8,128)S(1)}, u32[]{:S(2)}, u32[]{:S(2)}) collective-permute-start(f32[72,256]{1,0:T(8,128)S(1)} %get-tuple-element.48), channel_id=1, source_target_pairs={{0,2},{1,3},{2,0},{3,1},{4,6},{5,7},{6,4},{7,5},{8,10},{9,11},{10,... | collective-permute-start | bytes 221192 | tf_op jit(solution)/shard_map/ppermute | solution.py:30
  24.9 1.0 %collective-permute-done.8.refs_2_ = f32[72,256]{1,0:T(8,128)S(1)} collective-permute-done((f32[72,256]{1,0:T(8,128)S(1)}, f32[72,256]{1,0:T(8,128)S(1)}, u32[]{:S(2)}, u32[]{:S(2)}) %collective-permute-start.8) | collective-permute-done | bytes 73760 | tf_op jit(solution)/shard_map/ppermute | solution.py:25
  25.9 1.8 %collective-permute-done.7.refs_1_ = f32[72,256]{1,0:T(8,128)S(1)} collective-permute-done((f32[72,256]{1,0:T(8,128)S(1)}, f32[72,256]{1,0:T(8,128)S(1)}, u32[]{:S(2)}, u32[]{:S(2)}) %collective-permute-start.7) | collective-permute-done | bytes 73760 | tf_op jit(solution)/shard_map/ppermute | solution.py:30
  27.8 1.5 %collective-permute-start.10 = (f32[72,256]{1,0:T(8,128)S(1)}, f32[72,256]{1,0:T(8,128)S(1)}, u32[]{:S(2)}, u32[]{:S(2)}) collective-permute-start(f32[72,256]{1,0:T(8,128)S(1)} %get-tuple-element.51.block_ref), channel_id=1, source_target_pairs={{0,2},{1,3},{2,0},{3,1},{4,6},{5,7},{6,4},{7,5},{8,10},{9,11},{10,... | collective-permute-start | bytes 221192 | tf_op jit(solution)/shard_map/ppermute | solution.py:30
  29.4 0.3 collective-permute-start.12
  29.7 2.6 %collective-permute-done.10.refs_2_.across_ref = f32[72,256]{1,0:T(8,128)S(1)} collective-permute-done((f32[72,256]{1,0:T(8,128)S(1)}, f32[72,256]{1,0:T(8,128)S(1)}, u32[]{:S(2)}, u32[]{:S(2)}) %collective-permute-start.10) | collective-permute-done | bytes 73760 | tf_op jit(solution)/shard_map/ppermute | solution.py:30
  32.2 0.5 collective-permute-start.9
  32.8 0.9 %collective-permute-done.9.refs_1_ = f32[64,256]{1,0:T(8,128)S(1)} collective-permute-done((f32[64,256]{1,0:T(8,128)S(1)}, f32[64,256]{1,0:T(8,128)S(1)}, u32[]{:S(2)}, u32[]{:S(2)}) %collective-permute-start.9) | collective-permute-done | bytes 65568 | tf_op jit(solution)/shard_map/ppermute | solution.py:30
  33.7 0.4 shard_map.62
  34.1 1.3 %collective-permute-start.13 = (f32[72,256]{1,0:T(8,128)S(1)}, f32[72,256]{1,0:T(8,128)S(1)}, u32[]{:S(2)}, u32[]{:S(2)}) collective-permute-start(f32[72,256]{1,0:T(8,128)S(1)} %get-tuple-element.58), channel_id=1, source_target_pairs={{4,0},{8,4},{12,8},{16,12},{20,16},{24,20},{28,24},{5,1},{9,5},{13... | collective-permute-start | bytes 221192 | tf_op jit(solution)/shard_map/ppermute | solution.py:25
  35.4 1.1 %collective-permute-done.12.next_ref = f32[80,256]{1,0:T(8,128)S(1)} collective-permute-done((f32[80,256]{1,0:T(8,128)S(1)}, f32[80,256]{1,0:T(8,128)S(1)}, u32[]{:S(2)}, u32[]{:S(2)}) %collective-permute-start.12) | collective-permute-done | bytes 81952 | tf_op jit(solution)/shard_map/ppermute | solution.py:25
  36.5 0.3 shard_map.63
  36.8 0.1 collective-permute-start.14
  36.9 0.5 collective-permute-start.15
  37.4 0.7 %collective-permute-done.14.refs_0_ = f32[64,256]{1,0:T(8,128)S(1)} collective-permute-done((f32[64,256]{1,0:T(8,128)S(1)}, f32[64,256]{1,0:T(8,128)S(1)}, u32[]{:S(2)}, u32[]{:S(2)}) %collective-permute-start.14) | collective-permute-done | bytes 65568 | tf_op jit(solution)/shard_map/ppermute | solution.py:30
  38.1 0.2 collective-permute-done.15.refs_1_
  38.3 2.2 %collective-permute-done.13.back_ref = f32[72,256]{1,0:T(8,128)S(1)} collective-permute-done((f32[72,256]{1,0:T(8,128)S(1)}, f32[72,256]{1,0:T(8,128)S(1)}, u32[]{:S(2)}, u32[]{:S(2)}) %collective-permute-start.13) | collective-permute-done | bytes 73760 | tf_op jit(solution)/shard_map/ppermute | solution.py:25
  40.5 1.5 %collective-permute-start.16 = (f32[2,64,256]{2,1,0:T(8,128)S(1)}, f32[2,64,256]{2,1,0:T(8,128)S(1)}, u32[]{:S(2)}, u32[]{:S(2)}) collective-permute-start(f32[2,64,256]{2,1,0:T(8,128)S(1)} %shard_map.64.own_ref), channel_id=1, source_target_pairs={{0,2},{1,3},{2,0},{3,1},{4,6},{5,7},{6,4},{7,5},{8,10},{9,11},{10,... | collective-permute-start | bytes 393224 | tf_op jit(solution)/shard_map/ppermute | solution.py:30
  42.1 3.5 %collective-permute-done.16.came_ref = f32[2,64,256]{2,1,0:T(8,128)S(1)} collective-permute-done((f32[2,64,256]{2,1,0:T(8,128)S(1)}, f32[2,64,256]{2,1,0:T(8,128)S(1)}, u32[]{:S(2)}, u32[]{:S(2)}) %collective-permute-start.16) | collective-permute-done | bytes 131104 | tf_op jit(solution)/shard_map/ppermute | solution.py:30
  45.5 0.4 shard_map.65
  45.9 1.2 %collective-permute-start.18 = (f32[40,128]{1,0:T(8,128)S(1)}, f32[40,128]{1,0:T(8,128)S(1)}, u32[]{:S(2)}, u32[]{:S(2)}) collective-permute-start(f32[40,128]{1,0:T(8,128)S(1)} %get-tuple-element.62.refs_0_), channel_id=1, source_target_pairs={{0,4},{4,0},{8,12},{12,8},{16,20},{20,16},{24,28},{28,24},{1,5},{5... | collective-permute-start | bytes 61448 | tf_op jit(solution)/shard_map/ppermute | solution.py:30
  47.2 0.6 %collective-permute-start.17 = (f32[40,128]{1,0:T(8,128)S(1)}, f32[40,128]{1,0:T(8,128)S(1)}, u32[]{:S(2)}, u32[]{:S(2)}) collective-permute-start(f32[40,128]{1,0:T(8,128)S(1)} %get-tuple-element.62.refs_0_), channel_id=1, source_target_pairs={{0,1},{1,0},{2,3},{3,2},{4,5},{5,4},{6,7},{7,6},{8,9},{9,8},{10,11... | collective-permute-start | bytes 61448 | tf_op jit(solution)/shard_map/ppermute | solution.py:30
  47.8 2.0 %collective-permute-done.18.refs_2_ = f32[40,128]{1,0:T(8,128)S(1)} collective-permute-done((f32[40,128]{1,0:T(8,128)S(1)}, f32[40,128]{1,0:T(8,128)S(1)}, u32[]{:S(2)}, u32[]{:S(2)}) %collective-permute-start.18) | collective-permute-done | bytes 20512 | tf_op jit(solution)/shard_map/ppermute | solution.py:30
  49.8 0.2 collective-permute-start.20
  50.0 1.0 %collective-permute-start.23 = (f32[48,128]{1,0:T(8,128)S(1)}, f32[48,128]{1,0:T(8,128)S(1)}, u32[]{:S(2)}, u32[]{:S(2)}) collective-permute-start(f32[48,128]{1,0:T(8,128)S(1)} %get-tuple-element.68), channel_id=1, source_target_pairs={{0,24},{4,28},{8,16},{12,20},{16,8},{20,12},{24,0},{28,4},{1,25},{... | collective-permute-start | bytes 73736 | tf_op jit(solution)/shard_map/ppermute | solution.py:30
  51.0 0.5 collective-permute-start.22
  51.5 2.9 %collective-permute-start.21 = (f32[40,128]{1,0:T(8,128)S(1)}, f32[40,128]{1,0:T(8,128)S(1)}, u32[]{:S(2)}, u32[]{:S(2)}) collective-permute-start(f32[40,128]{1,0:T(8,128)S(1)} %get-tuple-element.67.refs_0_), channel_id=1, source_target_pairs={{0,8},{4,12},{8,0},{12,4},{16,24},{20,28},{24,16},{28,20},{1,9},{5... | collective-permute-start | bytes 61448 | tf_op jit(solution)/shard_map/ppermute | solution.py:30
  54.4 1.7 %collective-permute-done.22.refs_2_ = f32[40,128]{1,0:T(8,128)S(1)} collective-permute-done((f32[40,128]{1,0:T(8,128)S(1)}, f32[40,128]{1,0:T(8,128)S(1)}, u32[]{:S(2)}, u32[]{:S(2)}) %collective-permute-start.22) | collective-permute-done | bytes 20512 | tf_op jit(solution)/shard_map/ppermute | solution.py:30
  56.1 0.2 collective-permute-done.21.refs_1_
  56.3 4.2 %shard_map.67 = f32[64,1024]{1,0:T(8,128)} custom-call(f32[2,64,256]{2,1,0:T(8,128)S(1)} %get-tuple-element.66.here_ref, f32[2,64,256]{2,1,0:T(8,128)S(1)} %collective-permute-done.20.there_ref, f32[40,128]{1,0:T(8,128)S(1)} %get-tuple-element.67.refs_0_, f32[40,128]{1,0:T(8,128)S(1)} %collective-permute-done.21.refs_1_, ...), custom_call_target="tpu_custom_call" | custom-call | tf_op jit(solution)/shard_map/pallas_call | solution.py:365
  (21 shorter events, 0.2 us)
Async XLA Ops:
  1.1 18.4 %collective-permute-start.3 = (bf16[256,1024]{1,0:T(8,128)(2,1)S(1)}, bf16[256,1024]{1,0:T(8,128)(2,1)S(1)}, u32[]{:S(2)}, u32[]{:S(2)}) collective-permute-start(bf16[256,1024]{1,0:T(8,128)(2,1)S(1)} %constant_dynamic-slice_fusion), channel_id=1, source_target_pairs={{0,4},{4,8},{8,12},{12,16},{16,20},{20,24},{24,28},{28,0},{1,5},{5... | collective-permute-start | bytes 1572872 | tf_op jit(solution)/shard_map/ppermute | solution.py:25
  4.8 3.5 %collective-permute-start.2 = (s32[2,24]{1,0:T(2,128)S(1)}, s32[2,24]{1,0:T(2,128)S(1)}, u32[]{:S(2)}, u32[]{:S(2)}) collective-permute-start(s32[2,24]{1,0:T(2,128)S(1)} %pad_add_fusion.refs_0_), channel_id=1, source_target_pairs={{0,3},{1,2},{2,1},{3,0},{4,7},{5,6},{6,5},{7,4},{8,11},{9,10},{10,... | collective-permute-start | bytes 584 | tf_op jit(solution)/shard_map/ppermute | solution.py:30
  5.4 3.6 %collective-permute-start.1 = (s32[2,24]{1,0:T(2,128)S(1)}, s32[2,24]{1,0:T(2,128)S(1)}, u32[]{:S(2)}, u32[]{:S(2)}) collective-permute-start(s32[2,24]{1,0:T(2,128)S(1)} %pad_add_fusion.refs_0_), channel_id=1, source_target_pairs={{0,2},{1,3},{2,0},{3,1},{4,6},{5,7},{6,4},{7,5},{8,10},{9,11},{10,... | collective-permute-start | bytes 584 | tf_op jit(solution)/shard_map/ppermute | solution.py:30
  6.3 2.7 %collective-permute-start = (s32[2,24]{1,0:T(2,128)S(1)}, s32[2,24]{1,0:T(2,128)S(1)}, u32[]{:S(2)}, u32[]{:S(2)}) collective-permute-start(s32[2,24]{1,0:T(2,128)S(1)} %pad_add_fusion.refs_0_), channel_id=1, source_target_pairs={{0,1},{1,0},{2,3},{3,2},{4,5},{5,4},{6,7},{7,6},{8,9},{9,8},{10,11... | collective-permute-start | bytes 584 | tf_op jit(solution)/shard_map/ppermute | solution.py:30
  6.6 0.9 %copy-start.1 = (f32[64,1024]{1,0:T(8,128)S(1)}, f32[64,1024]{1,0:T(8,128)}, u32[]{:S(2)}) copy-start(f32[64,1024]{1,0:T(8,128)} %start_ref.1) | copy-start | bytes 786436
  7.6 0.7 %copy-start.2 = (bf16[1024]{0:T(1024)(128)(2,1)S(1)}, bf16[1024]{0:T(1024)(128)(2,1)}, u32[]{:S(2)}) copy-start(bf16[1024]{0:T(1024)(128)(2,1)} %param.7) | copy-start | bytes 6148
  9.1 11.2 %collective-permute-start.4 = (bf16[80,256]{1,0:T(8,128)(2,1)S(1)}, bf16[80,256]{1,0:T(8,128)(2,1)S(1)}, u32[]{:S(2)}, u32[]{:S(2)}) collective-permute-start(bf16[80,256]{1,0:T(8,128)(2,1)S(1)} %get-tuple-element.41), channel_id=1, source_target_pairs={{0,4},{4,8},{8,12},{12,16},{16,20},{20,24},{24,28},{28,0},{1,5},{5... | collective-permute-start | bytes 122888 | tf_op jit(solution)/shard_map/ppermute | solution.py:25
  10.7 1.6 %copy-start = (bf16[1024,1024]{1,0:T(8,128)(2,1)S(1)}, bf16[1024,1024]{1,0:T(8,128)(2,1)}, u32[]{:S(2)}) copy-start(bf16[1024,1024]{1,0:T(8,128)(2,1)} %cells_ref.1) | copy-start | bytes 6291460
  21.0 2.3 %collective-permute-start.5 = (f32[72,256]{1,0:T(8,128)S(1)}, f32[72,256]{1,0:T(8,128)S(1)}, u32[]{:S(2)}, u32[]{:S(2)}) collective-permute-start(f32[72,256]{1,0:T(8,128)S(1)} %get-tuple-element.45), channel_id=1, source_target_pairs={{0,1},{1,0},{2,3},{3,2},{4,5},{5,4},{6,7},{7,6},{8,9},{9,8},{10,11... | collective-permute-start | bytes 221192 | tf_op jit(solution)/shard_map/ppermute | solution.py:30
  21.1 2.3 %collective-permute-start.6 = (f32[72,256]{1,0:T(8,128)S(1)}, f32[72,256]{1,0:T(8,128)S(1)}, u32[]{:S(2)}, u32[]{:S(2)}) collective-permute-start(f32[72,256]{1,0:T(8,128)S(1)} %get-tuple-element.46), channel_id=1, source_target_pairs={{0,1},{1,0},{2,3},{3,2},{4,5},{5,4},{6,7},{7,6},{8,9},{9,8},{10,11... | collective-permute-start | bytes 221192 | tf_op jit(solution)/shard_map/ppermute | solution.py:30
  21.6 4.4 %collective-permute-start.8 = (f32[72,256]{1,0:T(8,128)S(1)}, f32[72,256]{1,0:T(8,128)S(1)}, u32[]{:S(2)}, u32[]{:S(2)}) collective-permute-start(f32[72,256]{1,0:T(8,128)S(1)} %get-tuple-element.49), channel_id=1, source_target_pairs={{0,28},{4,0},{8,4},{12,8},{16,12},{20,16},{24,20},{28,24},{1,29},{... | collective-permute-start | bytes 221192 | tf_op jit(solution)/shard_map/ppermute | solution.py:25
  23.4 4.4 %collective-permute-start.7 = (f32[72,256]{1,0:T(8,128)S(1)}, f32[72,256]{1,0:T(8,128)S(1)}, u32[]{:S(2)}, u32[]{:S(2)}) collective-permute-start(f32[72,256]{1,0:T(8,128)S(1)} %get-tuple-element.48), channel_id=1, source_target_pairs={{0,2},{1,3},{2,0},{3,1},{4,6},{5,7},{6,4},{7,5},{8,10},{9,11},{10,... | collective-permute-start | bytes 221192 | tf_op jit(solution)/shard_map/ppermute | solution.py:30
  27.8 4.4 %collective-permute-start.10 = (f32[72,256]{1,0:T(8,128)S(1)}, f32[72,256]{1,0:T(8,128)S(1)}, u32[]{:S(2)}, u32[]{:S(2)}) collective-permute-start(f32[72,256]{1,0:T(8,128)S(1)} %get-tuple-element.51.block_ref), channel_id=1, source_target_pairs={{0,2},{1,3},{2,0},{3,1},{4,6},{5,7},{6,4},{7,5},{8,10},{9,11},{10,... | collective-permute-start | bytes 221192 | tf_op jit(solution)/shard_map/ppermute | solution.py:30
  29.4 7.1 %collective-permute-start.12 = (f32[80,256]{1,0:T(8,128)S(1)}, f32[80,256]{1,0:T(8,128)S(1)}, u32[]{:S(2)}, u32[]{:S(2)}) collective-permute-start(f32[80,256]{1,0:T(8,128)S(1)} %get-tuple-element.56), channel_id=1, source_target_pairs={{0,4},{4,8},{8,12},{12,16},{16,20},{20,24},{24,28},{28,0},{1,5},{5... | collective-permute-start | bytes 245768 | tf_op jit(solution)/shard_map/ppermute | solution.py:25
  32.2 1.4 %collective-permute-start.11 = (f32[72,256]{1,0:T(8,128)S(1)}, f32[72,256]{1,0:T(8,128)S(1)}, u32[]{:S(2)}, u32[]{:S(2)}) collective-permute-start(f32[72,256]{1,0:T(8,128)S(1)} %collective-permute-done.10.refs_2_.across_ref), channel_id=1, source_target_pairs={{0,1},{1,0},{2,3},{3,2},{4,5},{5,4},{6,7},{7,6},{8,9},{9,8},{10,11... | collective-permute-start | bytes 221192 | tf_op jit(solution)/shard_map/ppermute | solution.py:30
  32.2 1.4 %collective-permute-start.9 = (f32[64,256]{1,0:T(8,128)S(1)}, f32[64,256]{1,0:T(8,128)S(1)}, u32[]{:S(2)}, u32[]{:S(2)}) collective-permute-start(f32[64,256]{1,0:T(8,128)S(1)} %get-tuple-element.50.refs_0_.lead_ref), channel_id=1, source_target_pairs={{0,1},{1,0},{2,3},{3,2},{4,5},{5,4},{6,7},{7,6},{8,9},{9,8},{10,11... | collective-permute-start | bytes 196616 | tf_op jit(solution)/shard_map/ppermute | solution.py:30
  34.1 6.4 %collective-permute-start.13 = (f32[72,256]{1,0:T(8,128)S(1)}, f32[72,256]{1,0:T(8,128)S(1)}, u32[]{:S(2)}, u32[]{:S(2)}) collective-permute-start(f32[72,256]{1,0:T(8,128)S(1)} %get-tuple-element.58), channel_id=1, source_target_pairs={{4,0},{8,4},{12,8},{16,12},{20,16},{24,20},{28,24},{5,1},{9,5},{13... | collective-permute-start | bytes 221192 | tf_op jit(solution)/shard_map/ppermute | solution.py:25
  36.8 1.3 %collective-permute-start.14 = (f32[64,256]{1,0:T(8,128)S(1)}, f32[64,256]{1,0:T(8,128)S(1)}, u32[]{:S(2)}, u32[]{:S(2)}) collective-permute-start(f32[64,256]{1,0:T(8,128)S(1)} %get-tuple-element.59), channel_id=1, source_target_pairs={{0,1},{1,0},{2,3},{3,2},{4,5},{5,4},{6,7},{7,6},{8,9},{9,8},{10,11... | collective-permute-start | bytes 196616 | tf_op jit(solution)/shard_map/ppermute | solution.py:30
  36.9 1.4 %collective-permute-start.15 = (f32[64,256]{1,0:T(8,128)S(1)}, f32[64,256]{1,0:T(8,128)S(1)}, u32[]{:S(2)}, u32[]{:S(2)}) collective-permute-start(f32[64,256]{1,0:T(8,128)S(1)} %get-tuple-element.60), channel_id=1, source_target_pairs={{0,1},{1,0},{2,3},{3,2},{4,5},{5,4},{6,7},{7,6},{8,9},{9,8},{10,11... | collective-permute-start | bytes 196616 | tf_op jit(solution)/shard_map/ppermute | solution.py:30
  40.5 5.0 %collective-permute-start.16 = (f32[2,64,256]{2,1,0:T(8,128)S(1)}, f32[2,64,256]{2,1,0:T(8,128)S(1)}, u32[]{:S(2)}, u32[]{:S(2)}) collective-permute-start(f32[2,64,256]{2,1,0:T(8,128)S(1)} %shard_map.64.own_ref), channel_id=1, source_target_pairs={{0,2},{1,3},{2,0},{3,1},{4,6},{5,7},{6,4},{7,5},{8,10},{9,11},{10,... | collective-permute-start | bytes 393224 | tf_op jit(solution)/shard_map/ppermute | solution.py:30
  45.9 3.9 %collective-permute-start.19 = (f32[48,128]{1,0:T(8,128)S(1)}, f32[48,128]{1,0:T(8,128)S(1)}, u32[]{:S(2)}, u32[]{:S(2)}) collective-permute-start(f32[48,128]{1,0:T(8,128)S(1)} %get-tuple-element.63), channel_id=1, source_target_pairs={{0,5},{1,4},{2,7},{3,6},{4,1},{5,0},{6,3},{7,2},{8,13},{9,12},{10,... | collective-permute-start | bytes 73736 | tf_op jit(solution)/shard_map/ppermute | solution.py:44
  45.9 3.8 %collective-permute-start.18 = (f32[40,128]{1,0:T(8,128)S(1)}, f32[40,128]{1,0:T(8,128)S(1)}, u32[]{:S(2)}, u32[]{:S(2)}) collective-permute-start(f32[40,128]{1,0:T(8,128)S(1)} %get-tuple-element.62.refs_0_), channel_id=1, source_target_pairs={{0,4},{4,0},{8,12},{12,8},{16,20},{20,16},{24,28},{28,24},{1,5},{5... | collective-permute-start | bytes 61448 | tf_op jit(solution)/shard_map/ppermute | solution.py:30
  47.2 2.6 %collective-permute-start.17 = (f32[40,128]{1,0:T(8,128)S(1)}, f32[40,128]{1,0:T(8,128)S(1)}, u32[]{:S(2)}, u32[]{:S(2)}) collective-permute-start(f32[40,128]{1,0:T(8,128)S(1)} %get-tuple-element.62.refs_0_), channel_id=1, source_target_pairs={{0,1},{1,0},{2,3},{3,2},{4,5},{5,4},{6,7},{7,6},{8,9},{9,8},{10,11... | collective-permute-start | bytes 61448 | tf_op jit(solution)/shard_map/ppermute | solution.py:30
  49.8 6.5 %collective-permute-start.20 = (f32[2,64,256]{2,1,0:T(8,128)S(1)}, f32[2,64,256]{2,1,0:T(8,128)S(1)}, u32[]{:S(2)}, u32[]{:S(2)}) collective-permute-start(f32[2,64,256]{2,1,0:T(8,128)S(1)} %get-tuple-element.66.here_ref), channel_id=1, source_target_pairs={{0,1},{1,0},{2,3},{3,2},{4,5},{5,4},{6,7},{7,6},{8,9},{9,8},{10,11... | collective-permute-start | bytes 393224 | tf_op jit(solution)/shard_map/ppermute | solution.py:30
  50.0 6.3 %collective-permute-start.23 = (f32[48,128]{1,0:T(8,128)S(1)}, f32[48,128]{1,0:T(8,128)S(1)}, u32[]{:S(2)}, u32[]{:S(2)}) collective-permute-start(f32[48,128]{1,0:T(8,128)S(1)} %get-tuple-element.68), channel_id=1, source_target_pairs={{0,24},{4,28},{8,16},{12,20},{16,8},{20,12},{24,0},{28,4},{1,25},{... | collective-permute-start | bytes 73736 | tf_op jit(solution)/shard_map/ppermute | solution.py:30
  51.0 5.1 %collective-permute-start.22 = (f32[40,128]{1,0:T(8,128)S(1)}, f32[40,128]{1,0:T(8,128)S(1)}, u32[]{:S(2)}, u32[]{:S(2)}) collective-permute-start(f32[40,128]{1,0:T(8,128)S(1)} %get-tuple-element.67.refs_0_), channel_id=1, source_target_pairs={{0,16},{4,20},{8,24},{12,28},{16,0},{20,4},{24,8},{28,12},{1,17},{... | collective-permute-start | bytes 61448 | tf_op jit(solution)/shard_map/ppermute | solution.py:30
  51.5 4.8 %collective-permute-start.21 = (f32[40,128]{1,0:T(8,128)S(1)}, f32[40,128]{1,0:T(8,128)S(1)}, u32[]{:S(2)}, u32[]{:S(2)}) collective-permute-start(f32[40,128]{1,0:T(8,128)S(1)} %get-tuple-element.67.refs_0_), channel_id=1, source_target_pairs={{0,8},{4,12},{8,0},{12,4},{16,24},{20,28},{24,16},{28,20},{1,9},{5... | collective-permute-start | bytes 61448 | tf_op jit(solution)/shard_map/ppermute | solution.py:30
